TPU v7x, 32 devices: a whole 2x2x4 slice. The times are simulated.
32 devices in a mesh: pair: 4 (over y, core), aux: 8 (over z, x).
Axes of the slice: x: 2, y: 2, z: 4, core: 2. Of those that a mesh axis runs over, the one named last changes fastest.
Arguments:
- three_index: float32 [8, 768, 8192], P('pair', None, 'aux'), may hold values from -0.6 to 0.6
- occupied_energy: float32 [8], P('pair'), may hold values from -2 to -0.5
- virtual_energy: float32 [768], replicated, may hold values from 0.2 to 3
- plan: int32 [2, 8], P(None, 'pair'), may hold values from 0 to 1, as said below
Outputs:
- gradient_blocks: float32 [8, 768, 8192], P('pair', None, 'aux')
- virtual_density: float32 [768, 768], P('aux', 'pair')
Inputs may be any that keep to these rules, and one draw needn't show every extreme that they name: For block p and round r with q = p XOR 2**r: the row plan[r, p * 2 : (p + 1) * 2] is a permutation of the slots, and plan[r, q * 2 + plan[r, p * 2 + k]] = k, so every orbital is paired with exactly one orbital of block q in each round.
All inputs are finite; a program needn't handle non-finite values.
Results may differ from a plain program's by a relative error of at most 0.0001.
Values sent between devices are 32-bit elements; how exact they have to be, the bound alone decides.
No kernel may reach another device: no remote copies, remote signals or barrier semaphores. Data moves between devices by JAX's collectives and lax.ppermute only.
A program may use at most 128 MiB of HBM per device.

v0:
```python
import jax
import jax.numpy as jnp
from jax import lax
from jax.sharding import PartitionSpec as P


def swapped(block, axis, bit):
    count = lax.axis_size(axis)
    route = []
    for low in range(count):
        high = low | 1 << bit
        if high != low and high < count:
            route += [(low, high), (high, low)]
    return lax.ppermute(block, axis, route)


def side_of(axis, bit):
    return lax.axis_index(axis) // 2**bit % 2


def fold(block, bit, dim):
    side = side_of("aux", bit)
    half = block.shape[dim] // 2
    keep = lax.dynamic_slice_in_dim(block, side * half, half, dim)
    give = lax.dynamic_slice_in_dim(block, (1 - side) * half, half, dim)
    return keep + swapped(give, "aux", bit)


def unfold(block, bit, dim):
    side = side_of("aux", bit)
    other = swapped(block, "aux", bit)
    return jnp.where(
        side == 1,
        jnp.concatenate([other, block], axis=dim),
        jnp.concatenate([block, other], axis=dim),
    )


def owned(block, bits, dim):
    for bit in range(bits):
        half = block.shape[dim] // 2
        block = lax.dynamic_slice_in_dim(block, side_of("aux", bit) * half, half, dim)
    return block


def dot(expr, left, right):
    return jnp.einsum(
        expr, left, right, precision=lax.Precision.HIGH, preferred_element_type=jnp.float32
    )


def body(three_index, occupied_energy, virtual_energy, plan):
    per_block = three_index.shape[0]
    half_count = per_block // 2
    width = three_index.shape[1]
    aux_count = lax.axis_size("aux")
    bits = aux_count.bit_length() - 1
    row_count = width // aux_count
    row_start = lax.axis_index("aux") * row_count
    slots = jnp.arange(per_block, dtype=jnp.int32)
    rounds = plan.shape[0]
    sends = []
    for turn in range(rounds):
        table = plan[turn]
        upper_side = side_of("pair", turn) == 1
        inverse = jnp.sum(jnp.where(table[None, :] == slots[:, None], slots[None, :], 0), axis=1)
        own_slots = jnp.where(upper_side, inverse[half_count:], slots[:half_count])
        send_slots = jnp.where(upper_side, inverse[:half_count], slots[half_count:])
        own = jnp.take(three_index, own_slots, axis=0)
        give = jnp.take(three_index, send_slots, axis=0)
        own_energy = jnp.take(occupied_energy, own_slots)
        give_energy = jnp.take(occupied_energy, send_slots)
        sends.append((own_slots, send_slots, own, give, own_energy, give_energy))
    peers = [None] * rounds
    for turn in reversed(range(rounds)):
        own_slots, send_slots, own, give, own_energy, give_energy = sends[turn]
        first, energy = swapped((give, give_energy), "pair", turn)
        second = swapped(own, "pair", turn)
        peers[turn] = (first, own_energy + energy, second)
    gradient = jnp.zeros(three_index.shape, jnp.float32)
    density = jnp.zeros((row_count, width), jnp.float32)
    owned_energy = owned(virtual_energy, bits, 0)
    for turn in range(rounds):
        own_slots, send_slots, own, _, _, _ = sends[turn]
        first, pair_energy, second = peers[turn]
        part = dot("hap,hbp->hab", own, first)
        for bit in range(bits):
            part = fold(part, bit, 1)
        gap = pair_energy[:, None, None] - owned_energy[None, :, None] - virtual_energy[None, None, :]
        amp = part / gap
        amp_peer = swapped(amp, "pair", turn)
        for bit in reversed(range(bits)):
            amp = unfold(amp, bit, 1)
            amp_peer = unfold(amp_peer, bit, 1)
        tilde = 2.0 * amp - jnp.swapaxes(amp, 1, 2)
        tilde_peer = 2.0 * jnp.swapaxes(amp_peer, 1, 2) - amp_peer
        gradient = gradient.at[own_slots].add(dot("hab,hbp->hap", tilde, first))
        gradient = gradient.at[send_slots].add(dot("hab,hbp->hap", tilde_peer, second))
        rows = lax.dynamic_slice_in_dim(amp, row_start, row_count, 1)
        columns = lax.dynamic_slice_in_dim(amp, row_start, row_count, 2)
        density = density + dot("hac,hbc->ab", rows, tilde) + dot("hca,hcb->ab", columns, tilde)
    density = lax.psum_scatter(density, "pair", scatter_dimension=1, tiled=True)
    return (gradient, density)


def solution(mesh):
    in_specs = (P("pair", None, "aux"), P("pair"), P(), P(None, "pair"))
    out_specs = (P("pair", None, "aux"), P("aux", "pair"))
    return jax.shard_map(body, mesh=mesh, in_specs=in_specs, out_specs=out_specs, check_vma=False)
```

profile of v0, /device:TPU:0, one launch (start us, length us, event | category | flops | bytes accessed | tf_op | source)
XLA Modules:
  0.0 386.1 jit_solution(5469991135697425578)
XLA Ops:
  14.0 11.1 %dynamic-slice_select_fusion.1 = (f32[1,768,1024]{2,1,0:T(8,128)}, f32[1,768,1024]{2,1,0:T(8,128)}, f32[1,768,1024]{2,1,0:T(8,128)}, f32[1,768,1024]{2,1,0:T(8,128)}) fusion(f32[2,768,1024]{2,1,0:T(8,128)} %param.14, s32[]{:T(128)} %bitcast.32, pred[]{:T(512)} %bitcast.33, s32[]{:T(128)} %bitcast.6, pred[]{:T(512)} %bitcast.5, s32[]{:T(128)} %bitcast.3, ...), kind=kLoop, calls=%fused_computation.22 | loop fusion | flops 3145728 | bytes 25165844 | tf_op jit(solution)/shard_map/jit(_take)/select_n | solution.py:69
  25.1 3.0 collective-permute-start.13
  28.0 68.3 %collective-permute-done.13 = f32[1,768,1024]{2,1,0:T(8,128)S(1)} collective-permute-done((f32[1,768,1024]{2,1,0:T(8,128)}, f32[1,768,1024]{2,1,0:T(8,128)S(1)}, u32[]{:S(2)}, u32[]{:S(2)}) %collective-permute-start.13) | collective-permute-done | bytes 3145760 | tf_op jit(solution)/shard_map/ppermute | solution.py:14
  96.4 7.0 %fusion.7 = f32[768,768]{1,0:T(8,128)S(1)} fusion(f32[1,768,1024]{2,1,0:T(8,128)S(1)} %collective-permute-done.13, f32[1,768,1024]{2,1,0:T(8,128)} %get-tuple-element.110), kind=kOutput, calls=%fused_computation.10 | convolution fusion | flops 3623878656 | bytes 8650752 | tf_op jit(solution)/shard_map/hap,hbp->hab/dot_general | solution.py:47
  104.6 1.7 collective-permute-start.14
  106.4 6.8 %fusion.14 = f32[768,768]{1,0:T(8,128)S(1)} fusion(f32[1,768,1024]{2,1,0:T(8,128)} %collective-permute-done, f32[1,768,1024]{2,1,0:T(8,128)} %get-tuple-element.112), kind=kOutput, calls=%fused_computation.18 | convolution fusion | flops 3623878656 | bytes 8650752 | tf_op jit(solution)/shard_map/hap,hbp->hab/dot_general | solution.py:47
  114.6 19.3 %collective-permute-done.14 = f32[1,384,768]{2,1,0:T(8,128)} collective-permute-done((f32[1,384,768]{2,1,0:T(8,128)}, f32[1,384,768]{2,1,0:T(8,128)}, u32[]{:S(2)}, u32[]{:S(2)}) %collective-permute-start.14) | collective-permute-done | bytes 1179680 | tf_op jit(solution)/shard_map/ppermute | solution.py:14
  133.9 1.8 bitcast_add_fusion
  136.5 1.8 collective-permute-start.15
  138.3 19.1 %collective-permute-done.1 = f32[1,384,768]{2,1,0:T(8,128)} collective-permute-done((f32[1,384,768]{2,1,0:T(8,128)}, f32[1,384,768]{2,1,0:T(8,128)}, u32[]{:S(2)}, u32[]{:S(2)}) %collective-permute-start.1) | collective-permute-done | bytes 1179680 | tf_op jit(solution)/shard_map/ppermute | solution.py:14
  157.4 1.4 bitcast_add_fusion.1
  159.9 1.5 collective-permute-start.2
  162.6 2.7 collective-permute-start.16
  165.3 14.7 %collective-permute-done.2 = f32[1,192,768]{2,1,0:T(8,128)} collective-permute-done((f32[1,192,768]{2,1,0:T(8,128)S(1)}, f32[1,192,768]{2,1,0:T(8,128)}, u32[]{:S(2)}, u32[]{:S(2)}) %collective-permute-start.2) | collective-permute-done | bytes 589856 | tf_op jit(solution)/shard_map/ppermute | solution.py:14
  183.7 2.9 collective-permute-start.17
  190.9 3.9 %collective-permute-done.3 = f32[1,96,768]{2,1,0:T(8,128)S(1)} collective-permute-done((f32[1,96,768]{2,1,0:T(8,128)S(1)}, f32[1,96,768]{2,1,0:T(8,128)S(1)}, u32[]{:S(2)}, u32[]{:S(2)}) %collective-permute-start.3) | collective-permute-done | bytes 294944 | tf_op jit(solution)/shard_map/ppermute | solution.py:14
  195.3 2.8 collective-permute-start.5
  200.0 17.0 %collective-permute-done.18 = f32[1,96,768]{2,1,0:T(8,128)S(1)} collective-permute-done((f32[1,96,768]{2,1,0:T(8,128)S(1)}, f32[1,96,768]{2,1,0:T(8,128)S(1)}, u32[]{:S(2)}, u32[]{:S(2)}) %collective-permute-start.18) | collective-permute-done | bytes 294944 | tf_op jit(solution)/shard_map/ppermute | solution.py:14
  217.1 1.8 collective-permute-start.9
  218.9 4.5 %collective-permute-done.5 = f32[1,96,768]{2,1,0:T(8,128)S(1)} collective-permute-done((f32[1,96,768]{2,1,0:T(8,128)S(1)}, f32[1,96,768]{2,1,0:T(8,128)S(1)}, u32[]{:S(2)}, u32[]{:S(2)}) %collective-permute-start.5) | collective-permute-done | bytes 294944 | tf_op jit(solution)/shard_map/ppermute | solution.py:14
  223.5 1.8 collective-permute-start.22
  225.5 11.7 %collective-permute-done.9 = f32[1,96,768]{2,1,0:T(8,128)S(1)} collective-permute-done((f32[1,96,768]{2,1,0:T(8,128)S(1)}, f32[1,96,768]{2,1,0:T(8,128)S(1)}, u32[]{:S(2)}, u32[]{:S(2)}) %collective-permute-start.9) | collective-permute-done | bytes 294944 | tf_op jit(solution)/shard_map/ppermute | solution.py:14
  237.2 2.4 collective-permute-start.10
  239.6 16.6 %collective-permute-done.22 = f32[1,96,768]{2,1,0:T(8,128)S(1)} collective-permute-done((f32[1,96,768]{2,1,0:T(8,128)S(1)}, f32[1,96,768]{2,1,0:T(8,128)S(1)}, u32[]{:S(2)}, u32[]{:S(2)}) %collective-permute-start.22) | collective-permute-done | bytes 294944 | tf_op jit(solution)/shard_map/ppermute | solution.py:14
  256.2 2.4 collective-permute-start.23
  258.6 1.5 collective-permute-start.20
  263.8 10.1 %collective-permute-done.10 = f32[1,192,768]{2,1,0:T(8,128)S(1)} collective-permute-done((f32[1,192,768]{2,1,0:T(8,128)S(1)}, f32[1,192,768]{2,1,0:T(8,128)S(1)}, u32[]{:S(2)}, u32[]{:S(2)}) %collective-permute-start.10) | collective-permute-done | bytes 589856 | tf_op jit(solution)/shard_map/ppermute | solution.py:14
  276.4 10.0 %collective-permute-done.23 = f32[1,192,768]{2,1,0:T(8,128)S(1)} collective-permute-done((f32[1,192,768]{2,1,0:T(8,128)S(1)}, f32[1,192,768]{2,1,0:T(8,128)S(1)}, u32[]{:S(2)}, u32[]{:S(2)}) %collective-permute-start.23) | collective-permute-done | bytes 589856 | tf_op jit(solution)/shard_map/ppermute | solution.py:14
  287.9 1.8 collective-permute-start.24
  289.9 2.0 copy.24
  291.9 4.0 %fusion.18 = f32[96,768]{1,0:T(8,128)} fusion(f32[1,768,768]{2,1,0:T(8,128)S(1)} %maximum_select_fusion.2, s32[]{:T(128)S(6)} %select_n.532, f32[1,768,768]{1,2,0:T(8,128)} %copy.24), kind=kOutput, calls=%fused_computation.31 | convolution fusion | flops 340918272 | bytes 5406724 | tf_op jit(solution)/shard_map/hca,hcb->ab/dot_general | solution.py:47
  295.8 17.1 %collective-permute-done.7 = f32[1,384,768]{2,1,0:T(8,128)} collective-permute-done((f32[1,384,768]{2,1,0:T(8,128)}, f32[1,384,768]{2,1,0:T(8,128)}, u32[]{:S(2)}, u32[]{:S(2)}) %collective-permute-start.7) | collective-permute-done | bytes 1179680 | tf_op jit(solution)/shard_map/ppermute | solution.py:14
  313.0 3.3 maximum_select_fusion
  316.3 3.1 copy.22
  319.4 2.7 fusion.20
  322.5 1.5 fusion.24
  324.0 1.6 fusion.59
  325.6 1.9 copy.26
  329.9 6.5 %bitcast_dynamic-update-slice_fusion = f32[2,768,1024]{2,1,0:T(8,128)S(1)} fusion(f32[2,768,1024]{2,1,0:T(8,128)S(1)} %broadcast_in_dim.57, s32[]{:T(128)} %bitcast.3, f32[1,768,1024]{2,1,0:T(8,128)} %collective-permute-done, pred[]{:T(512)} %get-tuple-element.124, f32[1,768,768]{2,1,0:T(8,128)S(1)} %copy-done.1, f32[1,768,768]{1,2,0:T(8,128)S(1)} %copy-done.5), kind=kOutput, calls=%fused_computation.15 | convolution fusion | flops 3625844736 | bytes 11010053 | tf_op jit(solution)/shard_map/hab,hbp->hap/dot_general | solution.py:47
  336.5 2.7 copy-done.2
  339.2 3.2 maximum_select_fusion.1
  342.4 3.1 copy.23
  345.5 11.0 %fusion = f32[2,768,1024]{2,1,0:T(8,128)} fusion(f32[2,768,1024]{2,1,0:T(8,128)} %copy-done.2, s32[]{:T(128)} %bitcast.6, pred[]{:T(512)} %get-tuple-element.125, f32[1,768,1024]{2,1,0:T(8,128)} %collective-permute-done.12, f32[1,768,768]{2,1,0:T(8,128)} %maximum_select_fusion.1, f32[1,768,768]{1,2,0:T(8,128)} %copy.23), kind=kOutput, calls=%fused_computation.3 | convolution fusion | flops 3626631168 | bytes 14156800 | tf_op jit(solution)/shard_map/hab,hbp->hap/dot_general | solution.py:47
  356.5 7.4 %fusion.1 = f32[2,768,1024]{2,1,0:T(8,128)} fusion(f32[2,768,1024]{2,1,0:T(8,128)} %fusion, s32[]{:T(128)} %bitcast.32, pred[]{:T(512)} %get-tuple-element.107, f32[1,768,1024]{2,1,0:T(8,128)S(1)} %copy-done.7, f32[1,768,768]{2,1,0:T(8,128)S(1)} %maximum_select_fusion.2, f32[1,768,768]{1,2,0:T(8,128)S(1)} %copy-done.3), kind=kOutput, calls=%fused_computation.4 | convolution fusion | flops 3626631168 | bytes 14156800 | tf_op jit(solution)/shard_map/hab,hbp->hap/dot_general | solution.py:47
  363.9 1.9 maximum_select_fusion.3
  365.8 2.0 copy.25
  367.8 9.8 %fusion.2 = f32[2,768,1024]{2,1,0:T(8,128)} fusion(f32[2,768,1024]{2,1,0:T(8,128)} %fusion.1, s32[]{:T(128)} %bitcast.37, pred[]{:T(512)} %get-tuple-element.106, f32[1,768,1024]{2,1,0:T(8,128)} %collective-permute-done.25, f32[1,768,768]{2,1,0:T(8,128)S(1)} %maximum_select_fusion.3, f32[1,768,768]{1,2,0:T(8,128)} %copy.25), kind=kOutput, calls=%fused_computation.5 | convolution fusion | flops 3626631168 | bytes 14156800 | tf_op jit(solution)/shard_map/hab,hbp->hap/dot_general | solution.py:47
  377.7 1.6 copy.27
  (100 shorter events, 26.3 us)
Async XLA Ops:
  7.2 370.5 %reduce-scatter.4.cloned.1.call-start = ((), (), s32[]{:S(2)}) async-start(), calls=%async_computation.1 | async-start | bytes 491520
  25.1 71.3 %collective-permute-start.13 = (f32[1,768,1024]{2,1,0:T(8,128)}, f32[1,768,1024]{2,1,0:T(8,128)S(1)}, u32[]{:S(2)}, u32[]{:S(2)}) collective-permute-start(f32[1,768,1024]{2,1,0:T(8,128)} %get-tuple-element.113), channel_id=1, source_target_pairs={{0,16},{16,0},{8,24},{24,8},{1,17},{17,1},{9,25},{25,9},{2,18},{18... | collective-permute-start | bytes 9437192 | tf_op jit(solution)/shard_map/ppermute | solution.py:14
  28.0 78.3 %collective-permute-start = (f32[1,768,1024]{2,1,0:T(8,128)}, f32[1,768,1024]{2,1,0:T(8,128)}, u32[]{:S(2)}, u32[]{:S(2)}) collective-permute-start(f32[1,768,1024]{2,1,0:T(8,128)} %get-tuple-element.111), channel_id=1, source_target_pairs={{0,8},{8,0},{16,24},{24,16},{1,9},{9,1},{17,25},{25,17},{2,10},{10... | collective-permute-start | bytes 9437192 | tf_op jit(solution)/shard_map/ppermute | solution.py:14
  96.3 7.0 %copy-start.6 = (f32[1,768,1024]{2,1,0:T(8,128)}, f32[1,768,1024]{2,1,0:T(8,128)S(1)}, u32[]{:S(2)}) copy-start(f32[1,768,1024]{2,1,0:T(8,128)S(1)} %collective-permute-done.13) | copy-start | bytes 9437188
  103.4 9.8 %copy-start.8 = (f32[768,768]{1,0:T(8,128)}, f32[768,768]{1,0:T(8,128)S(1)}, u32[]{:S(2)}) copy-start(f32[768,768]{1,0:T(8,128)S(1)} %fusion.7) | copy-start | bytes 7077892
  104.6 29.2 %collective-permute-start.14 = (f32[1,384,768]{2,1,0:T(8,128)}, f32[1,384,768]{2,1,0:T(8,128)}, u32[]{:S(2)}, u32[]{:S(2)}) collective-permute-start(f32[1,384,768]{2,1,0:T(8,128)} %dynamic-slice_bitcast_fusion), channel_id=1, source_target_pairs={{0,1},{1,0},{2,3},{3,2},{4,5},{5,4},{6,7},{7,6},{8,9},{9,8},{10,11... | collective-permute-start | bytes 3538952 | tf_op jit(solution)/shard_map/ppermute | solution.py:14
  114.3 43.1 %collective-permute-start.1 = (f32[1,384,768]{2,1,0:T(8,128)}, f32[1,384,768]{2,1,0:T(8,128)}, u32[]{:S(2)}, u32[]{:S(2)}) collective-permute-start(f32[1,384,768]{2,1,0:T(8,128)} %dynamic-slice_bitcast_fusion.1), channel_id=1, source_target_pairs={{0,1},{1,0},{2,3},{3,2},{4,5},{5,4},{6,7},{7,6},{8,9},{9,8},{10,11... | collective-permute-start | bytes 3538952 | tf_op jit(solution)/shard_map/ppermute | solution.py:14
  136.5 24.9 %collective-permute-start.15 = (f32[1,192,768]{2,1,0:T(8,128)}, f32[1,192,768]{2,1,0:T(8,128)}, u32[]{:S(2)}, u32[]{:S(2)}) collective-permute-start(f32[1,192,768]{2,1,0:T(8,128)} %constant_dynamic-slice_fusion.1), channel_id=1, source_target_pairs={{0,2},{2,0},{1,3},{3,1},{4,6},{6,4},{5,7},{7,5},{8,10},{10,8},{9,1... | collective-permute-start | bytes 1769480 | tf_op jit(solution)/shard_map/ppermute | solution.py:14
  158.8 1.0 copy-start.11
  159.9 20.1 %copy-start.12 = (f32[1,384,768]{2,1,0:T(8,128)S(1)}, f32[1,384,768]{2,1,0:T(8,128)}, u32[]{:S(2)}) copy-start(f32[1,384,768]{2,1,0:T(8,128)} %copy-done.11) | copy-start | bytes 3538948
  159.9 20.1 %collective-permute-start.2 = (f32[1,192,768]{2,1,0:T(8,128)S(1)}, f32[1,192,768]{2,1,0:T(8,128)}, u32[]{:S(2)}, u32[]{:S(2)}) collective-permute-start(f32[1,192,768]{2,1,0:T(8,128)S(1)} %constant_dynamic-slice_fusion.3), channel_id=1, source_target_pairs={{0,2},{2,0},{1,3},{3,1},{4,6},{6,4},{5,7},{7,5},{8,10},{10,8},{9,1... | collective-permute-start | bytes 1769480 | tf_op jit(solution)/shard_map/ppermute | solution.py:14
  161.4 20.9 %copy-start.14 = (f32[2]{0:T(128)S(1)}, f32[2]{0:T(128)}, u32[]{:S(2)}) copy-start(f32[2]{0:T(128)} %param.15) | copy-start | bytes 28
  161.4 29.4 %copy-start.15 = (f32[768]{0:T(1024)S(1)}, f32[768]{0:T(1024)}, u32[]{:S(2)}) copy-start(f32[768]{0:T(1024)} %param.16) | copy-start | bytes 9220
  162.6 36.6 %copy-start.16 = (s32[3]{0:T(128)S(1)}, s32[3]{0:T(128)}, u32[]{:S(2)}) copy-start(s32[3]{0:T(128)} %constant.290.clone.1) | copy-start | bytes 40
  162.6 28.2 %collective-permute-start.16 = (f32[1,96,768]{2,1,0:T(8,128)S(1)}, f32[1,96,768]{2,1,0:T(8,128)S(1)}, u32[]{:S(2)}, u32[]{:S(2)}) collective-permute-start(f32[1,96,768]{2,1,0:T(8,128)S(1)} %constant_dynamic-slice_fusion), channel_id=1, source_target_pairs={{0,4},{4,0},{1,5},{5,1},{2,6},{6,2},{3,7},{7,3},{8,12},{12,8},{9,1... | collective-permute-start | bytes 884744 | tf_op jit(solution)/shard_map/ppermute | solution.py:14
  181.1 13.6 %collective-permute-start.3 = (f32[1,96,768]{2,1,0:T(8,128)S(1)}, f32[1,96,768]{2,1,0:T(8,128)S(1)}, u32[]{:S(2)}, u32[]{:S(2)}) collective-permute-start(f32[1,96,768]{2,1,0:T(8,128)S(1)} %constant_dynamic-slice_fusion.2), channel_id=1, source_target_pairs={{0,4},{4,0},{1,5},{5,1},{2,6},{6,2},{3,7},{7,3},{8,12},{12,8},{9,1... | collective-permute-start | bytes 884744 | tf_op jit(solution)/shard_map/ppermute | solution.py:14
  183.7 5.8 %collective-permute-start.17 = (f32[1]{0:T(128)}, f32[1]{0:T(128)}, u32[]{:S(2)}, u32[]{:S(2)}) collective-permute-start(f32[1]{0:T(128)} %select_n.521), channel_id=1, source_target_pairs={{0,16},{16,0},{8,24},{24,8},{1,17},{17,1},{9,25},{25,9},{2,18},{18... | collective-permute-start | bytes 20 | tf_op jit(solution)/shard_map/ppermute | solution.py:14
  187.2 2.8 collective-permute-start.4
  194.9 22.1 %collective-permute-start.18 = (f32[1,96,768]{2,1,0:T(8,128)S(1)}, f32[1,96,768]{2,1,0:T(8,128)S(1)}, u32[]{:S(2)}, u32[]{:S(2)}) collective-permute-start(f32[1,96,768]{2,1,0:T(8,128)S(1)} %get-tuple-element.114), channel_id=1, source_target_pairs={{0,4},{4,0},{1,5},{5,1},{2,6},{6,2},{3,7},{7,3},{8,12},{12,8},{9,1... | collective-permute-start | bytes 884744 | tf_op jit(solution)/shard_map/ppermute | solution.py:14
  195.2 21.9 %collective-permute-start.8 = (f32[1,96,768]{2,1,0:T(8,128)S(1)}, f32[1,96,768]{2,1,0:T(8,128)S(1)}, u32[]{:S(2)}, u32[]{:S(2)}) collective-permute-start(f32[1,96,768]{2,1,0:T(8,128)S(1)} %get-tuple-element.115), channel_id=1, source_target_pairs={{0,8},{8,0},{16,24},{24,16},{1,9},{9,1},{17,25},{25,17},{2,10},{10... | collective-permute-start | bytes 884744 | tf_op jit(solution)/shard_map/ppermute | solution.py:14
  195.3 28.1 %collective-permute-start.5 = (f32[1,96,768]{2,1,0:T(8,128)S(1)}, f32[1,96,768]{2,1,0:T(8,128)S(1)}, u32[]{:S(2)}, u32[]{:S(2)}) collective-permute-start(f32[1,96,768]{2,1,0:T(8,128)S(1)} %get-tuple-element.115), channel_id=1, source_target_pairs={{0,4},{4,0},{1,5},{5,1},{2,6},{6,2},{3,7},{7,3},{8,12},{12,8},{9,1... | collective-permute-start | bytes 884744 | tf_op jit(solution)/shard_map/ppermute | solution.py:14
  198.1 147.4 %collective-permute-start.12 = (f32[1,768,1024]{2,1,0:T(8,128)}, f32[1,768,1024]{2,1,0:T(8,128)}, u32[]{:S(2)}, u32[]{:S(2)}) collective-permute-start(f32[1,768,1024]{2,1,0:T(8,128)} %get-tuple-element.112), channel_id=1, source_target_pairs={{0,8},{8,0},{16,24},{24,16},{1,9},{9,1},{17,25},{25,17},{2,10},{10... | collective-permute-start | bytes 9437192 | tf_op jit(solution)/shard_map/ppermute | solution.py:14
  198.3 25.2 %collective-permute-start.21 = (f32[1,96,768]{2,1,0:T(8,128)S(1)}, f32[1,96,768]{2,1,0:T(8,128)S(1)}, u32[]{:S(2)}, u32[]{:S(2)}) collective-permute-start(f32[1,96,768]{2,1,0:T(8,128)S(1)} %get-tuple-element.114), channel_id=1, source_target_pairs={{0,16},{16,0},{8,24},{24,8},{1,17},{17,1},{9,25},{25,9},{2,18},{18... | collective-permute-start | bytes 884744 | tf_op jit(solution)/shard_map/ppermute | solution.py:14
  217.0 41.5 %collective-permute-start.19 = (f32[1,192,768]{2,1,0:T(8,128)S(1)}, f32[1,192,768]{2,1,0:T(8,128)S(1)}, u32[]{:S(2)}, u32[]{:S(2)}) collective-permute-start(f32[1,192,768]{2,1,0:T(8,128)S(1)} %maximum_select_fusion.16), channel_id=1, source_target_pairs={{0,2},{2,0},{1,3},{3,1},{4,6},{6,4},{5,7},{7,5},{8,10},{10,8},{9,1... | collective-permute-start | bytes 1769480 | tf_op jit(solution)/shard_map/ppermute | solution.py:14
  217.1 20.0 %collective-permute-start.9 = (f32[1,96,768]{2,1,0:T(8,128)S(1)}, f32[1,96,768]{2,1,0:T(8,128)S(1)}, u32[]{:S(2)}, u32[]{:S(2)}) collective-permute-start(f32[1,96,768]{2,1,0:T(8,128)S(1)} %collective-permute-done.8), channel_id=1, source_target_pairs={{0,4},{4,0},{1,5},{5,1},{2,6},{6,2},{3,7},{7,3},{8,12},{12,8},{9,1... | collective-permute-start | bytes 884744 | tf_op jit(solution)/shard_map/ppermute | solution.py:14
  223.5 37.8 %collective-permute-start.6 = (f32[1,192,768]{2,1,0:T(8,128)S(1)}, f32[1,192,768]{2,1,0:T(8,128)S(1)}, u32[]{:S(2)}, u32[]{:S(2)}) collective-permute-start(f32[1,192,768]{2,1,0:T(8,128)S(1)} %maximum_select_fusion.12), channel_id=1, source_target_pairs={{0,2},{2,0},{1,3},{3,1},{4,6},{6,4},{5,7},{7,5},{8,10},{10,8},{9,1... | collective-permute-start | bytes 1769480 | tf_op jit(solution)/shard_map/ppermute | solution.py:14
  223.5 32.6 %collective-permute-start.22 = (f32[1,96,768]{2,1,0:T(8,128)S(1)}, f32[1,96,768]{2,1,0:T(8,128)S(1)}, u32[]{:S(2)}, u32[]{:S(2)}) collective-permute-start(f32[1,96,768]{2,1,0:T(8,128)S(1)} %collective-permute-done.21), channel_id=1, source_target_pairs={{0,4},{4,0},{1,5},{5,1},{2,6},{6,2},{3,7},{7,3},{8,12},{12,8},{9,1... | collective-permute-start | bytes 884744 | tf_op jit(solution)/shard_map/ppermute | solution.py:14
  237.2 36.7 %collective-permute-start.10 = (f32[1,192,768]{2,1,0:T(8,128)S(1)}, f32[1,192,768]{2,1,0:T(8,128)S(1)}, u32[]{:S(2)}, u32[]{:S(2)}) collective-permute-start(f32[1,192,768]{2,1,0:T(8,128)S(1)} %maximum_select_fusion.14), channel_id=1, source_target_pairs={{0,2},{2,0},{1,3},{3,1},{4,6},{6,4},{5,7},{7,5},{8,10},{10,8},{9,1... | collective-permute-start | bytes 1769480 | tf_op jit(solution)/shard_map/ppermute | solution.py:14
  256.2 30.2 %collective-permute-start.23 = (f32[1,192,768]{2,1,0:T(8,128)S(1)}, f32[1,192,768]{2,1,0:T(8,128)S(1)}, u32[]{:S(2)}, u32[]{:S(2)}) collective-permute-start(f32[1,192,768]{2,1,0:T(8,128)S(1)} %maximum_select_fusion.18), channel_id=1, source_target_pairs={{0,2},{2,0},{1,3},{3,1},{4,6},{6,4},{5,7},{7,5},{8,10},{10,8},{9,1... | collective-permute-start | bytes 1769480 | tf_op jit(solution)/shard_map/ppermute | solution.py:14
  258.6 29.3 %collective-permute-start.20 = (f32[1,384,768]{2,1,0:T(8,128)S(1)}, f32[1,384,768]{2,1,0:T(8,128)S(1)}, u32[]{:S(2)}, u32[]{:S(2)}) collective-permute-start(f32[1,384,768]{2,1,0:T(8,128)S(1)} %maximum_select_fusion.8), channel_id=1, source_target_pairs={{0,1},{1,0},{2,3},{3,2},{4,5},{5,4},{6,7},{7,6},{8,9},{9,8},{10,11... | collective-permute-start | bytes 3538952 | tf_op jit(solution)/shard_map/ppermute | solution.py:14
  262.3 50.6 %collective-permute-start.7 = (f32[1,384,768]{2,1,0:T(8,128)}, f32[1,384,768]{2,1,0:T(8,128)}, u32[]{:S(2)}, u32[]{:S(2)}) collective-permute-start(f32[1,384,768]{2,1,0:T(8,128)} %maximum_select_fusion.4), channel_id=1, source_target_pairs={{0,1},{1,0},{2,3},{3,2},{4,5},{5,4},{6,7},{7,6},{8,9},{9,8},{10,11... | collective-permute-start | bytes 3538952 | tf_op jit(solution)/shard_map/ppermute | solution.py:14
  273.9 94.0 %collective-permute-start.25 = (f32[1,768,1024]{2,1,0:T(8,128)}, f32[1,768,1024]{2,1,0:T(8,128)}, u32[]{:S(2)}, u32[]{:S(2)}) collective-permute-start(f32[1,768,1024]{2,1,0:T(8,128)} %get-tuple-element.110), channel_id=1, source_target_pairs={{0,16},{16,0},{8,24},{24,8},{1,17},{17,1},{9,25},{25,9},{2,18},{18... | collective-permute-start | bytes 9437192 | tf_op jit(solution)/shard_map/ppermute | solution.py:14
  286.4 52.7 %collective-permute-start.11 = (f32[1,384,768]{2,1,0:T(8,128)}, f32[1,384,768]{2,1,0:T(8,128)}, u32[]{:S(2)}, u32[]{:S(2)}) collective-permute-start(f32[1,384,768]{2,1,0:T(8,128)} %maximum_select_fusion.6), channel_id=1, source_target_pairs={{0,1},{1,0},{2,3},{3,2},{4,5},{5,4},{6,7},{7,6},{8,9},{9,8},{10,11... | collective-permute-start | bytes 3538952 | tf_op jit(solution)/shard_map/ppermute | solution.py:14
  287.9 76.0 %collective-permute-start.24 = (f32[1,384,768]{2,1,0:T(8,128)}, f32[1,384,768]{2,1,0:T(8,128)}, u32[]{:S(2)}, u32[]{:S(2)}) collective-permute-start(f32[1,384,768]{2,1,0:T(8,128)} %maximum_select_fusion.10), channel_id=1, source_target_pairs={{0,1},{1,0},{2,3},{3,2},{4,5},{5,4},{6,7},{7,6},{8,9},{9,8},{10,11... | collective-permute-start | bytes 3538952 | tf_op jit(solution)/shard_map/ppermute | solution.py:14
  291.9 21.1 %copy-start.10 = (f32[1,384,768]{2,1,0:T(8,128)S(1)}, f32[1,384,768]{2,1,0:T(8,128)}, u32[]{:S(2)}) copy-start(f32[1,384,768]{2,1,0:T(8,128)} %fusion.47) | copy-start | bytes 3538948
  319.4 2.7 copy-start
  319.4 3.1 copy-start.4
  322.5 1.5 copy-start.13
  327.5 1.7 copy-start.1
  327.5 2.4 copy-start.5
  329.9 9.2 %copy-start.9 = (f32[1,384,768]{2,1,0:T(8,128)S(1)}, f32[1,384,768]{2,1,0:T(8,128)}, u32[]{:S(2)}) copy-start(f32[1,384,768]{2,1,0:T(8,128)} %fusion.48) | copy-start | bytes 3538948
  336.4 2.7 copy-start.2
  345.5 11.0 %copy-start.3 = (f32[1,768,768]{1,2,0:T(8,128)S(1)}, f32[1,768,768]{1,2,0:T(8,128)}, u32[]{:S(2)}) copy-start(f32[1,768,768]{1,2,0:T(8,128)} %copy.24) | copy-start | bytes 7077892
  345.5 11.0 %copy-start.7 = (f32[1,768,1024]{2,1,0:T(8,128)S(1)}, f32[1,768,1024]{2,1,0:T(8,128)}, u32[]{:S(2)}) copy-start(f32[1,768,1024]{2,1,0:T(8,128)} %copy-done.6) | copy-start | bytes 9437188
Sparse Core Ops, SparseCore 0:
  327.6 21.1 reduce-scatter.3
where the time goes:
time: 387 us; the launch traced here: 386 us
  waiting for transfers between devices  213 us (55%)
  matrix products  58.4 us (15%)
  starting transfers between devices  32.8 us (8%)
  other arithmetic  32.6 us (8%)
  local copies, waits for them, and re-layouts  26.8 us (7%)
  between operations  22.3 us (6%)
    ppermute x26, waiting for transfers between devices, swapped(): return lax.ppermute(block, axis, route)  213 us
    dot_general x10, matrix products, dot(): jnp.einsum(expr, left, right, precision=lax.Precision.HIGH, preferred_ele...  58.4 us
    ppermute x26, starting transfers between devices, swapped(): return lax.ppermute(block, axis, route)  32.7 us
    select_n x16, other arithmetic, unfold(): jnp.where(side == 1, jnp.concatenate([other, block], axis=dim), jnp.conca...  12.5 us
    select_n x1, other arithmetic, body(): own = jnp.take(three_index, own_slots, axis=0)  11.1 us
    select_n x4, local copies, waits for them, and re-layouts, unfold(): jnp.where(side == 1, jnp.concatenate([other, block], axis=dim), jnp.conca...  10.1 us
    unnamed x36, local copies, waits for them, and re-layouts  9.24 us
  transfers between devices with their start and end apart: 27, of which 13 were waited for; matrix products, arithmetic and copies ran while one was open for 25% of the time, Pallas kernels for 0%

commit v1 on v0

v1 whole, which is shorter than its diff:
```python
import functools

import jax
import jax.numpy as jnp
from jax import lax
from jax.experimental import pallas as pl
from jax.experimental.pallas import tpu as pltpu
from jax.sharding import PartitionSpec as P


def swapped(block, axis, bit):
    count = lax.axis_size(axis)
    route = []
    for low in range(count):
        high = low | 1 << bit
        if high != low and high < count:
            route += [(low, high), (high, low)]
    return lax.ppermute(block, axis, route)


def after(value, *earlier):
    return lax.optimization_barrier((value, *earlier))[0]


def dot(expr, left, right):
    return jnp.einsum(
        expr, left, right, precision=lax.Precision.HIGH, preferred_element_type=jnp.float32
    )


def copy_kernel(plan_ref, side_ref, source_ref, target_ref):
    del plan_ref, side_ref
    target_ref[...] = source_ref[...]


def picked(three_index, plan, position, turn, own):
    per_block, width, depth = three_index.shape
    half_count = per_block // 2
    pieces = 4 if width % 32 == 0 else 1

    def source(h, piece, plan_ref, side_ref):
        upper = side_ref[0] // 2**turn % 2 == 1
        plain = h if own else half_count + h
        wanted = half_count + h if own else h
        inverse = 0
        for k in range(per_block):
            inverse += jnp.where(plan_ref[turn, k] == wanted, k, 0)
        return (jnp.where(upper, inverse, plain), piece, 0)

    return pl.pallas_call(
        copy_kernel,
        out_shape=jax.ShapeDtypeStruct((half_count, width, depth), jnp.float32),
        grid_spec=pltpu.PrefetchScalarGridSpec(
            num_scalar_prefetch=2,
            grid=(half_count, pieces),
            in_specs=[pl.BlockSpec((1, width // pieces, depth), source)],
            out_specs=pl.BlockSpec((1, width // pieces, depth), lambda h, piece, *_: (h, piece, 0)),
        ),
        compiler_params=pltpu.CompilerParams(vmem_limit_bytes=16 * 2**20),
        cost_estimate=pl.CostEstimate(
            flops=0, bytes_accessed=8 * half_count * width * depth, transcendentals=0
        ),
    )(plan, position, three_index)


def body(three_index, occupied_energy, virtual_energy, plan):
    per_block = three_index.shape[0]
    half_count = per_block // 2
    width = three_index.shape[1]
    aux_count = lax.axis_size("aux")
    row_count = width // aux_count
    row_start = lax.axis_index("aux") * row_count
    slots = jnp.arange(per_block, dtype=jnp.int32)
    rounds = plan.shape[0]
    position = lax.axis_index("pair").astype(jnp.int32)
    positions = position[None]
    gives = [None] * rounds
    firsts = [None] * rounds
    seconds = [None] * rounds
    for turn in range(1, rounds):
        gives[turn] = picked(three_index, plan, positions, turn, False)
        firsts[turn] = swapped(gives[turn], "pair", turn)
    other, = (swapped(three_index, "pair", 0),)
    owns = []
    energies = []
    where = []
    for turn in range(rounds):
        table = plan[turn]
        upper = position // 2**turn % 2 == 1
        inverse = jnp.sum(jnp.where(table[None, :] == slots[:, None], slots[None, :], 0), axis=1)
        own_slots = jnp.where(upper, inverse[half_count:], slots[:half_count])
        give_slots = jnp.where(upper, inverse[:half_count], slots[half_count:])
        where.append((own_slots, give_slots))
        peer_energy = swapped(occupied_energy[give_slots], "pair", turn)
        energies.append(occupied_energy[own_slots] + peer_energy)
        if turn == 0:
            owns.append(three_index[own_slots])
            firsts[0] = other[jnp.where(upper, slots[half_count:], table[:half_count])]
            seconds[0] = other[jnp.where(upper, slots[:half_count], table[half_count:])]
        else:
            owns.append(picked(three_index, plan, positions, turn, True))
            seconds[turn] = swapped(owns[turn], "pair", turn)
    rows_energy = lax.dynamic_slice_in_dim(virtual_energy, row_start, row_count, 0)
    gradient = jnp.zeros(three_index.shape, jnp.float32)
    density = jnp.zeros((row_count, width), jnp.float32)
    parts = []
    for turn in range(rounds):
        first = firsts[turn] if turn == 0 else after(firsts[turn], part)
        part = dot("hap,hbp->hab", owns[turn], first)
        parts.append(lax.psum_scatter(part, "aux", scatter_dimension=1, tiled=True))
    for turn in range(rounds):
        gap = energies[turn][:, None, None] - rows_energy[None, :, None] - virtual_energy[None, None, :]
        shard = parts[turn] / gap
        both = jnp.stack([shard, swapped(shard, "pair", turn)])
        amp, amp_peer = lax.all_gather(both, "aux", axis=2, tiled=True)
        tilde = 2.0 * amp - jnp.swapaxes(amp, 1, 2)
        tilde_peer = 2.0 * jnp.swapaxes(amp_peer, 1, 2) - amp_peer
        own_slots, give_slots = where[turn]
        gradient = gradient.at[own_slots].add(dot("hab,hbp->hap", tilde, firsts[turn]))
        gradient = gradient.at[give_slots].add(dot("hab,hbp->hap", tilde_peer, seconds[turn]))
        rows = lax.dynamic_slice_in_dim(amp, row_start, row_count, 1)
        columns = lax.dynamic_slice_in_dim(amp, row_start, row_count, 2)
        density = density + dot("hac,hbc->ab", rows, tilde) + dot("hca,hcb->ab", columns, tilde)
    density = lax.psum_scatter(density, "pair", scatter_dimension=1, tiled=True)
    return (gradient, density)


def solution(mesh):
    in_specs = (P("pair", None, "aux"), P("pair"), P(), P(None, "pair"))
    out_specs = (P("pair", None, "aux"), P("aux", "pair"))
    return jax.shard_map(body, mesh=mesh, in_specs=in_specs, out_specs=out_specs, check_vma=False)
```

time: 387 us -> 469 us (1.21)
  waiting for transfers between devices: 213 us -> 328 us
  other arithmetic: 32.6 us -> 3.99 us
  starting transfers between devices: 32.8 us -> 8.37 us
  local copies, waits for them, and re-layouts: 26.8 us -> 41.2 us
    ppermute x26 -> x7, waiting for transfers between devices: 213 us -> 63.4 us  [swapped(): return lax.ppermute(block, axis, route)]
    all_gather x0 -> x2, waiting for transfers between devices: none -> 134 us  [body(): amp, amp_peer = lax.all_gather(both, 'aux', axis=2, tiled=True)]
    reduce_scatter x0 -> x2, waiting for transfers between devices: none -> 130 us  [body(): parts.append(lax.psum_scatter(part, 'aux', scatter_dimension=1, tiled=True))]
    ppermute x26 -> x7, starting transfers between devices: 32.7 us -> 7.99 us  [swapped(): return lax.ppermute(block, axis, route)]
    another operation x0 -> x6, local copies, waits for them, and re-layouts: none -> 23.7 us  [body(): amp, amp_peer = lax.all_gather(both, 'aux', axis=2, tiled=True)]
    select_n x17 -> x0, other arithmetic: 23.6 us -> none  [the longest x16 12.5 us: unfold(): jnp.where(side == 1, jnp.concatenate([other, block], axis=dim), jnp.conca...]
    select_n x4 -> x0, local copies, waits for them, and re-layouts: 10.1 us -> none  [unfold(): jnp.where(side == 1, jnp.concatenate([other, block], axis=dim), jnp.conca...]
    add x4 -> x0, other arithmetic: 5.46 us -> none  [fold(): return keep + swapped(give, 'aux', bit)]
  transfers between devices with their start and end apart: 27 -> 12, of which waited for: 13 -> 8; matrix products, arithmetic and copies ran while one was open for 25% -> 18% of each run, Pallas kernels for 0% -> 1%
where the time goes in v1:
time: 469 us; the launch traced here: 468 us
  waiting for transfers between devices  328 us (70%)
  matrix products  60.2 us (13%)
  local copies, waits for them, and re-layouts  41.2 us (9%)
  between operations  22.3 us (5%)
  starting transfers between devices  8.37 us (2%)
    all_gather x2, waiting for transfers between devices, body(): amp, amp_peer = lax.all_gather(both, 'aux', axis=2, tiled=True)  134 us
    reduce_scatter x2, waiting for transfers between devices, body(): parts.append(lax.psum_scatter(part, 'aux', scatter_dimension=1, tiled=True))  130 us
    ppermute x7, waiting for transfers between devices, swapped(): return lax.ppermute(block, axis, route)  63.4 us
    dot_general x10, matrix products, dot(): jnp.einsum(expr, left, right, precision=lax.Precision.HIGH, preferred_ele...  60.2 us
    another operation x6, local copies, waits for them, and re-layouts, body(): amp, amp_peer = lax.all_gather(both, 'aux', axis=2, tiled=True)  23.7 us
    unnamed x40, local copies, waits for them, and re-layouts  13.4 us
  transfers between devices with their start and end apart: 12, of which 8 were waited for; matrix products, arithmetic and copies ran while one was open for 18% of the time, Pallas kernels for 1%

profile of v1, /device:TPU:0, one launch (start us, length us, event | category | flops | bytes accessed | tf_op | source)
XLA Modules:
  0.0 468.1 jit_solution(6729462059818148117)
XLA Ops:
  7.7 2.8 copy-done
  10.5 0.7 copy-done.3
  11.2 2.7 shard_map.60
  13.9 2.5 collective-permute-start.3
  16.6 0.6 fusion.82
  17.9 0.6 slice.129
  18.5 0.6 fusion.79
  20.5 2.8 copy-done.1
  23.2 0.9 shard_map.59
  24.2 1.9 copy-done.2
  26.0 7.3 %fusion.34 = f32[1,768,768]{2,1,0:T(8,128)} fusion(f32[2,768,1024]{2,1,0:T(8,128)} %collective-permute-done, s32[]{:T(128)} %bitcast.5, f32[2,768,1024]{2,1,0:T(8,128)S(1)} %copy-done.2, s32[]{:T(128)} %bitcast.2), kind=kOutput, calls=%fused_computation.38 | convolution fusion | flops 3623878656 | bytes 8651776 | tf_op jit(solution)/shard_map/hap,hbp->hab/dot_general | solution.py:26
  33.4 52.1 %collective-permute-done.3 = f32[1,768,1024]{2,1,0:T(8,128)} collective-permute-done((f32[1,768,1024]{2,1,0:T(8,128)}, f32[1,768,1024]{2,1,0:T(8,128)}, u32[]{:S(2)}, u32[]{:S(2)}) %collective-permute-start.3) | collective-permute-done | bytes 3145760 | tf_op jit(solution)/shard_map/ppermute | solution.py:18
  85.5 7.2 %fusion.29 = f32[1,768,768]{2,1,0:T(8,128)} fusion(f32[1,768,1024]{2,1,0:T(8,128)} %collective-permute-done.3, f32[1,768,1024]{2,1,0:T(8,128)S(1)} %shard_map.59), kind=kOutput, calls=%fused_computation.37 | convolution fusion | flops 3623878656 | bytes 8650752 | tf_op jit(solution)/shard_map/hap,hbp->hab/dot_general | solution.py:26
  92.8 0.7 reduce-scatter.6.cloned.1.call-update
  93.6 0.7 fusion.81
  97.4 0.7 fusion.80
  98.1 1.7 collective-permute-start.4
  99.8 2.1 collective-permute-done.4
  104.5 58.9 %reduce-scatter.8.cloned.1.call-done = f32[1,96,768]{2,1,0:T(8,128)} async-done(((f32[1,768,768]{2,1,0:T(8,128)}), f32[1,96,768]{2,1,0:T(8,128)}) %reduce-scatter.8.cloned.1.call-update) | async-done | bytes 294928 | tf_op jit(solution)/shard_map/reduce_scatter | solution.py:110
  163.4 71.5 %reduce-scatter.6.cloned.1.call-done = f32[1,96,768]{2,1,0:T(8,128)} async-done(((f32[1,768,768]{2,1,0:T(8,128)}), f32[1,96,768]{2,1,0:T(8,128)}) %reduce-scatter.6.cloned.1.call-update) | async-done | bytes 294928 | tf_op jit(solution)/shard_map/reduce_scatter | solution.py:110
  234.9 1.2 subtract_divide_fusion
  236.2 1.6 collective-permute-done.2
  237.8 0.9 pad_maximum_fusion
  238.7 1.6 collective-permute-start.5
  240.3 7.6 %collective-permute-done.5 = f32[1,96,768]{2,1,0:T(8,128)S(1)} collective-permute-done((f32[1,96,768]{2,1,0:T(8,128)S(1)}, f32[1,96,768]{2,1,0:T(8,128)S(1)}, u32[]{:S(2)}, u32[]{:S(2)}) %collective-permute-start.5) | collective-permute-done | bytes 294944 | tf_op jit(solution)/shard_map/ppermute | solution.py:18
  247.8 0.9 pad_maximum_fusion.1
  249.0 1.6 collective-permute-start.6
  251.2 0.8 and_reduce_fusion
  252.0 65.7 %all-gather.3.cloned.1.call-done = f32[2,1,768,768]{3,2,1,0:T(8,128)} async-done(((f32[2,1,96,768]{3,2,1,0:T(8,128)}), f32[2,1,768,768]{3,2,1,0:T(8,128)}) %all-gather.3.cloned.1.call-update) | async-done | bytes 4718608 | tf_op jit(solution)/shard_map/all_gather | solution.py:115
  317.8 5.7 %fusion.78 = (f32[1,1,768,768]{3,2,1,0:T(8,128)}, f32[1,768,768]{2,1,0:T(8,128)}, f32[1,768,768]{2,1,0:T(8,128)}) fusion(f32[2,1,768,768]{3,2,1,0:T(8,128)} %all-gather.3.cloned.1.call-done), kind=kLoop, calls=%fused_computation.89 | loop fusion | bytes 11796480 | tf_op jit(solution)/shard_map/unstack | solution.py:115
  323.4 3.1 copy.14
  326.6 3.2 copy.15
  329.8 68.1 %all-gather.5.cloned.1.call-done = f32[2,1,768,768]{3,2,1,0:T(8,128)} async-done(((f32[2,1,96,768]{3,2,1,0:T(8,128)}), f32[2,1,768,768]{3,2,1,0:T(8,128)}) %all-gather.5.cloned.1.call-update) | async-done | bytes 4718608 | tf_op jit(solution)/shard_map/all_gather | solution.py:115
  397.9 5.6 %fusion.77 = (f32[1,1,768,768]{3,2,1,0:T(8,128)}, f32[1,768,768]{2,1,0:T(8,128)}, f32[1,768,768]{2,1,0:T(8,128)}) fusion(f32[2,1,768,768]{3,2,1,0:T(8,128)} %all-gather.5.cloned.1.call-done), kind=kLoop, calls=%fused_computation.88 | loop fusion | bytes 11796480 | tf_op jit(solution)/shard_map/unstack | solution.py:115
  403.5 3.0 copy.16
  406.5 3.5 fusion.56
  410.0 3.6 convolution_add_fusion.2
  413.7 2.7 convolution_add_fusion.1
  416.4 2.7 convolution_add_fusion
  419.1 0.9 copy.18
  420.1 0.8 broadcast_in_dim.57
  420.9 9.0 %bitcast_dynamic-update-slice_fusion = f32[2,768,1024]{2,1,0:T(8,128)S(1)} fusion(f32[2,768,1024]{2,1,0:T(8,128)S(1)} %broadcast_in_dim.57, s32[]{:T(128)} %bitcast.2, f32[2,768,1024]{2,1,0:T(8,128)} %collective-permute-done, s32[]{:T(128)} %bitcast.5, pred[]{:T(512)} %get-tuple-element.151, f32[1,768,768]{1,2,0:T(8,128)} %copy.14, ...), kind=kOutput, calls=%fused_computation.15 | convolution fusion | flops 3625844736 | bytes 11011584 | tf_op jit(solution)/shard_map/hab,hbp->hap/dot_general | solution.py:26
  429.9 6.8 %fusion = f32[2,768,1024]{2,1,0:T(8,128)S(1)} fusion(f32[2,768,1024]{2,1,0:T(8,128)S(1)} %bitcast_dynamic-update-slice_fusion, s32[]{:T(128)} %bitcast.8, pred[]{:T(512)} %get-tuple-element.152, f32[2,768,1024]{2,1,0:T(8,128)} %collective-permute-done, s32[]{:T(128)} %bitcast.20, f32[1,768,768]{1,2,0:T(8,128)S(1)} %copy-done.9, ...), kind=kOutput, calls=%fused_computation.3 | convolution fusion | flops 3626631168 | bytes 14157312 | tf_op jit(solution)/shard_map/hab,hbp->hap/dot_general | solution.py:26
  436.8 6.9 %fusion.1 = f32[2,768,1024]{2,1,0:T(8,128)S(1)} fusion(f32[2,768,1024]{2,1,0:T(8,128)S(1)} %fusion, s32[]{:T(128)} %bitcast.25, pred[]{:T(512)} %get-tuple-element.130, f32[1,768,1024]{2,1,0:T(8,128)} %collective-permute-done.3, f32[1,768,768]{1,2,0:T(8,128)S(1)} %copy-done.8, f32[2,1,768,768]{3,2,1,0:T(8,128)S(1)} %bitcast.156), kind=kOutput, calls=%fused_computation.4 | convolution fusion | flops 3626631168 | bytes 14155781 | tf_op jit(solution)/shard_map/hab,hbp->hap/dot_general | solution.py:26
  443.7 2.7 copy-done.6
  446.4 3.1 copy.17
  449.5 10.4 %fusion.2 = f32[2,768,1024]{2,1,0:T(8,128)} fusion(f32[2,768,1024]{2,1,0:T(8,128)} %copy-done.6, s32[]{:T(128)} %bitcast.30, pred[]{:T(512)} %get-tuple-element.129, f32[1,768,1024]{2,1,0:T(8,128)} %collective-permute-done.6, f32[1,768,768]{1,2,0:T(8,128)} %copy.17, f32[2,1,768,768]{3,2,1,0:T(8,128)} %all-gather.5.cloned.1.call-done), kind=kOutput, calls=%fused_computation.5 | convolution fusion | flops 3626631168 | bytes 14156800 | tf_op jit(solution)/shard_map/hab,hbp->hap/dot_general | solution.py:26
  459.9 1.6 copy.19
  (57 shorter events, 1.4 us)
Async XLA Ops:
  7.2 156.2 %reduce-scatter.8.cloned.1.call-start = ((), (), s32[]{:S(2)}) async-start(), calls=%async_computation.5 | async-start | bytes 2654208 | tf_op jit(solution)/shard_map/reduce_scatter | solution.py:110
  7.2 16.9 %collective-permute-start = (f32[2,768,1024]{2,1,0:T(8,128)}, f32[2,768,1024]{2,1,0:T(8,128)}, u32[]{:S(2)}, u32[]{:S(2)}) collective-permute-start(f32[2,768,1024]{2,1,0:T(8,128)} %source_ref.3), channel_id=1, source_target_pairs={{0,8},{8,0},{16,24},{24,16},{1,9},{9,1},{17,25},{25,17},{2,10},{10... | collective-permute-start | bytes 18874376 | tf_op jit(solution)/shard_map/ppermute | solution.py:18
  7.7 2.8 copy-start
  10.5 0.7 copy-start.3
  11.2 5.3 %copy-start.4 = (s32[2,2]{1,0:T(2,128)S(1)}, s32[2,2]{1,0:T(2,128)}, u32[]{:S(2)}) copy-start(s32[2,2]{1,0:T(2,128)} %plan_ref.3) | copy-start | bytes 52
  13.9 71.6 %collective-permute-start.3 = (f32[1,768,1024]{2,1,0:T(8,128)}, f32[1,768,1024]{2,1,0:T(8,128)}, u32[]{:S(2)}, u32[]{:S(2)}) collective-permute-start(f32[1,768,1024]{2,1,0:T(8,128)} %shard_map.60), channel_id=1, source_target_pairs={{0,16},{16,0},{8,24},{24,8},{1,17},{17,1},{9,25},{25,9},{2,18},{18... | collective-permute-start | bytes 9437192 | tf_op jit(solution)/shard_map/ppermute | solution.py:18
  20.4 2.8 copy-start.1
  23.2 2.8 copy-start.2
  92.8 4.6 copy-start.10
  92.8 11.7 %copy-start.11 = (f32[768]{0:T(1024)S(1)}, f32[768]{0:T(1024)}, u32[]{:S(2)}) copy-start(f32[768]{0:T(1024)} %param.14) | copy-start | bytes 9220
  92.8 158.4 %copy-start.12 = (s32[3]{0:T(128)S(1)}, s32[3]{0:T(128)}, u32[]{:S(2)}) copy-start(s32[3]{0:T(128)} %constant.136.clone.1) | copy-start | bytes 40
  92.8 142.1 %reduce-scatter.6.cloned.1.call-start = ((), (), s32[]{:S(2)}) async-start(), calls=%async_computation.3 | async-start | bytes 2654208 | tf_op jit(solution)/shard_map/reduce_scatter | solution.py:110
  93.5 224.2 %all-gather.3.cloned.1.call-start = ((), (), s32[]{:S(2)}) async-start(), calls=%async_computation.4 | async-start | bytes 5308416 | tf_op jit(solution)/shard_map/all_gather | solution.py:115
  98.1 3.9 collective-permute-start.4
  99.8 3.4 collective-permute-start.1
  236.1 1.6 collective-permute-start.2
  238.7 159.2 %all-gather.5.cloned.1.call-start = ((), (), s32[]{:S(2)}) async-start(), calls=%async_computation.6 | async-start | bytes 5308416 | tf_op jit(solution)/shard_map/all_gather | solution.py:115
  238.7 9.1 %collective-permute-start.5 = (f32[1,96,768]{2,1,0:T(8,128)S(1)}, f32[1,96,768]{2,1,0:T(8,128)S(1)}, u32[]{:S(2)}, u32[]{:S(2)}) collective-permute-start(f32[1,96,768]{2,1,0:T(8,128)S(1)} %get-tuple-element.139), channel_id=1, source_target_pairs={{0,16},{16,0},{8,24},{24,8},{1,17},{17,1},{9,25},{25,9},{2,18},{18... | collective-permute-start | bytes 884744 | tf_op jit(solution)/shard_map/ppermute | solution.py:18
  248.7 211.2 %reduce-scatter.10.cloned.1.call-start = ((), (), s32[]{:S(2)}) async-start(), calls=%async_computation.7 | async-start | bytes 491520
  249.0 200.5 %collective-permute-start.6 = (f32[1,768,1024]{2,1,0:T(8,128)S(1)}, f32[1,768,1024]{2,1,0:T(8,128)}, u32[]{:S(2)}, u32[]{:S(2)}) collective-permute-start(f32[1,768,1024]{2,1,0:T(8,128)S(1)} %shard_map.59), channel_id=1, source_target_pairs={{0,16},{16,0},{8,24},{24,8},{1,17},{17,1},{9,25},{25,9},{2,18},{18... | collective-permute-start | bytes 9437192 | tf_op jit(solution)/shard_map/ppermute | solution.py:18
  406.5 3.5 copy-start.5
  406.5 9.9 %slice-start.2 = ((s8[4718592]{0:T(1024)(128)(4,1)}), s8[4194304]{0:T(1024)(128)(4,1)S(1)}, s32[]{:S(2)}) async-start(s8[4718592]{0:T(1024)(128)(4,1)} %bitcast.153), calls=%async_computation.10 | async-start | bytes 8388608
  410.0 3.7 copy-start.7
  410.0 6.4 %slice-start.3 = ((s8[4718592]{0:T(1024)(128)(4,1)}), s8[524288]{0:T(1024)(128)(4,1)S(1)}, s32[]{:S(2)}) async-start(s8[4718592]{0:T(1024)(128)(4,1)} %bitcast.153), calls=%async_computation.11 | async-start | bytes 1048576
  420.1 9.8 %slice-start = ((s8[4718592]{0:T(1024)(128)(4,1)}), s8[4194304]{0:T(1024)(128)(4,1)S(1)}, s32[]{:S(2)}) async-start(s8[4718592]{0:T(1024)(128)(4,1)} %bitcast.151), calls=%async_computation.8 | async-start | bytes 8388608
  420.1 16.7 %slice-start.4 = ((s8[4718592]{0:T(1024)(128)(4,1)}), s8[4194304]{0:T(1024)(128)(4,1)S(1)}, s32[]{:S(2)}) async-start(s8[4718592]{0:T(1024)(128)(4,1)} %bitcast.155), calls=%async_computation.12 | async-start | bytes 8388608
  420.9 9.0 %slice-start.1 = ((s8[4718592]{0:T(1024)(128)(4,1)}), s8[524288]{0:T(1024)(128)(4,1)S(1)}, s32[]{:S(2)}) async-start(s8[4718592]{0:T(1024)(128)(4,1)} %bitcast.151), calls=%async_computation.9 | async-start | bytes 1048576
  420.9 9.0 %copy-start.9 = (f32[1,768,768]{1,2,0:T(8,128)S(1)}, f32[1,768,768]{1,2,0:T(8,128)}, u32[]{:S(2)}) copy-start(f32[1,768,768]{1,2,0:T(8,128)} %copy.15) | copy-start | bytes 7077892
  420.9 15.9 %slice-start.5 = ((s8[4718592]{0:T(1024)(128)(4,1)}), s8[524288]{0:T(1024)(128)(4,1)S(1)}, s32[]{:S(2)}) async-start(s8[4718592]{0:T(1024)(128)(4,1)} %bitcast.155), calls=%async_computation.13 | async-start | bytes 1048576
  429.9 6.9 %copy-start.8 = (f32[1,768,768]{1,2,0:T(8,128)S(1)}, f32[1,768,768]{1,2,0:T(8,128)}, u32[]{:S(2)}) copy-start(f32[1,768,768]{1,2,0:T(8,128)} %copy.16) | copy-start | bytes 7077892
  443.7 2.7 copy-start.6
Sparse Core Ops, SparseCore 0:
  92.9 70.4 reduce-scatter.7
  166.9 67.9 reduce-scatter.5
  238.8 78.9 all-gather.2
  319.8 78.0 all-gather.4
  420.2 18.9 reduce-scatter.9

commit v2 on v1

v2 whole, which is shorter than its diff:
```python
import functools

import jax
import jax.numpy as jnp
from jax import lax
from jax.experimental import pallas as pl
from jax.experimental.pallas import tpu as pltpu
from jax.sharding import PartitionSpec as P

VMEM = pl.BlockSpec(memory_space=pltpu.VMEM)
SMEM = pl.BlockSpec(memory_space=pltpu.SMEM)


def params(mebibytes):
    return pltpu.CompilerParams(vmem_limit_bytes=mebibytes * 2**20)


def cost(flops, read):
    return pl.CostEstimate(flops=int(flops), bytes_accessed=int(read), transcendentals=0)


def swapped(block, axis, bit):
    count = lax.axis_size(axis)
    route = []
    for low in range(count):
        high = low | 1 << bit
        if high != low and high < count:
            route += [(low, high), (high, low)]
    return lax.ppermute(block, axis, route)


def orders(bits):
    return (list(range(bits)), list(range(1, bits)) + [0])


def across(block, step):
    pairs, auxes = lax.axis_size("pair"), lax.axis_size("aux")
    order = orders(auxes.bit_length() - 1)
    route = []
    for p in range(pairs):
        for m in range(auxes):
            route.append((p * auxes + m, p * auxes + (m ^ 1 << order[p % 2][step])))
    return lax.ppermute(block, ("pair", "aux"), route)


def after(value, *earlier):
    return lax.optimization_barrier((value, *earlier))[0]


def dot(expr, left, right):
    return jnp.einsum(
        expr, left, right, precision=lax.Precision.HIGH, preferred_element_type=jnp.float32
    )


def halves(value):
    high = value.astype(jnp.bfloat16)
    return high, (value - high.astype(jnp.float32)).astype(jnp.bfloat16)


def multiply(left, right, dims):
    (lh, ll), (rh, rl) = left, right
    one = functools.partial(
        lax.dot_general, dimension_numbers=(dims, ((), ())), preferred_element_type=jnp.float32
    )
    return one(lh, rh) + (one(lh, rl) + one(ll, rh))


def slot_of(plan_ref, side_ref, per_block, turn, h, own):
    half_count = per_block // 2
    upper = side_ref[0] // 2**turn % 2 == 1
    plain = h if own else half_count + h
    wanted = half_count + h if own else h
    inverse = 0
    for k in range(per_block):
        inverse += jnp.where(plan_ref[turn, k] == wanted, k, 0)
    return jnp.where(upper, inverse, plain)


def copy_kernel(plan_ref, side_ref, source_ref, target_ref):
    del plan_ref, side_ref
    target_ref[...] = source_ref[...]


def picked(three_index, plan, state, turn, own, start, count):
    per_block, width, depth = three_index.shape
    half_count = per_block // 2
    rows = count // 2 if count % 16 == 0 and start % (count // 2) == 0 else count

    def source(h, piece, plan_ref, side_ref):
        return (slot_of(plan_ref, side_ref, per_block, turn, h, own), start // rows + piece, 0)

    return pl.pallas_call(
        copy_kernel,
        out_shape=jax.ShapeDtypeStruct((half_count, count, depth), jnp.float32),
        grid_spec=pltpu.PrefetchScalarGridSpec(
            num_scalar_prefetch=2,
            grid=(half_count, count // rows),
            in_specs=[pl.BlockSpec((1, rows, depth), source)],
            out_specs=pl.BlockSpec((1, rows, depth), lambda h, piece, *_: (h, piece, 0)),
        ),
        compiler_params=params(24),
        cost_estimate=cost(0, 8 * half_count * count * depth),
    )(plan, state, three_index)


def integral_kernel(turn, blocks, plan_ref, state_ref, own_ref, peer_ref, keep_ref, give_ref, high, low):
    del plan_ref
    band = pl.program_id(1)

    @pl.when(band == 0)
    def _():
        high[...], low[...] = halves(peer_ref[0])

    own = halves(own_ref[0])
    value = multiply(own, (high[...], low[...]), ((1,), (1,)))
    rows = keep_ref.shape[1] * 2 // blocks
    core = state_ref[0] % 2
    inside = own_ref.shape[1] // rows
    for part in range(inside):
        index = band * inside + part
        side, place = index // (blocks // 2), index % (blocks // 2)
        piece = value[part * rows : (part + 1) * rows]

        @pl.when(side == core)
        def _():
            keep_ref[0, pl.ds(pl.multiple_of((place ^ state_ref[1]) * rows, rows), rows), :] = piece

        @pl.when(side != core)
        def _():
            give_ref[0, pl.ds(pl.multiple_of((place ^ state_ref[2]) * rows, rows), rows), :] = piece


def integral(three_index, peer, plan, state, turn, blocks):
    per_block, width, depth = three_index.shape
    half_count, count, _ = peer.shape
    bands = 4 if blocks % 4 == 0 else 1
    out = jax.ShapeDtypeStruct((half_count, width // 2, count), jnp.float32)
    whole = pl.BlockSpec((1, width // 2, count), lambda h, band, *_: (h, 0, 0))
    return pl.pallas_call(
        functools.partial(integral_kernel, turn, blocks),
        out_shape=(out, out),
        grid_spec=pltpu.PrefetchScalarGridSpec(
            num_scalar_prefetch=2,
            grid=(half_count, bands),
            in_specs=[
                pl.BlockSpec(
                    (1, width // bands, depth),
                    lambda h, band, p, s: (slot_of(p, s, per_block, turn, h, True), band, 0),
                ),
                pl.BlockSpec((1, count, depth), lambda h, band, *_: (h, 0, 0)),
            ],
            out_specs=(whole, whole),
            scratch_shapes=[pltpu.VMEM((count, depth), jnp.bfloat16)] * 2,
        ),
        compiler_params=params(40),
        cost_estimate=cost(
            6 * half_count * width * count * depth,
            4 * half_count * (width * depth + count * depth + width * count),
        ),
    )(plan, state, three_index, peer)


def amplitude_kernel(turn, per_block, rows_at, info_ref, state_ref, column_ref, row_ref, left_ref, right_ref, out_ref):
    half_count = per_block // 2
    rows = out_ref.shape[2]
    start = pl.multiple_of(rows_at(state_ref) * rows, rows)
    down = column_ref[pl.ds(start, rows), :]
    for who in range(2):
        p = state_ref[0] ^ who
        q = p ^ 2**turn
        upper = p // 2**turn % 2 == 1
        for h in range(half_count):
            low = info_ref[p, h]
            high = info_ref[q, half_count + h]
            for k in range(per_block):
                slot = info_ref[p, per_block * (turn + 1) + k]
                high += jnp.where(slot == half_count + h, info_ref[p, k], 0.0)
            wanted = info_ref[p, per_block * (turn + 1) + h]
            for k in range(per_block):
                low += jnp.where(wanted == k, info_ref[q, k], 0.0)
            energy = jnp.where(upper, high, low)
            gap = energy - down - row_ref[...]
            out_ref[who, h] = (left_ref[who, h] + right_ref[who, h]) / gap


def amplitude(info, state, column, row, left, right, turn, per_block):
    def rows_at(state_ref):
        return state_ref[0] % 2 * lax.div(column.shape[0], 2 * left.shape[2]) + state_ref[1]

    return pl.pallas_call(
        functools.partial(amplitude_kernel, turn, per_block, rows_at),
        out_shape=jax.ShapeDtypeStruct(left.shape, jnp.float32),
        in_specs=[SMEM, SMEM, VMEM, VMEM, VMEM, VMEM],
        out_specs=VMEM,
        compiler_params=params(16),
        cost_estimate=cost(8 * left.size, 12 * left.size),
    )(info, state, column, row, left, right)


def tilde_kernel(blocks, count, flips, state_ref, *refs):
    mine, came, (amp_ref, tilde_ref) = refs[:count], refs[count : 2 * count], refs[2 * count :]
    width = amp_ref.shape[2]
    rows = width // blocks
    core = state_ref[0] % 2
    for h in range(amp_ref.shape[0]):
        offset = 0
        for part in range(count):
            size = mine[part].shape[2]
            for place in range(blocks // 2):
                spot = pl.ds(pl.multiple_of((core * (blocks // 2) + (place ^ state_ref[1])) * rows, rows), rows)
                amp_ref[h, spot, offset : offset + size] = mine[part][h, place * rows : (place + 1) * rows, :]
                spot = pl.ds(pl.multiple_of(((1 - core) * (blocks // 2) + (place ^ state_ref[2])) * rows, rows), rows)
                amp_ref[h, spot, offset : offset + size] = came[part][h, place * rows : (place + 1) * rows, :]
            offset += size
        band = 128 if width % 128 == 0 else width
        for part in range(width // band):
            spot = slice(part * band, (part + 1) * band)
            straight, turned = amp_ref[h, spot, :], amp_ref[h, :, spot].T
            tilde_ref[h, spot, :] = 2.0 * turned - straight if flips else 2.0 * straight - turned


def tilde_of(state, mine, came, blocks, flips):
    half_count, half, _ = mine[0].shape
    out = jax.ShapeDtypeStruct((half_count, 2 * half, 2 * half), jnp.float32)
    return pl.pallas_call(
        functools.partial(tilde_kernel, blocks, len(mine), flips),
        out_shape=(out, out),
        in_specs=[SMEM] + [VMEM] * (2 * len(mine)),
        out_specs=(VMEM, VMEM),
        compiler_params=params(32),
        cost_estimate=cost(8 * half * half, 48 * half * half),
    )(state, *mine, *came)


def body(three_index, occupied_energy, virtual_energy, plan):
    per_block, width, depth = three_index.shape
    half_count = per_block // 2
    aux_count = lax.axis_size("aux")
    bits = aux_count.bit_length() - 1
    blocks = 2 * aux_count
    row_count = width // aux_count
    aux = lax.axis_index("aux").astype(jnp.int32)
    row_start = aux * row_count
    slots = jnp.arange(per_block, dtype=jnp.int32)
    rounds = plan.shape[0]
    position = lax.axis_index("pair").astype(jnp.int32)

    def mask(order):
        return sum((aux >> bit & 1) << bits - 1 - step for step, bit in enumerate(order))

    first_mask, second_mask = (mask(order) for order in orders(bits))
    core = position % 2
    state = jnp.stack(
        [
            position,
            jnp.where(core == 0, first_mask, second_mask),
            jnp.where(core == 0, second_mask, first_mask),
        ]
    ).astype(jnp.int32)

    cuts = 2
    step = width // cuts
    firsts = [None] * rounds
    seconds = [None] * rounds
    for turn in range(1, rounds):
        firsts[turn] = [
            swapped(picked(three_index, plan, state, turn, False, cut * step, step), "pair", turn)
            for cut in range(cuts)
        ]
    other = swapped(three_index, "pair", 0)
    info = lax.all_gather(
        jnp.concatenate([occupied_energy, plan.astype(jnp.float32).reshape(-1)]), "pair", axis=0
    )
    where = []
    for turn in range(rounds):
        table = plan[turn]
        upper = position // 2**turn % 2 == 1
        inverse = jnp.sum(jnp.where(table[None, :] == slots[:, None], slots[None, :], 0), axis=1)
        own_slots = jnp.where(upper, inverse[half_count:], slots[:half_count])
        give_slots = jnp.where(upper, inverse[:half_count], slots[half_count:])
        where.append((own_slots, give_slots))
        if turn == 0:
            firsts[0] = [other[jnp.where(upper, slots[half_count:], table[:half_count])]]
            seconds[0] = other[jnp.where(upper, slots[:half_count], table[half_count:])]
        else:
            own = picked(three_index, plan, state, turn, True, 0, width)
            seconds[turn] = swapped(own, "pair", turn)

    column = virtual_energy[:, None]
    gradient = jnp.zeros(three_index.shape, jnp.float32)
    density = jnp.zeros((row_count, width), jnp.float32)
    begun = []
    for turn in range(rounds):
        offset = 0
        for first in firsts[turn]:
            if begun:
                first = after(first, begun[-1][4])
            keep, give = integral(three_index, first, plan, state, turn, blocks)
            size = first.shape[1]
            begun.append((turn, offset, size, keep, give))
            offset += size
    gathered = [([], []) for _ in range(rounds)]
    for turn, offset, size, keep, give in begun:
        value = jnp.stack([keep, swapped(give, "pair", 0)])
        for stage in range(bits):
            half = value.shape[2] // 2
            came = across(value[:, :, half:], stage)
            if stage < bits - 1:
                value = value[:, :, :half] + came
            else:
                value = amplitude(
                    info, state, column, virtual_energy[None, offset : offset + size],
                    value[:, :, :half], came, turn, per_block,
                )
        if turn > 0:
            value = jnp.concatenate([value, swapped(value, "pair", turn)], axis=1)
        for stage in reversed(range(bits)):
            value = jnp.concatenate([value, across(value, stage)], axis=2)
        mine, came = gathered[turn]
        if turn == 0:
            both = swapped(value, "pair", 0)
            mine.append((value[0], value[1]))
            came.append((both[1], both[0]))
        else:
            both = swapped(value[1], "pair", 0)
            mine.append((value[0, :half_count], value[0, half_count:]))
            came.append((both[:half_count], both[half_count:]))
    for turn in range(rounds):
        mine, came = gathered[turn]
        amp, tilde = tilde_of(state, [m[0] for m in mine], [c[0] for c in came], blocks, False)
        _, tilde_peer = tilde_of(state, [m[1] for m in mine], [c[1] for c in came], blocks, True)
        own_slots, give_slots = where[turn]
        first = jnp.concatenate(firsts[turn], axis=1)
        gradient = gradient.at[own_slots].add(dot("hab,hbp->hap", tilde, first))
        gradient = gradient.at[give_slots].add(dot("hab,hbp->hap", tilde_peer, seconds[turn]))
        rows = lax.dynamic_slice_in_dim(amp, row_start, row_count, 1)
        columns = lax.dynamic_slice_in_dim(amp, row_start, row_count, 2)
        density = density + dot("hac,hbc->ab", rows, tilde) + dot("hca,hcb->ab", columns, tilde)
    density = lax.psum_scatter(density, "pair", scatter_dimension=1, tiled=True)
    return (gradient, density)


def solution(mesh):
    in_specs = (P("pair", None, "aux"), P("pair"), P(), P(None, "pair"))
    out_specs = (P("pair", None, "aux"), P("aux", "pair"))
    return jax.shard_map(body, mesh=mesh, in_specs=in_specs, out_specs=out_specs, check_vma=False)
```

time: 469 us -> 336 us (0.72)
  waiting for transfers between devices: 328 us -> 128 us
  starting transfers between devices: 8.37 us -> 61.6 us
  Pallas kernels: 3.59 us -> 34.5 us
  matrix products: 60.2 us -> 37 us
  other arithmetic: 3.99 us -> 13.2 us
  local copies, waits for them, and re-layouts: 41.2 us -> 32 us
  blocking collectives: 0 us -> 7.68 us
    all_gather x2 -> x0, waiting for transfers between devices: 134 us -> none  [body(): amp, amp_peer = lax.all_gather(both, 'aux', axis=2, tiled=True)]
    reduce_scatter x2 -> x0, waiting for transfers between devices: 130 us -> none  [body(): parts.append(lax.psum_scatter(part, 'aux', scatter_dimension=1, tiled=True))]
    ppermute x0 -> x18, waiting for transfers between devices: none -> 77.8 us  [across(): return lax.ppermute(block, ('pair', 'aux'), route)]
    ppermute x0 -> x18, starting transfers between devices: none -> 33.4 us  [across(): return lax.ppermute(block, ('pair', 'aux'), route)]
    pallas_call x2 -> x13, Pallas kernels: 3.59 us -> 34.5 us  [the longest x3 19.5 us: integral(): pl.pallas_call(functools.partial(integral_kernel, turn, blocks), out_shap...]
    another operation x6 -> x0, local copies, waits for them, and re-layouts: 23.7 us -> none  [body(): amp, amp_peer = lax.all_gather(both, 'aux', axis=2, tiled=True)]
    dot_general x10 -> x8, matrix products: 60.2 us -> 37 us  [dot(): jnp.einsum(expr, left, right, precision=lax.Precision.HIGH, preferred_ele...]
    ppermute x7 -> x12, starting transfers between devices: 7.99 us -> 28.1 us  [swapped(): return lax.ppermute(block, axis, route)]
  transfers between devices with their start and end apart: 12 -> 31, of which waited for: 8 -> 12; matrix products, arithmetic and copies ran while one was open for 18% -> 22% of each run, Pallas kernels for 1% -> 10%
where the time goes in v2:
time: 336 us; the launch traced here: 335 us
  waiting for transfers between devices  128 us (38%)
  starting transfers between devices  61.6 us (18%)
  matrix products  37 us (11%)
  Pallas kernels  34.5 us (10%)
  local copies, waits for them, and re-layouts  32 us (10%)
  between operations  21.3 us (6%)
  other arithmetic  13.2 us (4%)
  blocking collectives  7.68 us (2%)
    ppermute x18, waiting for transfers between devices, across(): return lax.ppermute(block, ('pair', 'aux'), route)  77.8 us
    ppermute x12, waiting for transfers between devices, swapped(): return lax.ppermute(block, axis, route)  50.2 us
    dot_general x8, matrix products, dot(): jnp.einsum(expr, left, right, precision=lax.Precision.HIGH, preferred_ele...  37 us
    ppermute x18, starting transfers between devices, across(): return lax.ppermute(block, ('pair', 'aux'), route)  33.4 us
    ppermute x12, starting transfers between devices, swapped(): return lax.ppermute(block, axis, route)  28.1 us
    pallas_call x3, Pallas kernels, integral(): pl.pallas_call(functools.partial(integral_kernel, turn, blocks), out_shap...  19.5 us
    unnamed x74, local copies, waits for them, and re-layouts  11.2 us
    unnamed x1, blocking collectives  7.68 us
  transfers between devices with their start and end apart: 31, of which 12 were waited for; matrix products, arithmetic and copies ran while one was open for 22% of the time, Pallas kernels for 10%

profile of v2, /device:TPU:0, one launch (start us, length us, event | category | flops | bytes accessed | tf_op | source)
XLA Modules:
  0.0 335.1 jit_solution(14168683267530211587)
XLA Ops:
  7.8 2.8 copy-done
  11.3 1.8 shard_map.63
  13.1 2.6 collective-permute-start.9
  15.6 1.8 shard_map.66
  20.0 2.4 constant_dynamic-slice_fusion.peer_ref
  23.7 9.4 %shard_map.59 = (f32[1,384,768]{2,1,0:T(8,128)S(1)}, f32[1,384,768]{2,1,0:T(8,128)}) custom-call(s32[2,2]{1,0:T(2,128)S(1)} %copy-done.21, s32[3]{0:T(128)S(1)} %pad_add_fusion.8.state_ref.side_ref, f32[2,768,1024]{2,1,0:T(8,128)S(1)} %copy-done.1, f32[1,768,1024]{2,1,0:T(8,128)S(1)} %constant_dynamic-slice_fusion.peer_ref), custom_call_target="tpu_custom_call" | custom-call | flops 3623878656 | bytes 8650752 | tf_op jit(solution)/shard_map/pallas_call | solution.py:140
  33.3 17.7 %collective-permute-done.9.peer_ref = f32[1,384,1024]{2,1,0:T(8,128)S(1)} collective-permute-done((f32[1,384,1024]{2,1,0:T(8,128)}, f32[1,384,1024]{2,1,0:T(8,128)S(1)}, u32[]{:S(2)}, u32[]{:S(2)}) %collective-permute-start.9) | collective-permute-done | bytes 1572896 | tf_op jit(solution)/shard_map/ppermute | solution.py:29
  51.1 5.0 %shard_map.64 = (f32[1,384,384]{2,1,0:T(8,128)S(1)}, f32[1,384,384]{2,1,0:T(8,128)S(1)}) custom-call(s32[2,2]{1,0:T(2,128)S(1)} %copy-done.21, s32[3]{0:T(128)S(1)} %pad_add_fusion.8.state_ref.side_ref, f32[2,768,1024]{2,1,0:T(8,128)S(1)} %copy-done.1, f32[1,384,1024]{2,1,0:T(8,128)S(1)} %collective-permute-done.9.peer_ref), custom_call_target="tpu_custom_call" | custom-call | flops 1811939328 | bytes 5898240 | tf_op jit(solution)/shard_map/pallas_call | solution.py:140
  56.2 28.3 %collective-permute-done.18.peer_ref = f32[1,384,1024]{2,1,0:T(8,128)S(1)} collective-permute-done((f32[1,384,1024]{2,1,0:T(8,128)}, f32[1,384,1024]{2,1,0:T(8,128)S(1)}, u32[]{:S(2)}, u32[]{:S(2)}) %collective-permute-start.18) | collective-permute-done | bytes 1572896 | tf_op jit(solution)/shard_map/ppermute | solution.py:29
  84.6 5.0 %shard_map.67 = (f32[1,384,384]{2,1,0:T(8,128)S(1)}, f32[1,384,384]{2,1,0:T(8,128)S(1)}) custom-call(s32[2,2]{1,0:T(2,128)S(1)} %copy-done.21, s32[3]{0:T(128)S(1)} %pad_add_fusion.8.state_ref.side_ref, f32[2,768,1024]{2,1,0:T(8,128)S(1)} %copy-done.1, f32[1,384,1024]{2,1,0:T(8,128)S(1)} %collective-permute-done.18.peer_ref), custom_call_target="tpu_custom_call" | custom-call | flops 1811939328 | bytes 5898240 | tf_op jit(solution)/shard_map/pallas_call | solution.py:140
  90.6 1.7 collective-permute-start.11
  98.0 2.2 pad_maximum_fusion.3
  103.0 1.6 collective-permute-start.12
  104.9 7.7 %all-reduce = f32[24]{0:T(128)S(1)} all-reduce(f32[24]{0:T(128)S(1)} %maximum_dynamic-update-slice_fusion), channel_id=2, replica_groups=mesh['pair'=4,'aux'=8] {'pair'}, use_global_device_ids=true, to_apply=%add | all-reduce | flops 24 | bytes 192
  117.3 4.7 %collective-permute-start.13 = (f32[2,1,48,384]{3,2,1,0:T(8,128)S(1)}, f32[2,1,48,384]{3,2,1,0:T(8,128)S(1)}, u32[]{:S(2)}, u32[]{:S(2)}) collective-permute-start(f32[2,1,48,384]{3,2,1,0:T(8,128)S(1)} %get-tuple-element.120), channel_id=1, source_target_pairs={{0,4},{1,5},{2,6},{3,7},{4,0},{5,1},{6,2},{7,3},{8,9},{9,8},{10,11... | collective-permute-start | bytes 442376 | tf_op jit(solution)/shard_map/ppermute | solution.py:43
  121.9 5.8 %collective-permute-done.21 = f32[2,1,96,384]{3,2,1,0:T(8,128)S(1)} collective-permute-done((f32[2,1,96,384]{3,2,1,0:T(8,128)S(1)}, f32[2,1,96,384]{3,2,1,0:T(8,128)S(1)}, u32[]{:S(2)}, u32[]{:S(2)}) %collective-permute-start.21) | collective-permute-done | bytes 294944 | tf_op jit(solution)/shard_map/ppermute | solution.py:43
  128.5 1.6 collective-permute-start.14
  130.1 1.5 fusion.40
  131.6 6.9 %collective-permute-start.3 = (f32[2,1,96,768]{3,2,1,0:T(8,128)S(1)}, f32[2,1,96,768]{3,2,1,0:T(8,128)S(1)}, u32[]{:S(2)}, u32[]{:S(2)}) collective-permute-start(f32[2,1,96,768]{3,2,1,0:T(8,128)S(1)} %slice.295), channel_id=1, source_target_pairs={{0,2},{1,3},{2,0},{3,1},{4,6},{5,7},{6,4},{7,5},{8,12},{9,13},{10,... | collective-permute-start | bytes 1769480 | tf_op jit(solution)/shard_map/ppermute | solution.py:43
  138.6 3.4 %collective-permute-start.22 = (f32[2,1,48,384]{3,2,1,0:T(8,128)S(1)}, f32[2,1,48,384]{3,2,1,0:T(8,128)S(1)}, u32[]{:S(2)}, u32[]{:S(2)}) collective-permute-start(f32[2,1,48,384]{3,2,1,0:T(8,128)S(1)} %get-tuple-element.118), channel_id=1, source_target_pairs={{0,4},{1,5},{2,6},{3,7},{4,0},{5,1},{6,2},{7,3},{8,9},{9,8},{10,11... | collective-permute-start | bytes 442376 | tf_op jit(solution)/shard_map/ppermute | solution.py:43
  142.1 11.0 %collective-permute-done.22.right_ref = f32[2,1,48,384]{3,2,1,0:T(8,128)S(1)} collective-permute-done((f32[2,1,48,384]{3,2,1,0:T(8,128)S(1)}, f32[2,1,48,384]{3,2,1,0:T(8,128)S(1)}, u32[]{:S(2)}, u32[]{:S(2)}) %collective-permute-start.22) | collective-permute-done | bytes 147488 | tf_op jit(solution)/shard_map/ppermute | solution.py:43
  154.9 4.1 %collective-permute-done.23 = f32[2,1,48,384]{3,2,1,0:T(8,128)S(1)} collective-permute-done((f32[2,1,48,384]{3,2,1,0:T(8,128)S(1)}, f32[2,1,48,384]{3,2,1,0:T(8,128)S(1)}, u32[]{:S(2)}, u32[]{:S(2)}) %collective-permute-start.23) | collective-permute-done | bytes 147488 | tf_op jit(solution)/shard_map/ppermute | solution.py:29
  159.0 3.5 %collective-permute-start.24 = (f32[2,2,48,384]{3,2,1,0:T(8,128)S(1)}, f32[2,2,48,384]{3,2,1,0:T(8,128)S(1)}, u32[]{:S(2)}, u32[]{:S(2)}) collective-permute-start(f32[2,2,48,384]{3,2,1,0:T(8,128)S(1)} %pad_maximum_fusion.13), channel_id=1, source_target_pairs={{0,4},{1,5},{2,6},{3,7},{4,0},{5,1},{6,2},{7,3},{8,9},{9,8},{10,11... | collective-permute-start | bytes 884744 | tf_op jit(solution)/shard_map/ppermute | solution.py:43
  162.5 11.0 %collective-permute-done.15 = f32[2,2,48,384]{3,2,1,0:T(8,128)S(1)} collective-permute-done((f32[2,2,48,384]{3,2,1,0:T(8,128)S(1)}, f32[2,2,48,384]{3,2,1,0:T(8,128)S(1)}, u32[]{:S(2)}, u32[]{:S(2)}) %collective-permute-start.15) | collective-permute-done | bytes 294944 | tf_op jit(solution)/shard_map/ppermute | solution.py:43
  173.8 3.0 collective-permute-start.4
  176.8 3.2 collective-permute-done.24
  180.1 15.7 %collective-permute-done.4.right_ref = f32[2,1,48,768]{3,2,1,0:T(8,128)S(1)} collective-permute-done((f32[2,1,48,768]{3,2,1,0:T(8,128)S(1)}, f32[2,1,48,768]{3,2,1,0:T(8,128)S(1)}, u32[]{:S(2)}, u32[]{:S(2)}) %collective-permute-start.4) | collective-permute-done | bytes 294944 | tf_op jit(solution)/shard_map/ppermute | solution.py:43
  198.2 12.1 %collective-permute-done.5 = f32[2,1,48,768]{3,2,1,0:T(8,128)S(1)} collective-permute-done((f32[2,1,48,768]{3,2,1,0:T(8,128)S(1)}, f32[2,1,48,768]{3,2,1,0:T(8,128)S(1)}, u32[]{:S(2)}, u32[]{:S(2)}) %collective-permute-start.5) | collective-permute-done | bytes 294944 | tf_op jit(solution)/shard_map/ppermute | solution.py:43
  210.5 7.8 %collective-permute-done.25 = f32[2,2,96,384]{3,2,1,0:T(8,128)S(1)} collective-permute-done((f32[2,2,96,384]{3,2,1,0:T(8,128)S(1)}, f32[2,2,96,384]{3,2,1,0:T(8,128)S(1)}, u32[]{:S(2)}, u32[]{:S(2)}) %collective-permute-start.25) | collective-permute-done | bytes 589856 | tf_op jit(solution)/shard_map/ppermute | solution.py:43
  218.4 1.6 collective-permute-start.26
  220.0 11.0 %collective-permute-done.6 = f32[2,1,96,768]{3,2,1,0:T(8,128)S(1)} collective-permute-done((f32[2,1,96,768]{3,2,1,0:T(8,128)S(1)}, f32[2,1,96,768]{3,2,1,0:T(8,128)S(1)}, u32[]{:S(2)}, u32[]{:S(2)}) %collective-permute-start.6) | collective-permute-done | bytes 589856 | tf_op jit(solution)/shard_map/ppermute | solution.py:43
  231.0 1.6 collective-permute-start.7
  232.6 2.3 shard_map.71
  238.3 10.3 %collective-permute-start.28 = (f32[2,384,384]{2,1,0:T(8,128)}, f32[2,384,384]{2,1,0:T(8,128)}, u32[]{:S(2)}, u32[]{:S(2)}) collective-permute-start(f32[2,384,384]{2,1,0:T(8,128)} %slice_bitcast_fusion), channel_id=1, source_target_pairs={{0,8},{8,0},{16,24},{24,16},{1,9},{9,1},{17,25},{25,17},{2,10},{10... | collective-permute-start | bytes 3538952 | tf_op jit(solution)/shard_map/ppermute | solution.py:29
  248.6 1.6 pad_maximum_fusion
  250.2 11.2 %collective-permute-start.8 = (f32[2,1,384,768]{3,2,1,0:T(8,128)}, f32[2,1,384,768]{3,2,1,0:T(8,128)}, u32[]{:S(2)}, u32[]{:S(2)}) collective-permute-start(f32[2,1,384,768]{3,2,1,0:T(8,128)} %pad_maximum_fusion), channel_id=1, source_target_pairs={{0,8},{8,0},{16,24},{24,16},{1,9},{9,1},{17,25},{25,17},{2,10},{10... | collective-permute-start | bytes 7077896 | tf_op jit(solution)/shard_map/ppermute | solution.py:29
  272.3 2.2 shard_map.70
  277.2 1.8 slice_bitcast_fusion.3
  279.0 2.8 slice_bitcast_fusion.2
  284.2 2.0 fusion.47
  286.2 1.9 copy.15
  289.4 2.1 shard_map.62
  291.5 3.5 %broadcast_in_dim.47 = f32[2,768,1024]{2,1,0:T(8,128)} broadcast(f32[]{:T(128)} %constant.128.clone.1), dimensions={} | broadcast | bytes 6291460 | tf_op jit(solution)/shard_map/broadcast_in_dim | solution.py:291
  295.0 6.5 %bitcast_dynamic-update-slice_fusion = f32[2,768,1024]{2,1,0:T(8,128)} fusion(f32[2,768,1024]{2,1,0:T(8,128)} %broadcast_in_dim.47, s32[]{:T(128)} %bitcast.15, f32[1,768,1024]{2,1,0:T(8,128)S(1)} %copy-done.5, f32[1,768,768]{2,1,0:T(8,128)S(1)} %get-tuple-element.66, pred[]{:T(512)} %get-tuple-element.128), kind=kOutput, calls=%fused_computation.14 | convolution fusion | flops 3624665088 | bytes 8651776 | tf_op jit(solution)/shard_map/hab,hbp->hap/dot_general | solution.py:51
  301.6 9.0 %fusion = f32[2,768,1024]{2,1,0:T(8,128)} fusion(f32[2,768,1024]{2,1,0:T(8,128)} %bitcast_dynamic-update-slice_fusion, s32[]{:T(128)} %bitcast.16, pred[]{:T(512)} %get-tuple-element.129, f32[2,768,1024]{2,1,0:T(8,128)} %collective-permute-done, s32[]{:T(128)} %bitcast.21, f32[1,768,768]{2,1,0:T(8,128)S(1)} %get-tuple-element.67), kind=kOutput, calls=%fused_computation.3 | convolution fusion | flops 3625451520 | bytes 11798016 | tf_op jit(solution)/shard_map/hab,hbp->hap/dot_general | solution.py:51
  310.6 7.5 %fusion.1 = f32[2,768,1024]{2,1,0:T(8,128)} fusion(f32[2,768,1024]{2,1,0:T(8,128)} %fusion, s32[]{:T(128)} %bitcast.26, pred[]{:T(512)} %get-tuple-element.101, f32[1,384,1024]{2,1,0:T(8,128)S(1)} %copy-done.9, f32[1,384,1024]{2,1,0:T(8,128)S(1)} %copy-done.7, f32[1,768,768]{2,1,0:T(8,128)S(1)} %copy-done.3), kind=kOutput, calls=%fused_computation.4 | convolution fusion | flops 3626237952 | bytes 11797504 | tf_op jit(solution)/shard_map/hab,hbp->hap/dot_general | solution.py:51
  318.1 8.6 %fusion.2 = f32[2,768,1024]{2,1,0:T(8,128)} fusion(f32[2,768,1024]{2,1,0:T(8,128)} %fusion.1, s32[]{:T(128)} %bitcast.38, pred[]{:T(512)} %get-tuple-element.100, f32[1,768,1024]{2,1,0:T(8,128)} %collective-permute-done.29, f32[1,768,768]{2,1,0:T(8,128)S(1)} %copy-done.19), kind=kOutput, calls=%fused_computation.5 | convolution fusion | flops 3625451520 | bytes 11797504 | tf_op jit(solution)/shard_map/hab,hbp->hap/dot_general | solution.py:51
  326.6 1.6 copy.16
  (167 shorter events, 39.5 us)
Async XLA Ops:
  7.2 319.5 %reduce-scatter.4.cloned.1.call-start = ((), (), s32[]{:S(2)}) async-start(), calls=%async_computation.1 | async-start | bytes 491520
  7.2 12.8 %collective-permute-start = (f32[2,768,1024]{2,1,0:T(8,128)}, f32[2,768,1024]{2,1,0:T(8,128)}, u32[]{:S(2)}, u32[]{:S(2)}) collective-permute-start(f32[2,768,1024]{2,1,0:T(8,128)} %source_ref.5), channel_id=1, source_target_pairs={{0,8},{8,0},{16,24},{24,16},{1,9},{9,1},{17,25},{25,17},{2,10},{10... | collective-permute-start | bytes 18874376 | tf_op jit(solution)/shard_map/ppermute | solution.py:29
  13.1 38.0 %collective-permute-start.9 = (f32[1,384,1024]{2,1,0:T(8,128)}, f32[1,384,1024]{2,1,0:T(8,128)S(1)}, u32[]{:S(2)}, u32[]{:S(2)}) collective-permute-start(f32[1,384,1024]{2,1,0:T(8,128)} %shard_map.63), channel_id=1, source_target_pairs={{0,16},{16,0},{8,24},{24,8},{1,17},{17,1},{9,25},{25,9},{2,18},{18... | collective-permute-start | bytes 4718600 | tf_op jit(solution)/shard_map/ppermute | solution.py:29
  17.4 67.2 %collective-permute-start.18 = (f32[1,384,1024]{2,1,0:T(8,128)}, f32[1,384,1024]{2,1,0:T(8,128)S(1)}, u32[]{:S(2)}, u32[]{:S(2)}) collective-permute-start(f32[1,384,1024]{2,1,0:T(8,128)} %shard_map.66), channel_id=1, source_target_pairs={{0,16},{16,0},{8,24},{24,8},{1,17},{17,1},{9,25},{25,9},{2,18},{18... | collective-permute-start | bytes 4718600 | tf_op jit(solution)/shard_map/ppermute | solution.py:29
  23.7 9.4 %copy-start.4 = (f32[1,768,1024]{2,1,0:T(8,128)}, f32[1,768,1024]{2,1,0:T(8,128)S(1)}, u32[]{:S(2)}) copy-start(f32[1,768,1024]{2,1,0:T(8,128)S(1)} %constant_dynamic-slice_fusion.peer_ref) | copy-start | bytes 9437188
  33.2 23.0 %copy-start.10 = (f32[1,384,768]{2,1,0:T(8,128)}, f32[1,384,768]{2,1,0:T(8,128)S(1)}, u32[]{:S(2)}) copy-start(f32[1,384,768]{2,1,0:T(8,128)S(1)} %get-tuple-element.64) | copy-start | bytes 3538948
  33.2 64.8 %collective-permute-start.1 = (f32[1,384,768]{2,1,0:T(8,128)}, f32[1,384,768]{2,1,0:T(8,128)}, u32[]{:S(2)}, u32[]{:S(2)}) collective-permute-start(f32[1,384,768]{2,1,0:T(8,128)} %get-tuple-element.65), channel_id=1, source_target_pairs={{0,8},{8,0},{16,24},{24,16},{1,9},{9,1},{17,25},{25,17},{2,10},{10... | collective-permute-start | bytes 3538952 | tf_op jit(solution)/shard_map/ppermute | solution.py:29
  56.2 33.6 %copy-start.16 = (f32[1,384,384]{2,1,0:T(8,128)}, f32[1,384,384]{2,1,0:T(8,128)S(1)}, u32[]{:S(2)}) copy-start(f32[1,384,384]{2,1,0:T(8,128)S(1)} %get-tuple-element.69) | copy-start | bytes 1769476
  56.2 33.6 %collective-permute-start.10 = (f32[1,384,384]{2,1,0:T(8,128)S(1)}, f32[1,384,384]{2,1,0:T(8,128)S(1)}, u32[]{:S(2)}, u32[]{:S(2)}) collective-permute-start(f32[1,384,384]{2,1,0:T(8,128)S(1)} %get-tuple-element.70), channel_id=1, source_target_pairs={{0,8},{8,0},{16,24},{24,16},{1,9},{9,1},{17,25},{25,17},{2,10},{10... | collective-permute-start | bytes 1769480 | tf_op jit(solution)/shard_map/ppermute | solution.py:29
  89.6 8.3 %copy-start.11 = (f32[1,384,768]{2,1,0:T(8,128)S(1)}, f32[1,384,768]{2,1,0:T(8,128)}, u32[]{:S(2)}) copy-start(f32[1,384,768]{2,1,0:T(8,128)} %copy-done.10) | copy-start | bytes 3538948
  89.7 2.7 collective-permute-start.19
  90.6 10.4 %collective-permute-start.11 = (f32[2,1,192,384]{3,2,1,0:T(8,128)}, f32[2,1,192,384]{3,2,1,0:T(8,128)}, u32[]{:S(2)}, u32[]{:S(2)}) collective-permute-start(f32[2,1,192,384]{3,2,1,0:T(8,128)} %pad_maximum_fusion.8), channel_id=1, source_target_pairs={{0,1},{1,0},{2,3},{3,2},{4,5},{5,4},{6,7},{7,6},{8,10},{9,11},{10,... | collective-permute-start | bytes 1769480 | tf_op jit(solution)/shard_map/ppermute | solution.py:43
  92.4 8.7 %copy-start.17 = (f32[1,384,384]{2,1,0:T(8,128)S(1)}, f32[1,384,384]{2,1,0:T(8,128)}, u32[]{:S(2)}) copy-start(f32[1,384,384]{2,1,0:T(8,128)} %copy-done.16) | copy-start | bytes 1769476
  92.4 21.0 %collective-permute-start.20 = (f32[2,1,192,384]{3,2,1,0:T(8,128)S(1)}, f32[2,1,192,384]{3,2,1,0:T(8,128)}, u32[]{:S(2)}, u32[]{:S(2)}) collective-permute-start(f32[2,1,192,384]{3,2,1,0:T(8,128)S(1)} %pad_maximum_fusion.7), channel_id=1, source_target_pairs={{0,1},{1,0},{2,3},{3,2},{4,5},{5,4},{6,7},{7,6},{8,10},{9,11},{10,... | collective-permute-start | bytes 1769480 | tf_op jit(solution)/shard_map/ppermute | solution.py:43
  93.6 7.5 %copy-start.26 = (f32[1,384,384]{2,1,0:T(8,128)S(1)}, f32[1,384,384]{2,1,0:T(8,128)}, u32[]{:S(2)}) copy-start(f32[1,384,384]{2,1,0:T(8,128)} %copy-done.25) | copy-start | bytes 1769476
  100.1 13.3 %copy-start.15 = (f32[1,384,384]{2,1,0:T(8,128)S(1)}, f32[1,384,384]{2,1,0:T(8,128)}, u32[]{:S(2)}) copy-start(f32[1,384,384]{2,1,0:T(8,128)} %copy-done.14) | copy-start | bytes 1769476
  100.1 29.9 %collective-permute-start.2 = (f32[2,1,192,768]{3,2,1,0:T(8,128)}, f32[2,1,192,768]{3,2,1,0:T(8,128)}, u32[]{:S(2)}, u32[]{:S(2)}) collective-permute-start(f32[2,1,192,768]{3,2,1,0:T(8,128)} %pad_maximum_fusion.3), channel_id=1, source_target_pairs={{0,1},{1,0},{2,3},{3,2},{4,5},{5,4},{6,7},{7,6},{8,10},{9,11},{10,... | collective-permute-start | bytes 3538952 | tf_op jit(solution)/shard_map/ppermute | solution.py:43
  103.0 13.2 %collective-permute-start.12 = (f32[2,1,96,384]{3,2,1,0:T(8,128)}, f32[2,1,96,384]{3,2,1,0:T(8,128)}, u32[]{:S(2)}, u32[]{:S(2)}) collective-permute-start(f32[2,1,96,384]{3,2,1,0:T(8,128)} %slice.305), channel_id=1, source_target_pairs={{0,2},{1,3},{2,0},{3,1},{4,6},{5,7},{6,4},{7,5},{8,12},{9,13},{10,... | collective-permute-start | bytes 884744 | tf_op jit(solution)/shard_map/ppermute | solution.py:43
  104.8 11.5 %copy-start.28 = (f32[2,1,192,384]{3,2,1,0:T(8,128)S(1)}, f32[2,1,192,384]{3,2,1,0:T(8,128)}, u32[]{:S(2)}) copy-start(f32[2,1,192,384]{3,2,1,0:T(8,128)} %copy-done.27) | copy-start | bytes 1769476
  114.6 15.5 %copy-start.12 = (f32[1,384,768]{2,1,0:T(8,128)S(1)}, f32[1,384,768]{2,1,0:T(8,128)}, u32[]{:S(2)}) copy-start(f32[1,384,768]{2,1,0:T(8,128)} %copy-done.10) | copy-start | bytes 3538948
  114.6 13.1 %collective-permute-start.21 = (f32[2,1,96,384]{3,2,1,0:T(8,128)S(1)}, f32[2,1,96,384]{3,2,1,0:T(8,128)S(1)}, u32[]{:S(2)}, u32[]{:S(2)}) collective-permute-start(f32[2,1,96,384]{3,2,1,0:T(8,128)S(1)} %slice.311), channel_id=1, source_target_pairs={{0,2},{1,3},{2,0},{3,1},{4,6},{5,7},{6,4},{7,5},{8,12},{9,13},{10,... | collective-permute-start | bytes 884744 | tf_op jit(solution)/shard_map/ppermute | solution.py:43
  117.3 10.5 %collective-permute-start.13 = (f32[2,1,48,384]{3,2,1,0:T(8,128)S(1)}, f32[2,1,48,384]{3,2,1,0:T(8,128)S(1)}, u32[]{:S(2)}, u32[]{:S(2)}) collective-permute-start(f32[2,1,48,384]{3,2,1,0:T(8,128)S(1)} %get-tuple-element.120), channel_id=1, source_target_pairs={{0,4},{1,5},{2,6},{3,7},{4,0},{5,1},{6,2},{7,3},{8,9},{9,8},{10,11... | collective-permute-start | bytes 442376 | tf_op jit(solution)/shard_map/ppermute | solution.py:43
  128.5 13.5 %collective-permute-start.14 = (f32[2,1,48,384]{3,2,1,0:T(8,128)S(1)}, f32[2,1,48,384]{3,2,1,0:T(8,128)S(1)}, u32[]{:S(2)}, u32[]{:S(2)}) collective-permute-start(f32[2,1,48,384]{3,2,1,0:T(8,128)S(1)} %shard_map.65), channel_id=1, source_target_pairs={{0,16},{16,0},{8,24},{24,8},{1,17},{17,1},{9,25},{25,9},{2,18},{18... | collective-permute-start | bytes 442376 | tf_op jit(solution)/shard_map/ppermute | solution.py:29
  131.6 42.0 %collective-permute-start.3 = (f32[2,1,96,768]{3,2,1,0:T(8,128)S(1)}, f32[2,1,96,768]{3,2,1,0:T(8,128)S(1)}, u32[]{:S(2)}, u32[]{:S(2)}) collective-permute-start(f32[2,1,96,768]{3,2,1,0:T(8,128)S(1)} %slice.295), channel_id=1, source_target_pairs={{0,2},{1,3},{2,0},{3,1},{4,6},{5,7},{6,4},{7,5},{8,12},{9,13},{10,... | collective-permute-start | bytes 1769480 | tf_op jit(solution)/shard_map/ppermute | solution.py:43
  138.6 14.6 %collective-permute-start.22 = (f32[2,1,48,384]{3,2,1,0:T(8,128)S(1)}, f32[2,1,48,384]{3,2,1,0:T(8,128)S(1)}, u32[]{:S(2)}, u32[]{:S(2)}) collective-permute-start(f32[2,1,48,384]{3,2,1,0:T(8,128)S(1)} %get-tuple-element.118), channel_id=1, source_target_pairs={{0,4},{1,5},{2,6},{3,7},{4,0},{5,1},{6,2},{7,3},{8,9},{9,8},{10,11... | collective-permute-start | bytes 442376 | tf_op jit(solution)/shard_map/ppermute | solution.py:43
  142.0 31.6 %collective-permute-start.15 = (f32[2,2,48,384]{3,2,1,0:T(8,128)S(1)}, f32[2,2,48,384]{3,2,1,0:T(8,128)S(1)}, u32[]{:S(2)}, u32[]{:S(2)}) collective-permute-start(f32[2,2,48,384]{3,2,1,0:T(8,128)S(1)} %pad_maximum_fusion.12), channel_id=1, source_target_pairs={{0,4},{1,5},{2,6},{3,7},{4,0},{5,1},{6,2},{7,3},{8,9},{9,8},{10,11... | collective-permute-start | bytes 884744 | tf_op jit(solution)/shard_map/ppermute | solution.py:43
  153.8 5.2 %collective-permute-start.23 = (f32[2,1,48,384]{3,2,1,0:T(8,128)S(1)}, f32[2,1,48,384]{3,2,1,0:T(8,128)S(1)}, u32[]{:S(2)}, u32[]{:S(2)}) collective-permute-start(f32[2,1,48,384]{3,2,1,0:T(8,128)S(1)} %shard_map.68), channel_id=1, source_target_pairs={{0,16},{16,0},{8,24},{24,8},{1,17},{17,1},{9,25},{25,9},{2,18},{18... | collective-permute-start | bytes 442376 | tf_op jit(solution)/shard_map/ppermute | solution.py:29
  159.0 20.9 %collective-permute-start.24 = (f32[2,2,48,384]{3,2,1,0:T(8,128)S(1)}, f32[2,2,48,384]{3,2,1,0:T(8,128)S(1)}, u32[]{:S(2)}, u32[]{:S(2)}) collective-permute-start(f32[2,2,48,384]{3,2,1,0:T(8,128)S(1)} %pad_maximum_fusion.13), channel_id=1, source_target_pairs={{0,4},{1,5},{2,6},{3,7},{4,0},{5,1},{6,2},{7,3},{8,9},{9,8},{10,11... | collective-permute-start | bytes 884744 | tf_op jit(solution)/shard_map/ppermute | solution.py:43
  173.6 23.0 %collective-permute-start.16 = (f32[2,2,96,384]{3,2,1,0:T(8,128)S(1)}, f32[2,2,96,384]{3,2,1,0:T(8,128)S(1)}, u32[]{:S(2)}, u32[]{:S(2)}) collective-permute-start(f32[2,2,96,384]{3,2,1,0:T(8,128)S(1)} %pad_maximum_fusion.10), channel_id=1, source_target_pairs={{0,2},{1,3},{2,0},{3,1},{4,6},{5,7},{6,4},{7,5},{8,12},{9,13},{10,... | collective-permute-start | bytes 1769480 | tf_op jit(solution)/shard_map/ppermute | solution.py:43
  173.8 58.9 %slice-start = ((s8[6291456]{0:T(1024)(128)(4,1)}), s8[4194304]{0:T(1024)(128)(4,1)S(1)}, s32[]{:S(2)}) async-start(s8[6291456]{0:T(1024)(128)(4,1)} %bitcast.121), calls=%async_computation.2 | async-start | bytes 8388608
  173.8 22.0 %collective-permute-start.4 = (f32[2,1,48,768]{3,2,1,0:T(8,128)S(1)}, f32[2,1,48,768]{3,2,1,0:T(8,128)S(1)}, u32[]{:S(2)}, u32[]{:S(2)}) collective-permute-start(f32[2,1,48,768]{3,2,1,0:T(8,128)S(1)} %get-tuple-element.116), channel_id=1, source_target_pairs={{0,4},{1,5},{2,6},{3,7},{4,0},{5,1},{6,2},{7,3},{8,9},{9,8},{10,11... | collective-permute-start | bytes 884744 | tf_op jit(solution)/shard_map/ppermute | solution.py:43
  180.0 38.3 %collective-permute-start.25 = (f32[2,2,96,384]{3,2,1,0:T(8,128)S(1)}, f32[2,2,96,384]{3,2,1,0:T(8,128)S(1)}, u32[]{:S(2)}, u32[]{:S(2)}) collective-permute-start(f32[2,2,96,384]{3,2,1,0:T(8,128)S(1)} %pad_maximum_fusion.11), channel_id=1, source_target_pairs={{0,2},{1,3},{2,0},{3,1},{4,6},{5,7},{6,4},{7,5},{8,12},{9,13},{10,... | collective-permute-start | bytes 1769480 | tf_op jit(solution)/shard_map/ppermute | solution.py:43
  196.5 36.1 %slice-start.1 = ((s8[6291456]{0:T(1024)(128)(4,1)}), s8[2097152]{0:T(1024)(128)(4,1)S(1)}, s32[]{:S(2)}) async-start(s8[6291456]{0:T(1024)(128)(4,1)} %bitcast.121), calls=%async_computation.3 | async-start | bytes 4194304
  196.5 13.8 %collective-permute-start.5 = (f32[2,1,48,768]{3,2,1,0:T(8,128)S(1)}, f32[2,1,48,768]{3,2,1,0:T(8,128)S(1)}, u32[]{:S(2)}, u32[]{:S(2)}) collective-permute-start(f32[2,1,48,768]{3,2,1,0:T(8,128)S(1)} %shard_map.60), channel_id=1, source_target_pairs={{0,4},{1,5},{2,6},{3,7},{4,0},{5,1},{6,2},{7,3},{8,9},{9,8},{10,11... | collective-permute-start | bytes 884744 | tf_op jit(solution)/shard_map/ppermute | solution.py:43
  196.7 38.8 %collective-permute-start.17 = (f32[2,2,192,384]{3,2,1,0:T(8,128)S(1)}, f32[2,2,192,384]{3,2,1,0:T(8,128)S(1)}, u32[]{:S(2)}, u32[]{:S(2)}) collective-permute-start(f32[2,2,192,384]{3,2,1,0:T(8,128)S(1)} %pad_maximum_fusion.5), channel_id=1, source_target_pairs={{0,1},{1,0},{2,3},{3,2},{4,5},{5,4},{6,7},{7,6},{8,10},{9,11},{10,... | collective-permute-start | bytes 3538952 | tf_op jit(solution)/shard_map/ppermute | solution.py:43
  210.4 20.5 %collective-permute-start.6 = (f32[2,1,96,768]{3,2,1,0:T(8,128)S(1)}, f32[2,1,96,768]{3,2,1,0:T(8,128)S(1)}, u32[]{:S(2)}, u32[]{:S(2)}) collective-permute-start(f32[2,1,96,768]{3,2,1,0:T(8,128)S(1)} %pad_maximum_fusion.9), channel_id=1, source_target_pairs={{0,2},{1,3},{2,0},{3,1},{4,6},{5,7},{6,4},{7,5},{8,12},{9,13},{10,... | collective-permute-start | bytes 1769480 | tf_op jit(solution)/shard_map/ppermute | solution.py:43
  218.4 18.5 %collective-permute-start.26 = (f32[2,2,192,384]{3,2,1,0:T(8,128)S(1)}, f32[2,2,192,384]{3,2,1,0:T(8,128)S(1)}, u32[]{:S(2)}, u32[]{:S(2)}) collective-permute-start(f32[2,2,192,384]{3,2,1,0:T(8,128)S(1)} %pad_maximum_fusion.6), channel_id=1, source_target_pairs={{0,1},{1,0},{2,3},{3,2},{4,5},{5,4},{6,7},{7,6},{8,10},{9,11},{10,... | collective-permute-start | bytes 3538952 | tf_op jit(solution)/shard_map/ppermute | solution.py:43
  231.0 17.6 %collective-permute-start.7 = (f32[2,1,192,768]{3,2,1,0:T(8,128)S(1)}, f32[2,1,192,768]{3,2,1,0:T(8,128)S(1)}, u32[]{:S(2)}, u32[]{:S(2)}) collective-permute-start(f32[2,1,192,768]{3,2,1,0:T(8,128)S(1)} %pad_maximum_fusion.4), channel_id=1, source_target_pairs={{0,1},{1,0},{2,3},{3,2},{4,5},{5,4},{6,7},{7,6},{8,10},{9,11},{10,... | collective-permute-start | bytes 3538952 | tf_op jit(solution)/shard_map/ppermute | solution.py:43
  234.9 83.1 %collective-permute-start.29 = (f32[1,768,1024]{2,1,0:T(8,128)}, f32[1,768,1024]{2,1,0:T(8,128)}, u32[]{:S(2)}, u32[]{:S(2)}) collective-permute-start(f32[1,768,1024]{2,1,0:T(8,128)} %shard_map.71), channel_id=1, source_target_pairs={{0,16},{16,0},{8,24},{24,8},{1,17},{17,1},{9,25},{25,9},{2,18},{18... | collective-permute-start | bytes 9437192 | tf_op jit(solution)/shard_map/ppermute | solution.py:29
  235.5 14.7 %copy-start.22 = (f32[2,2,192,384]{3,2,1,0:T(8,128)}, f32[2,2,192,384]{3,2,1,0:T(8,128)S(1)}, u32[]{:S(2)}) copy-start(f32[2,2,192,384]{3,2,1,0:T(8,128)S(1)} %collective-permute-done.17) | copy-start | bytes 3538948
  236.9 32.6 %collective-permute-start.27 = (f32[2,384,384]{2,1,0:T(8,128)}, f32[2,384,384]{2,1,0:T(8,128)S(1)}, u32[]{:S(2)}, u32[]{:S(2)}) collective-permute-start(f32[2,384,384]{2,1,0:T(8,128)} %slice_bitcast_fusion.1), channel_id=1, source_target_pairs={{0,8},{8,0},{16,24},{24,16},{1,9},{9,1},{17,25},{25,17},{2,10},{10... | collective-permute-start | bytes 3538952 | tf_op jit(solution)/shard_map/ppermute | solution.py:29
  236.9 24.5 %copy-start.23 = (f32[2,2,192,384]{3,2,1,0:T(8,128)}, f32[2,2,192,384]{3,2,1,0:T(8,128)S(1)}, u32[]{:S(2)}) copy-start(f32[2,2,192,384]{3,2,1,0:T(8,128)S(1)} %collective-permute-done.26) | copy-start | bytes 3538948
  238.3 29.2 %copy-start.30 = (s32[3]{0:T(128)S(1)}, s32[3]{0:T(128)}, u32[]{:S(2)}) copy-start(s32[3]{0:T(128)} %constant.135.clone.1) | copy-start | bytes 40
  238.3 31.3 %collective-permute-start.28 = (f32[2,384,384]{2,1,0:T(8,128)}, f32[2,384,384]{2,1,0:T(8,128)}, u32[]{:S(2)}, u32[]{:S(2)}) collective-permute-start(f32[2,384,384]{2,1,0:T(8,128)} %slice_bitcast_fusion), channel_id=1, source_target_pairs={{0,8},{8,0},{16,24},{24,16},{1,9},{9,1},{17,25},{25,17},{2,10},{10... | collective-permute-start | bytes 3538952 | tf_op jit(solution)/shard_map/ppermute | solution.py:29
  250.2 28.8 %collective-permute-start.8 = (f32[2,1,384,768]{3,2,1,0:T(8,128)}, f32[2,1,384,768]{3,2,1,0:T(8,128)}, u32[]{:S(2)}, u32[]{:S(2)}) collective-permute-start(f32[2,1,384,768]{3,2,1,0:T(8,128)} %pad_maximum_fusion), channel_id=1, source_target_pairs={{0,8},{8,0},{16,24},{24,16},{1,9},{9,1},{17,25},{25,17},{2,10},{10... | collective-permute-start | bytes 7077896 | tf_op jit(solution)/shard_map/ppermute | solution.py:29
  301.6 9.0 %copy-start.3 = (f32[1,768,768]{2,1,0:T(8,128)S(1)}, f32[1,768,768]{2,1,0:T(8,128)}, u32[]{:S(2)}) copy-start(f32[1,768,768]{2,1,0:T(8,128)} %copy-done.2) | copy-start | bytes 7077892
  301.6 9.0 %copy-start.7 = (f32[1,384,1024]{2,1,0:T(8,128)S(1)}, f32[1,384,1024]{2,1,0:T(8,128)}, u32[]{:S(2)}) copy-start(f32[1,384,1024]{2,1,0:T(8,128)} %copy-done.6) | copy-start | bytes 4718596
  301.6 9.0 %copy-start.9 = (f32[1,384,1024]{2,1,0:T(8,128)S(1)}, f32[1,384,1024]{2,1,0:T(8,128)}, u32[]{:S(2)}) copy-start(f32[1,384,1024]{2,1,0:T(8,128)} %copy-done.8) | copy-start | bytes 4718596
  (18 other events, 61.8 us)
Sparse Core Ops, SparseCore 0:
  288.3 19.8 reduce-scatter.3

commit v3 on v2

v3 whole, which is shorter than its diff:
```python
import functools

import jax
import jax.numpy as jnp
from jax import lax
from jax.experimental import pallas as pl
from jax.experimental.pallas import tpu as pltpu
from jax.sharding import PartitionSpec as P

VMEM = pl.BlockSpec(memory_space=pltpu.VMEM)
SMEM = pl.BlockSpec(memory_space=pltpu.SMEM)
ANY = pl.BlockSpec(memory_space=pl.ANY)


def params(mebibytes):
    return pltpu.CompilerParams(vmem_limit_bytes=mebibytes * 2**20)


def cost(flops, read):
    return pl.CostEstimate(flops=int(flops), bytes_accessed=int(read), transcendentals=0)


def swapped(block, axis, bit):
    count = lax.axis_size(axis)
    route = []
    for low in range(count):
        high = low | 1 << bit
        if high != low and high < count:
            route += [(low, high), (high, low)]
    return lax.ppermute(block, axis, route)


def orders(bits):
    return (list(range(bits)), list(range(1, bits)) + [0])


def across(block, step):
    pairs, auxes = lax.axis_size("pair"), lax.axis_size("aux")
    order = orders(auxes.bit_length() - 1)
    route = []
    for p in range(pairs):
        for m in range(auxes):
            route.append((p * auxes + m, p * auxes + (m ^ 1 << order[p % 2][step])))
    return lax.ppermute(block, ("pair", "aux"), route)


def halves(value):
    high = value.astype(jnp.bfloat16)
    return high, (value - high.astype(jnp.float32)).astype(jnp.bfloat16)


def multiply(left, right, dims):
    (lh, ll), (rh, rl) = left, right
    one = functools.partial(
        lax.dot_general, dimension_numbers=(dims, ((), ())), preferred_element_type=jnp.float32
    )
    if dims[0] == (1,):
        count = lh.shape[0]
        both = one(jnp.concatenate([lh, ll], axis=0), rh)
        return both[:count] + (both[count:] + one(lh, rl))
    return one(lh, rh) + (one(lh, rl) + one(ll, rh))


def upper_in(position, turn):
    return position // 2**turn % 2 == 1


def slot_of(plan_ref, state_ref, per_block, turn, h, own):
    half_count = per_block // 2
    plain = jnp.where(own, h, half_count + h)
    wanted = jnp.where(own, half_count + h, h)
    inverse = 0
    for k in range(per_block):
        inverse += jnp.where(plan_ref[turn, k] == wanted, k, 0)
    return jnp.where(upper_in(state_ref[0], turn), inverse, plain)


def peer_slot_of(plan_ref, state_ref, per_block, turn, h, own):
    half_count = per_block // 2
    plain = jnp.where(own, h, half_count + h)
    wanted = jnp.where(own, half_count + h, h)
    paired = 0
    for k in range(per_block):
        paired += jnp.where(plain == k, plan_ref[turn, k], 0)
    return jnp.where(upper_in(state_ref[0], turn), wanted, paired)


def copy_kernel(plan_ref, state_ref, source_ref, token_ref, target_ref):
    del plan_ref, state_ref, token_ref
    target_ref[...] = source_ref[...]


def picked(three_index, plan, state, token, turn, own, start, count):
    per_block, width, depth = three_index.shape
    half_count = per_block // 2
    rows = count // 2 if count % 16 == 0 and start % (count // 2) == 0 else count

    def source(h, piece, plan_ref, state_ref):
        return (slot_of(plan_ref, state_ref, per_block, turn, h, own), start // rows + piece, 0)

    return pl.pallas_call(
        copy_kernel,
        out_shape=jax.ShapeDtypeStruct((half_count, count, depth), jnp.float32),
        grid_spec=pltpu.PrefetchScalarGridSpec(
            num_scalar_prefetch=2,
            grid=(half_count, count // rows),
            in_specs=[pl.BlockSpec((1, rows, depth), source), ANY],
            out_specs=pl.BlockSpec((1, rows, depth), lambda h, piece, *_: (h, piece, 0)),
        ),
        compiler_params=params(24),
        cost_estimate=cost(0, 8 * half_count * count * depth),
    )(plan, state, three_index, token)


def integral_kernel(turn, blocks, plan_ref, state_ref, own_ref, peer_ref, token_ref, keep_ref, give_ref, high, low):
    del plan_ref, token_ref
    band = pl.program_id(1)

    @pl.when(band == 0)
    def _():
        high[...], low[...] = halves(peer_ref[0])

    own = halves(own_ref[0])
    value = multiply(own, (high[...], low[...]), ((1,), (1,)))
    rows = keep_ref.shape[1] * 2 // blocks
    core = state_ref[0] % 2
    inside = own_ref.shape[1] // rows
    for part in range(inside):
        index = band * inside + part
        side, place = index // (blocks // 2), index % (blocks // 2)
        piece = value[part * rows : (part + 1) * rows]

        @pl.when(side == core)
        def _():
            keep_ref[0, pl.ds(pl.multiple_of((place ^ state_ref[1]) * rows, rows), rows), :] = piece

        @pl.when(side != core)
        def _():
            give_ref[0, pl.ds(pl.multiple_of((place ^ state_ref[2]) * rows, rows), rows), :] = piece


def integral(three_index, peer, plan, state, token, turn, blocks):
    per_block, width, depth = three_index.shape
    half_count, count = per_block // 2, peer.shape[1]
    bands = 2
    out = jax.ShapeDtypeStruct((half_count, width // 2, count), jnp.float32)
    whole = pl.BlockSpec((1, width // 2, count), lambda h, band, *_: (h, 0, 0))
    chosen = peer.shape[0] == per_block

    def peer_at(h, band, p, s):
        return (peer_slot_of(p, s, per_block, turn, h, True) if chosen else h, 0, 0)

    return pl.pallas_call(
        functools.partial(integral_kernel, turn, blocks),
        out_shape=(out, out),
        grid_spec=pltpu.PrefetchScalarGridSpec(
            num_scalar_prefetch=2,
            grid=(half_count, bands),
            in_specs=[
                pl.BlockSpec(
                    (1, width // bands, depth),
                    lambda h, band, p, s: (slot_of(p, s, per_block, turn, h, True), band, 0),
                ),
                pl.BlockSpec((1, count, depth), peer_at),
                ANY,
            ],
            out_specs=(whole, whole),
            scratch_shapes=[pltpu.VMEM((count, depth), jnp.bfloat16)] * 2,
        ),
        compiler_params=params(44),
        cost_estimate=cost(
            6 * half_count * width * count * depth,
            4 * half_count * (width * depth + count * depth + width * count),
        ),
    )(plan, state, three_index, peer, token)


def part_kernel(keep_ref, came_ref, token_ref, low_ref, high_ref):
    del token_ref
    half = low_ref.shape[2]
    low_ref[0], low_ref[1] = keep_ref[:, :half], came_ref[:, :half]
    high_ref[0], high_ref[1] = keep_ref[:, half:], came_ref[:, half:]


def add_kernel(keep_ref, came_ref, token_ref, low_ref, high_ref):
    del token_ref
    half = low_ref.shape[2]
    low_ref[...] = keep_ref[:, :, :half] + came_ref[:, :, :half]
    high_ref[...] = keep_ref[:, :, half:] + came_ref[:, :, half:]


def parted(keep, came, token):
    joined = len(keep.shape) == 3
    shape = ((2,) if joined else ()) + keep.shape
    out = jax.ShapeDtypeStruct(shape[:2] + (shape[2] // 2,) + shape[3:], jnp.float32)
    return pl.pallas_call(
        part_kernel if joined else add_kernel,
        out_shape=(out, out),
        in_specs=[VMEM, VMEM, ANY],
        out_specs=(VMEM, VMEM),
        compiler_params=params(16),
        cost_estimate=cost(keep.size, 12 * keep.size),
    )(keep, came, token)


def join_kernel(axis, one_ref, two_ref, token_ref, out_ref):
    del token_ref
    half = one_ref.shape[axis]
    if axis == 1:
        out_ref[:, :half], out_ref[:, half:] = one_ref[...], two_ref[...]
    else:
        out_ref[:, :, :half], out_ref[:, :, half:] = one_ref[...], two_ref[...]


def joined(one, two, token, axis):
    shape = list(one.shape)
    shape[axis] *= 2
    return pl.pallas_call(
        functools.partial(join_kernel, axis),
        out_shape=jax.ShapeDtypeStruct(tuple(shape), jnp.float32),
        in_specs=[VMEM, VMEM, ANY],
        out_specs=VMEM,
        compiler_params=params(24),
        cost_estimate=cost(0, 16 * one.size),
    )(one, two, token)


def amplitude_kernel(turn, per_block, ours_ref, theirs_ref, state_ref, column_ref, row_ref, left_ref, right_ref, token_ref, out_ref):
    del token_ref
    half_count = per_block // 2
    rows = out_ref.shape[2]
    place = state_ref[0] % 2 * lax.div(column_ref.shape[0], 2 * rows) + state_ref[1]
    down = column_ref[pl.ds(pl.multiple_of(place * rows, rows), rows), :]
    for who in range(2):
        upper = upper_in(state_ref[0] ^ who, turn)
        for h in range(half_count):
            low = ours_ref[who, h]
            high = theirs_ref[who, half_count + h]
            wanted = ours_ref[who, per_block * (turn + 1) + h]
            for k in range(per_block):
                slot = ours_ref[who, per_block * (turn + 1) + k]
                high += jnp.where(slot == half_count + h, ours_ref[who, k], 0.0)
                low += jnp.where(wanted == k, theirs_ref[who, k], 0.0)
            gap = jnp.where(upper, high, low) - down - row_ref[...]
            out_ref[who, h] = (left_ref[who, h] + right_ref[who, h]) / gap


def amplitude(ours, theirs, state, column, row, left, right, token, turn, per_block):
    return pl.pallas_call(
        functools.partial(amplitude_kernel, turn, per_block),
        out_shape=jax.ShapeDtypeStruct(left.shape, jnp.float32),
        in_specs=[SMEM, SMEM, SMEM, VMEM, VMEM, VMEM, VMEM, ANY],
        out_specs=VMEM,
        compiler_params=params(16),
        cost_estimate=cost(8 * left.size, 12 * left.size),
    )(ours, theirs, state, column, row, left, right, token)


def tilde_kernel(blocks, count, state_ref, token_ref, *refs):
    del token_ref
    sources, (high_ref, low_ref, density_ref, amp, tilde) = refs[: 4 * count], refs[4 * count :]
    width = amp.shape[0]
    rows = width // blocks
    core = state_ref[0] % 2
    share = density_ref.shape[0]
    band = 128 if width % 128 == 0 else width
    for h in range(high_ref.shape[1]):
        for who in range(2):
            offset = 0
            for part in range(count):
                mine, came = sources[who * 2 * count + part], sources[who * 2 * count + count + part]
                size = mine.shape[2]
                for place in range(blocks // 2):
                    here = slice(place * rows, (place + 1) * rows)
                    spot = (core * (blocks // 2) + (place ^ state_ref[1])) * rows
                    amp[pl.ds(pl.multiple_of(spot, rows), rows), offset : offset + size] = mine[h, here, :]
                    spot = ((1 - core) * (blocks // 2) + (place ^ state_ref[2])) * rows
                    amp[pl.ds(pl.multiple_of(spot, rows), rows), offset : offset + size] = came[h, here, :]
                offset += size
            for part in range(width // band):
                spot = slice(part * band, (part + 1) * band)
                straight, turned = amp[spot, :], amp[:, spot].T
                value = 2.0 * straight - turned if who == 0 else 2.0 * turned - straight
                if who == 0:
                    tilde[spot, :] = value
                high_ref[who, h, spot, :], low_ref[who, h, spot, :] = halves(value)
            if who == 0:
                start = pl.ds(pl.multiple_of(state_ref[3] * share, share), share)
                straight = amp[start, :]
                turned = 2.0 * straight - tilde[start, :]
                both = (high_ref[0, h], low_ref[0, h])
                value = multiply(halves(straight), both, ((1,), (1,)))
                value += multiply(halves(turned), both, ((1,), (0,)))
                if h == 0:
                    density_ref[...] = value
                else:
                    density_ref[...] += value


def tildes(state, token, own, peer, blocks, share):
    sources = [x for x, _ in own] + [y for _, y in own] + [x for x, _ in peer] + [y for _, y in peer]
    half_count, half, _ = sources[0].shape
    width = 2 * half
    out = jax.ShapeDtypeStruct((2, half_count, width, width), jnp.bfloat16)
    return pl.pallas_call(
        functools.partial(tilde_kernel, blocks, len(own)),
        out_shape=(out, out, jax.ShapeDtypeStruct((share, width), jnp.float32)),
        in_specs=[SMEM, ANY] + [VMEM] * len(sources),
        out_specs=(VMEM, VMEM, VMEM),
        scratch_shapes=[pltpu.VMEM((width, width), jnp.float32)] * 2,
        compiler_params=params(48),
        cost_estimate=cost(24 * width * width * share, 24 * width * width),
    )(state, token, *sources)


def gradient_kernel(count, based, plan_ref, state_ref, high_ref, low_ref, token_ref, *refs):
    del plan_ref, state_ref, token_ref
    out_ref = refs[-1]
    tall = high_ref.shape[2]
    value = refs[count][0] if based else None
    offset = 0
    for source in refs[:count]:
        size = source.shape[1]
        spot = slice(offset, offset + size)
        term = multiply((high_ref[0, 0, :, spot], low_ref[0, 0, :, spot]), halves(source[0]), ((1,), (0,)))
        value = term if value is None else value + term
        offset += size
    out_ref[0] = value


def gradient_terms(plan, state, token, high, low, sources, base, turn, per_block, terms):
    width, depth = high.shape[2], sources[0].shape[2]
    half_count = per_block // 2
    tile = depth // 4 if depth % 512 == 0 else depth
    chosen = sources[0].shape[0] == per_block

    def block_at(term, h, piece, p, s):
        return (slot_of(p, s, per_block, turn, h, terms[0] + term == 0), 0, piece)

    def source_at(term, h, piece, p, s):
        if not chosen:
            return (h, 0, piece)
        return (peer_slot_of(p, s, per_block, turn, h, terms[0] + term == 0), 0, piece)

    square = pl.BlockSpec((1, 1, width, width), lambda term, h, piece, *_: (terms[0] + term, h, 0, 0))
    out_spec = pl.BlockSpec((1, width, tile), block_at)
    return pl.pallas_call(
        functools.partial(gradient_kernel, len(sources), base is not None),
        out_shape=jax.ShapeDtypeStruct((per_block, width, depth), jnp.float32),
        grid_spec=pltpu.PrefetchScalarGridSpec(
            num_scalar_prefetch=2,
            grid=(len(terms), half_count, depth // tile),
            in_specs=[square, square, ANY]
            + [pl.BlockSpec((1, x.shape[1], tile), source_at) for x in sources]
            + ([out_spec] if base is not None else []),
            out_specs=out_spec,
        ),
        input_output_aliases={} if base is None else {5 + len(sources): 0},
        compiler_params=params(40),
        cost_estimate=cost(
            6 * len(terms) * half_count * width * width * depth,
            4 * len(terms) * half_count * (width * depth * 3 + width * width),
        ),
    )(plan, state, high, low, token, *sources, *(() if base is None else (base,)))


def chain(env, turn, offset, first):
    bits, per_block = env["bits"], env["per_block"]
    half_count = per_block // 2
    token = yield None
    keep, give = integral(env["three_index"], first, env["plan"], env["state"], token, turn, env["blocks"])
    came = swapped(give, "pair", 0)
    token = yield give
    for stage in range(bits):
        keep, give = parted(keep, came, token)
        came = across(give, stage)
        token = yield give
    row = env["virtual"][None, offset : offset + first.shape[1]]
    value = amplitude(
        env["info"], env["peer_info"][turn], env["state"], env["column"], row, keep, came, token, turn, per_block
    )
    if turn > 0:
        came = swapped(value, "pair", turn)
        token = yield value
        value = joined(value, came, token, 1)
    for stage in reversed(range(bits)):
        came = across(value, stage)
        token = yield value
        value = joined(value, came, token, 2)
    if turn == 0:
        came = swapped(value, "pair", 0)
        env["gathered"][turn].append(((value[0], came[1]), (value[1], came[0])))
    else:
        came = swapped(value[1], "pair", 0)
        env["gathered"][turn].append(
            ((value[0, :half_count], came[:half_count]), (value[0, half_count:], came[half_count:]))
        )
    yield value


def body(three_index, occupied_energy, virtual_energy, plan):
    per_block, width, depth = three_index.shape
    half_count = per_block // 2
    aux_count = lax.axis_size("aux")
    bits = aux_count.bit_length() - 1
    blocks = 2 * aux_count
    row_count = width // aux_count
    aux = lax.axis_index("aux").astype(jnp.int32)
    rounds = plan.shape[0]
    position = lax.axis_index("pair").astype(jnp.int32)

    def mask(order):
        return sum((aux >> bit & 1) << bits - 1 - step for step, bit in enumerate(order))

    first_mask, second_mask = (mask(order) for order in orders(bits))
    core = position % 2
    state = jnp.stack(
        [
            position,
            jnp.where(core == 0, first_mask, second_mask),
            jnp.where(core == 0, second_mask, first_mask),
            aux,
        ]
    ).astype(jnp.int32)

    cuts = 2
    step = width // cuts
    firsts = [None] * rounds
    token = virtual_energy
    for turn in range(1, rounds):
        firsts[turn] = []
        for cut in range(cuts):
            token = picked(three_index, plan, state, token, turn, False, cut * step, step)
            firsts[turn].append(swapped(token, "pair", turn))
    other = swapped(three_index, "pair", 0)
    firsts[0] = [other]
    mine = jnp.concatenate([occupied_energy, plan.astype(jnp.float32).reshape(-1)])
    core_info = swapped(mine, "pair", 0)
    info = jnp.stack([mine, core_info])
    env = {
        "bits": bits,
        "per_block": per_block,
        "blocks": blocks,
        "plan": plan,
        "state": state,
        "three_index": three_index,
        "virtual": virtual_energy,
        "column": virtual_energy[:, None],
        "info": info,
        "peer_info": [jnp.stack([core_info, mine])]
        + [swapped(info, "pair", turn) for turn in range(1, rounds)],
        "gathered": [[] for _ in range(rounds)],
    }

    tasks = []
    for turn in range(rounds):
        for cut, first in enumerate(firsts[turn]):
            worker = chain(env, turn, cut * step if turn else 0, first)
            next(worker)
            share = first.shape[1] / width
            clock = 18.0 if turn == 0 else 40.0 + 34.0 * cut + 70.0 * (turn - 1)
            times = [clock, clock + 3 + 9 * share + 3]
            wide = 12.8 * share
            for stage in range(bits):
                times.append(times[-1] + 4 + (wide if stage < 2 else wide / 2))
            if turn > 0:
                wide *= 2
                times.append(times[-1] + 6)
            for stage in range(bits):
                times.append(times[-1] + 4 + (wide if stage > 0 else wide / 2))
            tasks += [(time, turn, cut, worker) for time in times]
            if cut == len(firsts[turn]) - 1:
                tasks.append((times[-1] + 6, turn, cut, None))
    for turn in range(1, rounds):
        tasks.append((62.0 + 70.0 * (turn - 1), turn, -1, None))
    tasks.sort(key=lambda task: task[:3])
    seconds = [other] + [None] * (rounds - 1)
    gradient = None
    densities = []
    for _, turn, cut, worker in tasks:
        if worker is not None:
            token = worker.send(token)
        elif cut < 0:
            token = picked(three_index, plan, state, token, turn, True, 0, width)
            seconds[turn] = swapped(token, "pair", turn)
        else:
            own, peer = zip(*env["gathered"][turn])
            high, low, density = tildes(state, token, own, peer, blocks, row_count)
            densities.append(density)
            if turn == 0:
                gradient = gradient_terms(
                    plan, state, density, high, low, [other], None, turn, per_block, (0, 1)
                )
            else:
                gradient = gradient_terms(
                    plan, state, density, high, low, firsts[turn], gradient, turn, per_block, (0,)
                )
                gradient = gradient_terms(
                    plan, state, density, high, low, [seconds[turn]], gradient, turn, per_block, (1,)
                )
            token = density
    density = sum(densities)
    for bit in reversed(range(lax.axis_size("pair").bit_length() - 1)):
        half = density.shape[1] // 2
        side = position >> bit & 1
        give = lax.dynamic_slice_in_dim(density, (1 - side) * half, half, 1)
        density = lax.dynamic_slice_in_dim(density, side * half, half, 1) + swapped(give, "pair", bit)
    return (gradient, density)


def solution(mesh):
    in_specs = (P("pair", None, "aux"), P("pair"), P(), P(None, "pair"))
    out_specs = (P("pair", None, "aux"), P("aux", "pair"))
    return jax.shard_map(body, mesh=mesh, in_specs=in_specs, out_specs=out_specs, check_vma=False)
```

time: 336 us -> 301 us (0.90)
  matrix products: 37 us -> 0 us
  waiting for transfers between devices: 128 us -> 163 us
  Pallas kernels: 34.5 us -> 67.7 us
  between operations: 21.3 us -> 1.18 us
  local copies, waits for them, and re-layouts: 32 us -> 13.9 us
  other arithmetic: 13.2 us -> 1.03 us
  starting transfers between devices: 61.6 us -> 52.9 us
  blocking collectives: 7.68 us -> 0 us
    pallas_call x7 -> x28, Pallas kernels: 9.12 us -> 47.3 us  [the longest x3 29 us: gradient_terms(): pl.pallas_call(functools.partial(gradient_kernel, len(sources), base is n...]
    dot_general x8 -> x0, matrix products: 37 us -> none  [dot(): jnp.einsum(expr, left, right, precision=lax.Precision.HIGH, preferred_ele...]
    ppermute x18, waiting for transfers between devices: 77.8 us -> 96.3 us  [across(): return lax.ppermute(block, ('pair', 'aux'), route)]
    ppermute x12 -> x16, waiting for transfers between devices: 50.2 us -> 66.7 us  [swapped(): return lax.ppermute(block, axis, route)]
    unnamed x1 -> x0, blocking collectives: 7.68 us -> none
    ppermute x18, starting transfers between devices: 33.4 us -> 26.8 us  [across(): return lax.ppermute(block, ('pair', 'aux'), route)]
    squeeze x4 -> x6, local copies, waits for them, and re-layouts: 7.08 us -> 0.62 us  [the longest x2 0.31 us: chain(): env['gathered'][turn].append(((value[0], came[1]), (value[1], came[0])))]
    slice x13 -> x3, local copies, waits for them, and re-layouts: 5.45 us -> 0.16 us  [the longest x2 0.16 us: chain(): came[half_count:]]
  transfers between devices with their start and end apart: 31 -> 34, of which waited for: 12 -> 20; matrix products, arithmetic and copies ran while one was open for 22% -> 0% of each run, Pallas kernels for 10% -> 20%
where the time goes in v3:
time: 301 us; the launch traced here: 300 us
  waiting for transfers between devices  163 us (54%)
  Pallas kernels  67.7 us (22%)
  starting transfers between devices  52.9 us (18%)
  local copies, waits for them, and re-layouts  13.9 us (5%)
    ppermute x18, waiting for transfers between devices, across(): return lax.ppermute(block, ('pair', 'aux'), route)  96.3 us
    ppermute x16, waiting for transfers between devices, swapped(): return lax.ppermute(block, axis, route)  66.7 us
    pallas_call x3, Pallas kernels, gradient_terms(): pl.pallas_call(functools.partial(gradient_kernel, len(sources), base is n...  29 us
    ppermute x18, starting transfers between devices, across(): return lax.ppermute(block, ('pair', 'aux'), route)  26.8 us
    ppermute x16, starting transfers between devices, swapped(): return lax.ppermute(block, axis, route)  26.1 us
    pallas_call x3, Pallas kernels, integral(): pl.pallas_call(functools.partial(integral_kernel, turn, blocks), out_shap...  17.1 us
    unnamed x52, local copies, waits for them, and re-layouts  12.8 us
    pallas_call x2, Pallas kernels, tildes(): pl.pallas_call(functools.partial(tilde_kernel, blocks, len(own)), out_sha...  9.04 us
  transfers between devices with their start and end apart: 34, of which 20 were waited for; matrix products, arithmetic and copies ran while one was open for 0% of the time, Pallas kernels for 20%

profile of v3, /device:TPU:0, one launch (start us, length us, event | category | flops | bytes accessed | tf_op | source)
XLA Modules:
  0.0 299.8 jit_solution(8755866715616965720)
XLA Ops:
  1.2 2.8 copy-done
  6.1 1.8 shard_map.60.token_ref
  7.9 3.3 %collective-permute-done.4.peer_ref.refs_0_ = f32[2,768,1024]{2,1,0:T(8,128)} collective-permute-done((f32[2,768,1024]{2,1,0:T(8,128)}, f32[2,768,1024]{2,1,0:T(8,128)}, u32[]{:S(2)}, u32[]{:S(2)}) %collective-permute-start.4) | collective-permute-done | bytes 6291488 | tf_op jit(solution)/shard_map/ppermute | solution.py:30
  11.3 7.5 %shard_map.61 = (f32[1,384,768]{2,1,0:T(8,128)S(1)}, f32[1,384,768]{2,1,0:T(8,128)S(1)}) custom-call(s32[2,2]{1,0:T(2,128)S(1)} %copy-done.16, s32[4]{0:T(128)S(1)} %pad_add_fusion.state_ref, f32[2,768,1024]{2,1,0:T(8,128)S(1)} %bitcast.28, f32[2,768,1024]{2,1,0:T(8,128)} %collective-permute-done.4.peer_ref.refs_0_, f32[1,384,1024]{2,1,0:T(8,128)} %shard_map.60.token_ref), custom_call_target="tpu_custom_call" | custom-call | flops 3623878656 | bytes 8650752 | tf_op jit(solution)/shard_map/pallas_call | solution.py:153
  19.2 2.7 collective-permute-start.3
  22.1 2.7 collective-permute-start.7
  26.3 30.8 %collective-permute-done.3.peer_ref.refs_0_ = f32[1,384,1024]{2,1,0:T(8,128)S(1)} collective-permute-done((f32[1,384,1024]{2,1,0:T(8,128)S(1)}, f32[1,384,1024]{2,1,0:T(8,128)S(1)}, u32[]{:S(2)}, u32[]{:S(2)}) %collective-permute-start.3) | collective-permute-done | bytes 1572896 | tf_op jit(solution)/shard_map/ppermute | solution.py:30
  57.1 4.0 %shard_map.63 = (f32[1,384,384]{2,1,0:T(8,128)S(1)}, f32[1,384,384]{2,1,0:T(8,128)S(1)}) custom-call(s32[2,2]{1,0:T(2,128)S(1)} %copy-done.16, s32[4]{0:T(128)S(1)} %pad_add_fusion.state_ref, f32[2,768,1024]{2,1,0:T(8,128)S(1)} %bitcast.28, f32[1,384,1024]{2,1,0:T(8,128)S(1)} %collective-permute-done.3.peer_ref.refs_0_, ...), custom_call_target="tpu_custom_call" | custom-call | flops 1811939328 | bytes 5898240 | tf_op jit(solution)/shard_map/pallas_call | solution.py:153
  61.4 1.8 collective-permute-done.6.came_ref
  63.3 2.0 collective-permute-start.8
  65.4 1.6 collective-permute-start.10
  66.9 6.3 %collective-permute-done.8.came_ref = f32[2,1,192,384]{3,2,1,0:T(8,128)S(1)} collective-permute-done((f32[2,1,192,384]{3,2,1,0:T(8,128)S(1)}, f32[2,1,192,384]{3,2,1,0:T(8,128)S(1)}, u32[]{:S(2)}, u32[]{:S(2)}) %collective-permute-start.8) | collective-permute-done | bytes 589856 | tf_op jit(solution)/shard_map/ppermute | solution.py:44
  74.8 2.0 collective-permute-start.9
  77.0 10.5 %collective-permute-start = (f32[6]{0:T(128)S(1)}, f32[6]{0:T(128)S(1)}, u32[]{:S(2)}, u32[]{:S(2)}) collective-permute-start(f32[6]{0:T(128)S(1)} %pad_maximum_fusion.2), channel_id=1, source_target_pairs={{0,8},{8,0},{16,24},{24,16},{1,9},{9,1},{17,25},{25,17},{2,10},{10... | collective-permute-start | bytes 80 | tf_op jit(solution)/shard_map/ppermute | solution.py:30
  87.7 2.8 copy-done.1
  91.3 2.7 shard_map.68
  95.4 5.6 %shard_map.70 = (f32[1,384,384]{2,1,0:T(8,128)S(1)}, f32[1,384,384]{2,1,0:T(8,128)S(1)}) custom-call(s32[2,2]{1,0:T(2,128)S(1)} %copy-done.16, s32[4]{0:T(128)S(1)} %pad_add_fusion.state_ref, f32[2,768,1024]{2,1,0:T(8,128)S(1)} %bitcast.30, f32[1,384,1024]{2,1,0:T(8,128)} %collective-permute-done.2.peer_ref.refs_1_, ...), custom_call_target="tpu_custom_call" | custom-call | flops 1811939328 | bytes 5898240 | tf_op jit(solution)/shard_map/pallas_call | solution.py:153
  101.0 2.0 collective-permute-start.11
  106.9 1.5 collective-permute-start.1
  108.4 2.0 collective-permute-done.1.theirs_ref
  111.5 1.6 collective-permute-start.16
  113.1 1.9 collective-permute-start.14
  115.0 1.7 collective-permute-done.16.two_ref
  118.1 4.1 %collective-permute-start.19 = (f32[2,2,48,384]{3,2,1,0:T(8,128)S(1)}, f32[2,2,48,384]{3,2,1,0:T(8,128)S(1)}, u32[]{:S(2)}, u32[]{:S(2)}) collective-permute-start(f32[2,2,48,384]{3,2,1,0:T(8,128)S(1)} %shard_map.74.token_ref.one_ref), channel_id=1, source_target_pairs={{0,4},{1,5},{2,6},{3,7},{4,0},{5,1},{6,2},{7,3},{8,9},{9,8},{10,11... | collective-permute-start | bytes 884744 | tf_op jit(solution)/shard_map/ppermute | solution.py:44
  122.1 4.1 %collective-permute-done.14.came_ref = f32[2,1,192,384]{3,2,1,0:T(8,128)S(1)} collective-permute-done((f32[2,1,192,384]{3,2,1,0:T(8,128)S(1)}, f32[2,1,192,384]{3,2,1,0:T(8,128)S(1)}, u32[]{:S(2)}, u32[]{:S(2)}) %collective-permute-start.14) | collective-permute-done | bytes 589856 | tf_op jit(solution)/shard_map/ppermute | solution.py:44
  126.3 7.8 %collective-permute-done.19.two_ref = f32[2,2,48,384]{3,2,1,0:T(8,128)S(1)} collective-permute-done((f32[2,2,48,384]{3,2,1,0:T(8,128)S(1)}, f32[2,2,48,384]{3,2,1,0:T(8,128)S(1)}, u32[]{:S(2)}, u32[]{:S(2)}) %collective-permute-start.19) | collective-permute-done | bytes 294944 | tf_op jit(solution)/shard_map/ppermute | solution.py:44
  134.2 4.0 %collective-permute-done.18.two_ref = f32[2,1,96,768]{3,2,1,0:T(8,128)S(1)} collective-permute-done((f32[2,1,96,768]{3,2,1,0:T(8,128)S(1)}, f32[2,1,96,768]{3,2,1,0:T(8,128)S(1)}, u32[]{:S(2)}, u32[]{:S(2)}) %collective-permute-start.18) | collective-permute-done | bytes 589856 | tf_op jit(solution)/shard_map/ppermute | solution.py:44
  138.3 1.8 collective-permute-start.25
  140.1 2.0 collective-permute-start.17
  142.1 27.3 %collective-permute-done.17.came_ref = f32[2,1,96,384]{3,2,1,0:T(8,128)S(1)} collective-permute-done((f32[2,1,96,384]{3,2,1,0:T(8,128)S(1)}, f32[2,1,96,384]{3,2,1,0:T(8,128)S(1)}, u32[]{:S(2)}, u32[]{:S(2)}) %collective-permute-start.17) | collective-permute-done | bytes 294944 | tf_op jit(solution)/shard_map/ppermute | solution.py:44
  169.6 6.5 %collective-permute-done.20.right_ref = f32[2,1,48,384]{3,2,1,0:T(8,128)S(1)} collective-permute-done((f32[2,1,48,384]{3,2,1,0:T(8,128)S(1)}, f32[2,1,48,384]{3,2,1,0:T(8,128)S(1)}, u32[]{:S(2)}, u32[]{:S(2)}) %collective-permute-start.20) | collective-permute-done | bytes 147488 | tf_op jit(solution)/shard_map/ppermute | solution.py:44
  176.8 1.8 collective-permute-start.22
  178.5 3.5 %collective-permute-done.22.two_ref = f32[2,1,48,384]{3,2,1,0:T(8,128)S(1)} collective-permute-done((f32[2,1,48,384]{3,2,1,0:T(8,128)S(1)}, f32[2,1,48,384]{3,2,1,0:T(8,128)S(1)}, u32[]{:S(2)}, u32[]{:S(2)}) %collective-permute-start.22) | collective-permute-done | bytes 147488 | tf_op jit(solution)/shard_map/ppermute | solution.py:30
  182.3 1.8 collective-permute-start.24
  187.0 4.5 %shard_map.84 = (bf16[2,1,768,768]{3,2,1,0:T(8,128)(2,1)}, bf16[2,1,768,768]{3,2,1,0:T(8,128)(2,1)}, f32[96,768]{1,0:T(8,128)S(1)}) custom-call(s32[4]{0:T(128)S(1)} %pad_add_fusion.state_ref, f32[2,1,384,768]{3,2,1,0:T(8,128)} %copy-done.2, f32[1,384,768]{2,1,0:T(8,128)S(1)} %get-tuple-element.69.refs_0_, f32[1,384,768]{2,1,0:T(8,128)S(1)} %get-tuple-element.67.refs_1_, ...), custom_call_target="tpu_custom_call" | custom-call | flops 1358954496 | bytes 14155776 | tf_op jit(solution)/shard_map/pallas_call | solution.py:305
  191.5 9.9 %collective-permute-done.24.two_ref = f32[2,2,192,384]{3,2,1,0:T(8,128)S(1)} collective-permute-done((f32[2,2,192,384]{3,2,1,0:T(8,128)S(1)}, f32[2,2,192,384]{3,2,1,0:T(8,128)S(1)}, u32[]{:S(2)}, u32[]{:S(2)}) %collective-permute-start.24) | collective-permute-done | bytes 1179680 | tf_op jit(solution)/shard_map/ppermute | solution.py:44
  202.5 15.4 %collective-permute-done.27.two_ref = f32[2,2,96,384]{3,2,1,0:T(8,128)S(1)} collective-permute-done((f32[2,2,96,384]{3,2,1,0:T(8,128)S(1)}, f32[2,2,96,384]{3,2,1,0:T(8,128)S(1)}, u32[]{:S(2)}, u32[]{:S(2)}) %collective-permute-start.27) | collective-permute-done | bytes 589856 | tf_op jit(solution)/shard_map/ppermute | solution.py:44
  218.0 1.6 collective-permute-start.28
  221.3 13.1 %collective-permute-done.28.two_ref = f32[2,2,192,384]{3,2,1,0:T(8,128)} collective-permute-done((f32[2,2,192,384]{3,2,1,0:T(8,128)S(1)}, f32[2,2,192,384]{3,2,1,0:T(8,128)}, u32[]{:S(2)}, u32[]{:S(2)}) %collective-permute-start.28) | collective-permute-done | bytes 1179680 | tf_op jit(solution)/shard_map/ppermute | solution.py:44
  234.3 1.6 shard_map.88.token_ref
  237.8 12.5 %shard_map.90.refs_2_ = f32[2,768,1024]{2,1,0:T(8,128)} custom-call(s32[2,2]{1,0:T(2,128)S(1)} %copy-done.16, s32[4]{0:T(128)S(1)} %pad_add_fusion.state_ref, bf16[2,1,768,768]{3,2,1,0:T(8,128)(2,1)S(1)} %copy-done.19, bf16[2,1,768,768]{3,2,1,0:T(8,128)(2,1)S(1)} %copy-done.20, f32[96,768]{1,0:T(8,128)S(1)} %copy-done.12, ...), custom_call_target="tpu_custom_call" | custom-call | flops 7247757312 | bytes 23592960 | tf_op jit(solution)/shard_map/pallas_call | solution.py:347
  250.6 4.5 %shard_map.89 = (bf16[2,1,768,768]{3,2,1,0:T(8,128)(2,1)}, bf16[2,1,768,768]{3,2,1,0:T(8,128)(2,1)}, f32[96,768]{1,0:T(8,128)S(1)}) custom-call(s32[4]{0:T(128)S(1)} %pad_add_fusion.state_ref, f32[2,2,384,384]{3,2,1,0:T(8,128)} %copy-done.3, f32[1,384,384]{2,1,0:T(8,128)S(1)} %get-tuple-element.65.refs_0_, f32[1,384,384]{2,1,0:T(8,128)S(1)} %get-tuple-element.63.refs_1_, ...), custom_call_target="tpu_custom_call" | custom-call | flops 1358954496 | bytes 14155776 | tf_op jit(solution)/shard_map/pallas_call | solution.py:305
  255.2 1.7 collective-permute-start.32
  257.0 1.7 copy-done.5
  258.6 1.7 copy-done.7
  260.3 8.8 %shard_map.91.refs_1_ = f32[2,768,1024]{2,1,0:T(8,128)} custom-call(s32[2,2]{1,0:T(2,128)S(1)} %copy-done.16, s32[4]{0:T(128)S(1)} %pad_add_fusion.state_ref, bf16[2,1,768,768]{3,2,1,0:T(8,128)(2,1)S(1)} %copy-done.5, bf16[2,1,768,768]{3,2,1,0:T(8,128)(2,1)S(1)} %copy-done.7, ...), custom_call_target="tpu_custom_call", output_to_operand_aliasing={{}: (7, {})} | custom-call | flops 3623878656 | bytes 11796480 | tf_op jit(solution)/shard_map/pallas_call | solution.py:347
  269.1 22.0 %collective-permute-done.32 = f32[96,384]{1,0:T(8,128)S(1)} collective-permute-done((f32[96,384]{1,0:T(8,128)S(1)}, f32[96,384]{1,0:T(8,128)S(1)}, u32[]{:S(2)}, u32[]{:S(2)}) %collective-permute-start.32) | collective-permute-done | bytes 147488 | tf_op jit(solution)/shard_map/ppermute | solution.py:30
  291.4 7.6 %shard_map.92 = f32[2,768,1024]{2,1,0:T(8,128)} custom-call(s32[2,2]{1,0:T(2,128)S(1)} %copy-done.16, s32[4]{0:T(128)S(1)} %pad_add_fusion.state_ref, bf16[2,1,768,768]{3,2,1,0:T(8,128)(2,1)S(1)} %copy-done.6, bf16[2,1,768,768]{3,2,1,0:T(8,128)(2,1)S(1)} %copy-done.8, f32[96,768]{1,0:T(8,128)S(1)} %get-tuple-element.59.token_ref, ...), custom_call_target="tpu_custom_call", output_to_operand_aliasing={{}: (6, {})} | custom-call | flops 3623878656 | bytes 11796480 | tf_op jit(solution)/shard_map/pallas_call | solution.py:347
  (132 shorter events, 25.6 us)
Async XLA Ops:
  0.6 10.6 %collective-permute-start.4 = (f32[2,768,1024]{2,1,0:T(8,128)}, f32[2,768,1024]{2,1,0:T(8,128)}, u32[]{:S(2)}, u32[]{:S(2)}) collective-permute-start(f32[2,768,1024]{2,1,0:T(8,128)} %own_ref.5), channel_id=1, source_target_pairs={{0,8},{8,0},{16,24},{24,16},{1,9},{9,1},{17,25},{25,17},{2,10},{10... | collective-permute-start | bytes 18874376 | tf_op jit(solution)/shard_map/ppermute | solution.py:30
  5.4 5.9 %slice-start = ((s8[6291456]{0:T(1024)(128)(4,1)}), s8[4194304]{0:T(1024)(128)(4,1)S(1)}, s32[]{:S(2)}) async-start(s8[6291456]{0:T(1024)(128)(4,1)} %bitcast.27), calls=%async_computation | async-start | bytes 8388608
  6.1 5.2 %slice-start.1 = ((s8[6291456]{0:T(1024)(128)(4,1)}), s8[2097152]{0:T(1024)(128)(4,1)S(1)}, s32[]{:S(2)}) async-start(s8[6291456]{0:T(1024)(128)(4,1)} %bitcast.27), calls=%async_computation.1 | async-start | bytes 4194304
  6.1 5.2 %copy-start.16 = (s32[2,2]{1,0:T(2,128)S(1)}, s32[2,2]{1,0:T(2,128)}, u32[]{:S(2)}) copy-start(s32[2,2]{1,0:T(2,128)} %plan_ref.17) | copy-start | bytes 52
  18.8 3.1 %collective-permute-start.5 = (f32[1,384,768]{2,1,0:T(8,128)S(1)}, f32[1,384,768]{2,1,0:T(8,128)S(1)}, u32[]{:S(2)}, u32[]{:S(2)}) collective-permute-start(f32[1,384,768]{2,1,0:T(8,128)S(1)} %get-tuple-element.33.token_ref), channel_id=1, source_target_pairs={{0,8},{8,0},{16,24},{24,16},{1,9},{9,1},{17,25},{25,17},{2,10},{10... | collective-permute-start | bytes 3538952 | tf_op jit(solution)/shard_map/ppermute | solution.py:30
  19.2 37.9 %collective-permute-start.3 = (f32[1,384,1024]{2,1,0:T(8,128)S(1)}, f32[1,384,1024]{2,1,0:T(8,128)S(1)}, u32[]{:S(2)}, u32[]{:S(2)}) collective-permute-start(f32[1,384,1024]{2,1,0:T(8,128)S(1)} %shard_map.59.token_ref), channel_id=1, source_target_pairs={{0,16},{16,0},{8,24},{24,8},{1,17},{17,1},{9,25},{25,9},{2,18},{18... | collective-permute-start | bytes 4718600 | tf_op jit(solution)/shard_map/ppermute | solution.py:30
  22.1 39.2 %collective-permute-start.7 = (f32[2,1,192,768]{3,2,1,0:T(8,128)S(1)}, f32[2,1,192,768]{3,2,1,0:T(8,128)S(1)}, u32[]{:S(2)}, u32[]{:S(2)}) collective-permute-start(f32[2,1,192,768]{3,2,1,0:T(8,128)S(1)} %get-tuple-element.34.token_ref), channel_id=1, source_target_pairs={{0,1},{1,0},{2,3},{3,2},{4,5},{5,4},{6,7},{7,6},{8,10},{9,11},{10,... | collective-permute-start | bytes 3538952 | tf_op jit(solution)/shard_map/ppermute | solution.py:44
  24.8 70.6 %collective-permute-start.2 = (f32[1,384,1024]{2,1,0:T(8,128)}, f32[1,384,1024]{2,1,0:T(8,128)}, u32[]{:S(2)}, u32[]{:S(2)}) collective-permute-start(f32[1,384,1024]{2,1,0:T(8,128)} %shard_map.60.token_ref), channel_id=1, source_target_pairs={{0,16},{16,0},{8,24},{24,8},{1,17},{17,1},{9,25},{25,9},{2,18},{18... | collective-permute-start | bytes 4718600 | tf_op jit(solution)/shard_map/ppermute | solution.py:30
  57.1 4.0 %copy-start.9 = (f32[1,384,1024]{2,1,0:T(8,128)}, f32[1,384,1024]{2,1,0:T(8,128)S(1)}, u32[]{:S(2)}) copy-start(f32[1,384,1024]{2,1,0:T(8,128)S(1)} %collective-permute-done.3.peer_ref.refs_0_) | copy-start | bytes 4718596
  61.2 2.1 collective-permute-start.6
  63.2 32.1 %slice-start.2 = ((s8[6291456]{0:T(1024)(128)(4,1)}), s8[2097152]{0:T(1024)(128)(4,1)S(1)}, s32[]{:S(2)}) async-start(s8[6291456]{0:T(1024)(128)(4,1)} %bitcast.29), calls=%async_computation.2 | async-start | bytes 4194304
  63.3 13.6 %copy-start.21 = (f32[2]{0:T(128)S(1)}, f32[2]{0:T(128)}, u32[]{:S(2)}) copy-start(f32[2]{0:T(128)} %param.5) | copy-start | bytes 28
  63.3 24.2 %copy-start.18 = (f32[768]{0:T(1024)S(1)}, f32[768]{0:T(1024)}, u32[]{:S(2)}) copy-start(f32[768]{0:T(1024)} %token_ref.1) | copy-start | bytes 9220
  63.3 9.9 %collective-permute-start.8 = (f32[2,1,192,384]{3,2,1,0:T(8,128)S(1)}, f32[2,1,192,384]{3,2,1,0:T(8,128)S(1)}, u32[]{:S(2)}, u32[]{:S(2)}) collective-permute-start(f32[2,1,192,384]{3,2,1,0:T(8,128)S(1)} %get-tuple-element.40.token_ref), channel_id=1, source_target_pairs={{0,1},{1,0},{2,3},{3,2},{4,5},{5,4},{6,7},{7,6},{8,10},{9,11},{10,... | collective-permute-start | bytes 1769480 | tf_op jit(solution)/shard_map/ppermute | solution.py:44
  65.4 25.9 %collective-permute-start.10 = (f32[2,1,96,768]{3,2,1,0:T(8,128)S(1)}, f32[2,1,96,768]{3,2,1,0:T(8,128)}, u32[]{:S(2)}, u32[]{:S(2)}) collective-permute-start(f32[2,1,96,768]{3,2,1,0:T(8,128)S(1)} %get-tuple-element.38.token_ref), channel_id=1, source_target_pairs={{0,2},{1,3},{2,0},{3,1},{4,6},{5,7},{6,4},{7,5},{8,12},{9,13},{10,... | collective-permute-start | bytes 1769480 | tf_op jit(solution)/shard_map/ppermute | solution.py:44
  74.8 19.6 %collective-permute-start.9 = (f32[2,1,96,384]{3,2,1,0:T(8,128)}, f32[2,1,96,384]{3,2,1,0:T(8,128)}, u32[]{:S(2)}, u32[]{:S(2)}) collective-permute-start(f32[2,1,96,384]{3,2,1,0:T(8,128)} %get-tuple-element.42.token_ref), channel_id=1, source_target_pairs={{0,2},{1,3},{2,0},{3,1},{4,6},{5,7},{6,4},{7,5},{8,12},{9,13},{10,... | collective-permute-start | bytes 884744 | tf_op jit(solution)/shard_map/ppermute | solution.py:44
  77.0 26.1 %collective-permute-start = (f32[6]{0:T(128)S(1)}, f32[6]{0:T(128)S(1)}, u32[]{:S(2)}, u32[]{:S(2)}) collective-permute-start(f32[6]{0:T(128)S(1)} %pad_maximum_fusion.2), channel_id=1, source_target_pairs={{0,8},{8,0},{16,24},{24,16},{1,9},{9,1},{17,25},{25,17},{2,10},{10... | collective-permute-start | bytes 80 | tf_op jit(solution)/shard_map/ppermute | solution.py:30
  90.4 4.9 %slice-start.3 = ((s8[6291456]{0:T(1024)(128)(4,1)}), s8[4194304]{0:T(1024)(128)(4,1)S(1)}, s32[]{:S(2)}) async-start(s8[6291456]{0:T(1024)(128)(4,1)} %bitcast.29), calls=%async_computation.3 | async-start | bytes 8388608
  94.0 10.8 %collective-permute-start.13 = (f32[2,1,48,768]{3,2,1,0:T(8,128)S(1)}, f32[2,1,48,768]{3,2,1,0:T(8,128)S(1)}, u32[]{:S(2)}, u32[]{:S(2)}) collective-permute-start(f32[2,1,48,768]{3,2,1,0:T(8,128)S(1)} %get-tuple-element.44.token_ref), channel_id=1, source_target_pairs={{0,4},{1,5},{2,6},{3,7},{4,0},{5,1},{6,2},{7,3},{8,9},{9,8},{10,11... | collective-permute-start | bytes 884744 | tf_op jit(solution)/shard_map/ppermute | solution.py:44
  101.0 12.1 %collective-permute-start.11 = (f32[1,384,384]{2,1,0:T(8,128)S(1)}, f32[1,384,384]{2,1,0:T(8,128)S(1)}, u32[]{:S(2)}, u32[]{:S(2)}) collective-permute-start(f32[1,384,384]{2,1,0:T(8,128)S(1)} %get-tuple-element.47.token_ref), channel_id=1, source_target_pairs={{0,8},{8,0},{16,24},{24,16},{1,9},{9,1},{17,25},{25,17},{2,10},{10... | collective-permute-start | bytes 1769480 | tf_op jit(solution)/shard_map/ppermute | solution.py:30
  103.1 7.7 %collective-permute-start.12 = (f32[2,1,48,384]{3,2,1,0:T(8,128)S(1)}, f32[2,1,48,384]{3,2,1,0:T(8,128)S(1)}, u32[]{:S(2)}, u32[]{:S(2)}) collective-permute-start(f32[2,1,48,384]{3,2,1,0:T(8,128)S(1)} %get-tuple-element.45.token_ref), channel_id=1, source_target_pairs={{0,4},{1,5},{2,6},{3,7},{4,0},{5,1},{6,2},{7,3},{8,9},{9,8},{10,11... | collective-permute-start | bytes 442376 | tf_op jit(solution)/shard_map/ppermute | solution.py:44
  105.5 11.7 %collective-permute-start.15 = (f32[2,1,48,768]{3,2,1,0:T(8,128)S(1)}, f32[2,1,48,768]{3,2,1,0:T(8,128)S(1)}, u32[]{:S(2)}, u32[]{:S(2)}) collective-permute-start(f32[2,1,48,768]{3,2,1,0:T(8,128)S(1)} %shard_map.71.token_ref.one_ref), channel_id=1, source_target_pairs={{0,4},{1,5},{2,6},{3,7},{4,0},{5,1},{6,2},{7,3},{8,9},{9,8},{10,11... | collective-permute-start | bytes 884744 | tf_op jit(solution)/shard_map/ppermute | solution.py:44
  106.9 3.6 %collective-permute-start.1 = (f32[2,6]{1,0:T(2,128)S(1)}, f32[2,6]{1,0:T(2,128)S(1)}, u32[]{:S(2)}, u32[]{:S(2)}) collective-permute-start(f32[2,6]{1,0:T(2,128)S(1)} %get-tuple-element.77.ours_ref), channel_id=1, source_target_pairs={{0,16},{16,0},{8,24},{24,8},{1,17},{17,1},{9,25},{25,9},{2,18},{18... | collective-permute-start | bytes 152 | tf_op jit(solution)/shard_map/ppermute | solution.py:30
  111.5 5.2 %collective-permute-start.16 = (f32[2,1,48,384]{3,2,1,0:T(8,128)S(1)}, f32[2,1,48,384]{3,2,1,0:T(8,128)S(1)}, u32[]{:S(2)}, u32[]{:S(2)}) collective-permute-start(f32[2,1,48,384]{3,2,1,0:T(8,128)S(1)} %shard_map.72.token_ref.one_ref), channel_id=1, source_target_pairs={{0,16},{16,0},{8,24},{24,8},{1,17},{17,1},{9,25},{25,9},{2,18},{18... | collective-permute-start | bytes 442376 | tf_op jit(solution)/shard_map/ppermute | solution.py:30
  113.1 13.1 %collective-permute-start.14 = (f32[2,1,192,384]{3,2,1,0:T(8,128)S(1)}, f32[2,1,192,384]{3,2,1,0:T(8,128)S(1)}, u32[]{:S(2)}, u32[]{:S(2)}) collective-permute-start(f32[2,1,192,384]{3,2,1,0:T(8,128)S(1)} %get-tuple-element.51.token_ref), channel_id=1, source_target_pairs={{0,1},{1,0},{2,3},{3,2},{4,5},{5,4},{6,7},{7,6},{8,10},{9,11},{10,... | collective-permute-start | bytes 1769480 | tf_op jit(solution)/shard_map/ppermute | solution.py:44
  117.3 21.0 %collective-permute-start.18 = (f32[2,1,96,768]{3,2,1,0:T(8,128)S(1)}, f32[2,1,96,768]{3,2,1,0:T(8,128)S(1)}, u32[]{:S(2)}, u32[]{:S(2)}) collective-permute-start(f32[2,1,96,768]{3,2,1,0:T(8,128)S(1)} %shard_map.75.token_ref.one_ref), channel_id=1, source_target_pairs={{0,2},{1,3},{2,0},{3,1},{4,6},{5,7},{6,4},{7,5},{8,12},{9,13},{10,... | collective-permute-start | bytes 1769480 | tf_op jit(solution)/shard_map/ppermute | solution.py:44
  118.1 16.1 %collective-permute-start.19 = (f32[2,2,48,384]{3,2,1,0:T(8,128)S(1)}, f32[2,2,48,384]{3,2,1,0:T(8,128)S(1)}, u32[]{:S(2)}, u32[]{:S(2)}) collective-permute-start(f32[2,2,48,384]{3,2,1,0:T(8,128)S(1)} %shard_map.74.token_ref.one_ref), channel_id=1, source_target_pairs={{0,4},{1,5},{2,6},{3,7},{4,0},{5,1},{6,2},{7,3},{8,9},{9,8},{10,11... | collective-permute-start | bytes 884744 | tf_op jit(solution)/shard_map/ppermute | solution.py:44
  138.3 43.7 %collective-permute-start.25 = (f32[2,1,192,768]{3,2,1,0:T(8,128)S(1)}, f32[2,1,192,768]{3,2,1,0:T(8,128)S(1)}, u32[]{:S(2)}, u32[]{:S(2)}) collective-permute-start(f32[2,1,192,768]{3,2,1,0:T(8,128)S(1)} %shard_map.78.token_ref.one_ref), channel_id=1, source_target_pairs={{0,1},{1,0},{2,3},{3,2},{4,5},{5,4},{6,7},{7,6},{8,10},{9,11},{10,... | collective-permute-start | bytes 3538952 | tf_op jit(solution)/shard_map/ppermute | solution.py:44
  140.1 29.4 %collective-permute-start.21 = (f32[2,2,96,384]{3,2,1,0:T(8,128)S(1)}, f32[2,2,96,384]{3,2,1,0:T(8,128)S(1)}, u32[]{:S(2)}, u32[]{:S(2)}) collective-permute-start(f32[2,2,96,384]{3,2,1,0:T(8,128)S(1)} %shard_map.77.token_ref.one_ref), channel_id=1, source_target_pairs={{0,2},{1,3},{2,0},{3,1},{4,6},{5,7},{6,4},{7,5},{8,12},{9,13},{10,... | collective-permute-start | bytes 1769480 | tf_op jit(solution)/shard_map/ppermute | solution.py:44
  140.1 29.3 %collective-permute-start.17 = (f32[2,1,96,384]{3,2,1,0:T(8,128)S(1)}, f32[2,1,96,384]{3,2,1,0:T(8,128)S(1)}, u32[]{:S(2)}, u32[]{:S(2)}) collective-permute-start(f32[2,1,96,384]{3,2,1,0:T(8,128)S(1)} %get-tuple-element.53.token_ref), channel_id=1, source_target_pairs={{0,2},{1,3},{2,0},{3,1},{4,6},{5,7},{6,4},{7,5},{8,12},{9,13},{10,... | collective-permute-start | bytes 884744 | tf_op jit(solution)/shard_map/ppermute | solution.py:44
  169.4 6.7 %collective-permute-start.20 = (f32[2,1,48,384]{3,2,1,0:T(8,128)S(1)}, f32[2,1,48,384]{3,2,1,0:T(8,128)S(1)}, u32[]{:S(2)}, u32[]{:S(2)}) collective-permute-start(f32[2,1,48,384]{3,2,1,0:T(8,128)S(1)} %get-tuple-element.55.token_ref), channel_id=1, source_target_pairs={{0,4},{1,5},{2,6},{3,7},{4,0},{5,1},{6,2},{7,3},{8,9},{9,8},{10,11... | collective-permute-start | bytes 442376 | tf_op jit(solution)/shard_map/ppermute | solution.py:44
  176.8 5.2 %collective-permute-start.22 = (f32[2,1,48,384]{3,2,1,0:T(8,128)S(1)}, f32[2,1,48,384]{3,2,1,0:T(8,128)S(1)}, u32[]{:S(2)}, u32[]{:S(2)}) collective-permute-start(f32[2,1,48,384]{3,2,1,0:T(8,128)S(1)} %shard_map.81.one_ref.token_ref), channel_id=1, source_target_pairs={{0,16},{16,0},{8,24},{24,8},{1,17},{17,1},{9,25},{25,9},{2,18},{18... | collective-permute-start | bytes 442376 | tf_op jit(solution)/shard_map/ppermute | solution.py:30
  182.2 4.6 %collective-permute-start.26 = (f32[2,1,384,768]{3,2,1,0:T(8,128)S(1)}, f32[2,1,384,768]{3,2,1,0:T(8,128)S(1)}, u32[]{:S(2)}, u32[]{:S(2)}) collective-permute-start(f32[2,1,384,768]{3,2,1,0:T(8,128)S(1)} %shard_map.83.token_ref), channel_id=1, source_target_pairs={{0,8},{8,0},{16,24},{24,16},{1,9},{9,1},{17,25},{25,17},{2,10},{10... | collective-permute-start | bytes 7077896 | tf_op jit(solution)/shard_map/ppermute | solution.py:30
  182.3 19.1 %collective-permute-start.24 = (f32[2,2,192,384]{3,2,1,0:T(8,128)S(1)}, f32[2,2,192,384]{3,2,1,0:T(8,128)S(1)}, u32[]{:S(2)}, u32[]{:S(2)}) collective-permute-start(f32[2,2,192,384]{3,2,1,0:T(8,128)S(1)} %shard_map.80.token_ref.one_ref), channel_id=1, source_target_pairs={{0,1},{1,0},{2,3},{3,2},{4,5},{5,4},{6,7},{7,6},{8,10},{9,11},{10,... | collective-permute-start | bytes 3538952 | tf_op jit(solution)/shard_map/ppermute | solution.py:44
  184.1 17.5 %collective-permute-start.23 = (f32[2,2,48,384]{3,2,1,0:T(8,128)S(1)}, f32[2,2,48,384]{3,2,1,0:T(8,128)S(1)}, u32[]{:S(2)}, u32[]{:S(2)}) collective-permute-start(f32[2,2,48,384]{3,2,1,0:T(8,128)S(1)} %shard_map.82.token_ref.one_ref), channel_id=1, source_target_pairs={{0,4},{1,5},{2,6},{3,7},{4,0},{5,1},{6,2},{7,3},{8,9},{9,8},{10,11... | collective-permute-start | bytes 884744 | tf_op jit(solution)/shard_map/ppermute | solution.py:44
  191.5 10.1 %copy-start.11 = (f32[96,768]{1,0:T(8,128)}, f32[96,768]{1,0:T(8,128)S(1)}, u32[]{:S(2)}) copy-start(f32[96,768]{1,0:T(8,128)S(1)} %get-tuple-element.56.token_ref) | copy-start | bytes 884740
  201.6 16.3 %collective-permute-start.27 = (f32[2,2,96,384]{3,2,1,0:T(8,128)S(1)}, f32[2,2,96,384]{3,2,1,0:T(8,128)S(1)}, u32[]{:S(2)}, u32[]{:S(2)}) collective-permute-start(f32[2,2,96,384]{3,2,1,0:T(8,128)S(1)} %shard_map.86.one_ref.token_ref), channel_id=1, source_target_pairs={{0,2},{1,3},{2,0},{3,1},{4,6},{5,7},{6,4},{7,5},{8,12},{9,13},{10,... | collective-permute-start | bytes 1769480 | tf_op jit(solution)/shard_map/ppermute | solution.py:44
  218.0 16.4 %collective-permute-start.28 = (f32[2,2,192,384]{3,2,1,0:T(8,128)S(1)}, f32[2,2,192,384]{3,2,1,0:T(8,128)}, u32[]{:S(2)}, u32[]{:S(2)}) collective-permute-start(f32[2,2,192,384]{3,2,1,0:T(8,128)S(1)} %shard_map.87.one_ref.token_ref), channel_id=1, source_target_pairs={{0,1},{1,0},{2,3},{3,2},{4,5},{5,4},{6,7},{7,6},{8,10},{9,11},{10,... | collective-permute-start | bytes 3538952 | tf_op jit(solution)/shard_map/ppermute | solution.py:44
  219.6 71.8 %collective-permute-start.31 = (f32[1,768,1024]{2,1,0:T(8,128)}, f32[1,768,1024]{2,1,0:T(8,128)S(1)}, u32[]{:S(2)}, u32[]{:S(2)}) collective-permute-start(f32[1,768,1024]{2,1,0:T(8,128)} %copy-done.4), channel_id=1, source_target_pairs={{0,16},{16,0},{8,24},{24,8},{1,17},{17,1},{9,25},{25,9},{2,18},{18... | collective-permute-start | bytes 9437192 | tf_op jit(solution)/shard_map/ppermute | solution.py:30
  221.1 29.3 %collective-permute-start.29 = (f32[2,384,384]{2,1,0:T(8,128)S(1)}, f32[2,384,384]{2,1,0:T(8,128)S(1)}, u32[]{:S(2)}, u32[]{:S(2)}) collective-permute-start(f32[2,384,384]{2,1,0:T(8,128)S(1)} %slice_bitcast_fusion.1), channel_id=1, source_target_pairs={{0,8},{8,0},{16,24},{24,16},{1,9},{9,1},{17,25},{25,17},{2,10},{10... | collective-permute-start | bytes 3538952 | tf_op jit(solution)/shard_map/ppermute | solution.py:30
  234.3 3.2 %copy-start.20 = (bf16[2,1,768,768]{3,2,1,0:T(8,128)(2,1)S(1)}, bf16[2,1,768,768]{3,2,1,0:T(8,128)(2,1)}, u32[]{:S(2)}) copy-start(bf16[2,1,768,768]{3,2,1,0:T(8,128)(2,1)} %get-tuple-element.61.low_ref) | copy-start | bytes 7077892
  235.9 14.5 %copy-start.3 = (f32[2,2,384,384]{3,2,1,0:T(8,128)}, f32[2,2,384,384]{3,2,1,0:T(8,128)S(1)}, u32[]{:S(2)}) copy-start(f32[2,2,384,384]{3,2,1,0:T(8,128)S(1)} %shard_map.88.token_ref) | copy-start | bytes 7077892
  236.0 14.5 %collective-permute-start.30 = (f32[2,384,384]{2,1,0:T(8,128)S(1)}, f32[2,384,384]{2,1,0:T(8,128)S(1)}, u32[]{:S(2)}, u32[]{:S(2)}) collective-permute-start(f32[2,384,384]{2,1,0:T(8,128)S(1)} %slice_bitcast_fusion), channel_id=1, source_target_pairs={{0,8},{8,0},{16,24},{24,16},{1,9},{9,1},{17,25},{25,17},{2,10},{10... | collective-permute-start | bytes 3538952 | tf_op jit(solution)/shard_map/ppermute | solution.py:30
  250.6 6.3 %copy-start.10 = (f32[1,384,1024]{2,1,0:T(8,128)S(1)}, f32[1,384,1024]{2,1,0:T(8,128)}, u32[]{:S(2)}) copy-start(f32[1,384,1024]{2,1,0:T(8,128)} %copy-done.9) | copy-start | bytes 4718596
  255.2 36.0 %collective-permute-start.32 = (f32[96,384]{1,0:T(8,128)S(1)}, f32[96,384]{1,0:T(8,128)S(1)}, u32[]{:S(2)}, u32[]{:S(2)}) collective-permute-start(f32[96,384]{1,0:T(8,128)S(1)} %constant_dynamic-slice_fusion.1), channel_id=1, source_target_pairs={{0,16},{16,0},{8,24},{24,8},{1,17},{17,1},{9,25},{25,9},{2,18},{18... | collective-permute-start | bytes 442376 | tf_op jit(solution)/shard_map/ppermute | solution.py:30
  260.3 31.1 %copy-start.6 = (bf16[2,1,768,768]{3,2,1,0:T(8,128)(2,1)S(1)}, bf16[2,1,768,768]{3,2,1,0:T(8,128)(2,1)}, u32[]{:S(2)}) copy-start(bf16[2,1,768,768]{3,2,1,0:T(8,128)(2,1)} %get-tuple-element.57.high_ref) | copy-start | bytes 7077892
  260.3 31.1 %copy-start.8 = (bf16[2,1,768,768]{3,2,1,0:T(8,128)(2,1)S(1)}, bf16[2,1,768,768]{3,2,1,0:T(8,128)(2,1)}, u32[]{:S(2)}) copy-start(bf16[2,1,768,768]{3,2,1,0:T(8,128)(2,1)} %get-tuple-element.58.low_ref) | copy-start | bytes 7077892
  291.3 7.7 %collective-permute-start.33 = (f32[96,192]{1,0:T(8,128)S(1)}, f32[96,192]{1,0:T(8,128)S(1)}, u32[]{:S(2)}, u32[]{:S(2)}) collective-permute-start(f32[96,192]{1,0:T(8,128)S(1)} %constant_dynamic-slice_fusion), channel_id=1, source_target_pairs={{0,8},{8,0},{16,24},{24,16},{1,9},{9,1},{17,25},{25,17},{2,10},{10... | collective-permute-start | bytes 221192 | tf_op jit(solution)/shard_map/ppermute | solution.py:30
  (12 other events, 23.8 us)

commit v4 on v3

--- a/solution.py
+++ b/solution.py
@@ -16,8 +16,8 @@
     return pltpu.CompilerParams(vmem_limit_bytes=mebibytes * 2**20)
 
 
-def cost(flops, read):
-    return pl.CostEstimate(flops=int(flops), bytes_accessed=int(read), transcendentals=0)
+def cost():
+    return pl.CostEstimate(flops=1, bytes_accessed=1, transcendentals=0)
 
 
 def swapped(block, axis, bit):
@@ -31,7 +31,7 @@
 
 
 def orders(bits):
-    return (list(range(bits)), list(range(1, bits)) + [0])
+    return (list(range(bits)), [1, 0] + list(range(2, bits)))
 
 
 def across(block, step):
@@ -90,13 +90,16 @@
     target_ref[...] = source_ref[...]
 
 
-def picked(three_index, plan, state, token, turn, own, start, count):
+def picked(three_index, plan, state, token, turn, own, part, parts):
     per_block, width, depth = three_index.shape
     half_count = per_block // 2
-    rows = count // 2 if count % 16 == 0 and start % (count // 2) == 0 else count
+    count = width if own else width // parts
+    depth = depth // parts if own else depth
+    rows = count // 2
 
     def source(h, piece, plan_ref, state_ref):
-        return (slot_of(plan_ref, state_ref, per_block, turn, h, own), start // rows + piece, 0)
+        slot = slot_of(plan_ref, state_ref, per_block, turn, h, own)
+        return (slot, piece, part) if own else (slot, part * 2 + piece, 0)
 
     return pl.pallas_call(
         copy_kernel,
@@ -108,7 +111,7 @@
             out_specs=pl.BlockSpec((1, rows, depth), lambda h, piece, *_: (h, piece, 0)),
         ),
         compiler_params=params(24),
-        cost_estimate=cost(0, 8 * half_count * count * depth),
+        cost_estimate=cost(),
     )(plan, state, three_index, token)
 
 
@@ -168,10 +171,7 @@
             scratch_shapes=[pltpu.VMEM((count, depth), jnp.bfloat16)] * 2,
         ),
         compiler_params=params(44),
-        cost_estimate=cost(
-            6 * half_count * width * count * depth,
-            4 * half_count * (width * depth + count * depth + width * count),
-        ),
+        cost_estimate=cost(),
     )(plan, state, three_index, peer, token)
 
 
@@ -199,8 +199,27 @@
         in_specs=[VMEM, VMEM, ANY],
         out_specs=(VMEM, VMEM),
         compiler_params=params(16),
-        cost_estimate=cost(keep.size, 12 * keep.size),
+        cost_estimate=cost(),
     )(keep, came, token)
+
+
+def last_kernel(one_ref, two_ref, token_ref, keep_ref, give_ref):
+    del token_ref
+    half = one_ref.shape[2]
+    keep_ref[:, :half], keep_ref[:, half:] = one_ref[0], two_ref[0]
+    give_ref[:, :half], give_ref[:, half:] = one_ref[1], two_ref[1]
+
+
+def last_joined(one, two, token):
+    out = jax.ShapeDtypeStruct((one.shape[1], 2 * one.shape[2], one.shape[3]), jnp.float32)
+    return pl.pallas_call(
+        last_kernel,
+        out_shape=(out, out),
+        in_specs=[VMEM, VMEM, ANY],
+        out_specs=(VMEM, VMEM),
+        compiler_params=params(24),
+        cost_estimate=cost(),
+    )(one, two, token)
 
 
 def join_kernel(axis, one_ref, two_ref, token_ref, out_ref):
@@ -221,7 +240,7 @@
         in_specs=[VMEM, VMEM, ANY],
         out_specs=VMEM,
         compiler_params=params(24),
-        cost_estimate=cost(0, 16 * one.size),
+        cost_estimate=cost(),
     )(one, two, token)
 
 
@@ -252,13 +271,14 @@
         in_specs=[SMEM, SMEM, SMEM, VMEM, VMEM, VMEM, VMEM, ANY],
         out_specs=VMEM,
         compiler_params=params(16),
-        cost_estimate=cost(8 * left.size, 12 * left.size),
+        cost_estimate=cost(),
     )(ours, theirs, state, column, row, left, right, token)
 
 
-def tilde_kernel(blocks, count, state_ref, token_ref, *refs):
+def tilde_kernel(blocks, places, state_ref, token_ref, *refs):
     del token_ref
-    sources, (high_ref, low_ref, density_ref, amp, tilde) = refs[: 4 * count], refs[4 * count :]
+    count = len(places)
+    sources, (high_ref, low_ref, density_ref, amp, tilde) = refs[: 2 * count], refs[2 * count :]
     width = amp.shape[0]
     rows = width // blocks
     core = state_ref[0] % 2
@@ -268,14 +288,15 @@
         for who in range(2):
             offset = 0
             for part in range(count):
-                mine, came = sources[who * 2 * count + part], sources[who * 2 * count + count + part]
+                mine, came = sources[2 * part], sources[2 * part + 1]
+                first, second = (start + h for start in places[part][who])
                 size = mine.shape[2]
                 for place in range(blocks // 2):
                     here = slice(place * rows, (place + 1) * rows)
                     spot = (core * (blocks // 2) + (place ^ state_ref[1])) * rows
-                    amp[pl.ds(pl.multiple_of(spot, rows), rows), offset : offset + size] = mine[h, here, :]
+                    amp[pl.ds(pl.multiple_of(spot, rows), rows), offset : offset + size] = mine[first, here, :]
                     spot = ((1 - core) * (blocks // 2) + (place ^ state_ref[2])) * rows
-                    amp[pl.ds(pl.multiple_of(spot, rows), rows), offset : offset + size] = came[h, here, :]
+                    amp[pl.ds(pl.multiple_of(spot, rows), rows), offset : offset + size] = came[second, here, :]
                 offset += size
             for part in range(width // band):
                 spot = slice(part * band, (part + 1) * band)
@@ -297,70 +318,78 @@
                     density_ref[...] += value
 
 
-def tildes(state, token, own, peer, blocks, share):
-    sources = [x for x, _ in own] + [y for _, y in own] + [x for x, _ in peer] + [y for _, y in peer]
-    half_count, half, _ = sources[0].shape
-    width = 2 * half
+def tildes(state, token, gathered, blocks, share, half_count):
+    sources = [array for mine, came, _, _ in gathered for array in (mine, came)]
+    places = [spots for _, _, *spots in gathered]
+    width = 2 * sources[0].shape[1]
     out = jax.ShapeDtypeStruct((2, half_count, width, width), jnp.bfloat16)
     return pl.pallas_call(
-        functools.partial(tilde_kernel, blocks, len(own)),
+        functools.partial(tilde_kernel, blocks, places),
         out_shape=(out, out, jax.ShapeDtypeStruct((share, width), jnp.float32)),
         in_specs=[SMEM, ANY] + [VMEM] * len(sources),
         out_specs=(VMEM, VMEM, VMEM),
         scratch_shapes=[pltpu.VMEM((width, width), jnp.float32)] * 2,
         compiler_params=params(48),
-        cost_estimate=cost(24 * width * width * share, 24 * width * width),
+        cost_estimate=cost(),
     )(state, token, *sources)
 
 
-def gradient_kernel(count, based, plan_ref, state_ref, high_ref, low_ref, token_ref, *refs):
+def gradient_kernel(count, based, columns, plan_ref, state_ref, high_ref, low_ref, token_ref, *refs):
     del plan_ref, state_ref, token_ref
     out_ref = refs[-1]
-    tall = high_ref.shape[2]
+
+    def term(spot, source):
+        tilde = (high_ref[0, 0, :, spot], low_ref[0, 0, :, spot])
+        return multiply(tilde, halves(source[0]), ((1,), (0,)))
+
+    if columns:
+        for piece, source in enumerate(refs[:count]):
+
+            @pl.when(pl.program_id(2) == piece)
+            def _():
+                out_ref[0] = refs[count][0] + term(slice(None), source)
+
+        return
     value = refs[count][0] if based else None
     offset = 0
     for source in refs[:count]:
-        size = source.shape[1]
-        spot = slice(offset, offset + size)
-        term = multiply((high_ref[0, 0, :, spot], low_ref[0, 0, :, spot]), halves(source[0]), ((1,), (0,)))
-        value = term if value is None else value + term
-        offset += size
+        added = term(slice(offset, offset + source.shape[1]), source)
+        value = added if value is None else value + added
+        offset += source.shape[1]
     out_ref[0] = value
 
 
-def gradient_terms(plan, state, token, high, low, sources, base, turn, per_block, terms):
-    width, depth = high.shape[2], sources[0].shape[2]
-    half_count = per_block // 2
-    tile = depth // 4 if depth % 512 == 0 else depth
+def gradient_terms(plan, state, token, high, low, sources, base, turn, own, three_index):
+    per_block, width, depth = three_index.shape
+    half_count = per_block // 2
+    columns = sources[0].shape[2] < depth
+    tile = sources[0].shape[2] if columns else depth // 4 if depth % 512 == 0 else depth
     chosen = sources[0].shape[0] == per_block
-
-    def block_at(term, h, piece, p, s):
-        return (slot_of(p, s, per_block, turn, h, terms[0] + term == 0), 0, piece)
-
-    def source_at(term, h, piece, p, s):
-        if not chosen:
-            return (h, 0, piece)
-        return (peer_slot_of(p, s, per_block, turn, h, terms[0] + term == 0), 0, piece)
-
-    square = pl.BlockSpec((1, 1, width, width), lambda term, h, piece, *_: (terms[0] + term, h, 0, 0))
+    at = 0 if own else 1
+
+    def block_at(h, _, piece, p, s):
+        return (slot_of(p, s, per_block, turn, h, own), 0, piece)
+
+    def source_at(h, _, piece, p, s):
+        slot = peer_slot_of(p, s, per_block, turn, h, own) if chosen else h
+        return (slot, 0, 0 if columns else piece)
+
+    square = pl.BlockSpec((1, 1, width, width), lambda h, *_: (at, h, 0, 0))
     out_spec = pl.BlockSpec((1, width, tile), block_at)
     return pl.pallas_call(
-        functools.partial(gradient_kernel, len(sources), base is not None),
+        functools.partial(gradient_kernel, len(sources), turn > 0, columns),
         out_shape=jax.ShapeDtypeStruct((per_block, width, depth), jnp.float32),
         grid_spec=pltpu.PrefetchScalarGridSpec(
             num_scalar_prefetch=2,
-            grid=(len(terms), half_count, depth // tile),
+            grid=(half_count, 1, depth // tile),
             in_specs=[square, square, ANY]
             + [pl.BlockSpec((1, x.shape[1], tile), source_at) for x in sources]
-            + ([out_spec] if base is not None else []),
+            + ([] if base is None else [out_spec] if turn > 0 else [ANY]),
             out_specs=out_spec,
         ),
         input_output_aliases={} if base is None else {5 + len(sources): 0},
-        compiler_params=params(40),
-        cost_estimate=cost(
-            6 * len(terms) * half_count * width * width * depth,
-            4 * len(terms) * half_count * (width * depth * 3 + width * width),
-        ),
+        compiler_params=params(44),
+        cost_estimate=cost(),
     )(plan, state, high, low, token, *sources, *(() if base is None else (base,)))
 
 
@@ -386,15 +415,17 @@
     for stage in reversed(range(bits)):
         came = across(value, stage)
         token = yield value
-        value = joined(value, came, token, 2)
+        if stage > 0 or turn == 0:
+            value = joined(value, came, token, 2)
+        else:
+            value, give = last_joined(value, came, token)
     if turn == 0:
+        value = value.reshape((2 * half_count,) + value.shape[2:])
         came = swapped(value, "pair", 0)
-        env["gathered"][turn].append(((value[0], came[1]), (value[1], came[0])))
+        env["gathered"][turn].append((value, came, (0, half_count), (half_count, 0)))
     else:
-        came = swapped(value[1], "pair", 0)
-        env["gathered"][turn].append(
-            ((value[0, :half_count], came[:half_count]), (value[0, half_count:], came[half_count:]))
-        )
+        came = swapped(give, "pair", 0)
+        env["gathered"][turn].append((value, came, (0, 0), (half_count, half_count)))
     yield value
 
 
@@ -423,20 +454,22 @@
         ]
     ).astype(jnp.int32)
 
-    cuts = 2
+    mine = jnp.concatenate([occupied_energy, plan.astype(jnp.float32).reshape(-1)])
+    core_info = swapped(mine, "pair", 0)
+    info = jnp.stack([mine, core_info])
+    peer_info = [jnp.stack([core_info, mine])]
+    peer_info += [swapped(info, "pair", turn) for turn in range(1, rounds)]
+    cuts, pieces = 2, 4
     step = width // cuts
     firsts = [None] * rounds
     token = virtual_energy
     for turn in range(1, rounds):
         firsts[turn] = []
         for cut in range(cuts):
-            token = picked(three_index, plan, state, token, turn, False, cut * step, step)
+            token = picked(three_index, plan, state, token, turn, False, cut, cuts)
             firsts[turn].append(swapped(token, "pair", turn))
     other = swapped(three_index, "pair", 0)
     firsts[0] = [other]
-    mine = jnp.concatenate([occupied_energy, plan.astype(jnp.float32).reshape(-1)])
-    core_info = swapped(mine, "pair", 0)
-    info = jnp.stack([mine, core_info])
     env = {
         "bits": bits,
         "per_block": per_block,
@@ -447,58 +480,72 @@
         "virtual": virtual_energy,
         "column": virtual_energy[:, None],
         "info": info,
-        "peer_info": [jnp.stack([core_info, mine])]
-        + [swapped(info, "pair", turn) for turn in range(1, rounds)],
+        "peer_info": peer_info,
         "gathered": [[] for _ in range(rounds)],
     }
+    seconds = [[other]] + [[] for _ in range(1, rounds)]
+    gradient = None
+    tilde = [None] * rounds
+    densities = []
+
+    def send_piece(turn, piece):
+        def run(token):
+            token = picked(three_index, plan, state, token, turn, True, piece, pieces)
+            seconds[turn].append(swapped(token, "pair", turn))
+            return token
+
+        return run
+
+    def make_tilde(turn):
+        def run(token):
+            high, low, density = tildes(state, token, env["gathered"][turn], blocks, row_count, half_count)
+            tilde[turn] = (high, low)
+            densities.append(density)
+            return density
+
+        return run
+
+    def add_terms(turn, own):
+        def run(token):
+            nonlocal gradient
+            sources = firsts[turn] if own else seconds[turn]
+            gradient = gradient_terms(
+                plan, state, token, *tilde[turn], sources, gradient, turn, own, three_index
+            )
+            return gradient
+
+        return run
 
     tasks = []
+    late = []
     for turn in range(rounds):
         for cut, first in enumerate(firsts[turn]):
             worker = chain(env, turn, cut * step if turn else 0, first)
             next(worker)
             share = first.shape[1] / width
-            clock = 18.0 if turn == 0 else 40.0 + 34.0 * cut + 70.0 * (turn - 1)
-            times = [clock, clock + 3 + 9 * share + 3]
+            clock = 12.0 if turn == 0 else 41.0 + 35.0 * cut + 137.0 * (turn - 1)
+            times = [clock, clock + 4 + 8 * share]
             wide = 12.8 * share
             for stage in range(bits):
-                times.append(times[-1] + 4 + (wide if stage < 2 else wide / 2))
+                times.append(times[-1] + 4 + (wide / 2 if stage == 1 else wide))
             if turn > 0:
                 wide *= 2
-                times.append(times[-1] + 6)
+                times.append(times[-1] + 8)
             for stage in range(bits):
-                times.append(times[-1] + 4 + (wide if stage > 0 else wide / 2))
-            tasks += [(time, turn, cut, worker) for time in times]
-            if cut == len(firsts[turn]) - 1:
-                tasks.append((times[-1] + 6, turn, cut, None))
+                times.append(times[-1] + 4 + (wide / 2 if stage == 1 else wide))
+            tasks += [(time, worker.send) for time in times]
+            late.append(times)
     for turn in range(1, rounds):
-        tasks.append((62.0 + 70.0 * (turn - 1), turn, -1, None))
-    tasks.sort(key=lambda task: task[:3])
-    seconds = [other] + [None] * (rounds - 1)
-    gradient = None
-    densities = []
-    for _, turn, cut, worker in tasks:
-        if worker is not None:
-            token = worker.send(token)
-        elif cut < 0:
-            token = picked(three_index, plan, state, token, turn, True, 0, width)
-            seconds[turn] = swapped(token, "pair", turn)
+        tasks += [(66.0 + 17.0 * piece + 137.0 * (turn - 1), send_piece(turn, piece)) for piece in range(pieces)]
+    for turn in range(rounds):
+        steps = [make_tilde(turn), add_terms(turn, True), add_terms(turn, False)]
+        if turn == 0 and rounds > 1:
+            tasks += [(time + 1, step_) for time, step_ in zip(late[cuts][-3:], steps)]
         else:
-            own, peer = zip(*env["gathered"][turn])
-            high, low, density = tildes(state, token, own, peer, blocks, row_count)
-            densities.append(density)
-            if turn == 0:
-                gradient = gradient_terms(
-                    plan, state, density, high, low, [other], None, turn, per_block, (0, 1)
-                )
-            else:
-                gradient = gradient_terms(
-                    plan, state, density, high, low, firsts[turn], gradient, turn, per_block, (0,)
-                )
-                gradient = gradient_terms(
-                    plan, state, density, high, low, [seconds[turn]], gradient, turn, per_block, (1,)
-                )
-            token = density
+            tasks += [(late[-1][-1] + 6 + index, step_) for index, step_ in enumerate(steps)]
+    tasks.sort(key=lambda task: task[0])
+    for _, task in tasks:
+        token = task(token)
     density = sum(densities)
     for bit in reversed(range(lax.axis_size("pair").bit_length() - 1)):
         half = density.shape[1] // 2

time: 301 us -> 331 us (1.100)
  local copies, waits for them, and re-layouts: 13.9 us -> 25.2 us
  starting transfers between devices: 52.9 us -> 60.6 us
  Pallas kernels: 67.7 us -> 75.1 us
  waiting for transfers between devices: 163 us -> 167 us
    ppermute x16 -> x19, waiting for transfers between devices: 66.7 us -> 81.8 us  [swapped(): return lax.ppermute(block, axis, route)]
    unnamed x52 -> x57, local copies, waits for them, and re-layouts: 12.8 us -> 24.8 us
    ppermute x18, waiting for transfers between devices: 96.3 us -> 84.8 us  [across(): return lax.ppermute(block, ('pair', 'aux'), route)]
    ppermute x18, starting transfers between devices: 26.8 us -> 32.5 us  [across(): return lax.ppermute(block, ('pair', 'aux'), route)]
    pallas_call x3 -> x6, Pallas kernels: 3.35 us -> 8.88 us  [picked(): pl.pallas_call(copy_kernel, out_shape=jax.ShapeDtypeStruct((half_count, c...]
    pallas_call x5 -> x8, Pallas kernels: 38 us -> 43 us  [the longest x4 32.3 us: gradient_terms(): pl.pallas_call(functools.partial(gradient_kernel, len(sources), turn > 0,...]
    ppermute x16 -> x19, starting transfers between devices: 26.1 us -> 28.1 us  [swapped(): return lax.ppermute(block, axis, route)]
  transfers between devices with their start and end apart: 34 -> 37, of which waited for: 20 -> 18; matrix products, arithmetic and copies ran while one was open for 0% -> 2% of each run, Pallas kernels for 20% -> 19%
where the time goes in v4:
time: 331 us; the launch traced here: 330 us
  waiting for transfers between devices  167 us (50%)
  Pallas kernels  75.1 us (23%)
  starting transfers between devices  60.6 us (18%)
  local copies, waits for them, and re-layouts  25.2 us (8%)
    ppermute x18, waiting for transfers between devices, across(): return lax.ppermute(block, ('pair', 'aux'), route)  84.8 us
    ppermute x19, waiting for transfers between devices, swapped(): return lax.ppermute(block, axis, route)  81.8 us
    ppermute x18, starting transfers between devices, across(): return lax.ppermute(block, ('pair', 'aux'), route)  32.5 us
    pallas_call x4, Pallas kernels, gradient_terms(): pl.pallas_call(functools.partial(gradient_kernel, len(sources), turn > 0,...  32.3 us
    ppermute x19, starting transfers between devices, swapped(): return lax.ppermute(block, axis, route)  28.1 us
    unnamed x57, local copies, waits for them, and re-layouts  24.8 us
    pallas_call x3, Pallas kernels, integral(): pl.pallas_call(functools.partial(integral_kernel, turn, blocks), out_shap...  16.9 us
    pallas_call x2, Pallas kernels, tildes(): pl.pallas_call(functools.partial(tilde_kernel, blocks, places), out_shape...  9.44 us
  transfers between devices with their start and end apart: 37, of which 18 were waited for; matrix products, arithmetic and copies ran while one was open for 2% of the time, Pallas kernels for 19%

profile of v4, /device:TPU:0, one launch (start us, length us, event | category | flops | bytes accessed | tf_op | source)
XLA Modules:
  0.0 329.6 jit_solution(18317806824101414375)
XLA Ops:
  1.2 2.8 copy-done
  6.1 1.8 shard_map.60.token_ref
  7.9 3.3 %collective-permute-done.3.peer_ref.refs_0_ = f32[2,768,1024]{2,1,0:T(8,128)} collective-permute-done((f32[2,768,1024]{2,1,0:T(8,128)}, f32[2,768,1024]{2,1,0:T(8,128)}, u32[]{:S(2)}, u32[]{:S(2)}) %collective-permute-start.3) | collective-permute-done | bytes 6291488 | tf_op jit(solution)/shard_map/ppermute | solution.py:30
  11.3 7.5 %shard_map.61 = (f32[1,384,768]{2,1,0:T(8,128)S(1)}, f32[1,384,768]{2,1,0:T(8,128)S(1)}) custom-call(s32[2,2]{1,0:T(2,128)S(1)} %copy-done.19, s32[4]{0:T(128)S(1)} %pad_add_fusion.state_ref, f32[2,768,1024]{2,1,0:T(8,128)S(1)} %bitcast.9, f32[2,768,1024]{2,1,0:T(8,128)} %collective-permute-done.3.peer_ref.refs_0_, f32[1,384,1024]{2,1,0:T(8,128)} %shard_map.60.token_ref), custom_call_target="tpu_custom_call" | custom-call | flops 1 | bytes 1 | tf_op jit(solution)/shard_map/pallas_call | solution.py:156
  19.2 2.7 collective-permute-start.7
  22.0 2.7 collective-permute-start.5
  26.3 12.7 %collective-permute-done.5.came_ref = f32[2,1,192,768]{3,2,1,0:T(8,128)S(1)} collective-permute-done((f32[2,1,192,768]{3,2,1,0:T(8,128)S(1)}, f32[2,1,192,768]{3,2,1,0:T(8,128)S(1)}, u32[]{:S(2)}, u32[]{:S(2)}) %collective-permute-start.5) | collective-permute-done | bytes 1179680 | tf_op jit(solution)/shard_map/ppermute | solution.py:44
  39.1 18.0 %collective-permute-done.7.peer_ref.refs_0_ = f32[1,384,1024]{2,1,0:T(8,128)S(1)} collective-permute-done((f32[1,384,1024]{2,1,0:T(8,128)S(1)}, f32[1,384,1024]{2,1,0:T(8,128)S(1)}, u32[]{:S(2)}, u32[]{:S(2)}) %collective-permute-start.7) | collective-permute-done | bytes 1572896 | tf_op jit(solution)/shard_map/ppermute | solution.py:30
  57.1 4.0 %shard_map.64 = (f32[1,384,384]{2,1,0:T(8,128)S(1)}, f32[1,384,384]{2,1,0:T(8,128)S(1)}) custom-call(s32[2,2]{1,0:T(2,128)S(1)} %copy-done.19, s32[4]{0:T(128)S(1)} %pad_add_fusion.state_ref, f32[2,768,1024]{2,1,0:T(8,128)S(1)} %bitcast.9, f32[1,384,1024]{2,1,0:T(8,128)S(1)} %collective-permute-done.7.peer_ref.refs_0_, ...), custom_call_target="tpu_custom_call" | custom-call | flops 1 | bytes 1 | tf_op jit(solution)/shard_map/pallas_call | solution.py:156
  61.2 2.1 collective-permute-start.6
  65.2 1.8 collective-permute-start.10
  67.1 7.0 %collective-permute-done.6.came_ref = f32[2,1,96,768]{3,2,1,0:T(8,128)} collective-permute-done((f32[2,1,96,768]{3,2,1,0:T(8,128)S(1)}, f32[2,1,96,768]{3,2,1,0:T(8,128)}, u32[]{:S(2)}, u32[]{:S(2)}) %collective-permute-start.6) | collective-permute-done | bytes 589856 | tf_op jit(solution)/shard_map/ppermute | solution.py:44
  75.3 3.4 %collective-permute-start.9 = (f32[2,1,48,768]{3,2,1,0:T(8,128)S(1)}, f32[2,1,48,768]{3,2,1,0:T(8,128)S(1)}, u32[]{:S(2)}, u32[]{:S(2)}) collective-permute-start(f32[2,1,48,768]{3,2,1,0:T(8,128)S(1)} %get-tuple-element.46.token_ref), channel_id=1, source_target_pairs={{0,4},{1,5},{2,6},{3,7},{4,0},{5,1},{6,2},{7,3},{8,12},{9,13},{10,... | collective-permute-start | bytes 884744 | tf_op jit(solution)/shard_map/ppermute | solution.py:44
  79.8 1.6 collective-permute-start.11
  83.8 2.8 copy-done.1
  88.2 2.3 collective-permute-done.11.came_ref
  91.3 5.4 %shard_map.71 = (f32[1,384,384]{2,1,0:T(8,128)S(1)}, f32[1,384,384]{2,1,0:T(8,128)S(1)}) custom-call(s32[2,2]{1,0:T(2,128)S(1)} %copy-done.19, s32[4]{0:T(128)S(1)} %pad_add_fusion.state_ref, f32[2,768,1024]{2,1,0:T(8,128)S(1)} %bitcast.11, f32[1,384,1024]{2,1,0:T(8,128)} %collective-permute-done.2.peer_ref.refs_1_, ...), custom_call_target="tpu_custom_call" | custom-call | flops 1 | bytes 1 | tf_op jit(solution)/shard_map/pallas_call | solution.py:156
  96.8 2.9 collective-permute-start.16
  101.4 2.0 collective-permute-done.1.theirs_ref
  103.4 16.6 %collective-permute-done.13.right_ref = f32[2,1,48,384]{3,2,1,0:T(8,128)S(1)} collective-permute-done((f32[2,1,48,384]{3,2,1,0:T(8,128)S(1)}, f32[2,1,48,384]{3,2,1,0:T(8,128)S(1)}, u32[]{:S(2)}, u32[]{:S(2)}) %collective-permute-start.13) | collective-permute-done | bytes 147488 | tf_op jit(solution)/shard_map/ppermute | solution.py:44
  120.6 1.6 shard_map.73.token_ref
  126.3 3.7 %collective-permute-done.15.two_ref = f32[2,1,48,384]{3,2,1,0:T(8,128)S(1)} collective-permute-done((f32[2,1,48,384]{3,2,1,0:T(8,128)S(1)}, f32[2,1,48,384]{3,2,1,0:T(8,128)S(1)}, u32[]{:S(2)}, u32[]{:S(2)}) %collective-permute-start.15) | collective-permute-done | bytes 147488 | tf_op jit(solution)/shard_map/ppermute | solution.py:30
  130.0 8.2 %collective-permute-done.14.came_ref = f32[2,1,192,384]{3,2,1,0:T(8,128)S(1)} collective-permute-done((f32[2,1,192,384]{3,2,1,0:T(8,128)S(1)}, f32[2,1,192,384]{3,2,1,0:T(8,128)S(1)}, u32[]{:S(2)}, u32[]{:S(2)}) %collective-permute-start.14) | collective-permute-done | bytes 589856 | tf_op jit(solution)/shard_map/ppermute | solution.py:44
  141.0 2.7 collective-permute-start.21
  143.6 1.6 shard_map.79.token_ref
  145.2 11.0 %collective-permute-done.17.came_ref = f32[2,1,96,384]{3,2,1,0:T(8,128)S(1)} collective-permute-done((f32[2,1,96,384]{3,2,1,0:T(8,128)S(1)}, f32[2,1,96,384]{3,2,1,0:T(8,128)S(1)}, u32[]{:S(2)}, u32[]{:S(2)}) %collective-permute-start.17) | collective-permute-done | bytes 294944 | tf_op jit(solution)/shard_map/ppermute | solution.py:44
  156.3 1.7 collective-permute-start.23
  158.2 8.6 %collective-permute-start.26 = (f32[2,384,768]{2,1,0:T(8,128)S(1)}, f32[2,384,768]{2,1,0:T(8,128)S(1)}, u32[]{:S(2)}, u32[]{:S(2)}) collective-permute-start(f32[2,384,768]{2,1,0:T(8,128)S(1)} %bitcast.12), channel_id=1, source_target_pairs={{0,8},{8,0},{16,24},{24,16},{1,9},{9,1},{17,25},{25,17},{2,10},{10... | collective-permute-start | bytes 7077896 | tf_op jit(solution)/shard_map/ppermute | solution.py:30
  166.8 3.1 collective-permute-start.19
  169.9 7.2 %collective-permute-done.19.right_ref = f32[2,1,48,384]{3,2,1,0:T(8,128)S(1)} collective-permute-done((f32[2,1,48,384]{3,2,1,0:T(8,128)S(1)}, f32[2,1,48,384]{3,2,1,0:T(8,128)S(1)}, u32[]{:S(2)}, u32[]{:S(2)}) %collective-permute-start.19) | collective-permute-done | bytes 147488 | tf_op jit(solution)/shard_map/ppermute | solution.py:44
  182.4 2.0 collective-permute-done.22.two_ref
  185.4 8.8 %collective-permute-done.25.two_ref = f32[2,2,192,384]{3,2,1,0:T(8,128)S(1)} collective-permute-done((f32[2,2,192,384]{3,2,1,0:T(8,128)S(1)}, f32[2,2,192,384]{3,2,1,0:T(8,128)S(1)}, u32[]{:S(2)}, u32[]{:S(2)}) %collective-permute-start.25) | collective-permute-done | bytes 1179680 | tf_op jit(solution)/shard_map/ppermute | solution.py:44
  197.6 4.2 %shard_map.89 = (bf16[2,1,768,768]{3,2,1,0:T(8,128)(2,1)S(1)}, bf16[2,1,768,768]{3,2,1,0:T(8,128)(2,1)S(1)}, f32[96,768]{1,0:T(8,128)S(1)}) custom-call(s32[4]{0:T(128)S(1)} %pad_add_fusion.state_ref, f32[2,2,96,384]{3,2,1,0:T(8,128)S(1)} %shard_map.88.token_ref.one_ref, f32[2,384,768]{2,1,0:T(8,128)} %bitcast.14, f32[2,384,768]{2,1,0:T(8,128)} %copy-done.22), custom_call_target="tpu_custom_call" | custom-call | flops 1 | bytes 1 | tf_op jit(solution)/shard_map/pallas_call | solution.py:326
  201.8 3.8 %collective-permute-done.27.two_ref = f32[2,2,96,384]{3,2,1,0:T(8,128)S(1)} collective-permute-done((f32[2,2,96,384]{3,2,1,0:T(8,128)S(1)}, f32[2,2,96,384]{3,2,1,0:T(8,128)S(1)}, u32[]{:S(2)}, u32[]{:S(2)}) %collective-permute-start.27) | collective-permute-done | bytes 589856 | tf_op jit(solution)/shard_map/ppermute | solution.py:44
  205.7 2.6 collective-permute-start.28
  209.1 7.4 %shard_map.91.token_ref.refs_1_ = f32[2,768,1024]{2,1,0:T(8,128)} custom-call(s32[2,2]{1,0:T(2,128)S(1)} %copy-done.19, s32[4]{0:T(128)S(1)} %pad_add_fusion.state_ref, bf16[2,1,768,768]{3,2,1,0:T(8,128)(2,1)S(1)} %get-tuple-element.61.high_ref, bf16[2,1,768,768]{3,2,1,0:T(8,128)(2,1)S(1)} %get-tuple-element.62.low_ref, ...), custom_call_target="tpu_custom_call" | custom-call | flops 1 | bytes 1 | tf_op jit(solution)/shard_map/pallas_call | solution.py:379
  216.5 6.0 %collective-permute-done.28.two_ref = f32[2,2,192,384]{3,2,1,0:T(8,128)S(1)} collective-permute-done((f32[2,2,192,384]{3,2,1,0:T(8,128)S(1)}, f32[2,2,192,384]{3,2,1,0:T(8,128)S(1)}, u32[]{:S(2)}, u32[]{:S(2)}) %collective-permute-start.28) | collective-permute-done | bytes 1179680 | tf_op jit(solution)/shard_map/ppermute | solution.py:44
  222.5 2.8 copy-done.2
  233.1 1.7 copy-done.7
  234.8 7.5 %shard_map.93.token_ref.refs_2_ = f32[2,768,1024]{2,1,0:T(8,128)} custom-call(s32[2,2]{1,0:T(2,128)S(1)} %copy-done.19, s32[4]{0:T(128)S(1)} %pad_add_fusion.state_ref, bf16[2,1,768,768]{3,2,1,0:T(8,128)(2,1)S(1)} %get-tuple-element.61.high_ref, bf16[2,1,768,768]{3,2,1,0:T(8,128)(2,1)S(1)} %copy-done.7, ...), custom_call_target="tpu_custom_call", output_to_operand_aliasing={{}: (6, {})} | custom-call | flops 1 | bytes 1 | tf_op jit(solution)/shard_map/pallas_call | solution.py:379
  242.4 5.2 %shard_map.94 = (bf16[2,1,768,768]{3,2,1,0:T(8,128)(2,1)}, bf16[2,1,768,768]{3,2,1,0:T(8,128)(2,1)}, f32[96,768]{1,0:T(8,128)S(1)}) custom-call(s32[4]{0:T(128)S(1)} %pad_add_fusion.state_ref, f32[2,768,1024]{2,1,0:T(8,128)} %shard_map.93.token_ref.refs_2_, f32[2,384,384]{2,1,0:T(8,128)S(1)} %copy-done.11, f32[2,384,384]{2,1,0:T(8,128)S(1)} %copy-done.15, ...), custom_call_target="tpu_custom_call" | custom-call | flops 1 | bytes 1 | tf_op jit(solution)/shard_map/pallas_call | solution.py:326
  247.7 1.6 collective-permute-start.35
  249.3 52.1 %collective-permute-done.35 = f32[96,384]{1,0:T(8,128)S(1)} collective-permute-done((f32[96,384]{1,0:T(8,128)S(1)}, f32[96,384]{1,0:T(8,128)S(1)}, u32[]{:S(2)}, u32[]{:S(2)}) %collective-permute-start.35) | collective-permute-done | bytes 147488 | tf_op jit(solution)/shard_map/ppermute | solution.py:30
  301.7 1.7 copy-done.4
  303.3 1.7 copy-done.5
  305.0 8.6 %shard_map.95.token_ref = f32[2,768,1024]{2,1,0:T(8,128)} custom-call(s32[2,2]{1,0:T(2,128)S(1)} %copy-done.19, s32[4]{0:T(128)S(1)} %pad_add_fusion.state_ref, bf16[2,1,768,768]{3,2,1,0:T(8,128)(2,1)S(1)} %copy-done.4, bf16[2,1,768,768]{3,2,1,0:T(8,128)(2,1)S(1)} %copy-done.5, ...), custom_call_target="tpu_custom_call", output_to_operand_aliasing={{}: (7, {})} | custom-call | flops 1 | bytes 1 | tf_op jit(solution)/shard_map/pallas_call | solution.py:379
  313.6 6.6 %copy.14.refs_4_ = f32[2,768,1024]{2,1,0:T(8,128)} copy(f32[2,768,1024]{2,1,0:T(8,128)} %shard_map.95.token_ref) | data formatting | bytes 12582912
  320.2 8.6 %shard_map.96 = f32[2,768,1024]{2,1,0:T(8,128)} custom-call(s32[2,2]{1,0:T(2,128)S(1)} %copy-done.19, s32[4]{0:T(128)S(1)} %pad_add_fusion.state_ref, bf16[2,1,768,768]{3,2,1,0:T(8,128)(2,1)S(1)} %copy-done.4, bf16[2,1,768,768]{3,2,1,0:T(8,128)(2,1)S(1)} %copy-done.5, f32[2,768,1024]{2,1,0:T(8,128)} %shard_map.95.token_ref, ...), custom_call_target="tpu_custom_call", output_to_operand_aliasing={{}: (9, {})} | custom-call | flops 1 | bytes 1 | tf_op jit(solution)/shard_map/pallas_call | solution.py:379
  (139 shorter events, 42.7 us)
Async XLA Ops:
  0.6 10.6 %collective-permute-start.3 = (f32[2,768,1024]{2,1,0:T(8,128)}, f32[2,768,1024]{2,1,0:T(8,128)}, u32[]{:S(2)}, u32[]{:S(2)}) collective-permute-start(f32[2,768,1024]{2,1,0:T(8,128)} %source_ref.11), channel_id=1, source_target_pairs={{0,8},{8,0},{16,24},{24,16},{1,9},{9,1},{17,25},{25,17},{2,10},{10... | collective-permute-start | bytes 18874376 | tf_op jit(solution)/shard_map/ppermute | solution.py:30
  5.4 5.9 %slice-start = ((s8[6291456]{0:T(1024)(128)(4,1)}), s8[4194304]{0:T(1024)(128)(4,1)S(1)}, s32[]{:S(2)}) async-start(s8[6291456]{0:T(1024)(128)(4,1)} %bitcast.8), calls=%async_computation | async-start | bytes 8388608
  18.8 3.1 collective-permute-start.4
  19.2 37.9 %collective-permute-start.7 = (f32[1,384,1024]{2,1,0:T(8,128)S(1)}, f32[1,384,1024]{2,1,0:T(8,128)S(1)}, u32[]{:S(2)}, u32[]{:S(2)}) collective-permute-start(f32[1,384,1024]{2,1,0:T(8,128)S(1)} %shard_map.59.token_ref), channel_id=1, source_target_pairs={{0,16},{16,0},{8,24},{24,8},{1,17},{17,1},{9,25},{25,9},{2,18},{18... | collective-permute-start | bytes 4718600 | tf_op jit(solution)/shard_map/ppermute | solution.py:30
  22.0 16.9 %collective-permute-start.5 = (f32[2,1,192,768]{3,2,1,0:T(8,128)S(1)}, f32[2,1,192,768]{3,2,1,0:T(8,128)S(1)}, u32[]{:S(2)}, u32[]{:S(2)}) collective-permute-start(f32[2,1,192,768]{3,2,1,0:T(8,128)S(1)} %get-tuple-element.39.token_ref), channel_id=1, source_target_pairs={{0,1},{1,0},{2,3},{3,2},{4,5},{5,4},{6,7},{7,6},{8,10},{9,11},{10,... | collective-permute-start | bytes 3538952 | tf_op jit(solution)/shard_map/ppermute | solution.py:44
  24.8 66.5 %collective-permute-start.2 = (f32[1,384,1024]{2,1,0:T(8,128)}, f32[1,384,1024]{2,1,0:T(8,128)}, u32[]{:S(2)}, u32[]{:S(2)}) collective-permute-start(f32[1,384,1024]{2,1,0:T(8,128)} %shard_map.60.token_ref), channel_id=1, source_target_pairs={{0,16},{16,0},{8,24},{24,8},{1,17},{17,1},{9,25},{25,9},{2,18},{18... | collective-permute-start | bytes 4718600 | tf_op jit(solution)/shard_map/ppermute | solution.py:30
  61.1 2.2 collective-permute-start.8
  61.2 12.9 %collective-permute-start.6 = (f32[2,1,96,768]{3,2,1,0:T(8,128)S(1)}, f32[2,1,96,768]{3,2,1,0:T(8,128)}, u32[]{:S(2)}, u32[]{:S(2)}) collective-permute-start(f32[2,1,96,768]{3,2,1,0:T(8,128)S(1)} %get-tuple-element.41.token_ref), channel_id=1, source_target_pairs={{0,2},{1,3},{2,0},{3,1},{4,6},{5,7},{6,4},{7,5},{8,9},{9,8},{10,11... | collective-permute-start | bytes 1769480 | tf_op jit(solution)/shard_map/ppermute | solution.py:44
  63.3 27.9 %slice-start.2 = ((s8[6291456]{0:T(1024)(128)(4,1)}), s8[2097152]{0:T(1024)(128)(4,1)S(1)}, s32[]{:S(2)}) async-start(s8[6291456]{0:T(1024)(128)(4,1)} %bitcast.10), calls=%async_computation.2 | async-start | bytes 4194304
  65.2 13.4 %collective-permute-start.10 = (f32[2,1,192,384]{3,2,1,0:T(8,128)}, f32[2,1,192,384]{3,2,1,0:T(8,128)}, u32[]{:S(2)}, u32[]{:S(2)}) collective-permute-start(f32[2,1,192,384]{3,2,1,0:T(8,128)} %get-tuple-element.44.token_ref), channel_id=1, source_target_pairs={{0,1},{1,0},{2,3},{3,2},{4,5},{5,4},{6,7},{7,6},{8,10},{9,11},{10,... | collective-permute-start | bytes 1769480 | tf_op jit(solution)/shard_map/ppermute | solution.py:44
  67.1 11.5 %copy-start.17 = (f32[2,1,192,384]{3,2,1,0:T(8,128)S(1)}, f32[2,1,192,384]{3,2,1,0:T(8,128)}, u32[]{:S(2)}) copy-start(f32[2,1,192,384]{3,2,1,0:T(8,128)} %copy-done.16) | copy-start | bytes 1769476
  75.2 6.2 %copy-start.23 = (f32[2]{0:T(128)S(1)}, f32[2]{0:T(128)}, u32[]{:S(2)}) copy-start(f32[2]{0:T(128)} %param.5) | copy-start | bytes 28
  75.3 7.7 %copy-start.21 = (f32[768]{0:T(1024)S(1)}, f32[768]{0:T(1024)}, u32[]{:S(2)}) copy-start(f32[768]{0:T(1024)} %token_ref.1) | copy-start | bytes 9220
  75.3 15.3 %collective-permute-start.9 = (f32[2,1,48,768]{3,2,1,0:T(8,128)S(1)}, f32[2,1,48,768]{3,2,1,0:T(8,128)S(1)}, u32[]{:S(2)}, u32[]{:S(2)}) collective-permute-start(f32[2,1,48,768]{3,2,1,0:T(8,128)S(1)} %get-tuple-element.46.token_ref), channel_id=1, source_target_pairs={{0,4},{1,5},{2,6},{3,7},{4,0},{5,1},{6,2},{7,3},{8,12},{9,13},{10,... | collective-permute-start | bytes 884744 | tf_op jit(solution)/shard_map/ppermute | solution.py:44
  79.8 10.7 %collective-permute-start.11 = (f32[2,1,96,384]{3,2,1,0:T(8,128)S(1)}, f32[2,1,96,384]{3,2,1,0:T(8,128)S(1)}, u32[]{:S(2)}, u32[]{:S(2)}) collective-permute-start(f32[2,1,96,384]{3,2,1,0:T(8,128)S(1)} %get-tuple-element.49.token_ref), channel_id=1, source_target_pairs={{0,2},{1,3},{2,0},{3,1},{4,6},{5,7},{6,4},{7,5},{8,9},{9,8},{10,11... | collective-permute-start | bytes 884744 | tf_op jit(solution)/shard_map/ppermute | solution.py:44
  81.5 2.3 collective-permute-start
  96.7 25.5 %collective-permute-start.12 = (f32[1,384,384]{2,1,0:T(8,128)S(1)}, f32[1,384,384]{2,1,0:T(8,128)S(1)}, u32[]{:S(2)}, u32[]{:S(2)}) collective-permute-start(f32[1,384,384]{2,1,0:T(8,128)S(1)} %get-tuple-element.52.token_ref), channel_id=1, source_target_pairs={{0,8},{8,0},{16,24},{24,16},{1,9},{9,1},{17,25},{25,17},{2,10},{10... | collective-permute-start | bytes 1769480 | tf_op jit(solution)/shard_map/ppermute | solution.py:30
  96.8 27.1 %collective-permute-start.16 = (f32[2,1,48,768]{3,2,1,0:T(8,128)S(1)}, f32[2,1,48,768]{3,2,1,0:T(8,128)S(1)}, u32[]{:S(2)}, u32[]{:S(2)}) collective-permute-start(f32[2,1,48,768]{3,2,1,0:T(8,128)S(1)} %shard_map.70.token_ref.one_ref), channel_id=1, source_target_pairs={{0,4},{1,5},{2,6},{3,7},{4,0},{5,1},{6,2},{7,3},{8,12},{9,13},{10,... | collective-permute-start | bytes 884744 | tf_op jit(solution)/shard_map/ppermute | solution.py:44
  99.7 20.2 %collective-permute-start.13 = (f32[2,1,48,384]{3,2,1,0:T(8,128)S(1)}, f32[2,1,48,384]{3,2,1,0:T(8,128)S(1)}, u32[]{:S(2)}, u32[]{:S(2)}) collective-permute-start(f32[2,1,48,384]{3,2,1,0:T(8,128)S(1)} %get-tuple-element.50.token_ref), channel_id=1, source_target_pairs={{0,4},{1,5},{2,6},{3,7},{4,0},{5,1},{6,2},{7,3},{8,12},{9,13},{10,... | collective-permute-start | bytes 442376 | tf_op jit(solution)/shard_map/ppermute | solution.py:44
  99.8 3.6 %collective-permute-start.1 = (f32[2,6]{1,0:T(2,128)S(1)}, f32[2,6]{1,0:T(2,128)S(1)}, u32[]{:S(2)}, u32[]{:S(2)}) collective-permute-start(f32[2,6]{1,0:T(2,128)S(1)} %get-tuple-element.73.ours_ref), channel_id=1, source_target_pairs={{0,16},{16,0},{8,24},{24,8},{1,17},{17,1},{9,25},{25,9},{2,18},{18... | collective-permute-start | bytes 152 | tf_op jit(solution)/shard_map/ppermute | solution.py:30
  122.3 15.9 %collective-permute-start.14 = (f32[2,1,192,384]{3,2,1,0:T(8,128)S(1)}, f32[2,1,192,384]{3,2,1,0:T(8,128)S(1)}, u32[]{:S(2)}, u32[]{:S(2)}) collective-permute-start(f32[2,1,192,384]{3,2,1,0:T(8,128)S(1)} %get-tuple-element.55.token_ref), channel_id=1, source_target_pairs={{0,1},{1,0},{2,3},{3,2},{4,5},{5,4},{6,7},{7,6},{8,10},{9,11},{10,... | collective-permute-start | bytes 1769480 | tf_op jit(solution)/shard_map/ppermute | solution.py:44
  123.9 14.4 %collective-permute-start.18 = (f32[2,1,96,768]{3,2,1,0:T(8,128)S(1)}, f32[2,1,96,768]{3,2,1,0:T(8,128)S(1)}, u32[]{:S(2)}, u32[]{:S(2)}) collective-permute-start(f32[2,1,96,768]{3,2,1,0:T(8,128)S(1)} %shard_map.75.token_ref.one_ref), channel_id=1, source_target_pairs={{0,2},{1,3},{2,0},{3,1},{4,6},{5,7},{6,4},{7,5},{8,9},{9,8},{10,11... | collective-permute-start | bytes 1769480 | tf_op jit(solution)/shard_map/ppermute | solution.py:44
  124.7 5.2 %collective-permute-start.15 = (f32[2,1,48,384]{3,2,1,0:T(8,128)S(1)}, f32[2,1,48,384]{3,2,1,0:T(8,128)S(1)}, u32[]{:S(2)}, u32[]{:S(2)}) collective-permute-start(f32[2,1,48,384]{3,2,1,0:T(8,128)S(1)} %shard_map.72.token_ref.one_ref), channel_id=1, source_target_pairs={{0,16},{16,0},{8,24},{24,8},{1,17},{17,1},{9,25},{25,9},{2,18},{18... | collective-permute-start | bytes 442376 | tf_op jit(solution)/shard_map/ppermute | solution.py:30
  138.4 19.7 %collective-permute-start.20 = (f32[2,1,192,768]{3,2,1,0:T(8,128)S(1)}, f32[2,1,192,768]{3,2,1,0:T(8,128)S(1)}, u32[]{:S(2)}, u32[]{:S(2)}) collective-permute-start(f32[2,1,192,768]{3,2,1,0:T(8,128)S(1)} %shard_map.78.token_ref.one_ref), channel_id=1, source_target_pairs={{0,1},{1,0},{2,3},{3,2},{4,5},{5,4},{6,7},{7,6},{8,10},{9,11},{10,... | collective-permute-start | bytes 3538952 | tf_op jit(solution)/shard_map/ppermute | solution.py:44
  140.0 16.3 %collective-permute-start.17 = (f32[2,1,96,384]{3,2,1,0:T(8,128)S(1)}, f32[2,1,96,384]{3,2,1,0:T(8,128)S(1)}, u32[]{:S(2)}, u32[]{:S(2)}) collective-permute-start(f32[2,1,96,384]{3,2,1,0:T(8,128)S(1)} %get-tuple-element.57.token_ref), channel_id=1, source_target_pairs={{0,2},{1,3},{2,0},{3,1},{4,6},{5,7},{6,4},{7,5},{8,9},{9,8},{10,11... | collective-permute-start | bytes 884744 | tf_op jit(solution)/shard_map/ppermute | solution.py:44
  141.0 15.3 %collective-permute-start.21 = (f32[2,2,48,384]{3,2,1,0:T(8,128)S(1)}, f32[2,2,48,384]{3,2,1,0:T(8,128)S(1)}, u32[]{:S(2)}, u32[]{:S(2)}) collective-permute-start(f32[2,2,48,384]{3,2,1,0:T(8,128)S(1)} %shard_map.76.token_ref.one_ref), channel_id=1, source_target_pairs={{0,4},{1,5},{2,6},{3,7},{4,0},{5,1},{6,2},{7,3},{8,12},{9,13},{10,... | collective-permute-start | bytes 884744 | tf_op jit(solution)/shard_map/ppermute | solution.py:44
  156.3 21.5 %collective-permute-start.23 = (f32[2,2,96,384]{3,2,1,0:T(8,128)S(1)}, f32[2,2,96,384]{3,2,1,0:T(8,128)S(1)}, u32[]{:S(2)}, u32[]{:S(2)}) collective-permute-start(f32[2,2,96,384]{3,2,1,0:T(8,128)S(1)} %shard_map.81.token_ref.one_ref), channel_id=1, source_target_pairs={{0,2},{1,3},{2,0},{3,1},{4,6},{5,7},{6,4},{7,5},{8,9},{9,8},{10,11... | collective-permute-start | bytes 1769480 | tf_op jit(solution)/shard_map/ppermute | solution.py:44
  158.2 19.6 %copy-start.3 = (f32[2,1,384,768]{3,2,1,0:T(8,128)}, f32[2,1,384,768]{3,2,1,0:T(8,128)S(1)}, u32[]{:S(2)}) copy-start(f32[2,1,384,768]{3,2,1,0:T(8,128)S(1)} %shard_map.82) | copy-start | bytes 7077892
  158.2 37.9 %collective-permute-start.26 = (f32[2,384,768]{2,1,0:T(8,128)S(1)}, f32[2,384,768]{2,1,0:T(8,128)S(1)}, u32[]{:S(2)}, u32[]{:S(2)}) collective-permute-start(f32[2,384,768]{2,1,0:T(8,128)S(1)} %bitcast.12), channel_id=1, source_target_pairs={{0,8},{8,0},{16,24},{24,16},{1,9},{9,1},{17,25},{25,17},{2,10},{10... | collective-permute-start | bytes 7077896 | tf_op jit(solution)/shard_map/ppermute | solution.py:30
  166.8 10.3 %collective-permute-start.19 = (f32[2,1,48,384]{3,2,1,0:T(8,128)S(1)}, f32[2,1,48,384]{3,2,1,0:T(8,128)S(1)}, u32[]{:S(2)}, u32[]{:S(2)}) collective-permute-start(f32[2,1,48,384]{3,2,1,0:T(8,128)S(1)} %get-tuple-element.59.token_ref), channel_id=1, source_target_pairs={{0,4},{1,5},{2,6},{3,7},{4,0},{5,1},{6,2},{7,3},{8,12},{9,13},{10,... | collective-permute-start | bytes 442376 | tf_op jit(solution)/shard_map/ppermute | solution.py:44
  177.9 16.3 %collective-permute-start.25 = (f32[2,2,192,384]{3,2,1,0:T(8,128)S(1)}, f32[2,2,192,384]{3,2,1,0:T(8,128)S(1)}, u32[]{:S(2)}, u32[]{:S(2)}) collective-permute-start(f32[2,2,192,384]{3,2,1,0:T(8,128)S(1)} %shard_map.84.token_ref.one_ref), channel_id=1, source_target_pairs={{0,1},{1,0},{2,3},{3,2},{4,5},{5,4},{6,7},{7,6},{8,10},{9,11},{10,... | collective-permute-start | bytes 3538952 | tf_op jit(solution)/shard_map/ppermute | solution.py:44
  179.3 5.1 %collective-permute-start.22 = (f32[2,1,48,384]{3,2,1,0:T(8,128)S(1)}, f32[2,1,48,384]{3,2,1,0:T(8,128)S(1)}, u32[]{:S(2)}, u32[]{:S(2)}) collective-permute-start(f32[2,1,48,384]{3,2,1,0:T(8,128)S(1)} %shard_map.83.token_ref.one_ref), channel_id=1, source_target_pairs={{0,16},{16,0},{8,24},{24,8},{1,17},{17,1},{9,25},{25,9},{2,18},{18... | collective-permute-start | bytes 442376 | tf_op jit(solution)/shard_map/ppermute | solution.py:30
  184.5 11.2 %collective-permute-start.24 = (f32[2,2,48,384]{3,2,1,0:T(8,128)S(1)}, f32[2,2,48,384]{3,2,1,0:T(8,128)S(1)}, u32[]{:S(2)}, u32[]{:S(2)}) collective-permute-start(f32[2,2,48,384]{3,2,1,0:T(8,128)S(1)} %shard_map.86.token_ref.one_ref), channel_id=1, source_target_pairs={{0,4},{1,5},{2,6},{3,7},{4,0},{5,1},{6,2},{7,3},{8,12},{9,13},{10,... | collective-permute-start | bytes 884744 | tf_op jit(solution)/shard_map/ppermute | solution.py:44
  195.7 9.9 %collective-permute-start.27 = (f32[2,2,96,384]{3,2,1,0:T(8,128)S(1)}, f32[2,2,96,384]{3,2,1,0:T(8,128)S(1)}, u32[]{:S(2)}, u32[]{:S(2)}) collective-permute-start(f32[2,2,96,384]{3,2,1,0:T(8,128)S(1)} %shard_map.88.token_ref.one_ref), channel_id=1, source_target_pairs={{0,2},{1,3},{2,0},{3,1},{4,6},{5,7},{6,4},{7,5},{8,9},{9,8},{10,11... | collective-permute-start | bytes 1769480 | tf_op jit(solution)/shard_map/ppermute | solution.py:44
  201.8 7.3 %copy-start.6 = (bf16[2,1,768,768]{3,2,1,0:T(8,128)(2,1)}, bf16[2,1,768,768]{3,2,1,0:T(8,128)(2,1)S(1)}, u32[]{:S(2)}) copy-start(bf16[2,1,768,768]{3,2,1,0:T(8,128)(2,1)S(1)} %get-tuple-element.62.low_ref) | copy-start | bytes 7077892
  205.7 16.8 %collective-permute-start.28 = (f32[2,2,192,384]{3,2,1,0:T(8,128)S(1)}, f32[2,2,192,384]{3,2,1,0:T(8,128)S(1)}, u32[]{:S(2)}, u32[]{:S(2)}) collective-permute-start(f32[2,2,192,384]{3,2,1,0:T(8,128)S(1)} %shard_map.90.token_ref.one_ref), channel_id=1, source_target_pairs={{0,1},{1,0},{2,3},{3,2},{4,5},{5,4},{6,7},{7,6},{8,10},{9,11},{10,... | collective-permute-start | bytes 3538952 | tf_op jit(solution)/shard_map/ppermute | solution.py:44
  208.3 23.3 %collective-permute-start.29 = (f32[2,384,384]{2,1,0:T(8,128)S(1)}, f32[2,384,384]{2,1,0:T(8,128)S(1)}, u32[]{:S(2)}, u32[]{:S(2)}) collective-permute-start(f32[2,384,384]{2,1,0:T(8,128)S(1)} %get-tuple-element.65), channel_id=1, source_target_pairs={{0,8},{8,0},{16,24},{24,16},{1,9},{9,1},{17,25},{25,17},{2,10},{10... | collective-permute-start | bytes 3538952 | tf_op jit(solution)/shard_map/ppermute | solution.py:30
  226.5 15.9 %collective-permute-start.30 = (f32[2,384,384]{2,1,0:T(8,128)}, f32[2,384,384]{2,1,0:T(8,128)}, u32[]{:S(2)}, u32[]{:S(2)}) collective-permute-start(f32[2,384,384]{2,1,0:T(8,128)} %get-tuple-element.66), channel_id=1, source_target_pairs={{0,8},{8,0},{16,24},{24,16},{1,9},{9,1},{17,25},{25,17},{2,10},{10... | collective-permute-start | bytes 3538952 | tf_op jit(solution)/shard_map/ppermute | solution.py:30
  228.0 92.2 %collective-permute-start.31 = (f32[1,768,256]{2,1,0:T(8,128)}, f32[1,768,256]{2,1,0:T(8,128)}, u32[]{:S(2)}, u32[]{:S(2)}) collective-permute-start(f32[1,768,256]{2,1,0:T(8,128)} %shard_map.68.token_ref), channel_id=1, source_target_pairs={{0,16},{16,0},{8,24},{24,8},{1,17},{17,1},{9,25},{25,9},{2,18},{18... | collective-permute-start | bytes 2359304 | tf_op jit(solution)/shard_map/ppermute | solution.py:30
  229.6 90.6 %collective-permute-start.32 = (f32[1,768,256]{2,1,0:T(8,128)}, f32[1,768,256]{2,1,0:T(8,128)}, u32[]{:S(2)}, u32[]{:S(2)}) collective-permute-start(f32[1,768,256]{2,1,0:T(8,128)} %shard_map.73.token_ref), channel_id=1, source_target_pairs={{0,16},{16,0},{8,24},{24,8},{1,17},{17,1},{9,25},{25,9},{2,18},{18... | collective-permute-start | bytes 2359304 | tf_op jit(solution)/shard_map/ppermute | solution.py:30
  230.1 90.1 %collective-permute-start.33 = (f32[1,768,256]{2,1,0:T(8,128)}, f32[1,768,256]{2,1,0:T(8,128)}, u32[]{:S(2)}, u32[]{:S(2)}) collective-permute-start(f32[1,768,256]{2,1,0:T(8,128)} %shard_map.79.token_ref), channel_id=1, source_target_pairs={{0,16},{16,0},{8,24},{24,8},{1,17},{17,1},{9,25},{25,9},{2,18},{18... | collective-permute-start | bytes 2359304 | tf_op jit(solution)/shard_map/ppermute | solution.py:30
  232.7 87.6 %collective-permute-start.34 = (f32[1,768,256]{2,1,0:T(8,128)}, f32[1,768,256]{2,1,0:T(8,128)}, u32[]{:S(2)}, u32[]{:S(2)}) collective-permute-start(f32[1,768,256]{2,1,0:T(8,128)} %shard_map.85.token_ref), channel_id=1, source_target_pairs={{0,16},{16,0},{8,24},{24,8},{1,17},{17,1},{9,25},{25,9},{2,18},{18... | collective-permute-start | bytes 2359304 | tf_op jit(solution)/shard_map/ppermute | solution.py:30
  234.8 7.6 %copy-start.11 = (f32[2,384,384]{2,1,0:T(8,128)S(1)}, f32[2,384,384]{2,1,0:T(8,128)}, u32[]{:S(2)}) copy-start(f32[2,384,384]{2,1,0:T(8,128)} %copy-done.10) | copy-start | bytes 3538948
  234.8 7.6 %copy-start.15 = (f32[2,384,384]{2,1,0:T(8,128)S(1)}, f32[2,384,384]{2,1,0:T(8,128)}, u32[]{:S(2)}) copy-start(f32[2,384,384]{2,1,0:T(8,128)} %copy-done.14) | copy-start | bytes 3538948
  242.3 5.3 %copy-start.13 = (f32[96,768]{1,0:T(8,128)S(1)}, f32[96,768]{1,0:T(8,128)}, u32[]{:S(2)}) copy-start(f32[96,768]{1,0:T(8,128)} %copy-done.12) | copy-start | bytes 884740
  247.6 54.0 %copy-start.9 = (f32[1,384,1024]{2,1,0:T(8,128)S(1)}, f32[1,384,1024]{2,1,0:T(8,128)}, u32[]{:S(2)}) copy-start(f32[1,384,1024]{2,1,0:T(8,128)} %copy-done.8) | copy-start | bytes 4718596
  247.7 53.8 %collective-permute-start.35 = (f32[96,384]{1,0:T(8,128)S(1)}, f32[96,384]{1,0:T(8,128)S(1)}, u32[]{:S(2)}, u32[]{:S(2)}) collective-permute-start(f32[96,384]{1,0:T(8,128)S(1)} %constant_dynamic-slice_fusion.1), channel_id=1, source_target_pairs={{0,16},{16,0},{8,24},{24,8},{1,17},{17,1},{9,25},{25,9},{2,18},{18... | collective-permute-start | bytes 442376 | tf_op jit(solution)/shard_map/ppermute | solution.py:30
  301.6 27.3 %collective-permute-start.36 = (f32[96,192]{1,0:T(8,128)S(1)}, f32[96,192]{1,0:T(8,128)S(1)}, u32[]{:S(2)}, u32[]{:S(2)}) collective-permute-start(f32[96,192]{1,0:T(8,128)S(1)} %constant_dynamic-slice_fusion), channel_id=1, source_target_pairs={{0,8},{8,0},{16,24},{24,16},{1,9},{9,1},{17,25},{25,17},{2,10},{10... | collective-permute-start | bytes 221192 | tf_op jit(solution)/shard_map/ppermute | solution.py:30
  (17 other events, 37.9 us)

commit v5 on v4

--- a/solution.py
+++ b/solution.py
@@ -115,13 +115,33 @@
     )(plan, state, three_index, token)
 
 
-def integral_kernel(turn, blocks, plan_ref, state_ref, own_ref, peer_ref, token_ref, keep_ref, give_ref, high, low):
+def gate_kernel(*refs):
+    refs[-1][...] = jnp.zeros_like(refs[-1])
+
+
+def gated(*tokens):
+    return pl.pallas_call(
+        gate_kernel,
+        out_shape=jax.ShapeDtypeStruct((8, 128), jnp.float32),
+        in_specs=[ANY] * len(tokens),
+        out_specs=VMEM,
+        compiler_params=params(16),
+        cost_estimate=cost(),
+    )(*tokens)
+
+
+def integral_kernel(turn, blocks, plan_ref, state_ref, own_ref, token_ref, *refs):
     del plan_ref, token_ref
+    keep_ref, give_ref, high, low = refs[-4:]
     band = pl.program_id(1)
 
     @pl.when(band == 0)
     def _():
-        high[...], low[...] = halves(peer_ref[0])
+        offset = 0
+        for peer_ref in refs[:-4]:
+            spot = slice(offset, offset + peer_ref.shape[1])
+            high[spot, :], low[spot, :] = halves(peer_ref[0])
+            offset += peer_ref.shape[1]
 
     own = halves(own_ref[0])
     value = multiply(own, (high[...], low[...]), ((1,), (1,)))
@@ -142,13 +162,13 @@
             give_ref[0, pl.ds(pl.multiple_of((place ^ state_ref[2]) * rows, rows), rows), :] = piece
 
 
-def integral(three_index, peer, plan, state, token, turn, blocks):
+def integral(three_index, peers, plan, state, token, turn, blocks):
     per_block, width, depth = three_index.shape
-    half_count, count = per_block // 2, peer.shape[1]
+    half_count, count = per_block // 2, sum(peer.shape[1] for peer in peers)
     bands = 2
     out = jax.ShapeDtypeStruct((half_count, width // 2, count), jnp.float32)
     whole = pl.BlockSpec((1, width // 2, count), lambda h, band, *_: (h, 0, 0))
-    chosen = peer.shape[0] == per_block
+    chosen = peers[0].shape[0] == per_block
 
     def peer_at(h, band, p, s):
         return (peer_slot_of(p, s, per_block, turn, h, True) if chosen else h, 0, 0)
@@ -164,15 +184,15 @@
                     (1, width // bands, depth),
                     lambda h, band, p, s: (slot_of(p, s, per_block, turn, h, True), band, 0),
                 ),
-                pl.BlockSpec((1, count, depth), peer_at),
                 ANY,
-            ],
+            ]
+            + [pl.BlockSpec((1, peer.shape[1], depth), peer_at) for peer in peers],
             out_specs=(whole, whole),
             scratch_shapes=[pltpu.VMEM((count, depth), jnp.bfloat16)] * 2,
         ),
         compiler_params=params(44),
         cost_estimate=cost(),
-    )(plan, state, three_index, peer, token)
+    )(plan, state, three_index, token, *peers)
 
 
 def part_kernel(keep_ref, came_ref, token_ref, low_ref, high_ref):
@@ -336,7 +356,8 @@
 
 def gradient_kernel(count, based, columns, plan_ref, state_ref, high_ref, low_ref, token_ref, *refs):
     del plan_ref, state_ref, token_ref
-    out_ref = refs[-1]
+    out_ref, done_ref = refs[-2:]
+    done_ref[...] = jnp.zeros_like(done_ref)
 
     def term(spot, source):
         tilde = (high_ref[0, 0, :, spot], low_ref[0, 0, :, spot])
@@ -378,14 +399,17 @@
     out_spec = pl.BlockSpec((1, width, tile), block_at)
     return pl.pallas_call(
         functools.partial(gradient_kernel, len(sources), turn > 0, columns),
-        out_shape=jax.ShapeDtypeStruct((per_block, width, depth), jnp.float32),
+        out_shape=(
+            jax.ShapeDtypeStruct((per_block, width, depth), jnp.float32),
+            jax.ShapeDtypeStruct((8, 128), jnp.float32),
+        ),
         grid_spec=pltpu.PrefetchScalarGridSpec(
             num_scalar_prefetch=2,
             grid=(half_count, 1, depth // tile),
             in_specs=[square, square, ANY]
             + [pl.BlockSpec((1, x.shape[1], tile), source_at) for x in sources]
             + ([] if base is None else [out_spec] if turn > 0 else [ANY]),
-            out_specs=out_spec,
+            out_specs=(out_spec, pl.BlockSpec((8, 128), lambda *_: (0, 0))),
         ),
         input_output_aliases={} if base is None else {5 + len(sources): 0},
         compiler_params=params(44),
@@ -393,18 +417,18 @@
     )(plan, state, high, low, token, *sources, *(() if base is None else (base,)))
 
 
-def chain(env, turn, offset, first):
+def chain(env, turn, offset, peers):
     bits, per_block = env["bits"], env["per_block"]
     half_count = per_block // 2
     token = yield None
-    keep, give = integral(env["three_index"], first, env["plan"], env["state"], token, turn, env["blocks"])
+    keep, give = integral(env["three_index"], peers, env["plan"], env["state"], token, turn, env["blocks"])
     came = swapped(give, "pair", 0)
     token = yield give
     for stage in range(bits):
         keep, give = parted(keep, came, token)
         came = across(give, stage)
         token = yield give
-    row = env["virtual"][None, offset : offset + first.shape[1]]
+    row = env["virtual"][None, offset : offset + keep.shape[3]]
     value = amplitude(
         env["info"], env["peer_info"][turn], env["state"], env["column"], row, keep, came, token, turn, per_block
     )
@@ -459,14 +483,14 @@
     info = jnp.stack([mine, core_info])
     peer_info = [jnp.stack([core_info, mine])]
     peer_info += [swapped(info, "pair", turn) for turn in range(1, rounds)]
-    cuts, pieces = 2, 4
+    cuts, rows, pieces = 2, 2, 4
     step = width // cuts
     firsts = [None] * rounds
     token = virtual_energy
     for turn in range(1, rounds):
         firsts[turn] = []
-        for cut in range(cuts):
-            token = picked(three_index, plan, state, token, turn, False, cut, cuts)
+        for piece in range(cuts * rows):
+            token = picked(three_index, plan, state, token, turn, False, piece, cuts * rows)
             firsts[turn].append(swapped(token, "pair", turn))
     other = swapped(three_index, "pair", 0)
     firsts[0] = [other]
@@ -488,6 +512,12 @@
     tilde = [None] * rounds
     densities = []
 
+    def gate(*arrived):
+        return lambda token: gated(token, *arrived)
+
+    def gate_piece(turn, piece):
+        return lambda token: gated(token, seconds[turn][piece])
+
     def send_piece(turn, piece):
         def run(token):
             token = picked(three_index, plan, state, token, turn, True, piece, pieces)
@@ -509,21 +539,22 @@
         def run(token):
             nonlocal gradient
             sources = firsts[turn] if own else seconds[turn]
-            gradient = gradient_terms(
+            gradient, token = gradient_terms(
                 plan, state, token, *tilde[turn], sources, gradient, turn, own, three_index
             )
-            return gradient
+            return token
 
         return run
 
-    tasks = []
+    tasks = [(20.0, gate(*peer_info))]
     late = []
     for turn in range(rounds):
-        for cut, first in enumerate(firsts[turn]):
-            worker = chain(env, turn, cut * step if turn else 0, first)
+        arrivals = [42.0 + 36.0 * cut + 137.0 * (turn - 1) for cut in range(cuts)] if turn else [11.0]
+        groups = [firsts[turn][cut * rows : (cut + 1) * rows] for cut in range(cuts)] if turn else [[other]]
+        for cut, (clock, peers) in enumerate(zip(arrivals, groups)):
+            worker = chain(env, turn, cut * step, peers)
             next(worker)
-            share = first.shape[1] / width
-            clock = 12.0 if turn == 0 else 41.0 + 35.0 * cut + 137.0 * (turn - 1)
+            share = 1 / len(groups)
             times = [clock, clock + 4 + 8 * share]
             wide = 12.8 * share
             for stage in range(bits):
@@ -535,8 +566,12 @@
                 times.append(times[-1] + 4 + (wide / 2 if stage == 1 else wide))
             tasks += [(time, worker.send) for time in times]
             late.append(times)
+            if turn > 0:
+                tasks.append((clock - 20.0, gate(peers[0])))
     for turn in range(1, rounds):
-        tasks += [(66.0 + 17.0 * piece + 137.0 * (turn - 1), send_piece(turn, piece)) for piece in range(pieces)]
+        for piece in range(pieces):
+            time = 94.0 + 17.0 * piece + 137.0 * (turn - 1) + (4.0 if piece == pieces - 1 else 0.0)
+            tasks += [(time - 20.0, send_piece(turn, piece)), (time, gate_piece(turn, piece))]
     for turn in range(rounds):
         steps = [make_tilde(turn), add_terms(turn, True), add_terms(turn, False)]
         if turn == 0 and rounds > 1:

time: 331 us -> 292 us (0.88)
  waiting for transfers between devices: 167 us -> 143 us
  starting transfers between devices: 60.6 us -> 52.2 us
  Pallas kernels: 75.1 us -> 71.2 us
  local copies, waits for them, and re-layouts: 25.2 us -> 21.6 us
    ppermute x19 -> x21, waiting for transfers between devices: 81.8 us -> 45.4 us  [swapped(): return lax.ppermute(block, axis, route)]
    ppermute x18, waiting for transfers between devices: 84.8 us -> 97.3 us  [across(): return lax.ppermute(block, ('pair', 'aux'), route)]
    ppermute x19 -> x21, starting transfers between devices: 28.1 us -> 19.7 us  [swapped(): return lax.ppermute(block, axis, route)]
    unnamed x57 -> x82, local copies, waits for them, and re-layouts: 24.8 us -> 21.3 us
    pallas_call x6 -> x8, Pallas kernels: 8.88 us -> 5.95 us  [picked(): pl.pallas_call(copy_kernel, out_shape=jax.ShapeDtypeStruct((half_count, c...]
  transfers between devices with their start and end apart: 37 -> 39, of which waited for: 18 -> 23; matrix products, arithmetic and copies ran while one was open for 2% -> 0% of each run, Pallas kernels for 19% -> 18%
where the time goes in v5:
time: 292 us; the launch traced here: 291 us
  waiting for transfers between devices  143 us (49%)
  Pallas kernels  71.2 us (24%)
  starting transfers between devices  52.2 us (18%)
  local copies, waits for them, and re-layouts  21.6 us (7%)
    ppermute x18, waiting for transfers between devices, across(): return lax.ppermute(block, ('pair', 'aux'), route)  97.3 us
    ppermute x21, waiting for transfers between devices, swapped(): return lax.ppermute(block, axis, route)  45.4 us
    ppermute x18, starting transfers between devices, across(): return lax.ppermute(block, ('pair', 'aux'), route)  32.5 us
    pallas_call x4, Pallas kernels, gradient_terms(): pl.pallas_call(functools.partial(gradient_kernel, len(sources), turn > 0,...  31.6 us
    unnamed x82, local copies, waits for them, and re-layouts  21.3 us
    ppermute x21, starting transfers between devices, swapped(): return lax.ppermute(block, axis, route)  19.7 us
    pallas_call x3, Pallas kernels, integral(): pl.pallas_call(functools.partial(integral_kernel, turn, blocks), out_shap...  16.6 us
    pallas_call x2, Pallas kernels, tildes(): pl.pallas_call(functools.partial(tilde_kernel, blocks, places), out_shape...  10 us
  transfers between devices with their start and end apart: 39, of which 23 were waited for; matrix products, arithmetic and copies ran while one was open for 0% of the time, Pallas kernels for 18%

profile of v5, /device:TPU:0, one launch (start us, length us, event | category | flops | bytes accessed | tf_op | source)
XLA Modules:
  0.0 290.9 jit_solution(5273789157469361644)
XLA Ops:
  1.2 2.8 copy-done
  8.2 3.1 %collective-permute-done.2.refs_0_ = f32[2,768,1024]{2,1,0:T(8,128)} collective-permute-done((f32[2,768,1024]{2,1,0:T(8,128)}, f32[2,768,1024]{2,1,0:T(8,128)}, u32[]{:S(2)}, u32[]{:S(2)}) %collective-permute-start.2) | collective-permute-done | bytes 6291488 | tf_op jit(solution)/shard_map/ppermute | solution.py:30
  11.3 8.5 %shard_map.63 = (f32[1,384,768]{2,1,0:T(8,128)S(1)}, f32[1,384,768]{2,1,0:T(8,128)}) custom-call(s32[2,2]{1,0:T(2,128)S(1)} %copy-done.33, s32[4]{0:T(128)S(1)} %pad_add_fusion.state_ref, f32[2,768,1024]{2,1,0:T(8,128)S(1)} %bitcast.9, f32[1,192,1024]{2,1,0:T(8,128)S(1)} %shard_map.62.token_ref, f32[2,768,1024]{2,1,0:T(8,128)} %collective-permute-done.2.refs_0_), custom_call_target="tpu_custom_call" | custom-call | flops 1 | bytes 1 | tf_op jit(solution)/shard_map/pallas_call | solution.py:176
  21.3 2.7 collective-permute-start.4
  26.7 15.4 %collective-permute-done.1.refs_2_.theirs_ref = f32[2,6]{1,0:T(2,128)S(1)} collective-permute-done((f32[2,6]{1,0:T(2,128)S(1)}, f32[2,6]{1,0:T(2,128)S(1)}, u32[]{:S(2)}, u32[]{:S(2)}) %collective-permute-start.1) | collective-permute-done | bytes 80 | tf_op jit(solution)/shard_map/ppermute | solution.py:30
  43.6 1.8 collective-permute-start.5
  45.3 1.5 collective-permute-start.6
  46.9 13.0 %collective-permute-done.5.came_ref = f32[2,1,192,768]{3,2,1,0:T(8,128)S(1)} collective-permute-done((f32[2,1,192,768]{3,2,1,0:T(8,128)S(1)}, f32[2,1,192,768]{3,2,1,0:T(8,128)S(1)}, u32[]{:S(2)}, u32[]{:S(2)}) %collective-permute-start.5) | collective-permute-done | bytes 1179680 | tf_op jit(solution)/shard_map/ppermute | solution.py:44
  59.9 4.2 %collective-permute-done.6.refs_1_ = f32[1,192,1024]{2,1,0:T(8,128)S(1)} collective-permute-done((f32[1,192,1024]{2,1,0:T(8,128)S(1)}, f32[1,192,1024]{2,1,0:T(8,128)S(1)}, u32[]{:S(2)}, u32[]{:S(2)}) %collective-permute-start.6) | collective-permute-done | bytes 786464 | tf_op jit(solution)/shard_map/ppermute | solution.py:30
  64.1 3.1 %copy-done.1 = f32[2,768,1024]{2,1,0:T(8,128)S(1)} copy-done((f32[2,768,1024]{2,1,0:T(8,128)S(1)}, f32[2,768,1024]{2,1,0:T(8,128)}, u32[]{:S(2)}) %copy-start.1) | copy-done | bytes 6291480
  67.2 4.0 %shard_map.68 = (f32[1,384,384]{2,1,0:T(8,128)S(1)}, f32[1,384,384]{2,1,0:T(8,128)S(1)}) custom-call(s32[2,2]{1,0:T(2,128)S(1)} %copy-done.33, s32[4]{0:T(128)S(1)} %pad_add_fusion.state_ref, f32[2,768,1024]{2,1,0:T(8,128)S(1)} %copy-done.1, f32[2,1,96,768]{3,2,1,0:T(8,128)S(1)} %get-tuple-element.47.token_ref, ...), custom_call_target="tpu_custom_call" | custom-call | flops 1 | bytes 1 | tf_op jit(solution)/shard_map/pallas_call | solution.py:176
  71.3 1.6 collective-permute-start.10
  73.4 1.6 collective-permute-start.8
  76.5 12.1 %collective-permute-done.9.came_ref = f32[2,1,96,768]{3,2,1,0:T(8,128)S(1)} collective-permute-done((f32[2,1,96,768]{3,2,1,0:T(8,128)S(1)}, f32[2,1,96,768]{3,2,1,0:T(8,128)S(1)}, u32[]{:S(2)}, u32[]{:S(2)}) %collective-permute-start.9) | collective-permute-done | bytes 589856 | tf_op jit(solution)/shard_map/ppermute | solution.py:44
  88.7 2.7 collective-permute-start.12
  92.5 10.8 %collective-permute-done.12.right_ref = f32[2,1,48,768]{3,2,1,0:T(8,128)S(1)} collective-permute-done((f32[2,1,48,768]{3,2,1,0:T(8,128)S(1)}, f32[2,1,48,768]{3,2,1,0:T(8,128)S(1)}, u32[]{:S(2)}, u32[]{:S(2)}) %collective-permute-start.12) | collective-permute-done | bytes 294944 | tf_op jit(solution)/shard_map/ppermute | solution.py:44
  105.1 2.8 collective-permute-start.16
  108.1 4.0 %shard_map.76 = (f32[1,384,384]{2,1,0:T(8,128)S(1)}, f32[1,384,384]{2,1,0:T(8,128)S(1)}) custom-call(s32[2,2]{1,0:T(2,128)S(1)} %copy-done.33, s32[4]{0:T(128)S(1)} %pad_add_fusion.state_ref, f32[2,768,1024]{2,1,0:T(8,128)S(1)} %copy-done.1, f32[1,768,256]{2,1,0:T(8,128)S(1)} %shard_map.75.token_ref, ...), custom_call_target="tpu_custom_call" | custom-call | flops 1 | bytes 1 | tf_op jit(solution)/shard_map/pallas_call | solution.py:176
  112.3 10.7 %collective-permute-done.16.right_ref = f32[2,1,48,384]{3,2,1,0:T(8,128)S(1)} collective-permute-done((f32[2,1,48,384]{3,2,1,0:T(8,128)S(1)}, f32[2,1,48,384]{3,2,1,0:T(8,128)S(1)}, u32[]{:S(2)}, u32[]{:S(2)}) %collective-permute-start.16) | collective-permute-done | bytes 147488 | tf_op jit(solution)/shard_map/ppermute | solution.py:44
  123.8 1.6 collective-permute-start.19
  125.4 4.9 %collective-permute-done.19.two_ref = f32[2,1,48,384]{3,2,1,0:T(8,128)S(1)} collective-permute-done((f32[2,1,48,384]{3,2,1,0:T(8,128)S(1)}, f32[2,1,48,384]{3,2,1,0:T(8,128)S(1)}, u32[]{:S(2)}, u32[]{:S(2)}) %collective-permute-start.19) | collective-permute-done | bytes 147488 | tf_op jit(solution)/shard_map/ppermute | solution.py:30
  131.1 2.5 collective-permute-done.18.two_ref
  133.7 1.6 collective-permute-start.25
  137.0 19.3 %collective-permute-done.17.came_ref = f32[2,1,192,384]{3,2,1,0:T(8,128)S(1)} collective-permute-done((f32[2,1,192,384]{3,2,1,0:T(8,128)S(1)}, f32[2,1,192,384]{3,2,1,0:T(8,128)S(1)}, u32[]{:S(2)}, u32[]{:S(2)}) %collective-permute-start.17) | collective-permute-done | bytes 589856 | tf_op jit(solution)/shard_map/ppermute | solution.py:44
  156.5 1.6 collective-permute-start.26
  158.1 2.0 collective-permute-start.24
  160.1 3.9 %collective-permute-done.21.came_ref = f32[2,1,96,384]{3,2,1,0:T(8,128)S(1)} collective-permute-done((f32[2,1,96,384]{3,2,1,0:T(8,128)S(1)}, f32[2,1,96,384]{3,2,1,0:T(8,128)S(1)}, u32[]{:S(2)}, u32[]{:S(2)}) %collective-permute-start.21) | collective-permute-done | bytes 294944 | tf_op jit(solution)/shard_map/ppermute | solution.py:44
  165.0 3.8 %collective-permute-start.31 = (f32[2,384,768]{2,1,0:T(8,128)S(1)}, f32[2,384,768]{2,1,0:T(8,128)S(1)}, u32[]{:S(2)}, u32[]{:S(2)}) collective-permute-start(f32[2,384,768]{2,1,0:T(8,128)S(1)} %bitcast.10), channel_id=1, source_target_pairs={{0,8},{8,0},{16,24},{24,16},{1,9},{9,1},{17,25},{25,17},{2,10},{10... | collective-permute-start | bytes 7077896 | tf_op jit(solution)/shard_map/ppermute | solution.py:30
  168.8 2.5 collective-permute-done.26.refs_1_
  172.2 2.7 collective-permute-start.29
  176.4 5.9 %collective-permute-start.23 = (f32[2,1,48,384]{3,2,1,0:T(8,128)S(1)}, f32[2,1,48,384]{3,2,1,0:T(8,128)S(1)}, u32[]{:S(2)}, u32[]{:S(2)}) collective-permute-start(f32[2,1,48,384]{3,2,1,0:T(8,128)S(1)} %get-tuple-element.66.token_ref), channel_id=1, source_target_pairs={{0,4},{1,5},{2,6},{3,7},{4,0},{5,1},{6,2},{7,3},{8,12},{9,13},{10,... | collective-permute-start | bytes 442376 | tf_op jit(solution)/shard_map/ppermute | solution.py:44
  182.4 6.1 %collective-permute-done.23.right_ref = f32[2,1,48,384]{3,2,1,0:T(8,128)S(1)} collective-permute-done((f32[2,1,48,384]{3,2,1,0:T(8,128)S(1)}, f32[2,1,48,384]{3,2,1,0:T(8,128)S(1)}, u32[]{:S(2)}, u32[]{:S(2)}) %collective-permute-start.23) | collective-permute-done | bytes 147488 | tf_op jit(solution)/shard_map/ppermute | solution.py:44
  190.3 5.7 %collective-permute-done.27.two_ref = f32[2,1,48,384]{3,2,1,0:T(8,128)S(1)} collective-permute-done((f32[2,1,48,384]{3,2,1,0:T(8,128)S(1)}, f32[2,1,48,384]{3,2,1,0:T(8,128)S(1)}, u32[]{:S(2)}, u32[]{:S(2)}) %collective-permute-start.27) | collective-permute-done | bytes 147488 | tf_op jit(solution)/shard_map/ppermute | solution.py:30
  196.0 6.2 %collective-permute-start.28 = (f32[2,2,48,384]{3,2,1,0:T(8,128)S(1)}, f32[2,2,48,384]{3,2,1,0:T(8,128)S(1)}, u32[]{:S(2)}, u32[]{:S(2)}) collective-permute-start(f32[2,2,48,384]{3,2,1,0:T(8,128)S(1)} %shard_map.92.refs_0_.one_ref), channel_id=1, source_target_pairs={{0,4},{1,5},{2,6},{3,7},{4,0},{5,1},{6,2},{7,3},{8,12},{9,13},{10,... | collective-permute-start | bytes 884744 | tf_op jit(solution)/shard_map/ppermute | solution.py:44
  204.6 10.8 %collective-permute-done.28.two_ref = f32[2,2,48,384]{3,2,1,0:T(8,128)S(1)} collective-permute-done((f32[2,2,48,384]{3,2,1,0:T(8,128)S(1)}, f32[2,2,48,384]{3,2,1,0:T(8,128)S(1)}, u32[]{:S(2)}, u32[]{:S(2)}) %collective-permute-start.28) | collective-permute-done | bytes 294944 | tf_op jit(solution)/shard_map/ppermute | solution.py:44
  217.1 4.4 %shard_map.97 = (bf16[2,1,768,768]{3,2,1,0:T(8,128)(2,1)S(1)}, bf16[2,1,768,768]{3,2,1,0:T(8,128)(2,1)S(1)}, f32[96,768]{1,0:T(8,128)S(1)}) custom-call(s32[4]{0:T(128)S(1)} %pad_add_fusion.state_ref, f32[2,2,96,384]{3,2,1,0:T(8,128)S(1)} %shard_map.96.token_ref.one_ref, f32[2,384,768]{2,1,0:T(8,128)} %bitcast.12, f32[2,384,768]{2,1,0:T(8,128)} %copy-done.36), custom_call_target="tpu_custom_call" | custom-call | flops 1 | bytes 1 | tf_op jit(solution)/shard_map/pallas_call | solution.py:346
  221.4 1.8 collective-permute-done.33.refs_1_.refs_3_
  225.5 2.2 collective-permute-start.34
  227.8 7.5 %shard_map.100 = (f32[2,768,1024]{2,1,0:T(8,128)}, f32[8,128]{1,0:T(8,128)S(1)}) custom-call(s32[2,2]{1,0:T(2,128)S(1)} %copy-done.33, s32[4]{0:T(128)S(1)} %pad_add_fusion.state_ref, bf16[2,1,768,768]{3,2,1,0:T(8,128)(2,1)S(1)} %get-tuple-element.68.high_ref, bf16[2,1,768,768]{3,2,1,0:T(8,128)(2,1)S(1)} %get-tuple-element.69.low_ref, ...), custom_call_target="tpu_custom_call" | custom-call | flops 1 | bytes 1 | tf_op jit(solution)/shard_map/pallas_call | solution.py:400
  235.2 6.7 %collective-permute-done.34.two_ref = f32[2,2,192,384]{3,2,1,0:T(8,128)S(1)} collective-permute-done((f32[2,2,192,384]{3,2,1,0:T(8,128)S(1)}, f32[2,2,192,384]{3,2,1,0:T(8,128)S(1)}, u32[]{:S(2)}, u32[]{:S(2)}) %collective-permute-start.34) | collective-permute-done | bytes 1179680 | tf_op jit(solution)/shard_map/ppermute | solution.py:44
  244.2 1.7 copy-done.6
  247.1 7.6 %shard_map.102 = (f32[2,768,1024]{2,1,0:T(8,128)}, f32[8,128]{1,0:T(8,128)S(1)}) custom-call(s32[2,2]{1,0:T(2,128)S(1)} %copy-done.33, s32[4]{0:T(128)S(1)} %pad_add_fusion.state_ref, bf16[2,1,768,768]{3,2,1,0:T(8,128)(2,1)S(1)} %get-tuple-element.68.high_ref, bf16[2,1,768,768]{3,2,1,0:T(8,128)(2,1)S(1)} %copy-done.6, ...), custom_call_target="tpu_custom_call", output_to_operand_aliasing={{0}: (6, {})} | custom-call | flops 1 | bytes 1 | tf_op jit(solution)/shard_map/pallas_call | solution.py:400
  254.8 5.7 %shard_map.103 = (bf16[2,1,768,768]{3,2,1,0:T(8,128)(2,1)}, bf16[2,1,768,768]{3,2,1,0:T(8,128)(2,1)}, f32[96,768]{1,0:T(8,128)S(1)}) custom-call(s32[4]{0:T(128)S(1)} %pad_add_fusion.state_ref, f32[8,128]{1,0:T(8,128)S(1)} %get-tuple-element.74.token_ref, f32[2,384,384]{2,1,0:T(8,128)S(1)} %copy-done.13, f32[2,384,384]{2,1,0:T(8,128)} %collective-permute-done.35.refs_1_, ...), custom_call_target="tpu_custom_call" | custom-call | flops 1 | bytes 1 | tf_op jit(solution)/shard_map/pallas_call | solution.py:346
  261.9 6.3 %collective-permute-done.37 = f32[96,384]{1,0:T(8,128)S(1)} collective-permute-done((f32[96,384]{1,0:T(8,128)S(1)}, f32[96,384]{1,0:T(8,128)S(1)}, u32[]{:S(2)}, u32[]{:S(2)}) %collective-permute-start.37) | collective-permute-done | bytes 147488 | tf_op jit(solution)/shard_map/ppermute | solution.py:30
  269.3 1.7 copy-done.3
  270.9 1.7 copy-done.4
  273.6 9.0 %shard_map.104 = (f32[2,768,1024]{2,1,0:T(8,128)}, f32[8,128]{1,0:T(8,128)S(1)}) custom-call(s32[2,2]{1,0:T(2,128)S(1)} %copy-done.33, s32[4]{0:T(128)S(1)} %pad_add_fusion.state_ref, bf16[2,1,768,768]{3,2,1,0:T(8,128)(2,1)S(1)} %copy-done.3, bf16[2,1,768,768]{3,2,1,0:T(8,128)(2,1)S(1)} %copy-done.4, ...), custom_call_target="tpu_custom_call", output_to_operand_aliasing={{0}: (9, {})} | custom-call | flops 1 | bytes 1 | tf_op jit(solution)/shard_map/pallas_call | solution.py:400
  282.6 7.5 %shard_map.105 = (f32[2,768,1024]{2,1,0:T(8,128)}, f32[8,128]{1,0:T(8,128)}) custom-call(s32[2,2]{1,0:T(2,128)S(1)} %copy-done.33, s32[4]{0:T(128)S(1)} %pad_add_fusion.state_ref, bf16[2,1,768,768]{3,2,1,0:T(8,128)(2,1)S(1)} %copy-done.3, bf16[2,1,768,768]{3,2,1,0:T(8,128)(2,1)S(1)} %copy-done.4, ...), custom_call_target="tpu_custom_call", output_to_operand_aliasing={{0}: (9, {})} | custom-call | flops 1 | bytes 1 | tf_op jit(solution)/shard_map/pallas_call | solution.py:400
  (176 shorter events, 38.7 us)
Async XLA Ops:
  0.6 10.6 %collective-permute-start.2 = (f32[2,768,1024]{2,1,0:T(8,128)}, f32[2,768,1024]{2,1,0:T(8,128)}, u32[]{:S(2)}, u32[]{:S(2)}) collective-permute-start(f32[2,768,1024]{2,1,0:T(8,128)} %source_ref.15), channel_id=1, source_target_pairs={{0,8},{8,0},{16,24},{24,16},{1,9},{9,1},{17,25},{25,17},{2,10},{10... | collective-permute-start | bytes 18874376 | tf_op jit(solution)/shard_map/ppermute | solution.py:30
  8.2 11.6 %copy-start.26 = (f32[1,192,1024]{2,1,0:T(8,128)}, f32[1,192,1024]{2,1,0:T(8,128)S(1)}, u32[]{:S(2)}) copy-start(f32[1,192,1024]{2,1,0:T(8,128)S(1)} %shard_map.62.token_ref) | copy-start | bytes 2359300
  8.2 15.9 %copy-start.38 = (f32[2]{0:T(128)S(1)}, f32[2]{0:T(128)}, u32[]{:S(2)}) copy-start(f32[2]{0:T(128)} %param.5) | copy-start | bytes 28
  20.9 21.2 %collective-permute-start.3 = (f32[1,384,768]{2,1,0:T(8,128)}, f32[1,384,768]{2,1,0:T(8,128)}, u32[]{:S(2)}, u32[]{:S(2)}) collective-permute-start(f32[1,384,768]{2,1,0:T(8,128)} %get-tuple-element.44.refs_0_), channel_id=1, source_target_pairs={{0,8},{8,0},{16,24},{24,16},{1,9},{9,1},{17,25},{25,17},{2,10},{10... | collective-permute-start | bytes 3538952 | tf_op jit(solution)/shard_map/ppermute | solution.py:30
  21.3 20.8 %collective-permute-start.4 = (f32[1,192,1024]{2,1,0:T(8,128)S(1)}, f32[1,192,1024]{2,1,0:T(8,128)S(1)}, u32[]{:S(2)}, u32[]{:S(2)}) collective-permute-start(f32[1,192,1024]{2,1,0:T(8,128)S(1)} %shard_map.59.token_ref), channel_id=1, source_target_pairs={{0,16},{16,0},{8,24},{24,8},{1,17},{17,1},{9,25},{25,9},{2,18},{18... | collective-permute-start | bytes 2359304 | tf_op jit(solution)/shard_map/ppermute | solution.py:30
  24.1 18.0 %copy-start.29 = (f32[1,384,768]{2,1,0:T(8,128)S(1)}, f32[1,384,768]{2,1,0:T(8,128)}, u32[]{:S(2)}) copy-start(f32[1,384,768]{2,1,0:T(8,128)} %copy-done.28) | copy-start | bytes 3538948
  24.1 1.1 collective-permute-start
  25.3 16.8 %collective-permute-start.1 = (f32[2,6]{1,0:T(2,128)S(1)}, f32[2,6]{1,0:T(2,128)S(1)}, u32[]{:S(2)}, u32[]{:S(2)}) collective-permute-start(f32[2,6]{1,0:T(2,128)S(1)} %get-tuple-element.87.ours_ref), channel_id=1, source_target_pairs={{0,16},{16,0},{8,24},{24,8},{1,17},{17,1},{9,25},{25,9},{2,18},{18... | collective-permute-start | bytes 152 | tf_op jit(solution)/shard_map/ppermute | solution.py:30
  43.6 16.3 %collective-permute-start.5 = (f32[2,1,192,768]{3,2,1,0:T(8,128)S(1)}, f32[2,1,192,768]{3,2,1,0:T(8,128)S(1)}, u32[]{:S(2)}, u32[]{:S(2)}) collective-permute-start(f32[2,1,192,768]{3,2,1,0:T(8,128)S(1)} %get-tuple-element.46.token_ref), channel_id=1, source_target_pairs={{0,1},{1,0},{2,3},{3,2},{4,5},{5,4},{6,7},{7,6},{8,10},{9,11},{10,... | collective-permute-start | bytes 3538952 | tf_op jit(solution)/shard_map/ppermute | solution.py:44
  45.3 18.8 %collective-permute-start.6 = (f32[1,192,1024]{2,1,0:T(8,128)S(1)}, f32[1,192,1024]{2,1,0:T(8,128)S(1)}, u32[]{:S(2)}, u32[]{:S(2)}) collective-permute-start(f32[1,192,1024]{2,1,0:T(8,128)S(1)} %shard_map.60.token_ref), channel_id=1, source_target_pairs={{0,16},{16,0},{8,24},{24,8},{1,17},{17,1},{9,25},{25,9},{2,18},{18... | collective-permute-start | bytes 2359304 | tf_op jit(solution)/shard_map/ppermute | solution.py:30
  71.2 2.1 collective-permute-start.7
  71.3 20.4 %collective-permute-start.10 = (f32[1,192,1024]{2,1,0:T(8,128)S(1)}, f32[1,192,1024]{2,1,0:T(8,128)S(1)}, u32[]{:S(2)}, u32[]{:S(2)}) collective-permute-start(f32[1,192,1024]{2,1,0:T(8,128)S(1)} %shard_map.61.token_ref), channel_id=1, source_target_pairs={{0,16},{16,0},{8,24},{24,8},{1,17},{17,1},{9,25},{25,9},{2,18},{18... | collective-permute-start | bytes 2359304 | tf_op jit(solution)/shard_map/ppermute | solution.py:30
  72.9 15.7 %collective-permute-start.9 = (f32[2,1,96,768]{3,2,1,0:T(8,128)S(1)}, f32[2,1,96,768]{3,2,1,0:T(8,128)S(1)}, u32[]{:S(2)}, u32[]{:S(2)}) collective-permute-start(f32[2,1,96,768]{3,2,1,0:T(8,128)S(1)} %get-tuple-element.47.token_ref), channel_id=1, source_target_pairs={{0,2},{1,3},{2,0},{3,1},{4,6},{5,7},{6,4},{7,5},{8,9},{9,8},{10,11... | collective-permute-start | bytes 1769480 | tf_op jit(solution)/shard_map/ppermute | solution.py:44
  73.4 18.3 %collective-permute-start.8 = (f32[2,1,192,384]{3,2,1,0:T(8,128)S(1)}, f32[2,1,192,384]{3,2,1,0:T(8,128)S(1)}, u32[]{:S(2)}, u32[]{:S(2)}) collective-permute-start(f32[2,1,192,384]{3,2,1,0:T(8,128)S(1)} %get-tuple-element.51.token_ref), channel_id=1, source_target_pairs={{0,1},{1,0},{2,3},{3,2},{4,5},{5,4},{6,7},{7,6},{8,10},{9,11},{10,... | collective-permute-start | bytes 1769480 | tf_op jit(solution)/shard_map/ppermute | solution.py:44
  75.0 33.1 %collective-permute-start.13 = (f32[1,192,1024]{2,1,0:T(8,128)S(1)}, f32[1,192,1024]{2,1,0:T(8,128)S(1)}, u32[]{:S(2)}, u32[]{:S(2)}) collective-permute-start(f32[1,192,1024]{2,1,0:T(8,128)S(1)} %copy-done.27), channel_id=1, source_target_pairs={{0,16},{16,0},{8,24},{24,8},{1,17},{17,1},{9,25},{25,9},{2,18},{18... | collective-permute-start | bytes 2359304 | tf_op jit(solution)/shard_map/ppermute | solution.py:30
  88.7 14.6 %collective-permute-start.12 = (f32[2,1,48,768]{3,2,1,0:T(8,128)S(1)}, f32[2,1,48,768]{3,2,1,0:T(8,128)S(1)}, u32[]{:S(2)}, u32[]{:S(2)}) collective-permute-start(f32[2,1,48,768]{3,2,1,0:T(8,128)S(1)} %get-tuple-element.53.refs_0_), channel_id=1, source_target_pairs={{0,4},{1,5},{2,6},{3,7},{4,0},{5,1},{6,2},{7,3},{8,12},{9,13},{10,... | collective-permute-start | bytes 884744 | tf_op jit(solution)/shard_map/ppermute | solution.py:44
  91.7 16.4 %copy-start.7 = (f32[1,192,1024]{2,1,0:T(8,128)}, f32[1,192,1024]{2,1,0:T(8,128)S(1)}, u32[]{:S(2)}) copy-start(f32[1,192,1024]{2,1,0:T(8,128)S(1)} %collective-permute-done.10.refs_1_.refs_0_.refs_2_) | copy-start | bytes 2359300
  91.8 12.4 %collective-permute-start.11 = (f32[2,1,96,384]{3,2,1,0:T(8,128)S(1)}, f32[2,1,96,384]{3,2,1,0:T(8,128)S(1)}, u32[]{:S(2)}, u32[]{:S(2)}) collective-permute-start(f32[2,1,96,384]{3,2,1,0:T(8,128)S(1)} %get-tuple-element.55.token_ref), channel_id=1, source_target_pairs={{0,2},{1,3},{2,0},{3,1},{4,6},{5,7},{6,4},{7,5},{8,9},{9,8},{10,11... | collective-permute-start | bytes 884744 | tf_op jit(solution)/shard_map/ppermute | solution.py:44
  104.0 19.6 %collective-permute-start.15 = (f32[2,1,48,768]{3,2,1,0:T(8,128)S(1)}, f32[2,1,48,768]{3,2,1,0:T(8,128)S(1)}, u32[]{:S(2)}, u32[]{:S(2)}) collective-permute-start(f32[2,1,48,768]{3,2,1,0:T(8,128)S(1)} %shard_map.73.token_ref.one_ref), channel_id=1, source_target_pairs={{0,4},{1,5},{2,6},{3,7},{4,0},{5,1},{6,2},{7,3},{8,12},{9,13},{10,... | collective-permute-start | bytes 884744 | tf_op jit(solution)/shard_map/ppermute | solution.py:44
  105.1 17.9 %collective-permute-start.16 = (f32[2,1,48,384]{3,2,1,0:T(8,128)S(1)}, f32[2,1,48,384]{3,2,1,0:T(8,128)S(1)}, u32[]{:S(2)}, u32[]{:S(2)}) collective-permute-start(f32[2,1,48,384]{3,2,1,0:T(8,128)S(1)} %get-tuple-element.57.token_ref), channel_id=1, source_target_pairs={{0,4},{1,5},{2,6},{3,7},{4,0},{5,1},{6,2},{7,3},{8,12},{9,13},{10,... | collective-permute-start | bytes 442376 | tf_op jit(solution)/shard_map/ppermute | solution.py:44
  107.9 23.2 %collective-permute-start.20 = (f32[1,768,256]{2,1,0:T(8,128)S(1)}, f32[1,768,256]{2,1,0:T(8,128)S(1)}, u32[]{:S(2)}, u32[]{:S(2)}) collective-permute-start(f32[1,768,256]{2,1,0:T(8,128)S(1)} %shard_map.75.token_ref), channel_id=1, source_target_pairs={{0,16},{16,0},{8,24},{24,8},{1,17},{17,1},{9,25},{25,9},{2,18},{18... | collective-permute-start | bytes 2359304 | tf_op jit(solution)/shard_map/ppermute | solution.py:30
  112.2 13.2 %collective-permute-start.14 = (f32[1,384,384]{2,1,0:T(8,128)S(1)}, f32[1,384,384]{2,1,0:T(8,128)S(1)}, u32[]{:S(2)}, u32[]{:S(2)}) collective-permute-start(f32[1,384,384]{2,1,0:T(8,128)S(1)} %get-tuple-element.59.token_ref), channel_id=1, source_target_pairs={{0,8},{8,0},{16,24},{24,16},{1,9},{9,1},{17,25},{25,17},{2,10},{10... | collective-permute-start | bytes 1769480 | tf_op jit(solution)/shard_map/ppermute | solution.py:30
  123.7 9.9 %collective-permute-start.18 = (f32[2,1,96,768]{3,2,1,0:T(8,128)S(1)}, f32[2,1,96,768]{3,2,1,0:T(8,128)S(1)}, u32[]{:S(2)}, u32[]{:S(2)}) collective-permute-start(f32[2,1,96,768]{3,2,1,0:T(8,128)S(1)} %shard_map.78.token_ref.one_ref), channel_id=1, source_target_pairs={{0,2},{1,3},{2,0},{3,1},{4,6},{5,7},{6,4},{7,5},{8,9},{9,8},{10,11... | collective-permute-start | bytes 1769480 | tf_op jit(solution)/shard_map/ppermute | solution.py:44
  123.8 6.5 %collective-permute-start.19 = (f32[2,1,48,384]{3,2,1,0:T(8,128)S(1)}, f32[2,1,48,384]{3,2,1,0:T(8,128)S(1)}, u32[]{:S(2)}, u32[]{:S(2)}) collective-permute-start(f32[2,1,48,384]{3,2,1,0:T(8,128)S(1)} %shard_map.77.token_ref.one_ref), channel_id=1, source_target_pairs={{0,16},{16,0},{8,24},{24,8},{1,17},{17,1},{9,25},{25,9},{2,18},{18... | collective-permute-start | bytes 442376 | tf_op jit(solution)/shard_map/ppermute | solution.py:30
  133.7 31.1 %collective-permute-start.25 = (f32[2,1,192,768]{3,2,1,0:T(8,128)S(1)}, f32[2,1,192,768]{3,2,1,0:T(8,128)S(1)}, u32[]{:S(2)}, u32[]{:S(2)}) collective-permute-start(f32[2,1,192,768]{3,2,1,0:T(8,128)S(1)} %shard_map.83.token_ref.one_ref), channel_id=1, source_target_pairs={{0,1},{1,0},{2,3},{3,2},{4,5},{5,4},{6,7},{7,6},{8,10},{9,11},{10,... | collective-permute-start | bytes 3538952 | tf_op jit(solution)/shard_map/ppermute | solution.py:44
  135.4 21.0 %collective-permute-start.17 = (f32[2,1,192,384]{3,2,1,0:T(8,128)S(1)}, f32[2,1,192,384]{3,2,1,0:T(8,128)S(1)}, u32[]{:S(2)}, u32[]{:S(2)}) collective-permute-start(f32[2,1,192,384]{3,2,1,0:T(8,128)S(1)} %get-tuple-element.62.token_ref), channel_id=1, source_target_pairs={{0,1},{1,0},{2,3},{3,2},{4,5},{5,4},{6,7},{7,6},{8,10},{9,11},{10,... | collective-permute-start | bytes 1769480 | tf_op jit(solution)/shard_map/ppermute | solution.py:44
  135.8 22.2 %collective-permute-start.22 = (f32[2,2,48,384]{3,2,1,0:T(8,128)S(1)}, f32[2,2,48,384]{3,2,1,0:T(8,128)S(1)}, u32[]{:S(2)}, u32[]{:S(2)}) collective-permute-start(f32[2,2,48,384]{3,2,1,0:T(8,128)S(1)} %shard_map.80.token_ref.one_ref), channel_id=1, source_target_pairs={{0,4},{1,5},{2,6},{3,7},{4,0},{5,1},{6,2},{7,3},{8,12},{9,13},{10,... | collective-permute-start | bytes 884744 | tf_op jit(solution)/shard_map/ppermute | solution.py:44
  156.4 7.6 %collective-permute-start.21 = (f32[2,1,96,384]{3,2,1,0:T(8,128)S(1)}, f32[2,1,96,384]{3,2,1,0:T(8,128)S(1)}, u32[]{:S(2)}, u32[]{:S(2)}) collective-permute-start(f32[2,1,96,384]{3,2,1,0:T(8,128)S(1)} %get-tuple-element.64.token_ref), channel_id=1, source_target_pairs={{0,2},{1,3},{2,0},{3,1},{4,6},{5,7},{6,4},{7,5},{8,9},{9,8},{10,11... | collective-permute-start | bytes 884744 | tf_op jit(solution)/shard_map/ppermute | solution.py:44
  156.5 14.8 %collective-permute-start.26 = (f32[1,768,256]{2,1,0:T(8,128)S(1)}, f32[1,768,256]{2,1,0:T(8,128)S(1)}, u32[]{:S(2)}, u32[]{:S(2)}) collective-permute-start(f32[1,768,256]{2,1,0:T(8,128)S(1)} %shard_map.81.refs_0_), channel_id=1, source_target_pairs={{0,16},{16,0},{8,24},{24,8},{1,17},{17,1},{9,25},{25,9},{2,18},{18... | collective-permute-start | bytes 2359304 | tf_op jit(solution)/shard_map/ppermute | solution.py:30
  158.1 14.1 %collective-permute-start.24 = (f32[2,2,96,384]{3,2,1,0:T(8,128)S(1)}, f32[2,2,96,384]{3,2,1,0:T(8,128)S(1)}, u32[]{:S(2)}, u32[]{:S(2)}) collective-permute-start(f32[2,2,96,384]{3,2,1,0:T(8,128)S(1)} %shard_map.85.token_ref.one_ref), channel_id=1, source_target_pairs={{0,2},{1,3},{2,0},{3,1},{4,6},{5,7},{6,4},{7,5},{8,9},{9,8},{10,11... | collective-permute-start | bytes 1769480 | tf_op jit(solution)/shard_map/ppermute | solution.py:44
  165.0 50.6 %collective-permute-start.31 = (f32[2,384,768]{2,1,0:T(8,128)S(1)}, f32[2,384,768]{2,1,0:T(8,128)S(1)}, u32[]{:S(2)}, u32[]{:S(2)}) collective-permute-start(f32[2,384,768]{2,1,0:T(8,128)S(1)} %bitcast.10), channel_id=1, source_target_pairs={{0,8},{8,0},{16,24},{24,16},{1,9},{9,1},{17,25},{25,17},{2,10},{10... | collective-permute-start | bytes 7077896 | tf_op jit(solution)/shard_map/ppermute | solution.py:30
  172.2 31.2 %collective-permute-start.29 = (f32[2,2,192,384]{3,2,1,0:T(8,128)S(1)}, f32[2,2,192,384]{3,2,1,0:T(8,128)S(1)}, u32[]{:S(2)}, u32[]{:S(2)}) collective-permute-start(f32[2,2,192,384]{3,2,1,0:T(8,128)S(1)} %shard_map.90.token_ref.one_ref), channel_id=1, source_target_pairs={{0,1},{1,0},{2,3},{3,2},{4,5},{5,4},{6,7},{7,6},{8,10},{9,11},{10,... | collective-permute-start | bytes 3538952 | tf_op jit(solution)/shard_map/ppermute | solution.py:44
  175.0 27.2 %collective-permute-start.30 = (f32[1,768,256]{2,1,0:T(8,128)S(1)}, f32[1,768,256]{2,1,0:T(8,128)S(1)}, u32[]{:S(2)}, u32[]{:S(2)}) collective-permute-start(f32[1,768,256]{2,1,0:T(8,128)S(1)} %shard_map.87.token_ref), channel_id=1, source_target_pairs={{0,16},{16,0},{8,24},{24,8},{1,17},{17,1},{9,25},{25,9},{2,18},{18... | collective-permute-start | bytes 2359304 | tf_op jit(solution)/shard_map/ppermute | solution.py:30
  176.4 12.0 %collective-permute-start.23 = (f32[2,1,48,384]{3,2,1,0:T(8,128)S(1)}, f32[2,1,48,384]{3,2,1,0:T(8,128)S(1)}, u32[]{:S(2)}, u32[]{:S(2)}) collective-permute-start(f32[2,1,48,384]{3,2,1,0:T(8,128)S(1)} %get-tuple-element.66.token_ref), channel_id=1, source_target_pairs={{0,4},{1,5},{2,6},{3,7},{4,0},{5,1},{6,2},{7,3},{8,12},{9,13},{10,... | collective-permute-start | bytes 442376 | tf_op jit(solution)/shard_map/ppermute | solution.py:44
  189.1 6.9 %collective-permute-start.27 = (f32[2,1,48,384]{3,2,1,0:T(8,128)S(1)}, f32[2,1,48,384]{3,2,1,0:T(8,128)S(1)}, u32[]{:S(2)}, u32[]{:S(2)}) collective-permute-start(f32[2,1,48,384]{3,2,1,0:T(8,128)S(1)} %shard_map.91.one_ref.token_ref), channel_id=1, source_target_pairs={{0,16},{16,0},{8,24},{24,8},{1,17},{17,1},{9,25},{25,9},{2,18},{18... | collective-permute-start | bytes 442376 | tf_op jit(solution)/shard_map/ppermute | solution.py:30
  196.0 19.5 %collective-permute-start.28 = (f32[2,2,48,384]{3,2,1,0:T(8,128)S(1)}, f32[2,2,48,384]{3,2,1,0:T(8,128)S(1)}, u32[]{:S(2)}, u32[]{:S(2)}) collective-permute-start(f32[2,2,48,384]{3,2,1,0:T(8,128)S(1)} %shard_map.92.refs_0_.one_ref), channel_id=1, source_target_pairs={{0,4},{1,5},{2,6},{3,7},{4,0},{5,1},{6,2},{7,3},{8,12},{9,13},{10,... | collective-permute-start | bytes 884744 | tf_op jit(solution)/shard_map/ppermute | solution.py:44
  203.1 20.2 %collective-permute-start.33 = (f32[1,768,256]{2,1,0:T(8,128)S(1)}, f32[1,768,256]{2,1,0:T(8,128)S(1)}, u32[]{:S(2)}, u32[]{:S(2)}) collective-permute-start(f32[1,768,256]{2,1,0:T(8,128)S(1)} %shard_map.94.token_ref), channel_id=1, source_target_pairs={{0,16},{16,0},{8,24},{24,8},{1,17},{17,1},{9,25},{25,9},{2,18},{18... | collective-permute-start | bytes 2359304 | tf_op jit(solution)/shard_map/ppermute | solution.py:30
  204.6 10.8 %copy-start.12 = (f32[2,384,384]{2,1,0:T(8,128)}, f32[2,384,384]{2,1,0:T(8,128)S(1)}, u32[]{:S(2)}) copy-start(f32[2,384,384]{2,1,0:T(8,128)S(1)} %get-tuple-element.67.token_ref.refs_0_) | copy-start | bytes 3538948
  215.5 9.9 %collective-permute-start.32 = (f32[2,2,96,384]{3,2,1,0:T(8,128)S(1)}, f32[2,2,96,384]{3,2,1,0:T(8,128)S(1)}, u32[]{:S(2)}, u32[]{:S(2)}) collective-permute-start(f32[2,2,96,384]{3,2,1,0:T(8,128)S(1)} %shard_map.96.token_ref.one_ref), channel_id=1, source_target_pairs={{0,2},{1,3},{2,0},{3,1},{4,6},{5,7},{6,4},{7,5},{8,9},{9,8},{10,11... | collective-permute-start | bytes 1769480 | tf_op jit(solution)/shard_map/ppermute | solution.py:44
  225.5 16.4 %collective-permute-start.34 = (f32[2,2,192,384]{3,2,1,0:T(8,128)S(1)}, f32[2,2,192,384]{3,2,1,0:T(8,128)S(1)}, u32[]{:S(2)}, u32[]{:S(2)}) collective-permute-start(f32[2,2,192,384]{3,2,1,0:T(8,128)S(1)} %shard_map.99.token_ref.one_ref), channel_id=1, source_target_pairs={{0,1},{1,0},{2,3},{3,2},{4,5},{5,4},{6,7},{7,6},{8,10},{9,11},{10,... | collective-permute-start | bytes 3538952 | tf_op jit(solution)/shard_map/ppermute | solution.py:44
  227.8 27.0 %collective-permute-start.35 = (f32[2,384,384]{2,1,0:T(8,128)}, f32[2,384,384]{2,1,0:T(8,128)}, u32[]{:S(2)}, u32[]{:S(2)}) collective-permute-start(f32[2,384,384]{2,1,0:T(8,128)} %get-tuple-element.75), channel_id=1, source_target_pairs={{0,8},{8,0},{16,24},{24,16},{1,9},{9,1},{17,25},{25,17},{2,10},{10... | collective-permute-start | bytes 3538952 | tf_op jit(solution)/shard_map/ppermute | solution.py:30
  244.2 10.6 %collective-permute-start.36 = (f32[2,384,384]{2,1,0:T(8,128)}, f32[2,384,384]{2,1,0:T(8,128)}, u32[]{:S(2)}, u32[]{:S(2)}) collective-permute-start(f32[2,384,384]{2,1,0:T(8,128)} %get-tuple-element.76), channel_id=1, source_target_pairs={{0,8},{8,0},{16,24},{24,16},{1,9},{9,1},{17,25},{25,17},{2,10},{10... | collective-permute-start | bytes 3538952 | tf_op jit(solution)/shard_map/ppermute | solution.py:30
  254.7 14.5 %copy-start.17 = (f32[1,192,1024]{2,1,0:T(8,128)S(1)}, f32[1,192,1024]{2,1,0:T(8,128)}, u32[]{:S(2)}) copy-start(f32[1,192,1024]{2,1,0:T(8,128)} %copy-done.16) | copy-start | bytes 2359300
  261.9 6.3 %collective-permute-start.37 = (f32[96,384]{1,0:T(8,128)S(1)}, f32[96,384]{1,0:T(8,128)S(1)}, u32[]{:S(2)}, u32[]{:S(2)}) collective-permute-start(f32[96,384]{1,0:T(8,128)S(1)} %constant_dynamic-slice_fusion.1), channel_id=1, source_target_pairs={{0,16},{16,0},{8,24},{24,8},{1,17},{17,1},{9,25},{25,9},{2,18},{18... | collective-permute-start | bytes 442376 | tf_op jit(solution)/shard_map/ppermute | solution.py:30
  269.2 21.0 %collective-permute-start.38 = (f32[96,192]{1,0:T(8,128)S(1)}, f32[96,192]{1,0:T(8,128)S(1)}, u32[]{:S(2)}, u32[]{:S(2)}) collective-permute-start(f32[96,192]{1,0:T(8,128)S(1)} %constant_dynamic-slice_fusion), channel_id=1, source_target_pairs={{0,8},{8,0},{16,24},{24,16},{1,9},{9,1},{17,25},{25,17},{2,10},{10... | collective-permute-start | bytes 221192 | tf_op jit(solution)/shard_map/ppermute | solution.py:30
  273.6 9.0 %copy-start.21 = (f32[1,768,256]{2,1,0:T(8,128)S(1)}, f32[1,768,256]{2,1,0:T(8,128)}, u32[]{:S(2)}) copy-start(f32[1,768,256]{2,1,0:T(8,128)} %copy-done.20) | copy-start | bytes 2359300
  273.6 9.0 %copy-start.23 = (f32[1,768,256]{2,1,0:T(8,128)S(1)}, f32[1,768,256]{2,1,0:T(8,128)}, u32[]{:S(2)}) copy-start(f32[1,768,256]{2,1,0:T(8,128)} %copy-done.22) | copy-start | bytes 2359300
  273.6 9.0 %copy-start.25 = (f32[1,768,256]{2,1,0:T(8,128)S(1)}, f32[1,768,256]{2,1,0:T(8,128)}, u32[]{:S(2)}) copy-start(f32[1,768,256]{2,1,0:T(8,128)} %copy-done.24) | copy-start | bytes 2359300
  (32 other events, 110.2 us)

commit v6 on v5

v6 whole, which is shorter than its diff:
```python
import functools

import jax
import jax.numpy as jnp
from jax import lax
from jax.experimental import pallas as pl
from jax.experimental.pallas import tpu as pltpu
from jax.sharding import PartitionSpec as P

VMEM = pl.BlockSpec(memory_space=pltpu.VMEM)
SMEM = pl.BlockSpec(memory_space=pltpu.SMEM)
ANY = pl.BlockSpec(memory_space=pl.ANY)


def params(mebibytes):
    return pltpu.CompilerParams(vmem_limit_bytes=mebibytes * 2**20)


def cost():
    return pl.CostEstimate(flops=1, bytes_accessed=1, transcendentals=0)


def swapped(block, axis, bit):
    count = lax.axis_size(axis)
    route = []
    for low in range(count):
        high = low | 1 << bit
        if high != low and high < count:
            route += [(low, high), (high, low)]
    return lax.ppermute(block, axis, route)


def orders(bits):
    return (list(range(bits)), [1, 0] + list(range(2, bits)))


def across(block, step):
    pairs, auxes = lax.axis_size("pair"), lax.axis_size("aux")
    order = orders(auxes.bit_length() - 1)
    route = []
    for p in range(pairs):
        for m in range(auxes):
            route.append((p * auxes + m, p * auxes + (m ^ 1 << order[p % 2][step])))
    return lax.ppermute(block, ("pair", "aux"), route)


def halves(value):
    high = value.astype(jnp.bfloat16)
    return high, (value - high.astype(jnp.float32)).astype(jnp.bfloat16)


def multiply(left, right, dims):
    rh, rl = right
    one = functools.partial(
        lax.dot_general, dimension_numbers=(dims, ((), ())), preferred_element_type=jnp.float32
    )
    count = left.shape[0] // 2
    both = one(left, rh)
    return both[:count] + (both[count:] + one(left[:count], rl))


def stacked(value):
    return jnp.concatenate(halves(value), axis=0)


def upper_in(position, turn):
    return position // 2**turn % 2 == 1


def slot_of(plan_ref, state_ref, per_block, turn, h, own):
    half_count = per_block // 2
    plain = jnp.where(own, h, half_count + h)
    wanted = jnp.where(own, half_count + h, h)
    inverse = 0
    for k in range(per_block):
        inverse += jnp.where(plan_ref[turn, k] == wanted, k, 0)
    return jnp.where(upper_in(state_ref[0], turn), inverse, plain)


def peer_slot_of(plan_ref, state_ref, per_block, turn, h, own):
    half_count = per_block // 2
    plain = jnp.where(own, h, half_count + h)
    wanted = jnp.where(own, half_count + h, h)
    paired = 0
    for k in range(per_block):
        paired += jnp.where(plain == k, plan_ref[turn, k], 0)
    return jnp.where(upper_in(state_ref[0], turn), wanted, paired)


def copy_kernel(extra, plan_ref, state_ref, source_ref, *refs):
    del plan_ref, state_ref
    rows = source_ref.shape[1]
    refs[-1][:, :rows] = source_ref[...]
    if extra:
        refs[-1][:, rows:] = refs[0][...][None]


def picked(three_index, plan, state, token, turn, own, part, parts, extra=None):
    per_block, width, depth = three_index.shape
    half_count = per_block // 2
    rows = width if own else width // parts
    depth = depth // parts if own else depth
    count = rows + (0 if extra is None else extra.shape[0])

    def source(h, plan_ref, state_ref):
        slot = slot_of(plan_ref, state_ref, per_block, turn, h, own)
        return (slot, 0, part) if own else (slot, part, 0)

    return pl.pallas_call(
        functools.partial(copy_kernel, extra is not None),
        out_shape=jax.ShapeDtypeStruct((half_count, count, depth), jnp.float32),
        grid_spec=pltpu.PrefetchScalarGridSpec(
            num_scalar_prefetch=2,
            grid=(half_count,),
            in_specs=[pl.BlockSpec((1, rows, depth), source)]
            + ([] if extra is None else [VMEM])
            + [ANY],
            out_specs=pl.BlockSpec((1, count, depth), lambda h, *_: (h, 0, 0)),
        ),
        compiler_params=params(24),
        cost_estimate=cost(),
    )(plan, state, three_index, *(() if extra is None else (extra,)), token)


def gate_kernel(*refs):
    refs[-1][...] = jnp.zeros_like(refs[-1])


def gated(*tokens):
    return pl.pallas_call(
        gate_kernel,
        out_shape=jax.ShapeDtypeStruct((8, 128), jnp.float32),
        in_specs=[ANY] * len(tokens),
        out_specs=VMEM,
        compiler_params=params(16),
        cost_estimate=cost(),
    )(*tokens)


def integral_kernel(turn, blocks, plan_ref, state_ref, own_ref, token_ref, *refs):
    del plan_ref, token_ref
    keep_ref, give_ref, high, low = refs[-4:]
    band = pl.program_id(1)
    count = high.shape[0] // (len(refs) - 4)

    @pl.when(band == 0)
    def _():
        for index, peer_ref in enumerate(refs[:-4]):
            spot = slice(index * count, (index + 1) * count)
            high[spot, :], low[spot, :] = halves(peer_ref[0, :count])

    value = multiply(stacked(own_ref[0]), (high[...], low[...]), ((1,), (1,)))
    rows = keep_ref.shape[1] * 2 // blocks
    inside = own_ref.shape[1] // rows
    for part in range(inside):
        place = (band * inside + part) ^ state_ref[1]
        piece = value[part * rows : (part + 1) * rows]

        @pl.when(place < blocks // 2)
        def _():
            keep_ref[0, pl.ds(pl.multiple_of(place * rows, rows), rows), :] = piece

        @pl.when(place >= blocks // 2)
        def _():
            spot = (place - blocks // 2) * rows
            give_ref[0, pl.ds(pl.multiple_of(spot, rows), rows), :] = piece


def integral(three_index, peers, plan, state, token, turn, blocks, count):
    per_block, width, depth = three_index.shape
    half_count = per_block // 2
    bands = 2
    out = jax.ShapeDtypeStruct((half_count, width // 2, count), jnp.float32)
    whole = pl.BlockSpec((1, width // 2, count), lambda h, band, *_: (h, 0, 0))
    chosen = peers[0].shape[0] == per_block

    def peer_at(h, band, p, s):
        return (peer_slot_of(p, s, per_block, turn, h, True) if chosen else h, 0, 0)

    return pl.pallas_call(
        functools.partial(integral_kernel, turn, blocks),
        out_shape=(out, out),
        grid_spec=pltpu.PrefetchScalarGridSpec(
            num_scalar_prefetch=2,
            grid=(half_count, bands),
            in_specs=[
                pl.BlockSpec(
                    (1, width // bands, depth),
                    lambda h, band, p, s: (slot_of(p, s, per_block, turn, h, True), band, 0),
                ),
                ANY,
            ]
            + [pl.BlockSpec((1, peer.shape[1], depth), peer_at) for peer in peers],
            out_specs=(whole, whole),
            scratch_shapes=[pltpu.VMEM((count, depth), jnp.bfloat16)] * 2,
        ),
        compiler_params=params(44),
        cost_estimate=cost(),
    )(plan, state, three_index, token, *peers)


def add_kernel(keep_ref, came_ref, token_ref, low_ref, high_ref):
    del token_ref
    half = low_ref.shape[1]
    low_ref[...] = keep_ref[:, :half] + came_ref[:, :half]
    high_ref[...] = keep_ref[:, half:] + came_ref[:, half:]


def parted(keep, came, token):
    out = jax.ShapeDtypeStruct((keep.shape[0], keep.shape[1] // 2, keep.shape[2]), jnp.float32)
    return pl.pallas_call(
        add_kernel,
        out_shape=(out, out),
        in_specs=[VMEM, VMEM, ANY],
        out_specs=(VMEM, VMEM),
        compiler_params=params(16),
        cost_estimate=cost(),
    )(keep, came, token)


def join_kernel(axis, one_ref, two_ref, token_ref, out_ref):
    del token_ref
    half = one_ref.shape[axis]
    if axis == 0:
        out_ref[:half], out_ref[half:] = one_ref[...], two_ref[...]
    else:
        out_ref[:, :half], out_ref[:, half:] = one_ref[...], two_ref[...]


def joined(one, two, token, axis):
    shape = list(one.shape)
    shape[axis] *= 2
    return pl.pallas_call(
        functools.partial(join_kernel, axis),
        out_shape=jax.ShapeDtypeStruct(tuple(shape), jnp.float32),
        in_specs=[VMEM, VMEM, ANY],
        out_specs=VMEM,
        compiler_params=params(24),
        cost_estimate=cost(),
    )(one, two, token)


def amplitude_kernel(turn, per_block, ours_ref, theirs_ref, state_ref, column_ref, row_ref, left_ref, right_ref, token_ref, out_ref):
    del token_ref
    half_count = per_block // 2
    rows = out_ref.shape[1]
    down = column_ref[pl.ds(pl.multiple_of(state_ref[1] * rows, rows), rows), :]
    theirs = theirs_ref[...].reshape(theirs_ref.shape[-2:])
    upper = upper_in(state_ref[0], turn)
    for h in range(half_count):
        low = ours_ref[0, h] + jnp.zeros((1, 1), jnp.float32)
        high = theirs[0:1, half_count + h : half_count + h + 1]
        wanted = ours_ref[0, per_block * (turn + 1) + h]
        for k in range(per_block):
            slot = ours_ref[0, per_block * (turn + 1) + k]
            high = high + jnp.where(slot == half_count + h, ours_ref[0, k], 0.0)
            low = low + jnp.where(wanted == k, 1.0, 0.0) * theirs[0:1, k : k + 1]
        gap = jnp.where(upper, high, low) - down - row_ref[...]
        out_ref[h] = (left_ref[h] + right_ref[h]) / gap


def amplitude(ours, theirs, theirs_spec, state, column, row, left, right, token, turn, per_block):
    return pl.pallas_call(
        functools.partial(amplitude_kernel, turn, per_block),
        out_shape=jax.ShapeDtypeStruct(left.shape, jnp.float32),
        grid=(1,),
        in_specs=[SMEM, theirs_spec, SMEM, VMEM, VMEM, VMEM, VMEM, ANY],
        out_specs=VMEM,
        compiler_params=params(16),
        cost_estimate=cost(),
    )(ours, theirs, state, column, row, left, right, token)


def tilde_kernel(blocks, places, state_ref, token_ref, *refs):
    del token_ref
    count = len(places)
    sources, (tall_ref, density_ref, amp, tilde) = refs[: 2 * count], refs[2 * count :]
    width = amp.shape[0]
    rows = width // blocks
    share = density_ref.shape[0]
    band = 128 if width % 128 == 0 else width
    for h in range(tall_ref.shape[1]):
        for who in range(2):
            offset = 0
            for part in range(count):
                first, order = places[part][who]
                source = sources[2 * part + who]
                size = source.shape[2]
                for place in range(blocks):
                    spot = pl.ds(pl.multiple_of((place ^ state_ref[order]) * rows, rows), rows)
                    amp[spot, offset : offset + size] = source[first + h, place * rows : (place + 1) * rows, :]
                offset += size
            for part in range(width // band):
                spot = slice(part * band, (part + 1) * band)
                straight, turned = amp[spot, :], amp[:, spot].T
                value = 2.0 * straight - turned if who == 0 else 2.0 * turned - straight
                if who == 0:
                    tilde[spot, :] = value
                below = slice(width + part * band, width + (part + 1) * band)
                tall_ref[who, h, spot, :], tall_ref[who, h, below, :] = halves(value)
            if who == 0:
                start = pl.ds(pl.multiple_of(state_ref[3] * share, share), share)
                straight = amp[start, :]
                turned = 2.0 * straight - tilde[start, :]
                both = (tall_ref[0, h, :width], tall_ref[0, h, width:])
                value = multiply(stacked(straight), both, ((1,), (1,)))
                value += multiply(stacked(turned), both, ((1,), (0,)))
                if h == 0:
                    density_ref[...] = value
                else:
                    density_ref[...] += value


def tildes(state, token, gathered, blocks, share, half_count):
    sources = [array for own, peer, _ in gathered for array in (own, peer)]
    places = [spots for _, _, spots in gathered]
    width = sources[0].shape[1]
    return pl.pallas_call(
        functools.partial(tilde_kernel, blocks, places),
        out_shape=(
            jax.ShapeDtypeStruct((2, half_count, 2 * width, width), jnp.bfloat16),
            jax.ShapeDtypeStruct((share, width), jnp.float32),
        ),
        in_specs=[SMEM, ANY] + [VMEM] * len(sources),
        out_specs=(VMEM, VMEM),
        scratch_shapes=[pltpu.VMEM((width, width), jnp.float32)] * 2,
        compiler_params=params(48),
        cost_estimate=cost(),
    )(state, token, *sources)


def gradient_kernel(count, based, columns, plan_ref, state_ref, tall_ref, token_ref, *refs):
    del plan_ref, state_ref, token_ref
    out_ref, done_ref = refs[-2:]
    done_ref[...] = jnp.zeros_like(done_ref)

    def term(offset, source):
        size = min(source.shape[1], tall_ref.shape[3] // (1 if columns else count))
        tilde = tall_ref[0, 0, :, offset : offset + size]
        return multiply(tilde, halves(source[0, :size]), ((1,), (0,)))

    if columns:
        for piece, source in enumerate(refs[:count]):

            @pl.when(pl.program_id(2) == piece)
            def _():
                out_ref[0] = refs[count][0] + term(0, source)

        return
    value = refs[count][0] if based else None
    for index, source in enumerate(refs[:count]):
        added = term(index * (tall_ref.shape[3] // count), source)
        value = added if value is None else value + added
    out_ref[0] = value


def gradient_terms(plan, state, token, tall, sources, base, turn, own, three_index):
    per_block, width, depth = three_index.shape
    half_count = per_block // 2
    columns = sources[0].shape[2] < depth
    tile = sources[0].shape[2] if columns else depth // 4 if depth % 512 == 0 else depth
    chosen = sources[0].shape[0] == per_block
    at = 0 if own else 1

    def block_at(h, _, piece, p, s):
        return (slot_of(p, s, per_block, turn, h, own), 0, piece)

    def source_at(h, _, piece, p, s):
        slot = peer_slot_of(p, s, per_block, turn, h, own) if chosen else h
        return (slot, 0, 0 if columns else piece)

    tilde_spec = pl.BlockSpec((1, 1, 2 * width, width), lambda h, *_: (at, h, 0, 0))
    out_spec = pl.BlockSpec((1, width, tile), block_at)
    return pl.pallas_call(
        functools.partial(gradient_kernel, len(sources), turn > 0, columns),
        out_shape=(
            jax.ShapeDtypeStruct((per_block, width, depth), jnp.float32),
            jax.ShapeDtypeStruct((8, 128), jnp.float32),
        ),
        grid_spec=pltpu.PrefetchScalarGridSpec(
            num_scalar_prefetch=2,
            grid=(half_count, 1, depth // tile),
            in_specs=[tilde_spec, ANY]
            + [pl.BlockSpec((1, x.shape[1], tile), source_at) for x in sources]
            + ([] if base is None else [out_spec] if turn > 0 else [ANY]),
            out_specs=(out_spec, pl.BlockSpec((8, 128), lambda *_: (0, 0))),
        ),
        input_output_aliases={} if base is None else {4 + len(sources): 0},
        compiler_params=params(44),
        cost_estimate=cost(),
    )(plan, state, tall, token, *sources, *(() if base is None else (base,)))


def chain(env, turn, offset, size, peers):
    bits, per_block, state = env["bits"], env["per_block"], env["state"]
    half_count = per_block // 2
    count = size // len(peers)
    token = yield None
    keep, give = integral(
        env["three_index"], peers, env["plan"], state, token, turn, env["blocks"], count
    )
    for stage in range(bits - 1):
        came = across(give, stage)
        token = yield give
        keep, give = parted(keep, came, token)
    came = across(give, bits - 1)
    token = yield give
    row = env["virtual"][None, offset : offset + size]
    theirs, spec = env["theirs"][turn]
    value = amplitude(
        env["ours"], theirs, spec, state, env["column"], row, keep, came, token, turn, per_block
    )
    if turn > 0:
        came = swapped(value, "pair", turn)
        token = yield value
        value = joined(value, came, token, 0)
    for stage in reversed(range(bits)):
        came = across(value, stage)
        token = yield value
        value = joined(value, came, token, 1)
    if turn == 0:
        came = swapped(value, "pair", 0)
        env["gathered"][turn].append((value, came, ((0, 1), (0, 2))))
    else:
        env["gathered"][turn].append((value, value, ((0, 1), (half_count, 1))))
    yield value


def body(three_index, occupied_energy, virtual_energy, plan):
    per_block, width, depth = three_index.shape
    half_count = per_block // 2
    aux_count = lax.axis_size("aux")
    bits = aux_count.bit_length() - 1
    blocks = aux_count
    row_count = width // aux_count
    aux = lax.axis_index("aux").astype(jnp.int32)
    rounds = plan.shape[0]
    position = lax.axis_index("pair").astype(jnp.int32)

    def mask(order):
        return sum((aux >> bit & 1) << bits - 1 - step for step, bit in enumerate(order))

    first_mask, second_mask = (mask(order) for order in orders(bits))
    core = position % 2
    state = jnp.stack(
        [
            position,
            jnp.where(core == 0, first_mask, second_mask),
            jnp.where(core == 0, second_mask, first_mask),
            aux,
        ]
    ).astype(jnp.int32)

    mine = jnp.concatenate([occupied_energy, plan.astype(jnp.float32).reshape(-1)])[None]
    extra = jnp.pad(mine, ((0, 7), (0, depth - mine.shape[1])))
    cuts, pieces = 2, 4
    step = width // cuts
    firsts = [None] * rounds
    theirs = [(swapped(mine, "pair", 0), VMEM)]
    token = virtual_energy
    for turn in range(1, rounds):
        firsts[turn] = []
        for cut in range(cuts):
            token = picked(
                three_index, plan, state, token, turn, False, cut, cuts, None if cut else extra
            )
            firsts[turn].append(swapped(token, "pair", turn))
        theirs.append((firsts[turn][0], pl.BlockSpec((1, 8, depth), lambda _: (0, step // 8, 0))))
    other = swapped(three_index, "pair", 0)
    firsts[0] = [other]
    env = {
        "bits": bits,
        "per_block": per_block,
        "blocks": blocks,
        "plan": plan,
        "state": state,
        "three_index": three_index,
        "virtual": virtual_energy,
        "column": virtual_energy[:, None],
        "ours": mine,
        "theirs": theirs,
        "gathered": [[] for _ in range(rounds)],
    }
    seconds = [[other]] + [[] for _ in range(1, rounds)]
    gradient = None
    tilde = [None] * rounds
    densities = []

    def gate_piece(turn, piece):
        return lambda token: gated(token, seconds[turn][piece])

    def send_piece(turn, piece):
        def run(token):
            token = picked(three_index, plan, state, token, turn, True, piece, pieces)
            seconds[turn].append(swapped(token, "pair", turn))
            return token

        return run

    def make_tilde(turn):
        def run(token):
            tilde[turn], density = tildes(
                state, token, env["gathered"][turn], blocks, row_count, half_count
            )
            densities.append(density)
            return density

        return run

    def add_terms(turn, own):
        def run(token):
            nonlocal gradient
            sources = firsts[turn] if own else seconds[turn]
            gradient, token = gradient_terms(
                plan, state, token, tilde[turn], sources, gradient, turn, own, three_index
            )
            return token

        return run

    tasks = []
    late = []
    for turn in range(rounds):
        groups = [[first] for first in firsts[turn]]
        for cut, peers in enumerate(groups):
            clock = 42.0 + 36.0 * cut + 137.0 * (turn - 1) if turn else 11.0
            share = 1 / len(groups)
            worker = chain(env, turn, cut * step, width // len(groups), peers)
            next(worker)
            wide = 12.8 * share
            times = [clock, clock + 3 + 8 * share + wide]
            for stage in range(1, bits):
                times.append(times[-1] + 3 + (wide / 2 if stage == 1 else wide))
            if turn > 0:
                wide *= 2
                times.append(times[-1] + 7)
            for stage in range(bits):
                times.append(times[-1] + 3 + (wide / 2 if stage == 1 else wide))
            tasks += [(time, worker.send) for time in times]
            late.append(times)
    for turn in range(1, rounds):
        begin = 74.0 + 137.0 * (turn - 1)
        for piece, (send, there) in enumerate(((0, 20), (17, 37), (34, 56), (51, 75))):
            tasks += [(begin + send, send_piece(turn, piece)), (begin + there, gate_piece(turn, piece))]
    for turn in range(rounds):
        steps = [make_tilde(turn), add_terms(turn, True), add_terms(turn, False)]
        if turn == 0 and rounds > 1:
            tasks += [(time + 1, step_) for time, step_ in zip(late[cuts][-4:-1], steps)]
        else:
            tasks += [(late[-1][-1] + 6 + index, step_) for index, step_ in enumerate(steps)]
    tasks.sort(key=lambda task: task[0])
    for _, task in tasks:
        token = task(token)
    density = sum(densities)
    for bit in reversed(range(lax.axis_size("pair").bit_length() - 1)):
        half = density.shape[1] // 2
        side = position >> bit & 1
        give = lax.dynamic_slice_in_dim(density, (1 - side) * half, half, 1)
        density = lax.dynamic_slice_in_dim(density, side * half, half, 1) + swapped(give, "pair", bit)
    return (gradient, density)


def solution(mesh):
    in_specs = (P("pair", None, "aux"), P("pair"), P(), P(None, "pair"))
    out_specs = (P("pair", None, "aux"), P("aux", "pair"))
    return jax.shard_map(body, mesh=mesh, in_specs=in_specs, out_specs=out_specs, check_vma=False)
```

time: 292 us -> 254 us (0.87)
  waiting for transfers between devices: 143 us -> 119 us
  starting transfers between devices: 52.2 us -> 47.2 us
  Pallas kernels: 71.2 us -> 66.8 us
  local copies, waits for them, and re-layouts: 21.6 us -> 17.7 us
    ppermute x18, waiting for transfers between devices: 97.3 us -> 80.1 us  [across(): return lax.ppermute(block, ('pair', 'aux'), route)]
    ppermute x18, starting transfers between devices: 32.5 us -> 23.4 us  [across(): return lax.ppermute(block, ('pair', 'aux'), route)]
    ppermute x21 -> x13, waiting for transfers between devices: 45.4 us -> 38.5 us  [swapped(): return lax.ppermute(block, axis, route)]
    pallas_call x19 -> x12, Pallas kernels: 10.3 us -> 5.14 us  [the longest x6 4.72 us: picked(): pl.pallas_call(functools.partial(copy_kernel, extra is not None), out_sha...]
    ppermute x21 -> x13, starting transfers between devices: 19.7 us -> 23.8 us  [swapped(): return lax.ppermute(block, axis, route)]
    unnamed x82 -> x56, local copies, waits for them, and re-layouts: 21.3 us -> 17.3 us
    pallas_call x9 -> x11, Pallas kernels: 0.54 us -> 3.55 us  [joined(): pl.pallas_call(functools.partial(join_kernel, axis), out_shape=jax.ShapeD...]
  transfers between devices with their start and end apart: 39 -> 31, of which waited for: 23 -> 18; matrix products, arithmetic and copies ran while one was open for 0% -> 1% of each run, Pallas kernels for 18% -> 24%
where the time goes in v6:
time: 254 us
  waiting for transfers between devices  119 us (47%)
  Pallas kernels  66.8 us (26%)
  starting transfers between devices  47.2 us (19%)
  local copies, waits for them, and re-layouts  17.7 us (7%)
    ppermute x18, waiting for transfers between devices, across(): return lax.ppermute(block, ('pair', 'aux'), route)  80.1 us
    ppermute x13, waiting for transfers between devices, swapped(): return lax.ppermute(block, axis, route)  38.5 us
    pallas_call x4, Pallas kernels, gradient_terms(): pl.pallas_call(functools.partial(gradient_kernel, len(sources), turn > 0,...  31.8 us
    ppermute x13, starting transfers between devices, swapped(): return lax.ppermute(block, axis, route)  23.8 us
    ppermute x18, starting transfers between devices, across(): return lax.ppermute(block, ('pair', 'aux'), route)  23.4 us
    unnamed x56, local copies, waits for them, and re-layouts  17.3 us
    pallas_call x3, Pallas kernels, integral(): pl.pallas_call(functools.partial(integral_kernel, turn, blocks), out_shap...  15 us
    pallas_call x2, Pallas kernels, tildes(): pl.pallas_call(functools.partial(tilde_kernel, blocks, places), out_shape...  8.97 us
  transfers between devices with their start and end apart: 31, of which 18 were waited for; matrix products, arithmetic and copies ran while one was open for 1% of the time, Pallas kernels for 24%

profile of v6, /device:TPU:0, one launch (start us, length us, event | category | flops | bytes accessed | tf_op | source)
XLA Modules:
  0.0 253.6 jit_solution(6851370166785018011)
XLA Ops:
  2.7 2.8 %copy-done = f32[2,768,1024]{2,1,0:T(8,128)S(1)} copy-done((f32[2,768,1024]{2,1,0:T(8,128)S(1)}, f32[2,768,1024]{2,1,0:T(8,128)}, u32[]{:S(2)}) %copy-start) | copy-done | bytes 6291480
  7.6 2.6 %collective-permute-start = (f32[1,392,1024]{2,1,0:T(8,128)S(1)}, f32[1,392,1024]{2,1,0:T(8,128)S(1)}, u32[]{:S(2)}, u32[]{:S(2)}) collective-permute-start(f32[1,392,1024]{2,1,0:T(8,128)S(1)} %shard_map.59.refs_0_), channel_id=1, source_target_pairs={{0,16},{16,0},{8,24},{24,8},{1,17},{17,1},{9,25},{25,9},{2,18},{18... | collective-permute-start | bytes 4816904 | tf_op jit(solution)/shard_map/ppermute | solution.py:30
  11.3 7.3 %shard_map.61 = (f32[1,384,768]{2,1,0:T(8,128)S(1)}, f32[1,384,768]{2,1,0:T(8,128)S(1)}) custom-call(s32[2,2]{1,0:T(2,128)S(1)} %copy-done.21, s32[4]{0:T(128)S(1)} %pad_add_fusion.state_ref, f32[2,768,1024]{2,1,0:T(8,128)S(1)} %bitcast.7, f32[1,384,1024]{2,1,0:T(8,128)S(1)} %shard_map.60.token_ref, f32[2,768,1024]{2,1,0:T(8,128)} %collective-permute-done.1.refs_0_), custom_call_target="tpu_custom_call" | custom-call | flops 1 | bytes 1 | tf_op jit(solution)/shard_map/pallas_call | solution.py:180
  18.6 2.9 %collective-permute-start.2 = (f32[1,384,768]{2,1,0:T(8,128)S(1)}, f32[1,384,768]{2,1,0:T(8,128)S(1)}, u32[]{:S(2)}, u32[]{:S(2)}) collective-permute-start(f32[1,384,768]{2,1,0:T(8,128)S(1)} %get-tuple-element.32.token_ref), channel_id=1, source_target_pairs={{0,1},{1,0},{2,3},{3,2},{4,5},{5,4},{6,7},{7,6},{8,10},{9,11},{10,... | collective-permute-start | bytes 3538952 | tf_op jit(solution)/shard_map/ppermute | solution.py:44
  21.6 14.2 %collective-permute-done.2.came_ref = f32[1,384,768]{2,1,0:T(8,128)S(1)} collective-permute-done((f32[1,384,768]{2,1,0:T(8,128)S(1)}, f32[1,384,768]{2,1,0:T(8,128)S(1)}, u32[]{:S(2)}, u32[]{:S(2)}) %collective-permute-start.2) | collective-permute-done | bytes 1179680 | tf_op jit(solution)/shard_map/ppermute | solution.py:44
  35.9 2.2 collective-permute-start.4
  38.1 7.9 %collective-permute-done.refs_0_.theirs_ref = f32[1,392,1024]{2,1,0:T(8,128)S(1)} collective-permute-done((f32[1,392,1024]{2,1,0:T(8,128)S(1)}, f32[1,392,1024]{2,1,0:T(8,128)S(1)}, u32[]{:S(2)}, u32[]{:S(2)}) %collective-permute-start) | collective-permute-done | bytes 1605664 | tf_op jit(solution)/shard_map/ppermute | solution.py:30
  45.9 3.8 %shard_map.63 = (f32[1,384,384]{2,1,0:T(8,128)S(1)}, f32[1,384,384]{2,1,0:T(8,128)S(1)}) custom-call(s32[2,2]{1,0:T(2,128)S(1)} %copy-done.21, s32[4]{0:T(128)S(1)} %pad_add_fusion.state_ref, f32[2,768,1024]{2,1,0:T(8,128)S(1)} %bitcast.7, f32[1,192,768]{2,1,0:T(8,128)S(1)} %get-tuple-element.33.token_ref, ...), custom_call_target="tpu_custom_call" | custom-call | flops 1 | bytes 1 | tf_op jit(solution)/shard_map/pallas_call | solution.py:180
  49.8 1.8 collective-permute-start.3
  51.5 1.5 collective-permute-start.11
  53.1 2.6 %collective-permute-start.7 = (f32[1,96,768]{2,1,0:T(8,128)S(1)}, f32[1,96,768]{2,1,0:T(8,128)S(1)}, u32[]{:S(2)}, u32[]{:S(2)}) collective-permute-start(f32[1,96,768]{2,1,0:T(8,128)S(1)} %get-tuple-element.37.token_ref), channel_id=1, source_target_pairs={{0,4},{1,5},{2,6},{3,7},{4,0},{5,1},{6,2},{7,3},{8,12},{9,13},{10,... | collective-permute-start | bytes 884744 | tf_op jit(solution)/shard_map/ppermute | solution.py:44
  55.8 3.9 %collective-permute-done.3.came_ref = f32[1,384,384]{2,1,0:T(8,128)S(1)} collective-permute-done((f32[1,384,384]{2,1,0:T(8,128)S(1)}, f32[1,384,384]{2,1,0:T(8,128)S(1)}, u32[]{:S(2)}, u32[]{:S(2)}) %collective-permute-start.3) | collective-permute-done | bytes 589856 | tf_op jit(solution)/shard_map/ppermute | solution.py:44
  59.8 1.9 collective-permute-start.5
  61.7 3.0 %collective-permute-start.6 = (f32[1,6]{1,0:T(1,128)S(1)}, f32[1,6]{1,0:T(1,128)S(1)}, u32[]{:S(2)}, u32[]{:S(2)}) collective-permute-start(f32[1,6]{1,0:T(1,128)S(1)} %maximum_bitcast_fusion.ours_ref), channel_id=1, source_target_pairs={{0,8},{8,0},{16,24},{24,16},{1,9},{9,1},{17,25},{25,17},{2,10},{10... | collective-permute-start | bytes 80 | tf_op jit(solution)/shard_map/ppermute | solution.py:30
  65.5 3.1 %collective-permute-done.7.right_ref = f32[1,96,768]{2,1,0:T(8,128)S(1)} collective-permute-done((f32[1,96,768]{2,1,0:T(8,128)S(1)}, f32[1,96,768]{2,1,0:T(8,128)S(1)}, u32[]{:S(2)}, u32[]{:S(2)}) %collective-permute-start.7) | collective-permute-done | bytes 294944 | tf_op jit(solution)/shard_map/ppermute | solution.py:44
  69.5 3.0 %collective-permute-start.8 = (f32[1,96,384]{2,1,0:T(8,128)S(1)}, f32[1,96,384]{2,1,0:T(8,128)S(1)}, u32[]{:S(2)}, u32[]{:S(2)}) collective-permute-start(f32[1,96,384]{2,1,0:T(8,128)S(1)} %get-tuple-element.42.token_ref), channel_id=1, source_target_pairs={{0,4},{1,5},{2,6},{3,7},{4,0},{5,1},{6,2},{7,3},{8,12},{9,13},{10,... | collective-permute-start | bytes 442376 | tf_op jit(solution)/shard_map/ppermute | solution.py:44
  72.5 16.6 %collective-permute-done.8.right_ref = f32[1,96,384]{2,1,0:T(8,128)S(1)} collective-permute-done((f32[1,96,384]{2,1,0:T(8,128)S(1)}, f32[1,96,384]{2,1,0:T(8,128)S(1)}, u32[]{:S(2)}, u32[]{:S(2)}) %collective-permute-start.8) | collective-permute-done | bytes 147488 | tf_op jit(solution)/shard_map/ppermute | solution.py:44
  90.7 3.3 %collective-permute-start.9 = (f32[1,96,384]{2,1,0:T(8,128)S(1)}, f32[1,96,384]{2,1,0:T(8,128)S(1)}, u32[]{:S(2)}, u32[]{:S(2)}) collective-permute-start(f32[1,96,384]{2,1,0:T(8,128)S(1)} %shard_map.68.refs_0_.one_ref), channel_id=1, source_target_pairs={{0,16},{16,0},{8,24},{24,8},{1,17},{17,1},{9,25},{25,9},{2,18},{18... | collective-permute-start | bytes 442376 | tf_op jit(solution)/shard_map/ppermute | solution.py:30
  94.0 4.4 %collective-permute-done.9.two_ref = f32[1,96,384]{2,1,0:T(8,128)S(1)} collective-permute-done((f32[1,96,384]{2,1,0:T(8,128)S(1)}, f32[1,96,384]{2,1,0:T(8,128)S(1)}, u32[]{:S(2)}, u32[]{:S(2)}) %collective-permute-start.9) | collective-permute-done | bytes 147488 | tf_op jit(solution)/shard_map/ppermute | solution.py:30
  98.4 3.8 %shard_map.72 = (f32[1,384,384]{2,1,0:T(8,128)S(1)}, f32[1,384,384]{2,1,0:T(8,128)S(1)}) custom-call(s32[2,2]{1,0:T(2,128)S(1)} %copy-done.21, s32[4]{0:T(128)S(1)} %pad_add_fusion.state_ref, f32[2,768,1024]{2,1,0:T(8,128)S(1)} %bitcast.7, f32[2,96,384]{2,1,0:T(8,128)S(1)} %shard_map.71.token_ref.one_ref, ...), custom_call_target="tpu_custom_call" | custom-call | flops 1 | bytes 1 | tf_op jit(solution)/shard_map/pallas_call | solution.py:180
  104.5 1.5 collective-permute-start.16
  108.0 16.9 %collective-permute-done.12.came_ref = f32[1,384,384]{2,1,0:T(8,128)S(1)} collective-permute-done((f32[1,384,384]{2,1,0:T(8,128)S(1)}, f32[1,384,384]{2,1,0:T(8,128)S(1)}, u32[]{:S(2)}, u32[]{:S(2)}) %collective-permute-start.12) | collective-permute-done | bytes 589856 | tf_op jit(solution)/shard_map/ppermute | solution.py:44
  125.8 7.4 %collective-permute-done.14.came_ref = f32[1,192,384]{2,1,0:T(8,128)S(1)} collective-permute-done((f32[1,192,384]{2,1,0:T(8,128)S(1)}, f32[1,192,384]{2,1,0:T(8,128)S(1)}, u32[]{:S(2)}, u32[]{:S(2)}) %collective-permute-start.14) | collective-permute-done | bytes 294944 | tf_op jit(solution)/shard_map/ppermute | solution.py:44
  133.5 4.1 %collective-permute-start.24 = (f32[1,768,768]{2,1,0:T(8,128)S(1)}, f32[1,768,768]{2,1,0:T(8,128)S(1)}, u32[]{:S(2)}, u32[]{:S(2)}) collective-permute-start(f32[1,768,768]{2,1,0:T(8,128)S(1)} %shard_map.79.token_ref.refs_0_), channel_id=1, source_target_pairs={{0,8},{8,0},{16,24},{24,16},{1,9},{9,1},{17,25},{25,17},{2,10},{10... | collective-permute-start | bytes 7077896 | tf_op jit(solution)/shard_map/ppermute | solution.py:30
  137.6 9.9 %collective-permute-done.18.two_ref = f32[2,192,384]{2,1,0:T(8,128)S(1)} collective-permute-done((f32[2,192,384]{2,1,0:T(8,128)S(1)}, f32[2,192,384]{2,1,0:T(8,128)S(1)}, u32[]{:S(2)}, u32[]{:S(2)}) %collective-permute-start.18) | collective-permute-done | bytes 589856 | tf_op jit(solution)/shard_map/ppermute | solution.py:44
  147.9 1.8 collective-permute-start.21
  149.7 1.5 collective-permute-start.17
  151.2 6.0 %collective-permute-done.17.right_ref = f32[1,96,384]{2,1,0:T(8,128)S(1)} collective-permute-done((f32[1,96,384]{2,1,0:T(8,128)S(1)}, f32[1,96,384]{2,1,0:T(8,128)S(1)}, u32[]{:S(2)}, u32[]{:S(2)}) %collective-permute-start.17) | collective-permute-done | bytes 147488 | tf_op jit(solution)/shard_map/ppermute | solution.py:44
  159.1 7.3 %collective-permute-done.21.refs_1_ = f32[1,768,256]{2,1,0:T(8,128)S(1)} collective-permute-done((f32[1,768,256]{2,1,0:T(8,128)S(1)}, f32[1,768,256]{2,1,0:T(8,128)S(1)}, u32[]{:S(2)}, u32[]{:S(2)}) %collective-permute-start.21) | collective-permute-done | bytes 786464 | tf_op jit(solution)/shard_map/ppermute | solution.py:30
  167.3 2.0 collective-permute-done.20.two_ref
  170.6 2.3 collective-permute-start.26
  174.3 1.7 copy-done.17
  176.0 4.5 %shard_map.85 = (bf16[2,1,1536,768]{3,2,1,0:T(8,128)(2,1)}, f32[96,768]{1,0:T(8,128)S(1)}) custom-call(s32[4]{0:T(128)S(1)} %pad_add_fusion.state_ref, f32[2,96,384]{2,1,0:T(8,128)S(1)} %shard_map.84.token_ref.one_ref, f32[1,768,768]{2,1,0:T(8,128)S(1)} %shard_map.79.token_ref.refs_0_, f32[1,768,768]{2,1,0:T(8,128)S(1)} %copy-done.17), custom_call_target="tpu_custom_call" | custom-call | flops 1 | bytes 1 | tf_op jit(solution)/shard_map/pallas_call | solution.py:318
  180.5 1.6 shard_map.86.refs_0_.refs_1_
  182.1 1.5 shard_map.87.token_ref
  183.6 2.0 collective-permute-done.22.two_ref
  185.7 5.1 %collective-permute-done.26.refs_1_.refs_2_ = f32[1,768,256]{2,1,0:T(8,128)S(1)} collective-permute-done((f32[1,768,256]{2,1,0:T(8,128)S(1)}, f32[1,768,256]{2,1,0:T(8,128)S(1)}, u32[]{:S(2)}, u32[]{:S(2)}) %collective-permute-start.26) | collective-permute-done | bytes 786464 | tf_op jit(solution)/shard_map/ppermute | solution.py:30
  190.8 7.5 %shard_map.90 = (f32[2,768,1024]{2,1,0:T(8,128)}, f32[8,128]{1,0:T(8,128)S(1)}) custom-call(s32[2,2]{1,0:T(2,128)S(1)} %copy-done.21, s32[4]{0:T(128)S(1)} %pad_add_fusion.state_ref, bf16[2,1,1536,768]{3,2,1,0:T(8,128)(2,1)S(1)} %bitcast.9, f32[8,128]{1,0:T(8,128)S(1)} %shard_map.89.token_ref, f32[2,768,1024]{2,1,0:T(8,128)} %collective-permute-done.1.refs_0_), custom_call_target="tpu_custom_call" | custom-call | flops 1 | bytes 1 | tf_op jit(solution)/shard_map/pallas_call | solution.py:374
  199.8 1.7 collective-permute-start.28
  201.6 2.3 copy-done.7
  203.9 7.7 %shard_map.92 = (f32[2,768,1024]{2,1,0:T(8,128)}, f32[8,128]{1,0:T(8,128)S(1)}) custom-call(s32[2,2]{1,0:T(2,128)S(1)} %copy-done.21, s32[4]{0:T(128)S(1)} %pad_add_fusion.state_ref, bf16[2,1,1536,768]{3,2,1,0:T(8,128)(2,1)S(1)} %copy-done.7, f32[2,384,384]{2,1,0:T(8,128)S(1)} %shard_map.91.token_ref.one_ref, ...), custom_call_target="tpu_custom_call", output_to_operand_aliasing={{0}: (5, {})} | custom-call | flops 1 | bytes 1 | tf_op jit(solution)/shard_map/pallas_call | solution.py:374
  211.6 6.4 %collective-permute-done.28.refs_1_.refs_3_ = f32[1,768,256]{2,1,0:T(8,128)} collective-permute-done((f32[1,768,256]{2,1,0:T(8,128)}, f32[1,768,256]{2,1,0:T(8,128)}, u32[]{:S(2)}, u32[]{:S(2)}) %collective-permute-start.28) | collective-permute-done | bytes 786464 | tf_op jit(solution)/shard_map/ppermute | solution.py:30
  220.8 1.7 copy-done.2
  222.4 4.5 %shard_map.95 = (bf16[2,1,1536,768]{3,2,1,0:T(8,128)(2,1)}, f32[96,768]{1,0:T(8,128)S(1)}) custom-call(s32[4]{0:T(128)S(1)} %pad_add_fusion.state_ref, f32[2,768,384]{2,1,0:T(8,128)S(1)} %copy-done.2, f32[2,768,384]{2,1,0:T(8,128)S(1)} %shard_map.86.refs_0_.refs_1_, f32[2,768,384]{2,1,0:T(8,128)S(1)} %shard_map.86.refs_0_.refs_1_, ...), custom_call_target="tpu_custom_call" | custom-call | flops 1 | bytes 1 | tf_op jit(solution)/shard_map/pallas_call | solution.py:318
  227.8 4.4 %collective-permute-done.29 = f32[96,384]{1,0:T(8,128)S(1)} collective-permute-done((f32[96,384]{1,0:T(8,128)S(1)}, f32[96,384]{1,0:T(8,128)S(1)}, u32[]{:S(2)}, u32[]{:S(2)}) %collective-permute-start.29) | collective-permute-done | bytes 147488 | tf_op jit(solution)/shard_map/ppermute | solution.py:30
  232.4 2.3 copy-done.5
  236.2 8.9 %shard_map.96 = (f32[2,768,1024]{2,1,0:T(8,128)}, f32[8,128]{1,0:T(8,128)S(1)}) custom-call(s32[2,2]{1,0:T(2,128)S(1)} %copy-done.21, s32[4]{0:T(128)S(1)} %pad_add_fusion.state_ref, bf16[2,1,1536,768]{3,2,1,0:T(8,128)(2,1)S(1)} %copy-done.5, f32[96,768]{1,0:T(8,128)S(1)} %get-tuple-element.55.token_ref, ...), custom_call_target="tpu_custom_call", output_to_operand_aliasing={{0}: (6, {})} | custom-call | flops 1 | bytes 1 | tf_op jit(solution)/shard_map/pallas_call | solution.py:374
  245.1 7.8 %shard_map.97 = (f32[2,768,1024]{2,1,0:T(8,128)}, f32[8,128]{1,0:T(8,128)}) custom-call(s32[2,2]{1,0:T(2,128)S(1)} %copy-done.21, s32[4]{0:T(128)S(1)} %pad_add_fusion.state_ref, bf16[2,1,1536,768]{3,2,1,0:T(8,128)(2,1)S(1)} %copy-done.6, f32[8,128]{1,0:T(8,128)S(1)} %get-tuple-element.57.token_ref, ...), custom_call_target="tpu_custom_call", output_to_operand_aliasing={{0}: (8, {})} | custom-call | flops 1 | bytes 1 | tf_op jit(solution)/shard_map/pallas_call | solution.py:374
  (126 shorter events, 27.6 us)
Async XLA Ops:
  0.6 10.6 %collective-permute-start.1 = (f32[2,768,1024]{2,1,0:T(8,128)}, f32[2,768,1024]{2,1,0:T(8,128)}, u32[]{:S(2)}, u32[]{:S(2)}) collective-permute-start(f32[2,768,1024]{2,1,0:T(8,128)} %source_ref.11), channel_id=1, source_target_pairs={{0,8},{8,0},{16,24},{24,16},{1,9},{9,1},{17,25},{25,17},{2,10},{10... | collective-permute-start | bytes 18874376 | tf_op jit(solution)/shard_map/ppermute | solution.py:30
  2.7 2.8 %copy-start = (f32[2,768,1024]{2,1,0:T(8,128)S(1)}, f32[2,768,1024]{2,1,0:T(8,128)}, u32[]{:S(2)}) copy-start(f32[2,768,1024]{2,1,0:T(8,128)} %source_ref.11) | copy-start | bytes 18874372
  6.9 4.4 %slice-start = ((s8[6291456]{0:T(1024)(128)(4,1)}), s8[4194304]{0:T(1024)(128)(4,1)S(1)}, s32[]{:S(2)}) async-start(s8[6291456]{0:T(1024)(128)(4,1)} %bitcast.6), calls=%async_computation | async-start | bytes 8388608
  7.6 3.7 %slice-start.1 = ((s8[6291456]{0:T(1024)(128)(4,1)}), s8[2097152]{0:T(1024)(128)(4,1)S(1)}, s32[]{:S(2)}) async-start(s8[6291456]{0:T(1024)(128)(4,1)} %bitcast.6), calls=%async_computation.1 | async-start | bytes 4194304
  7.6 3.7 %copy-start.21 = (s32[2,2]{1,0:T(2,128)S(1)}, s32[2,2]{1,0:T(2,128)}, u32[]{:S(2)}) copy-start(s32[2,2]{1,0:T(2,128)} %plan_ref.25) | copy-start | bytes 52
  7.6 38.4 %collective-permute-start = (f32[1,392,1024]{2,1,0:T(8,128)S(1)}, f32[1,392,1024]{2,1,0:T(8,128)S(1)}, u32[]{:S(2)}, u32[]{:S(2)}) collective-permute-start(f32[1,392,1024]{2,1,0:T(8,128)S(1)} %shard_map.59.refs_0_), channel_id=1, source_target_pairs={{0,16},{16,0},{8,24},{24,8},{1,17},{17,1},{9,25},{25,9},{2,18},{18... | collective-permute-start | bytes 4816904 | tf_op jit(solution)/shard_map/ppermute | solution.py:30
  18.6 17.1 %collective-permute-start.2 = (f32[1,384,768]{2,1,0:T(8,128)S(1)}, f32[1,384,768]{2,1,0:T(8,128)S(1)}, u32[]{:S(2)}, u32[]{:S(2)}) collective-permute-start(f32[1,384,768]{2,1,0:T(8,128)S(1)} %get-tuple-element.32.token_ref), channel_id=1, source_target_pairs={{0,1},{1,0},{2,3},{3,2},{4,5},{5,4},{6,7},{7,6},{8,10},{9,11},{10,... | collective-permute-start | bytes 3538952 | tf_op jit(solution)/shard_map/ppermute | solution.py:44
  35.9 17.2 %collective-permute-start.4 = (f32[1,192,768]{2,1,0:T(8,128)S(1)}, f32[1,192,768]{2,1,0:T(8,128)S(1)}, u32[]{:S(2)}, u32[]{:S(2)}) collective-permute-start(f32[1,192,768]{2,1,0:T(8,128)S(1)} %get-tuple-element.33.token_ref), channel_id=1, source_target_pairs={{0,2},{1,3},{2,0},{3,1},{4,6},{5,7},{6,4},{7,5},{8,9},{9,8},{10,11... | collective-permute-start | bytes 1769480 | tf_op jit(solution)/shard_map/ppermute | solution.py:44
  45.9 111.3 %copy-start.3 = (f32[1,392,1024]{2,1,0:T(8,128)}, f32[1,392,1024]{2,1,0:T(8,128)S(1)}, u32[]{:S(2)}) copy-start(f32[1,392,1024]{2,1,0:T(8,128)S(1)} %collective-permute-done.refs_0_.theirs_ref) | copy-start | bytes 4816900
  49.8 9.9 %collective-permute-start.3 = (f32[1,384,384]{2,1,0:T(8,128)S(1)}, f32[1,384,384]{2,1,0:T(8,128)S(1)}, u32[]{:S(2)}, u32[]{:S(2)}) collective-permute-start(f32[1,384,384]{2,1,0:T(8,128)S(1)} %get-tuple-element.35.token_ref), channel_id=1, source_target_pairs={{0,1},{1,0},{2,3},{3,2},{4,5},{5,4},{6,7},{7,6},{8,10},{9,11},{10,... | collective-permute-start | bytes 1769480 | tf_op jit(solution)/shard_map/ppermute | solution.py:44
  51.5 46.9 %collective-permute-start.11 = (f32[1,384,1024]{2,1,0:T(8,128)S(1)}, f32[1,384,1024]{2,1,0:T(8,128)S(1)}, u32[]{:S(2)}, u32[]{:S(2)}) collective-permute-start(f32[1,384,1024]{2,1,0:T(8,128)S(1)} %shard_map.60.token_ref), channel_id=1, source_target_pairs={{0,16},{16,0},{8,24},{24,8},{1,17},{17,1},{9,25},{25,9},{2,18},{18... | collective-permute-start | bytes 4718600 | tf_op jit(solution)/shard_map/ppermute | solution.py:30
  53.1 11.6 %copy-start.23 = (f32[768]{0:T(1024)S(1)}, f32[768]{0:T(1024)}, u32[]{:S(2)}) copy-start(f32[768]{0:T(1024)} %refs_1_.1) | copy-start | bytes 9220
  53.1 15.4 %collective-permute-start.7 = (f32[1,96,768]{2,1,0:T(8,128)S(1)}, f32[1,96,768]{2,1,0:T(8,128)S(1)}, u32[]{:S(2)}, u32[]{:S(2)}) collective-permute-start(f32[1,96,768]{2,1,0:T(8,128)S(1)} %get-tuple-element.37.token_ref), channel_id=1, source_target_pairs={{0,4},{1,5},{2,6},{3,7},{4,0},{5,1},{6,2},{7,3},{8,12},{9,13},{10,... | collective-permute-start | bytes 884744 | tf_op jit(solution)/shard_map/ppermute | solution.py:44
  59.8 9.7 %collective-permute-start.5 = (f32[1,192,384]{2,1,0:T(8,128)S(1)}, f32[1,192,384]{2,1,0:T(8,128)S(1)}, u32[]{:S(2)}, u32[]{:S(2)}) collective-permute-start(f32[1,192,384]{2,1,0:T(8,128)S(1)} %get-tuple-element.39.token_ref), channel_id=1, source_target_pairs={{0,2},{1,3},{2,0},{3,1},{4,6},{5,7},{6,4},{7,5},{8,9},{9,8},{10,11... | collective-permute-start | bytes 884744 | tf_op jit(solution)/shard_map/ppermute | solution.py:44
  61.7 3.8 %collective-permute-start.6 = (f32[1,6]{1,0:T(1,128)S(1)}, f32[1,6]{1,0:T(1,128)S(1)}, u32[]{:S(2)}, u32[]{:S(2)}) collective-permute-start(f32[1,6]{1,0:T(1,128)S(1)} %maximum_bitcast_fusion.ours_ref), channel_id=1, source_target_pairs={{0,8},{8,0},{16,24},{24,16},{1,9},{9,1},{17,25},{25,17},{2,10},{10... | collective-permute-start | bytes 80 | tf_op jit(solution)/shard_map/ppermute | solution.py:30
  69.4 21.1 %collective-permute-start.10 = (f32[1,96,768]{2,1,0:T(8,128)S(1)}, f32[1,96,768]{2,1,0:T(8,128)S(1)}, u32[]{:S(2)}, u32[]{:S(2)}) collective-permute-start(f32[1,96,768]{2,1,0:T(8,128)S(1)} %shard_map.66.token_ref.one_ref), channel_id=1, source_target_pairs={{0,4},{1,5},{2,6},{3,7},{4,0},{5,1},{6,2},{7,3},{8,12},{9,13},{10,... | collective-permute-start | bytes 884744 | tf_op jit(solution)/shard_map/ppermute | solution.py:44
  69.5 19.6 %collective-permute-start.8 = (f32[1,96,384]{2,1,0:T(8,128)S(1)}, f32[1,96,384]{2,1,0:T(8,128)S(1)}, u32[]{:S(2)}, u32[]{:S(2)}) collective-permute-start(f32[1,96,384]{2,1,0:T(8,128)S(1)} %get-tuple-element.42.token_ref), channel_id=1, source_target_pairs={{0,4},{1,5},{2,6},{3,7},{4,0},{5,1},{6,2},{7,3},{8,12},{9,13},{10,... | collective-permute-start | bytes 442376 | tf_op jit(solution)/shard_map/ppermute | solution.py:44
  90.6 11.7 %collective-permute-start.13 = (f32[1,192,768]{2,1,0:T(8,128)S(1)}, f32[1,192,768]{2,1,0:T(8,128)S(1)}, u32[]{:S(2)}, u32[]{:S(2)}) collective-permute-start(f32[1,192,768]{2,1,0:T(8,128)S(1)} %shard_map.70.token_ref.one_ref), channel_id=1, source_target_pairs={{0,2},{1,3},{2,0},{3,1},{4,6},{5,7},{6,4},{7,5},{8,9},{9,8},{10,11... | collective-permute-start | bytes 1769480 | tf_op jit(solution)/shard_map/ppermute | solution.py:44
  90.7 7.7 %collective-permute-start.9 = (f32[1,96,384]{2,1,0:T(8,128)S(1)}, f32[1,96,384]{2,1,0:T(8,128)S(1)}, u32[]{:S(2)}, u32[]{:S(2)}) collective-permute-start(f32[1,96,384]{2,1,0:T(8,128)S(1)} %shard_map.68.refs_0_.one_ref), channel_id=1, source_target_pairs={{0,16},{16,0},{8,24},{24,8},{1,17},{17,1},{9,25},{25,9},{2,18},{18... | collective-permute-start | bytes 442376 | tf_op jit(solution)/shard_map/ppermute | solution.py:30
  98.4 3.8 %copy-start.8 = (f32[1,384,1024]{2,1,0:T(8,128)}, f32[1,384,1024]{2,1,0:T(8,128)S(1)}, u32[]{:S(2)}) copy-start(f32[1,384,1024]{2,1,0:T(8,128)S(1)} %collective-permute-done.11.refs_0_.refs_1_) | copy-start | bytes 4718596
  102.4 30.9 %collective-permute-start.19 = (f32[1,384,768]{2,1,0:T(8,128)S(1)}, f32[1,384,768]{2,1,0:T(8,128)S(1)}, u32[]{:S(2)}, u32[]{:S(2)}) collective-permute-start(f32[1,384,768]{2,1,0:T(8,128)S(1)} %shard_map.73.refs_0_.one_ref), channel_id=1, source_target_pairs={{0,1},{1,0},{2,3},{3,2},{4,5},{5,4},{6,7},{7,6},{8,10},{9,11},{10,... | collective-permute-start | bytes 3538952 | tf_op jit(solution)/shard_map/ppermute | solution.py:44
  103.8 21.2 %collective-permute-start.12 = (f32[1,384,384]{2,1,0:T(8,128)S(1)}, f32[1,384,384]{2,1,0:T(8,128)S(1)}, u32[]{:S(2)}, u32[]{:S(2)}) collective-permute-start(f32[1,384,384]{2,1,0:T(8,128)S(1)} %get-tuple-element.44.token_ref), channel_id=1, source_target_pairs={{0,1},{1,0},{2,3},{3,2},{4,5},{5,4},{6,7},{7,6},{8,10},{9,11},{10,... | collective-permute-start | bytes 1769480 | tf_op jit(solution)/shard_map/ppermute | solution.py:44
  104.5 21.4 %collective-permute-start.16 = (f32[1,768,256]{2,1,0:T(8,128)S(1)}, f32[1,768,256]{2,1,0:T(8,128)S(1)}, u32[]{:S(2)}, u32[]{:S(2)}) collective-permute-start(f32[1,768,256]{2,1,0:T(8,128)S(1)} %shard_map.69.token_ref), channel_id=1, source_target_pairs={{0,16},{16,0},{8,24},{24,8},{1,17},{17,1},{9,25},{25,9},{2,18},{18... | collective-permute-start | bytes 2359304 | tf_op jit(solution)/shard_map/ppermute | solution.py:30
  106.0 19.8 %collective-permute-start.15 = (f32[2,96,384]{2,1,0:T(8,128)S(1)}, f32[2,96,384]{2,1,0:T(8,128)S(1)}, u32[]{:S(2)}, u32[]{:S(2)}) collective-permute-start(f32[2,96,384]{2,1,0:T(8,128)S(1)} %shard_map.71.token_ref.one_ref), channel_id=1, source_target_pairs={{0,4},{1,5},{2,6},{3,7},{4,0},{5,1},{6,2},{7,3},{8,12},{9,13},{10,... | collective-permute-start | bytes 884744 | tf_op jit(solution)/shard_map/ppermute | solution.py:44
  125.0 8.2 %collective-permute-start.14 = (f32[1,192,384]{2,1,0:T(8,128)S(1)}, f32[1,192,384]{2,1,0:T(8,128)S(1)}, u32[]{:S(2)}, u32[]{:S(2)}) collective-permute-start(f32[1,192,384]{2,1,0:T(8,128)S(1)} %get-tuple-element.46.token_ref), channel_id=1, source_target_pairs={{0,2},{1,3},{2,0},{3,1},{4,6},{5,7},{6,4},{7,5},{8,9},{9,8},{10,11... | collective-permute-start | bytes 884744 | tf_op jit(solution)/shard_map/ppermute | solution.py:44
  125.8 7.5 %copy-start.12 = (f32[1,768,256]{2,1,0:T(8,128)}, f32[1,768,256]{2,1,0:T(8,128)S(1)}, u32[]{:S(2)}) copy-start(f32[1,768,256]{2,1,0:T(8,128)S(1)} %collective-permute-done.16.refs_1_.refs_0_) | copy-start | bytes 2359300
  133.5 39.4 %collective-permute-start.24 = (f32[1,768,768]{2,1,0:T(8,128)S(1)}, f32[1,768,768]{2,1,0:T(8,128)S(1)}, u32[]{:S(2)}, u32[]{:S(2)}) collective-permute-start(f32[1,768,768]{2,1,0:T(8,128)S(1)} %shard_map.79.token_ref.refs_0_), channel_id=1, source_target_pairs={{0,8},{8,0},{16,24},{24,16},{1,9},{9,1},{17,25},{25,17},{2,10},{10... | collective-permute-start | bytes 7077896 | tf_op jit(solution)/shard_map/ppermute | solution.py:30
  137.6 9.9 %collective-permute-start.18 = (f32[2,192,384]{2,1,0:T(8,128)S(1)}, f32[2,192,384]{2,1,0:T(8,128)S(1)}, u32[]{:S(2)}, u32[]{:S(2)}) collective-permute-start(f32[2,192,384]{2,1,0:T(8,128)S(1)} %shard_map.76.refs_0_.one_ref), channel_id=1, source_target_pairs={{0,2},{1,3},{2,0},{3,1},{4,6},{5,7},{6,4},{7,5},{8,9},{9,8},{10,11... | collective-permute-start | bytes 1769480 | tf_op jit(solution)/shard_map/ppermute | solution.py:44
  147.6 32.9 %collective-permute-start.23 = (f32[2,384,384]{2,1,0:T(8,128)S(1)}, f32[2,384,384]{2,1,0:T(8,128)}, u32[]{:S(2)}, u32[]{:S(2)}) collective-permute-start(f32[2,384,384]{2,1,0:T(8,128)S(1)} %shard_map.80.token_ref.one_ref), channel_id=1, source_target_pairs={{0,1},{1,0},{2,3},{3,2},{4,5},{5,4},{6,7},{7,6},{8,10},{9,11},{10,... | collective-permute-start | bytes 3538952 | tf_op jit(solution)/shard_map/ppermute | solution.py:44
  147.9 18.5 %collective-permute-start.21 = (f32[1,768,256]{2,1,0:T(8,128)S(1)}, f32[1,768,256]{2,1,0:T(8,128)S(1)}, u32[]{:S(2)}, u32[]{:S(2)}) collective-permute-start(f32[1,768,256]{2,1,0:T(8,128)S(1)} %shard_map.74.token_ref), channel_id=1, source_target_pairs={{0,16},{16,0},{8,24},{24,8},{1,17},{17,1},{9,25},{25,9},{2,18},{18... | collective-permute-start | bytes 2359304 | tf_op jit(solution)/shard_map/ppermute | solution.py:30
  149.7 7.5 %collective-permute-start.17 = (f32[1,96,384]{2,1,0:T(8,128)S(1)}, f32[1,96,384]{2,1,0:T(8,128)S(1)}, u32[]{:S(2)}, u32[]{:S(2)}) collective-permute-start(f32[1,96,384]{2,1,0:T(8,128)S(1)} %get-tuple-element.48.token_ref), channel_id=1, source_target_pairs={{0,4},{1,5},{2,6},{3,7},{4,0},{5,1},{6,2},{7,3},{8,12},{9,13},{10,... | collective-permute-start | bytes 442376 | tf_op jit(solution)/shard_map/ppermute | solution.py:44
  158.0 11.2 %collective-permute-start.20 = (f32[1,96,384]{2,1,0:T(8,128)S(1)}, f32[1,96,384]{2,1,0:T(8,128)S(1)}, u32[]{:S(2)}, u32[]{:S(2)}) collective-permute-start(f32[1,96,384]{2,1,0:T(8,128)S(1)} %shard_map.81.refs_0_.one_ref), channel_id=1, source_target_pairs={{0,16},{16,0},{8,24},{24,8},{1,17},{17,1},{9,25},{25,9},{2,18},{18... | collective-permute-start | bytes 442376 | tf_op jit(solution)/shard_map/ppermute | solution.py:30
  169.3 16.3 %collective-permute-start.22 = (f32[2,96,384]{2,1,0:T(8,128)S(1)}, f32[2,96,384]{2,1,0:T(8,128)S(1)}, u32[]{:S(2)}, u32[]{:S(2)}) collective-permute-start(f32[2,96,384]{2,1,0:T(8,128)S(1)} %shard_map.84.token_ref.one_ref), channel_id=1, source_target_pairs={{0,4},{1,5},{2,6},{3,7},{4,0},{5,1},{6,2},{7,3},{8,12},{9,13},{10,... | collective-permute-start | bytes 884744 | tf_op jit(solution)/shard_map/ppermute | solution.py:44
  170.6 20.2 %collective-permute-start.26 = (f32[1,768,256]{2,1,0:T(8,128)S(1)}, f32[1,768,256]{2,1,0:T(8,128)S(1)}, u32[]{:S(2)}, u32[]{:S(2)}) collective-permute-start(f32[1,768,256]{2,1,0:T(8,128)S(1)} %shard_map.82.refs_0_), channel_id=1, source_target_pairs={{0,16},{16,0},{8,24},{24,8},{1,17},{17,1},{9,25},{25,9},{2,18},{18... | collective-permute-start | bytes 2359304 | tf_op jit(solution)/shard_map/ppermute | solution.py:30
  180.5 10.3 %slice-start.2 = ((s8[4718592]{0:T(1024)(128)(4,1)}), s8[4194304]{0:T(1024)(128)(4,1)S(1)}, s32[]{:S(2)}) async-start(s8[4718592]{0:T(1024)(128)(4,1)} %bitcast.8), calls=%async_computation.2 | async-start | bytes 8388608
  182.1 8.7 %slice-start.3 = ((s8[4718592]{0:T(1024)(128)(4,1)}), s8[524288]{0:T(1024)(128)(4,1)S(1)}, s32[]{:S(2)}) async-start(s8[4718592]{0:T(1024)(128)(4,1)} %bitcast.8), calls=%async_computation.3 | async-start | bytes 1048576
  185.6 12.7 %collective-permute-start.25 = (f32[2,192,384]{2,1,0:T(8,128)S(1)}, f32[2,192,384]{2,1,0:T(8,128)S(1)}, u32[]{:S(2)}, u32[]{:S(2)}) collective-permute-start(f32[2,192,384]{2,1,0:T(8,128)S(1)} %shard_map.88.refs_0_.one_ref), channel_id=1, source_target_pairs={{0,2},{1,3},{2,0},{3,1},{4,6},{5,7},{6,4},{7,5},{8,9},{9,8},{10,11... | collective-permute-start | bytes 1769480 | tf_op jit(solution)/shard_map/ppermute | solution.py:44
  190.8 7.5 %copy-start.14 = (f32[1,768,256]{2,1,0:T(8,128)}, f32[1,768,256]{2,1,0:T(8,128)S(1)}, u32[]{:S(2)}) copy-start(f32[1,768,256]{2,1,0:T(8,128)S(1)} %collective-permute-done.26.refs_1_.refs_2_) | copy-start | bytes 2359300
  198.4 19.6 %collective-permute-start.27 = (f32[2,384,384]{2,1,0:T(8,128)S(1)}, f32[2,384,384]{2,1,0:T(8,128)}, u32[]{:S(2)}, u32[]{:S(2)}) collective-permute-start(f32[2,384,384]{2,1,0:T(8,128)S(1)} %shard_map.91.token_ref.one_ref), channel_id=1, source_target_pairs={{0,1},{1,0},{2,3},{3,2},{4,5},{5,4},{6,7},{7,6},{8,10},{9,11},{10,... | collective-permute-start | bytes 3538952 | tf_op jit(solution)/shard_map/ppermute | solution.py:44
  199.8 18.1 %collective-permute-start.28 = (f32[1,768,256]{2,1,0:T(8,128)}, f32[1,768,256]{2,1,0:T(8,128)}, u32[]{:S(2)}, u32[]{:S(2)}) collective-permute-start(f32[1,768,256]{2,1,0:T(8,128)} %shard_map.87.token_ref), channel_id=1, source_target_pairs={{0,16},{16,0},{8,24},{24,8},{1,17},{17,1},{9,25},{25,9},{2,18},{18... | collective-permute-start | bytes 2359304 | tf_op jit(solution)/shard_map/ppermute | solution.py:30
  222.4 4.5 %copy-start.19 = (f32[96,768]{1,0:T(8,128)S(1)}, f32[96,768]{1,0:T(8,128)}, u32[]{:S(2)}) copy-start(f32[96,768]{1,0:T(8,128)} %copy-done.18) | copy-start | bytes 884740
  226.9 5.5 %copy-start.4 = (f32[1,392,1024]{2,1,0:T(8,128)S(1)}, f32[1,392,1024]{2,1,0:T(8,128)}, u32[]{:S(2)}) copy-start(f32[1,392,1024]{2,1,0:T(8,128)} %copy-done.3) | copy-start | bytes 4816900
  227.0 5.2 %collective-permute-start.29 = (f32[96,384]{1,0:T(8,128)S(1)}, f32[96,384]{1,0:T(8,128)S(1)}, u32[]{:S(2)}, u32[]{:S(2)}) collective-permute-start(f32[96,384]{1,0:T(8,128)S(1)} %constant_dynamic-slice_fusion.1), channel_id=1, source_target_pairs={{0,16},{16,0},{8,24},{24,8},{1,17},{17,1},{9,25},{25,9},{2,18},{18... | collective-permute-start | bytes 442376 | tf_op jit(solution)/shard_map/ppermute | solution.py:30
  232.3 20.5 %collective-permute-start.30 = (f32[96,192]{1,0:T(8,128)S(1)}, f32[96,192]{1,0:T(8,128)S(1)}, u32[]{:S(2)}, u32[]{:S(2)}) collective-permute-start(f32[96,192]{1,0:T(8,128)S(1)} %constant_dynamic-slice_fusion), channel_id=1, source_target_pairs={{0,8},{8,0},{16,24},{24,16},{1,9},{9,1},{17,25},{25,17},{2,10},{10... | collective-permute-start | bytes 221192 | tf_op jit(solution)/shard_map/ppermute | solution.py:30
  236.2 8.9 %copy-start.6 = (bf16[2,1,1536,768]{3,2,1,0:T(8,128)(2,1)S(1)}, bf16[2,1,1536,768]{3,2,1,0:T(8,128)(2,1)}, u32[]{:S(2)}) copy-start(bf16[2,1,1536,768]{3,2,1,0:T(8,128)(2,1)} %get-tuple-element.54.tall_ref) | copy-start | bytes 14155780
  236.2 8.9 %copy-start.11 = (f32[1,768,256]{2,1,0:T(8,128)S(1)}, f32[1,768,256]{2,1,0:T(8,128)}, u32[]{:S(2)}) copy-start(f32[1,768,256]{2,1,0:T(8,128)} %copy-done.10) | copy-start | bytes 2359300
  236.2 8.9 %copy-start.13 = (f32[1,768,256]{2,1,0:T(8,128)S(1)}, f32[1,768,256]{2,1,0:T(8,128)}, u32[]{:S(2)}) copy-start(f32[1,768,256]{2,1,0:T(8,128)} %copy-done.12) | copy-start | bytes 2359300
  236.2 8.9 %copy-start.15 = (f32[1,768,256]{2,1,0:T(8,128)S(1)}, f32[1,768,256]{2,1,0:T(8,128)}, u32[]{:S(2)}) copy-start(f32[1,768,256]{2,1,0:T(8,128)} %copy-done.14) | copy-start | bytes 2359300
  (11 other events, 16.0 us)

commit v7 on v6

--- a/solution.py
+++ b/solution.py
@@ -135,6 +135,22 @@
         compiler_params=params(16),
         cost_estimate=cost(),
     )(*tokens)
+
+
+def pass_kernel(value_ref, token_ref, out_ref):
+    del token_ref
+    out_ref[...] = value_ref[...]
+
+
+def passed(value, token):
+    return pl.pallas_call(
+        pass_kernel,
+        out_shape=jax.ShapeDtypeStruct(value.shape, value.dtype),
+        in_specs=[VMEM, ANY],
+        out_specs=VMEM,
+        compiler_params=params(16),
+        cost_estimate=cost(),
+    )(value, token)
 
 
 def integral_kernel(turn, blocks, plan_ref, state_ref, own_ref, token_ref, *refs):
@@ -520,6 +536,7 @@
 
     tasks = []
     late = []
+    tuned = bits == 3 and rounds == 2 and cuts == 2
     for turn in range(rounds):
         groups = [[first] for first in firsts[turn]]
         for cut, peers in enumerate(groups):
@@ -536,27 +553,37 @@
                 times.append(times[-1] + 7)
             for stage in range(bits):
                 times.append(times[-1] + 3 + (wide / 2 if stage == 1 else wide))
+            if tuned and turn > 0 and cut == cuts - 1:
+                times = [70.0, 80.0, 87.0, 95.0, 101.5, 104.0, 120.0, 130.0]
             tasks += [(time, worker.send) for time in times]
             late.append(times)
     for turn in range(1, rounds):
-        begin = 74.0 + 137.0 * (turn - 1)
-        for piece, (send, there) in enumerate(((0, 20), (17, 37), (34, 56), (51, 75))):
+        begin = 0.0 if tuned else 74.0 + 137.0 * (turn - 1)
+        plain = ((0.0, 20.0), (17.0, 37.0), (34.0, 56.0), (51.0, 75.0))
+        ordered = ((79.0, 94.5), (86.0, 101.2), (102.0, 119.7), (102.1, 129.0))
+        for piece, (send, there) in enumerate(ordered if tuned else plain):
             tasks += [(begin + send, send_piece(turn, piece)), (begin + there, gate_piece(turn, piece))]
     for turn in range(rounds):
         steps = [make_tilde(turn), add_terms(turn, True), add_terms(turn, False)]
         if turn == 0 and rounds > 1:
-            tasks += [(time + 1, step_) for time, step_ in zip(late[cuts][-4:-1], steps)]
+            times = [119.5, 121.0, 122.0] if tuned else [time + 1 for time in late[cuts][-4:-1]]
+            tasks += list(zip(times, steps))
         else:
             tasks += [(late[-1][-1] + 6 + index, step_) for index, step_ in enumerate(steps)]
     tasks.sort(key=lambda task: task[0])
-    for _, task in tasks:
+    for _, task in tasks[:-1]:
         token = task(token)
     density = sum(densities)
     for bit in reversed(range(lax.axis_size("pair").bit_length() - 1)):
         half = density.shape[1] // 2
         side = position >> bit & 1
         give = lax.dynamic_slice_in_dim(density, (1 - side) * half, half, 1)
-        density = lax.dynamic_slice_in_dim(density, side * half, half, 1) + swapped(give, "pair", bit)
+        came = swapped(give, "pair", bit)
+        if tasks:
+            came = passed(came, token)
+            token = tasks.pop()[1](token)
+            tasks = []
+        density = lax.dynamic_slice_in_dim(density, side * half, half, 1) + came
     return (gradient, density)
 
 

time: 254 us -> 251 us (0.988)
  waiting for transfers between devices: 119 us -> 112 us
  starting transfers between devices: 47.2 us -> 51.2 us
    ppermute x18, waiting for transfers between devices: 80.1 us -> 69.2 us  [across(): return lax.ppermute(block, ('pair', 'aux'), route)]
    ppermute x13, waiting for transfers between devices: 38.5 us -> 42.7 us  [swapped(): return lax.ppermute(block, axis, route)]
    ppermute x13, starting transfers between devices: 23.8 us -> 27.1 us  [swapped(): return lax.ppermute(block, axis, route)]
    unnamed x56 -> x48, local copies, waits for them, and re-layouts: 17.3 us -> 17.1 us
  transfers between devices with their start and end apart: 31 -> 31, of which waited for: 18 -> 16; matrix products, arithmetic and copies ran while one was open for 1% -> 1% of each run, Pallas kernels for 24% -> 24%
where the time goes in v7:
time: 251 us; the launch traced here: 250 us
  waiting for transfers between devices  112 us (45%)
  Pallas kernels  66.3 us (26%)
  starting transfers between devices  51.2 us (20%)
  local copies, waits for them, and re-layouts  17.5 us (7%)
    ppermute x18, waiting for transfers between devices, across(): return lax.ppermute(block, ('pair', 'aux'), route)  69.2 us
    ppermute x13, waiting for transfers between devices, swapped(): return lax.ppermute(block, axis, route)  42.7 us
    pallas_call x4, Pallas kernels, gradient_terms(): pl.pallas_call(functools.partial(gradient_kernel, len(sources), turn > 0,...  31.6 us
    ppermute x13, starting transfers between devices, swapped(): return lax.ppermute(block, axis, route)  27.1 us
    ppermute x18, starting transfers between devices, across(): return lax.ppermute(block, ('pair', 'aux'), route)  24.1 us
    unnamed x48, local copies, waits for them, and re-layouts  17.1 us
    pallas_call x3, Pallas kernels, integral(): pl.pallas_call(functools.partial(integral_kernel, turn, blocks), out_shap...  15 us
    pallas_call x2, Pallas kernels, tildes(): pl.pallas_call(functools.partial(tilde_kernel, blocks, places), out_shape...  10.1 us
  transfers between devices with their start and end apart: 31, of which 16 were waited for; matrix products, arithmetic and copies ran while one was open for 1% of the time, Pallas kernels for 24%

profile of v7, /device:TPU:0, one launch (start us, length us, event | category | flops | bytes accessed | tf_op | source)
XLA Modules:
  0.0 250.2 jit_solution(15225710877560791076)
XLA Ops:
  2.7 2.8 %copy-done = f32[2,768,1024]{2,1,0:T(8,128)S(1)} copy-done((f32[2,768,1024]{2,1,0:T(8,128)S(1)}, f32[2,768,1024]{2,1,0:T(8,128)}, u32[]{:S(2)}) %copy-start) | copy-done | bytes 6291480
  7.6 2.6 %collective-permute-start = (f32[1,392,1024]{2,1,0:T(8,128)S(1)}, f32[1,392,1024]{2,1,0:T(8,128)S(1)}, u32[]{:S(2)}, u32[]{:S(2)}) collective-permute-start(f32[1,392,1024]{2,1,0:T(8,128)S(1)} %shard_map.59.refs_0_), channel_id=1, source_target_pairs={{0,16},{16,0},{8,24},{24,8},{1,17},{17,1},{9,25},{25,9},{2,18},{18... | collective-permute-start | bytes 4816904 | tf_op jit(solution)/shard_map/ppermute | solution.py:30
  11.3 7.3 %shard_map.61 = (f32[1,384,768]{2,1,0:T(8,128)S(1)}, f32[1,384,768]{2,1,0:T(8,128)S(1)}) custom-call(s32[2,2]{1,0:T(2,128)S(1)} %copy-done.19, s32[4]{0:T(128)S(1)} %pad_add_fusion.state_ref, f32[2,768,1024]{2,1,0:T(8,128)S(1)} %bitcast.7, f32[1,384,1024]{2,1,0:T(8,128)S(1)} %shard_map.60.token_ref, f32[2,768,1024]{2,1,0:T(8,128)} %collective-permute-done.1.refs_0_), custom_call_target="tpu_custom_call" | custom-call | flops 1 | bytes 1 | tf_op jit(solution)/shard_map/pallas_call | solution.py:196
  18.6 2.9 %collective-permute-start.2 = (f32[1,384,768]{2,1,0:T(8,128)S(1)}, f32[1,384,768]{2,1,0:T(8,128)S(1)}, u32[]{:S(2)}, u32[]{:S(2)}) collective-permute-start(f32[1,384,768]{2,1,0:T(8,128)S(1)} %get-tuple-element.32.token_ref), channel_id=1, source_target_pairs={{0,1},{1,0},{2,3},{3,2},{4,5},{5,4},{6,7},{7,6},{8,10},{9,11},{10,... | collective-permute-start | bytes 3538952 | tf_op jit(solution)/shard_map/ppermute | solution.py:44
  21.6 1.5 collective-permute-start.8
  23.1 12.7 %collective-permute-done.2.came_ref = f32[1,384,768]{2,1,0:T(8,128)S(1)} collective-permute-done((f32[1,384,768]{2,1,0:T(8,128)S(1)}, f32[1,384,768]{2,1,0:T(8,128)S(1)}, u32[]{:S(2)}, u32[]{:S(2)}) %collective-permute-start.2) | collective-permute-done | bytes 1179680 | tf_op jit(solution)/shard_map/ppermute | solution.py:44
  35.9 2.2 collective-permute-start.4
  38.1 8.1 %collective-permute-done.refs_0_.theirs_ref = f32[1,392,1024]{2,1,0:T(8,128)S(1)} collective-permute-done((f32[1,392,1024]{2,1,0:T(8,128)S(1)}, f32[1,392,1024]{2,1,0:T(8,128)S(1)}, u32[]{:S(2)}, u32[]{:S(2)}) %collective-permute-start) | collective-permute-done | bytes 1605664 | tf_op jit(solution)/shard_map/ppermute | solution.py:30
  46.2 3.8 %shard_map.63 = (f32[1,384,384]{2,1,0:T(8,128)S(1)}, f32[1,384,384]{2,1,0:T(8,128)S(1)}) custom-call(s32[2,2]{1,0:T(2,128)S(1)} %copy-done.19, s32[4]{0:T(128)S(1)} %pad_add_fusion.state_ref, f32[2,768,1024]{2,1,0:T(8,128)S(1)} %bitcast.7, f32[1,192,768]{2,1,0:T(8,128)S(1)} %get-tuple-element.33.token_ref, ...), custom_call_target="tpu_custom_call" | custom-call | flops 1 | bytes 1 | tf_op jit(solution)/shard_map/pallas_call | solution.py:196
  50.0 2.0 collective-permute-start.3
  52.1 2.7 %collective-permute-start.7 = (f32[1,96,768]{2,1,0:T(8,128)S(1)}, f32[1,96,768]{2,1,0:T(8,128)S(1)}, u32[]{:S(2)}, u32[]{:S(2)}) collective-permute-start(f32[1,96,768]{2,1,0:T(8,128)S(1)} %get-tuple-element.37.token_ref), channel_id=1, source_target_pairs={{0,4},{1,5},{2,6},{3,7},{4,0},{5,1},{6,2},{7,3},{8,12},{9,13},{10,... | collective-permute-start | bytes 884744 | tf_op jit(solution)/shard_map/ppermute | solution.py:44
  54.7 5.2 %collective-permute-done.3.came_ref = f32[1,384,384]{2,1,0:T(8,128)S(1)} collective-permute-done((f32[1,384,384]{2,1,0:T(8,128)S(1)}, f32[1,384,384]{2,1,0:T(8,128)S(1)}, u32[]{:S(2)}, u32[]{:S(2)}) %collective-permute-start.3) | collective-permute-done | bytes 589856 | tf_op jit(solution)/shard_map/ppermute | solution.py:44
  60.0 2.1 collective-permute-start.5
  62.1 4.6 %collective-permute-start.6 = (f32[1,6]{1,0:T(1,128)S(1)}, f32[1,6]{1,0:T(1,128)S(1)}, u32[]{:S(2)}, u32[]{:S(2)}) collective-permute-start(f32[1,6]{1,0:T(1,128)S(1)} %maximum_bitcast_fusion.ours_ref), channel_id=1, source_target_pairs={{0,8},{8,0},{16,24},{24,16},{1,9},{9,1},{17,25},{25,17},{2,10},{10... | collective-permute-start | bytes 80 | tf_op jit(solution)/shard_map/ppermute | solution.py:30
  68.5 3.0 %collective-permute-start.10 = (f32[1,96,384]{2,1,0:T(8,128)S(1)}, f32[1,96,384]{2,1,0:T(8,128)S(1)}, u32[]{:S(2)}, u32[]{:S(2)}) collective-permute-start(f32[1,96,384]{2,1,0:T(8,128)S(1)} %get-tuple-element.41.token_ref), channel_id=1, source_target_pairs={{0,4},{1,5},{2,6},{3,7},{4,0},{5,1},{6,2},{7,3},{8,12},{9,13},{10,... | collective-permute-start | bytes 442376 | tf_op jit(solution)/shard_map/ppermute | solution.py:44
  71.5 8.2 %collective-permute-done.8.refs_0_.refs_1_ = f32[1,384,1024]{2,1,0:T(8,128)S(1)} collective-permute-done((f32[1,384,1024]{2,1,0:T(8,128)S(1)}, f32[1,384,1024]{2,1,0:T(8,128)S(1)}, u32[]{:S(2)}, u32[]{:S(2)}) %collective-permute-start.8) | collective-permute-done | bytes 1572896 | tf_op jit(solution)/shard_map/ppermute | solution.py:30
  79.6 3.8 %shard_map.68 = (f32[1,384,384]{2,1,0:T(8,128)S(1)}, f32[1,384,384]{2,1,0:T(8,128)S(1)}) custom-call(s32[2,2]{1,0:T(2,128)S(1)} %copy-done.19, s32[4]{0:T(128)S(1)} %pad_add_fusion.state_ref, f32[2,768,1024]{2,1,0:T(8,128)S(1)} %bitcast.7, f32[1,96,384]{2,1,0:T(8,128)S(1)} %get-tuple-element.41.token_ref, ...), custom_call_target="tpu_custom_call" | custom-call | flops 1 | bytes 1 | tf_op jit(solution)/shard_map/pallas_call | solution.py:196
  83.5 1.8 collective-permute-start.9
  85.3 5.9 %collective-permute-done.10.right_ref = f32[1,96,384]{2,1,0:T(8,128)S(1)} collective-permute-done((f32[1,96,384]{2,1,0:T(8,128)S(1)}, f32[1,96,384]{2,1,0:T(8,128)S(1)}, u32[]{:S(2)}, u32[]{:S(2)}) %collective-permute-start.10) | collective-permute-done | bytes 147488 | tf_op jit(solution)/shard_map/ppermute | solution.py:44
  92.1 1.6 collective-permute-start.11
  93.6 4.4 %collective-permute-done.11.two_ref = f32[1,96,384]{2,1,0:T(8,128)S(1)} collective-permute-done((f32[1,96,384]{2,1,0:T(8,128)S(1)}, f32[1,96,384]{2,1,0:T(8,128)S(1)}, u32[]{:S(2)}, u32[]{:S(2)}) %collective-permute-start.11) | collective-permute-done | bytes 147488 | tf_op jit(solution)/shard_map/ppermute | solution.py:30
  98.8 4.9 %collective-permute-done.14.two_ref = f32[1,192,768]{2,1,0:T(8,128)S(1)} collective-permute-done((f32[1,192,768]{2,1,0:T(8,128)S(1)}, f32[1,192,768]{2,1,0:T(8,128)S(1)}, u32[]{:S(2)}, u32[]{:S(2)}) %collective-permute-start.14) | collective-permute-done | bytes 589856 | tf_op jit(solution)/shard_map/ppermute | solution.py:44
  106.0 2.3 collective-permute-start.16
  109.0 12.8 %collective-permute-done.13.came_ref = f32[1,192,384]{2,1,0:T(8,128)S(1)} collective-permute-done((f32[1,192,384]{2,1,0:T(8,128)S(1)}, f32[1,192,384]{2,1,0:T(8,128)S(1)}, u32[]{:S(2)}, u32[]{:S(2)}) %collective-permute-start.13) | collective-permute-done | bytes 294944 | tf_op jit(solution)/shard_map/ppermute | solution.py:44
  122.5 9.0 %collective-permute-done.15.right_ref = f32[1,96,384]{2,1,0:T(8,128)S(1)} collective-permute-done((f32[1,96,384]{2,1,0:T(8,128)S(1)}, f32[1,96,384]{2,1,0:T(8,128)S(1)}, u32[]{:S(2)}, u32[]{:S(2)}) %collective-permute-start.15) | collective-permute-done | bytes 147488 | tf_op jit(solution)/shard_map/ppermute | solution.py:44
  132.6 1.6 collective-permute-start.20
  134.7 18.3 %collective-permute-done.20.refs_1_ = f32[1,768,256]{2,1,0:T(8,128)S(1)} collective-permute-done((f32[1,768,256]{2,1,0:T(8,128)S(1)}, f32[1,768,256]{2,1,0:T(8,128)S(1)}, u32[]{:S(2)}, u32[]{:S(2)}) %collective-permute-start.20) | collective-permute-done | bytes 786464 | tf_op jit(solution)/shard_map/ppermute | solution.py:30
  153.0 2.7 %collective-permute-done.18.two_ref = f32[1,96,384]{2,1,0:T(8,128)S(1)} collective-permute-done((f32[1,96,384]{2,1,0:T(8,128)S(1)}, f32[1,96,384]{2,1,0:T(8,128)S(1)}, u32[]{:S(2)}, u32[]{:S(2)}) %collective-permute-start.18) | collective-permute-done | bytes 147488 | tf_op jit(solution)/shard_map/ppermute | solution.py:30
  156.4 1.5 shard_map.84.token_ref
  158.0 1.6 collective-permute-start.24
  159.6 1.5 collective-permute-start.26
  161.1 9.8 %collective-permute-done.21.two_ref = f32[2,96,384]{2,1,0:T(8,128)S(1)} collective-permute-done((f32[2,96,384]{2,1,0:T(8,128)S(1)}, f32[2,96,384]{2,1,0:T(8,128)S(1)}, u32[]{:S(2)}, u32[]{:S(2)}) %collective-permute-start.21) | collective-permute-done | bytes 294944 | tf_op jit(solution)/shard_map/ppermute | solution.py:44
  171.0 3.3 %collective-permute-done.24.two_ref = f32[2,384,384]{2,1,0:T(8,128)S(1)} collective-permute-done((f32[2,384,384]{2,1,0:T(8,128)S(1)}, f32[2,384,384]{2,1,0:T(8,128)S(1)}, u32[]{:S(2)}, u32[]{:S(2)}) %collective-permute-start.24) | collective-permute-done | bytes 1179680 | tf_op jit(solution)/shard_map/ppermute | solution.py:44
  174.4 5.6 %shard_map.88 = (bf16[2,1,1536,768]{3,2,1,0:T(8,128)(2,1)}, f32[96,768]{1,0:T(8,128)S(1)}) custom-call(s32[4]{0:T(128)S(1)} %pad_add_fusion.state_ref, f32[2,768,384]{2,1,0:T(8,128)S(1)} %shard_map.87.token_ref.refs_0_.refs_1_, f32[1,768,768]{2,1,0:T(8,128)S(1)} %shard_map.80.refs_0_, f32[1,768,768]{2,1,0:T(8,128)} %collective-permute-done.25.refs_1_), custom_call_target="tpu_custom_call" | custom-call | flops 1 | bytes 1 | tf_op jit(solution)/shard_map/pallas_call | solution.py:334
  180.1 5.5 %collective-permute-done.23.two_ref = f32[2,192,384]{2,1,0:T(8,128)S(1)} collective-permute-done((f32[2,192,384]{2,1,0:T(8,128)S(1)}, f32[2,192,384]{2,1,0:T(8,128)S(1)}, u32[]{:S(2)}, u32[]{:S(2)}) %collective-permute-start.23) | collective-permute-done | bytes 589856 | tf_op jit(solution)/shard_map/ppermute | solution.py:44
  185.7 1.6 collective-permute-start.27
  187.3 1.5 collective-permute-start.28
  188.8 2.3 copy-done.7
  191.1 7.5 %shard_map.91 = (f32[2,768,1024]{2,1,0:T(8,128)}, f32[8,128]{1,0:T(8,128)S(1)}) custom-call(s32[2,2]{1,0:T(2,128)S(1)} %copy-done.19, s32[4]{0:T(128)S(1)} %pad_add_fusion.state_ref, bf16[2,1,1536,768]{3,2,1,0:T(8,128)(2,1)S(1)} %copy-done.7, f32[2,384,384]{2,1,0:T(8,128)S(1)} %shard_map.90.token_ref.one_ref, f32[2,768,1024]{2,1,0:T(8,128)} %collective-permute-done.1.refs_0_), custom_call_target="tpu_custom_call" | custom-call | flops 1 | bytes 1 | tf_op jit(solution)/shard_map/pallas_call | solution.py:390
  198.6 7.7 %shard_map.92 = (f32[2,768,1024]{2,1,0:T(8,128)}, f32[8,128]{1,0:T(8,128)S(1)}) custom-call(s32[2,2]{1,0:T(2,128)S(1)} %copy-done.19, s32[4]{0:T(128)S(1)} %pad_add_fusion.state_ref, bf16[2,1,1536,768]{3,2,1,0:T(8,128)(2,1)S(1)} %copy-done.7, f32[8,128]{1,0:T(8,128)S(1)} %get-tuple-element.51.token_ref, ...), custom_call_target="tpu_custom_call", output_to_operand_aliasing={{0}: (5, {})} | custom-call | flops 1 | bytes 1 | tf_op jit(solution)/shard_map/pallas_call | solution.py:390
  206.3 1.4 shard_map.94.token_ref.refs_2_.refs_3_
  209.1 1.7 copy-done.2
  210.8 4.5 %shard_map.95 = (bf16[2,1,1536,768]{3,2,1,0:T(8,128)(2,1)}, f32[96,768]{1,0:T(8,128)S(1)}) custom-call(s32[4]{0:T(128)S(1)} %pad_add_fusion.state_ref, f32[2,768,384]{2,1,0:T(8,128)S(1)} %copy-done.2, f32[2,768,384]{2,1,0:T(8,128)S(1)} %shard_map.87.token_ref.refs_0_.refs_1_, f32[2,768,384]{2,1,0:T(8,128)S(1)} %shard_map.87.token_ref.refs_0_.refs_1_, ...), custom_call_target="tpu_custom_call" | custom-call | flops 1 | bytes 1 | tf_op jit(solution)/shard_map/pallas_call | solution.py:334
  217.3 2.3 copy-done.5
  221.1 8.6 %shard_map.96 = (f32[2,768,1024]{2,1,0:T(8,128)}, f32[8,128]{1,0:T(8,128)S(1)}) custom-call(s32[2,2]{1,0:T(2,128)S(1)} %copy-done.19, s32[4]{0:T(128)S(1)} %pad_add_fusion.state_ref, bf16[2,1,1536,768]{3,2,1,0:T(8,128)(2,1)S(1)} %copy-done.5, f32[96,768]{1,0:T(8,128)S(1)} %get-tuple-element.55.token_ref, ...), custom_call_target="tpu_custom_call", output_to_operand_aliasing={{0}: (6, {})} | custom-call | flops 1 | bytes 1 | tf_op jit(solution)/shard_map/pallas_call | solution.py:390
  229.8 9.5 %collective-permute-start.30 = (f32[96,192]{1,0:T(8,128)S(1)}, f32[96,192]{1,0:T(8,128)S(1)}, u32[]{:S(2)}, u32[]{:S(2)}) collective-permute-start(f32[96,192]{1,0:T(8,128)S(1)} %constant_dynamic-slice_fusion), channel_id=1, source_target_pairs={{0,8},{8,0},{16,24},{24,16},{1,9},{9,1},{17,25},{25,17},{2,10},{10... | collective-permute-start | bytes 221192 | tf_op jit(solution)/shard_map/ppermute | solution.py:30
  239.3 2.3 copy-done.6
  241.6 7.8 %shard_map.97 = (f32[2,768,1024]{2,1,0:T(8,128)}, f32[8,128]{1,0:T(8,128)}) custom-call(s32[2,2]{1,0:T(2,128)S(1)} %copy-done.19, s32[4]{0:T(128)S(1)} %pad_add_fusion.state_ref, bf16[2,1,1536,768]{3,2,1,0:T(8,128)(2,1)S(1)} %copy-done.6, f32[8,128]{1,0:T(8,128)S(1)} %get-tuple-element.57.token_ref, ...), custom_call_target="tpu_custom_call", output_to_operand_aliasing={{0}: (8, {})} | custom-call | flops 1 | bytes 1 | tf_op jit(solution)/shard_map/pallas_call | solution.py:390
  (118 shorter events, 20.8 us)
Async XLA Ops:
  0.6 10.6 %collective-permute-start.1 = (f32[2,768,1024]{2,1,0:T(8,128)}, f32[2,768,1024]{2,1,0:T(8,128)}, u32[]{:S(2)}, u32[]{:S(2)}) collective-permute-start(f32[2,768,1024]{2,1,0:T(8,128)} %source_ref.11), channel_id=1, source_target_pairs={{0,8},{8,0},{16,24},{24,16},{1,9},{9,1},{17,25},{25,17},{2,10},{10... | collective-permute-start | bytes 18874376 | tf_op jit(solution)/shard_map/ppermute | solution.py:30
  2.7 2.8 %copy-start = (f32[2,768,1024]{2,1,0:T(8,128)S(1)}, f32[2,768,1024]{2,1,0:T(8,128)}, u32[]{:S(2)}) copy-start(f32[2,768,1024]{2,1,0:T(8,128)} %source_ref.11) | copy-start | bytes 18874372
  6.9 4.4 %slice-start = ((s8[6291456]{0:T(1024)(128)(4,1)}), s8[4194304]{0:T(1024)(128)(4,1)S(1)}, s32[]{:S(2)}) async-start(s8[6291456]{0:T(1024)(128)(4,1)} %bitcast.6), calls=%async_computation | async-start | bytes 8388608
  7.6 3.7 %slice-start.1 = ((s8[6291456]{0:T(1024)(128)(4,1)}), s8[2097152]{0:T(1024)(128)(4,1)S(1)}, s32[]{:S(2)}) async-start(s8[6291456]{0:T(1024)(128)(4,1)} %bitcast.6), calls=%async_computation.1 | async-start | bytes 4194304
  7.6 3.7 %copy-start.19 = (s32[2,2]{1,0:T(2,128)S(1)}, s32[2,2]{1,0:T(2,128)}, u32[]{:S(2)}) copy-start(s32[2,2]{1,0:T(2,128)} %plan_ref.25) | copy-start | bytes 52
  7.6 38.6 %collective-permute-start = (f32[1,392,1024]{2,1,0:T(8,128)S(1)}, f32[1,392,1024]{2,1,0:T(8,128)S(1)}, u32[]{:S(2)}, u32[]{:S(2)}) collective-permute-start(f32[1,392,1024]{2,1,0:T(8,128)S(1)} %shard_map.59.refs_0_), channel_id=1, source_target_pairs={{0,16},{16,0},{8,24},{24,8},{1,17},{17,1},{9,25},{25,9},{2,18},{18... | collective-permute-start | bytes 4816904 | tf_op jit(solution)/shard_map/ppermute | solution.py:30
  18.6 17.1 %collective-permute-start.2 = (f32[1,384,768]{2,1,0:T(8,128)S(1)}, f32[1,384,768]{2,1,0:T(8,128)S(1)}, u32[]{:S(2)}, u32[]{:S(2)}) collective-permute-start(f32[1,384,768]{2,1,0:T(8,128)S(1)} %get-tuple-element.32.token_ref), channel_id=1, source_target_pairs={{0,1},{1,0},{2,3},{3,2},{4,5},{5,4},{6,7},{7,6},{8,10},{9,11},{10,... | collective-permute-start | bytes 3538952 | tf_op jit(solution)/shard_map/ppermute | solution.py:44
  21.6 58.1 %collective-permute-start.8 = (f32[1,384,1024]{2,1,0:T(8,128)S(1)}, f32[1,384,1024]{2,1,0:T(8,128)S(1)}, u32[]{:S(2)}, u32[]{:S(2)}) collective-permute-start(f32[1,384,1024]{2,1,0:T(8,128)S(1)} %shard_map.60.token_ref), channel_id=1, source_target_pairs={{0,16},{16,0},{8,24},{24,8},{1,17},{17,1},{9,25},{25,9},{2,18},{18... | collective-permute-start | bytes 4718600 | tf_op jit(solution)/shard_map/ppermute | solution.py:30
  35.9 16.1 %collective-permute-start.4 = (f32[1,192,768]{2,1,0:T(8,128)S(1)}, f32[1,192,768]{2,1,0:T(8,128)S(1)}, u32[]{:S(2)}, u32[]{:S(2)}) collective-permute-start(f32[1,192,768]{2,1,0:T(8,128)S(1)} %get-tuple-element.33.token_ref), channel_id=1, source_target_pairs={{0,2},{1,3},{2,0},{3,1},{4,6},{5,7},{6,4},{7,5},{8,9},{9,8},{10,11... | collective-permute-start | bytes 1769480 | tf_op jit(solution)/shard_map/ppermute | solution.py:44
  46.2 85.4 %copy-start.3 = (f32[1,392,1024]{2,1,0:T(8,128)}, f32[1,392,1024]{2,1,0:T(8,128)S(1)}, u32[]{:S(2)}) copy-start(f32[1,392,1024]{2,1,0:T(8,128)S(1)} %collective-permute-done.refs_0_.theirs_ref) | copy-start | bytes 4816900
  50.0 9.9 %collective-permute-start.3 = (f32[1,384,384]{2,1,0:T(8,128)S(1)}, f32[1,384,384]{2,1,0:T(8,128)S(1)}, u32[]{:S(2)}, u32[]{:S(2)}) collective-permute-start(f32[1,384,384]{2,1,0:T(8,128)S(1)} %get-tuple-element.35.token_ref), channel_id=1, source_target_pairs={{0,1},{1,0},{2,3},{3,2},{4,5},{5,4},{6,7},{7,6},{8,10},{9,11},{10,... | collective-permute-start | bytes 1769480 | tf_op jit(solution)/shard_map/ppermute | solution.py:44
  52.0 14.7 %copy-start.21 = (f32[768]{0:T(1024)S(1)}, f32[768]{0:T(1024)}, u32[]{:S(2)}) copy-start(f32[768]{0:T(1024)} %refs_1_.1) | copy-start | bytes 9220
  52.1 15.5 %collective-permute-start.7 = (f32[1,96,768]{2,1,0:T(8,128)S(1)}, f32[1,96,768]{2,1,0:T(8,128)S(1)}, u32[]{:S(2)}, u32[]{:S(2)}) collective-permute-start(f32[1,96,768]{2,1,0:T(8,128)S(1)} %get-tuple-element.37.token_ref), channel_id=1, source_target_pairs={{0,4},{1,5},{2,6},{3,7},{4,0},{5,1},{6,2},{7,3},{8,12},{9,13},{10,... | collective-permute-start | bytes 884744 | tf_op jit(solution)/shard_map/ppermute | solution.py:44
  60.0 8.4 %collective-permute-start.5 = (f32[1,192,384]{2,1,0:T(8,128)S(1)}, f32[1,192,384]{2,1,0:T(8,128)S(1)}, u32[]{:S(2)}, u32[]{:S(2)}) collective-permute-start(f32[1,192,384]{2,1,0:T(8,128)S(1)} %get-tuple-element.39.token_ref), channel_id=1, source_target_pairs={{0,2},{1,3},{2,0},{3,1},{4,6},{5,7},{6,4},{7,5},{8,9},{9,8},{10,11... | collective-permute-start | bytes 884744 | tf_op jit(solution)/shard_map/ppermute | solution.py:44
  62.1 5.5 %collective-permute-start.6 = (f32[1,6]{1,0:T(1,128)S(1)}, f32[1,6]{1,0:T(1,128)S(1)}, u32[]{:S(2)}, u32[]{:S(2)}) collective-permute-start(f32[1,6]{1,0:T(1,128)S(1)} %maximum_bitcast_fusion.ours_ref), channel_id=1, source_target_pairs={{0,8},{8,0},{16,24},{24,16},{1,9},{9,1},{17,25},{25,17},{2,10},{10... | collective-permute-start | bytes 80 | tf_op jit(solution)/shard_map/ppermute | solution.py:30
  68.4 23.6 %collective-permute-start.12 = (f32[1,96,768]{2,1,0:T(8,128)S(1)}, f32[1,96,768]{2,1,0:T(8,128)S(1)}, u32[]{:S(2)}, u32[]{:S(2)}) collective-permute-start(f32[1,96,768]{2,1,0:T(8,128)S(1)} %shard_map.66.token_ref.one_ref), channel_id=1, source_target_pairs={{0,4},{1,5},{2,6},{3,7},{4,0},{5,1},{6,2},{7,3},{8,12},{9,13},{10,... | collective-permute-start | bytes 884744 | tf_op jit(solution)/shard_map/ppermute | solution.py:44
  68.5 22.6 %collective-permute-start.10 = (f32[1,96,384]{2,1,0:T(8,128)S(1)}, f32[1,96,384]{2,1,0:T(8,128)S(1)}, u32[]{:S(2)}, u32[]{:S(2)}) collective-permute-start(f32[1,96,384]{2,1,0:T(8,128)S(1)} %get-tuple-element.41.token_ref), channel_id=1, source_target_pairs={{0,4},{1,5},{2,6},{3,7},{4,0},{5,1},{6,2},{7,3},{8,12},{9,13},{10,... | collective-permute-start | bytes 442376 | tf_op jit(solution)/shard_map/ppermute | solution.py:44
  79.6 3.8 %copy-start.8 = (f32[1,384,1024]{2,1,0:T(8,128)}, f32[1,384,1024]{2,1,0:T(8,128)S(1)}, u32[]{:S(2)}) copy-start(f32[1,384,1024]{2,1,0:T(8,128)S(1)} %collective-permute-done.8.refs_0_.refs_1_) | copy-start | bytes 4718596
  83.5 15.2 %collective-permute-start.9 = (f32[1,384,384]{2,1,0:T(8,128)S(1)}, f32[1,384,384]{2,1,0:T(8,128)S(1)}, u32[]{:S(2)}, u32[]{:S(2)}) collective-permute-start(f32[1,384,384]{2,1,0:T(8,128)S(1)} %get-tuple-element.43.token_ref), channel_id=1, source_target_pairs={{0,1},{1,0},{2,3},{3,2},{4,5},{5,4},{6,7},{7,6},{8,10},{9,11},{10,... | collective-permute-start | bytes 1769480 | tf_op jit(solution)/shard_map/ppermute | solution.py:44
  92.0 11.7 %collective-permute-start.14 = (f32[1,192,768]{2,1,0:T(8,128)S(1)}, f32[1,192,768]{2,1,0:T(8,128)S(1)}, u32[]{:S(2)}, u32[]{:S(2)}) collective-permute-start(f32[1,192,768]{2,1,0:T(8,128)S(1)} %shard_map.70.token_ref.one_ref), channel_id=1, source_target_pairs={{0,2},{1,3},{2,0},{3,1},{4,6},{5,7},{6,4},{7,5},{8,9},{9,8},{10,11... | collective-permute-start | bytes 1769480 | tf_op jit(solution)/shard_map/ppermute | solution.py:44
  92.1 6.0 %collective-permute-start.11 = (f32[1,96,384]{2,1,0:T(8,128)S(1)}, f32[1,96,384]{2,1,0:T(8,128)S(1)}, u32[]{:S(2)}, u32[]{:S(2)}) collective-permute-start(f32[1,96,384]{2,1,0:T(8,128)S(1)} %shard_map.69.token_ref.one_ref), channel_id=1, source_target_pairs={{0,16},{16,0},{8,24},{24,8},{1,17},{17,1},{9,25},{25,9},{2,18},{18... | collective-permute-start | bytes 442376 | tf_op jit(solution)/shard_map/ppermute | solution.py:30
  103.8 28.6 %collective-permute-start.19 = (f32[1,384,768]{2,1,0:T(8,128)S(1)}, f32[1,384,768]{2,1,0:T(8,128)S(1)}, u32[]{:S(2)}, u32[]{:S(2)}) collective-permute-start(f32[1,384,768]{2,1,0:T(8,128)S(1)} %shard_map.74.refs_0_.one_ref), channel_id=1, source_target_pairs={{0,1},{1,0},{2,3},{3,2},{4,5},{5,4},{6,7},{7,6},{8,10},{9,11},{10,... | collective-permute-start | bytes 3538952 | tf_op jit(solution)/shard_map/ppermute | solution.py:44
  105.1 17.4 %collective-permute-start.17 = (f32[1,768,256]{2,1,0:T(8,128)S(1)}, f32[1,768,256]{2,1,0:T(8,128)S(1)}, u32[]{:S(2)}, u32[]{:S(2)}) collective-permute-start(f32[1,768,256]{2,1,0:T(8,128)S(1)} %shard_map.72.token_ref), channel_id=1, source_target_pairs={{0,16},{16,0},{8,24},{24,8},{1,17},{17,1},{9,25},{25,9},{2,18},{18... | collective-permute-start | bytes 2359304 | tf_op jit(solution)/shard_map/ppermute | solution.py:30
  106.0 15.8 %collective-permute-start.13 = (f32[1,192,384]{2,1,0:T(8,128)S(1)}, f32[1,192,384]{2,1,0:T(8,128)S(1)}, u32[]{:S(2)}, u32[]{:S(2)}) collective-permute-start(f32[1,192,384]{2,1,0:T(8,128)S(1)} %get-tuple-element.46.token_ref), channel_id=1, source_target_pairs={{0,2},{1,3},{2,0},{3,1},{4,6},{5,7},{6,4},{7,5},{8,9},{9,8},{10,11... | collective-permute-start | bytes 884744 | tf_op jit(solution)/shard_map/ppermute | solution.py:44
  106.0 16.4 %collective-permute-start.16 = (f32[2,96,384]{2,1,0:T(8,128)S(1)}, f32[2,96,384]{2,1,0:T(8,128)S(1)}, u32[]{:S(2)}, u32[]{:S(2)}) collective-permute-start(f32[2,96,384]{2,1,0:T(8,128)S(1)} %shard_map.71.refs_0_.one_ref), channel_id=1, source_target_pairs={{0,4},{1,5},{2,6},{3,7},{4,0},{5,1},{6,2},{7,3},{8,12},{9,13},{10,... | collective-permute-start | bytes 884744 | tf_op jit(solution)/shard_map/ppermute | solution.py:44
  121.8 9.7 %collective-permute-start.15 = (f32[1,96,384]{2,1,0:T(8,128)S(1)}, f32[1,96,384]{2,1,0:T(8,128)S(1)}, u32[]{:S(2)}, u32[]{:S(2)}) collective-permute-start(f32[1,96,384]{2,1,0:T(8,128)S(1)} %get-tuple-element.48.token_ref), channel_id=1, source_target_pairs={{0,4},{1,5},{2,6},{3,7},{4,0},{5,1},{6,2},{7,3},{8,12},{9,13},{10,... | collective-permute-start | bytes 442376 | tf_op jit(solution)/shard_map/ppermute | solution.py:44
  122.5 9.9 %copy-start.10 = (f32[1,768,256]{2,1,0:T(8,128)}, f32[1,768,256]{2,1,0:T(8,128)S(1)}, u32[]{:S(2)}) copy-start(f32[1,768,256]{2,1,0:T(8,128)S(1)} %collective-permute-done.17.refs_1_.refs_0_) | copy-start | bytes 2359300
  132.5 41.9 %collective-permute-start.25 = (f32[1,768,768]{2,1,0:T(8,128)S(1)}, f32[1,768,768]{2,1,0:T(8,128)}, u32[]{:S(2)}, u32[]{:S(2)}) collective-permute-start(f32[1,768,768]{2,1,0:T(8,128)S(1)} %shard_map.80.refs_0_), channel_id=1, source_target_pairs={{0,8},{8,0},{16,24},{24,16},{1,9},{9,1},{17,25},{25,17},{2,10},{10... | collective-permute-start | bytes 7077896 | tf_op jit(solution)/shard_map/ppermute | solution.py:30
  132.6 20.4 %collective-permute-start.20 = (f32[1,768,256]{2,1,0:T(8,128)S(1)}, f32[1,768,256]{2,1,0:T(8,128)S(1)}, u32[]{:S(2)}, u32[]{:S(2)}) collective-permute-start(f32[1,768,256]{2,1,0:T(8,128)S(1)} %shard_map.75.token_ref), channel_id=1, source_target_pairs={{0,16},{16,0},{8,24},{24,8},{1,17},{17,1},{9,25},{25,9},{2,18},{18... | collective-permute-start | bytes 2359304 | tf_op jit(solution)/shard_map/ppermute | solution.py:30
  134.2 23.7 %collective-permute-start.22 = (f32[2,192,384]{2,1,0:T(8,128)S(1)}, f32[2,192,384]{2,1,0:T(8,128)S(1)}, u32[]{:S(2)}, u32[]{:S(2)}) collective-permute-start(f32[2,192,384]{2,1,0:T(8,128)S(1)} %shard_map.77.refs_0_.one_ref), channel_id=1, source_target_pairs={{0,2},{1,3},{2,0},{3,1},{4,6},{5,7},{6,4},{7,5},{8,9},{9,8},{10,11... | collective-permute-start | bytes 1769480 | tf_op jit(solution)/shard_map/ppermute | solution.py:44
  134.2 21.5 %collective-permute-start.18 = (f32[1,96,384]{2,1,0:T(8,128)S(1)}, f32[1,96,384]{2,1,0:T(8,128)S(1)}, u32[]{:S(2)}, u32[]{:S(2)}) collective-permute-start(f32[1,96,384]{2,1,0:T(8,128)S(1)} %shard_map.79.token_ref.one_ref), channel_id=1, source_target_pairs={{0,16},{16,0},{8,24},{24,8},{1,17},{17,1},{9,25},{25,9},{2,18},{18... | collective-permute-start | bytes 442376 | tf_op jit(solution)/shard_map/ppermute | solution.py:30
  153.0 2.7 %copy-start.12 = (f32[1,768,256]{2,1,0:T(8,128)}, f32[1,768,256]{2,1,0:T(8,128)S(1)}, u32[]{:S(2)}) copy-start(f32[1,768,256]{2,1,0:T(8,128)S(1)} %collective-permute-done.20.refs_1_) | copy-start | bytes 2359300
  158.0 16.3 %collective-permute-start.24 = (f32[2,384,384]{2,1,0:T(8,128)S(1)}, f32[2,384,384]{2,1,0:T(8,128)S(1)}, u32[]{:S(2)}, u32[]{:S(2)}) collective-permute-start(f32[2,384,384]{2,1,0:T(8,128)S(1)} %shard_map.85.token_ref.one_ref), channel_id=1, source_target_pairs={{0,1},{1,0},{2,3},{3,2},{4,5},{5,4},{6,7},{7,6},{8,10},{9,11},{10,... | collective-permute-start | bytes 3538952 | tf_op jit(solution)/shard_map/ppermute | solution.py:44
  159.6 11.3 %collective-permute-start.21 = (f32[2,96,384]{2,1,0:T(8,128)S(1)}, f32[2,96,384]{2,1,0:T(8,128)S(1)}, u32[]{:S(2)}, u32[]{:S(2)}) collective-permute-start(f32[2,96,384]{2,1,0:T(8,128)S(1)} %shard_map.82.refs_0_.one_ref), channel_id=1, source_target_pairs={{0,4},{1,5},{2,6},{3,7},{4,0},{5,1},{6,2},{7,3},{8,12},{9,13},{10,... | collective-permute-start | bytes 884744 | tf_op jit(solution)/shard_map/ppermute | solution.py:44
  159.6 20.5 %collective-permute-start.26 = (f32[1,768,256]{2,1,0:T(8,128)S(1)}, f32[1,768,256]{2,1,0:T(8,128)S(1)}, u32[]{:S(2)}, u32[]{:S(2)}) collective-permute-start(f32[1,768,256]{2,1,0:T(8,128)S(1)} %shard_map.83.refs_0_), channel_id=1, source_target_pairs={{0,16},{16,0},{8,24},{24,8},{1,17},{17,1},{9,25},{25,9},{2,18},{18... | collective-permute-start | bytes 2359304 | tf_op jit(solution)/shard_map/ppermute | solution.py:30
  170.9 14.7 %collective-permute-start.23 = (f32[2,192,384]{2,1,0:T(8,128)S(1)}, f32[2,192,384]{2,1,0:T(8,128)S(1)}, u32[]{:S(2)}, u32[]{:S(2)}) collective-permute-start(f32[2,192,384]{2,1,0:T(8,128)S(1)} %shard_map.86.token_ref.one_ref), channel_id=1, source_target_pairs={{0,2},{1,3},{2,0},{3,1},{4,6},{5,7},{6,4},{7,5},{8,9},{9,8},{10,11... | collective-permute-start | bytes 1769480 | tf_op jit(solution)/shard_map/ppermute | solution.py:44
  180.1 5.6 %copy-start.16 = (f32[96,768]{1,0:T(8,128)}, f32[96,768]{1,0:T(8,128)S(1)}, u32[]{:S(2)}) copy-start(f32[96,768]{1,0:T(8,128)S(1)} %get-tuple-element.49.refs_0_) | copy-start | bytes 884740
  180.1 5.6 %copy-start.14 = (f32[1,768,256]{2,1,0:T(8,128)}, f32[1,768,256]{2,1,0:T(8,128)S(1)}, u32[]{:S(2)}) copy-start(f32[1,768,256]{2,1,0:T(8,128)S(1)} %collective-permute-done.26.refs_1_.refs_2_) | copy-start | bytes 2359300
  185.7 20.6 %collective-permute-start.27 = (f32[2,384,384]{2,1,0:T(8,128)S(1)}, f32[2,384,384]{2,1,0:T(8,128)}, u32[]{:S(2)}, u32[]{:S(2)}) collective-permute-start(f32[2,384,384]{2,1,0:T(8,128)S(1)} %shard_map.90.token_ref.one_ref), channel_id=1, source_target_pairs={{0,1},{1,0},{2,3},{3,2},{4,5},{5,4},{6,7},{7,6},{8,10},{9,11},{10,... | collective-permute-start | bytes 3538952 | tf_op jit(solution)/shard_map/ppermute | solution.py:44
  187.3 19.0 %collective-permute-start.28 = (f32[1,768,256]{2,1,0:T(8,128)}, f32[1,768,256]{2,1,0:T(8,128)}, u32[]{:S(2)}, u32[]{:S(2)}) collective-permute-start(f32[1,768,256]{2,1,0:T(8,128)} %shard_map.84.token_ref), channel_id=1, source_target_pairs={{0,16},{16,0},{8,24},{24,8},{1,17},{17,1},{9,25},{25,9},{2,18},{18... | collective-permute-start | bytes 2359304 | tf_op jit(solution)/shard_map/ppermute | solution.py:30
  188.8 2.3 copy-start.7
  210.8 4.5 %copy-start.17 = (f32[96,768]{1,0:T(8,128)S(1)}, f32[96,768]{1,0:T(8,128)}, u32[]{:S(2)}) copy-start(f32[96,768]{1,0:T(8,128)} %copy-done.16) | copy-start | bytes 884740
  215.3 14.4 %collective-permute-start.29 = (f32[96,384]{1,0:T(8,128)S(1)}, f32[96,384]{1,0:T(8,128)S(1)}, u32[]{:S(2)}, u32[]{:S(2)}) collective-permute-start(f32[96,384]{1,0:T(8,128)S(1)} %constant_dynamic-slice_fusion.1), channel_id=1, source_target_pairs={{0,16},{16,0},{8,24},{24,8},{1,17},{17,1},{9,25},{25,9},{2,18},{18... | collective-permute-start | bytes 442376 | tf_op jit(solution)/shard_map/ppermute | solution.py:30
  221.1 18.2 %copy-start.11 = (f32[1,768,256]{2,1,0:T(8,128)S(1)}, f32[1,768,256]{2,1,0:T(8,128)}, u32[]{:S(2)}) copy-start(f32[1,768,256]{2,1,0:T(8,128)} %copy-done.10) | copy-start | bytes 2359300
  221.1 18.2 %copy-start.13 = (f32[1,768,256]{2,1,0:T(8,128)S(1)}, f32[1,768,256]{2,1,0:T(8,128)}, u32[]{:S(2)}) copy-start(f32[1,768,256]{2,1,0:T(8,128)} %copy-done.12) | copy-start | bytes 2359300
  221.1 18.2 %copy-start.15 = (f32[1,768,256]{2,1,0:T(8,128)S(1)}, f32[1,768,256]{2,1,0:T(8,128)}, u32[]{:S(2)}) copy-start(f32[1,768,256]{2,1,0:T(8,128)} %copy-done.14) | copy-start | bytes 2359300
  229.8 19.6 %collective-permute-start.30 = (f32[96,192]{1,0:T(8,128)S(1)}, f32[96,192]{1,0:T(8,128)S(1)}, u32[]{:S(2)}, u32[]{:S(2)}) collective-permute-start(f32[96,192]{1,0:T(8,128)S(1)} %constant_dynamic-slice_fusion), channel_id=1, source_target_pairs={{0,8},{8,0},{16,24},{24,16},{1,9},{9,1},{17,25},{25,17},{2,10},{10... | collective-permute-start | bytes 221192 | tf_op jit(solution)/shard_map/ppermute | solution.py:30
  239.3 2.3 copy-start.6
  (7 other events, 9.6 us)

commit v8 on v7

--- a/solution.py
+++ b/solution.py
@@ -554,13 +554,17 @@
             for stage in range(bits):
                 times.append(times[-1] + 3 + (wide / 2 if stage == 1 else wide))
             if tuned and turn > 0 and cut == cuts - 1:
-                times = [70.0, 80.0, 87.0, 95.0, 101.5, 104.0, 120.0, 130.0]
+                times = [70.0, 80.0, 84.0, 95.0, 101.5, 104.0, 120.0, 130.0]
+            elif tuned and turn == 0:
+                times[-1] = 104.2
+            elif tuned:
+                times[-1] = 120.2
             tasks += [(time, worker.send) for time in times]
             late.append(times)
     for turn in range(1, rounds):
         begin = 0.0 if tuned else 74.0 + 137.0 * (turn - 1)
         plain = ((0.0, 20.0), (17.0, 37.0), (34.0, 56.0), (51.0, 75.0))
-        ordered = ((79.0, 94.5), (86.0, 101.2), (102.0, 119.7), (102.1, 129.0))
+        ordered = ((79.0, 101.1), (102.0, 119.7), (104.5, 129.0), (120.5, 136.5))
         for piece, (send, there) in enumerate(ordered if tuned else plain):
             tasks += [(begin + send, send_piece(turn, piece)), (begin + there, gate_piece(turn, piece))]
     for turn in range(rounds):

time: 251 us -> 248 us (0.988)
  waiting for transfers between devices: 112 us -> 107 us
  local copies, waits for them, and re-layouts: 17.5 us -> 22 us
  starting transfers between devices: 51.2 us -> 48.2 us
    ppermute x18, waiting for transfers between devices: 69.2 us -> 64.6 us  [across(): return lax.ppermute(block, ('pair', 'aux'), route)]
    unnamed x48 -> x56, local copies, waits for them, and re-layouts: 17.1 us -> 21.6 us
  transfers between devices with their start and end apart: 31 -> 31, of which waited for: 16 -> 17; matrix products, arithmetic and copies ran while one was open for 1% -> 1% of each run, Pallas kernels for 24% -> 26%
where the time goes in v8:
time: 248 us
  waiting for transfers between devices  107 us (43%)
  Pallas kernels  67.5 us (27%)
  starting transfers between devices  48.2 us (19%)
  local copies, waits for them, and re-layouts  22 us (9%)
    ppermute x18, waiting for transfers between devices, across(): return lax.ppermute(block, ('pair', 'aux'), route)  64.6 us
    ppermute x13, waiting for transfers between devices, swapped(): return lax.ppermute(block, axis, route)  41.9 us
    pallas_call x4, Pallas kernels, gradient_terms(): pl.pallas_call(functools.partial(gradient_kernel, len(sources), turn > 0,...  31.7 us
    ppermute x13, starting transfers between devices, swapped(): return lax.ppermute(block, axis, route)  24.7 us
    ppermute x18, starting transfers between devices, across(): return lax.ppermute(block, ('pair', 'aux'), route)  23.5 us
    unnamed x56, local copies, waits for them, and re-layouts  21.6 us
    pallas_call x3, Pallas kernels, integral(): pl.pallas_call(functools.partial(integral_kernel, turn, blocks), out_shap...  15 us
    pallas_call x2, Pallas kernels, tildes(): pl.pallas_call(functools.partial(tilde_kernel, blocks, places), out_shape...  8.96 us
  transfers between devices with their start and end apart: 31, of which 17 were waited for; matrix products, arithmetic and copies ran while one was open for 1% of the time, Pallas kernels for 26%

profile of v8, /device:TPU:0, one launch (start us, length us, event | category | flops | bytes accessed | tf_op | source)
XLA Modules:
  0.0 247.6 jit_solution(6768040802355837062)
XLA Ops:
  2.7 2.8 %copy-done = f32[2,768,1024]{2,1,0:T(8,128)S(1)} copy-done((f32[2,768,1024]{2,1,0:T(8,128)S(1)}, f32[2,768,1024]{2,1,0:T(8,128)}, u32[]{:S(2)}) %copy-start) | copy-done | bytes 6291480
  7.6 2.6 %collective-permute-start = (f32[1,392,1024]{2,1,0:T(8,128)S(1)}, f32[1,392,1024]{2,1,0:T(8,128)S(1)}, u32[]{:S(2)}, u32[]{:S(2)}) collective-permute-start(f32[1,392,1024]{2,1,0:T(8,128)S(1)} %shard_map.59.refs_0_), channel_id=1, source_target_pairs={{0,16},{16,0},{8,24},{24,8},{1,17},{17,1},{9,25},{25,9},{2,18},{18... | collective-permute-start | bytes 4816904 | tf_op jit(solution)/shard_map/ppermute | solution.py:30
  11.3 7.3 %shard_map.61 = (f32[1,384,768]{2,1,0:T(8,128)S(1)}, f32[1,384,768]{2,1,0:T(8,128)S(1)}) custom-call(s32[2,2]{1,0:T(2,128)S(1)} %copy-done.21, s32[4]{0:T(128)S(1)} %pad_add_fusion.state_ref, f32[2,768,1024]{2,1,0:T(8,128)S(1)} %bitcast.7, f32[1,384,1024]{2,1,0:T(8,128)S(1)} %shard_map.60.token_ref, f32[2,768,1024]{2,1,0:T(8,128)} %collective-permute-done.1.refs_0_), custom_call_target="tpu_custom_call" | custom-call | flops 1 | bytes 1 | tf_op jit(solution)/shard_map/pallas_call | solution.py:196
  18.6 2.9 %collective-permute-start.2 = (f32[1,384,768]{2,1,0:T(8,128)S(1)}, f32[1,384,768]{2,1,0:T(8,128)S(1)}, u32[]{:S(2)}, u32[]{:S(2)}) collective-permute-start(f32[1,384,768]{2,1,0:T(8,128)S(1)} %get-tuple-element.32.token_ref), channel_id=1, source_target_pairs={{0,1},{1,0},{2,3},{3,2},{4,5},{5,4},{6,7},{7,6},{8,10},{9,11},{10,... | collective-permute-start | bytes 3538952 | tf_op jit(solution)/shard_map/ppermute | solution.py:44
  21.6 1.5 collective-permute-start.8
  23.1 12.7 %collective-permute-done.2.came_ref = f32[1,384,768]{2,1,0:T(8,128)S(1)} collective-permute-done((f32[1,384,768]{2,1,0:T(8,128)S(1)}, f32[1,384,768]{2,1,0:T(8,128)S(1)}, u32[]{:S(2)}, u32[]{:S(2)}) %collective-permute-start.2) | collective-permute-done | bytes 1179680 | tf_op jit(solution)/shard_map/ppermute | solution.py:44
  35.9 2.2 collective-permute-start.4
  38.1 8.1 %collective-permute-done.refs_0_.theirs_ref = f32[1,392,1024]{2,1,0:T(8,128)S(1)} collective-permute-done((f32[1,392,1024]{2,1,0:T(8,128)S(1)}, f32[1,392,1024]{2,1,0:T(8,128)S(1)}, u32[]{:S(2)}, u32[]{:S(2)}) %collective-permute-start) | collective-permute-done | bytes 1605664 | tf_op jit(solution)/shard_map/ppermute | solution.py:30
  46.2 3.8 %shard_map.63 = (f32[1,384,384]{2,1,0:T(8,128)S(1)}, f32[1,384,384]{2,1,0:T(8,128)S(1)}) custom-call(s32[2,2]{1,0:T(2,128)S(1)} %copy-done.21, s32[4]{0:T(128)S(1)} %pad_add_fusion.state_ref, f32[2,768,1024]{2,1,0:T(8,128)S(1)} %bitcast.7, f32[1,192,768]{2,1,0:T(8,128)S(1)} %get-tuple-element.33.token_ref, ...), custom_call_target="tpu_custom_call" | custom-call | flops 1 | bytes 1 | tf_op jit(solution)/shard_map/pallas_call | solution.py:196
  50.0 2.0 collective-permute-start.3
  52.1 2.7 %collective-permute-start.7 = (f32[1,96,768]{2,1,0:T(8,128)S(1)}, f32[1,96,768]{2,1,0:T(8,128)S(1)}, u32[]{:S(2)}, u32[]{:S(2)}) collective-permute-start(f32[1,96,768]{2,1,0:T(8,128)S(1)} %get-tuple-element.37.token_ref), channel_id=1, source_target_pairs={{0,4},{1,5},{2,6},{3,7},{4,0},{5,1},{6,2},{7,3},{8,12},{9,13},{10,... | collective-permute-start | bytes 884744 | tf_op jit(solution)/shard_map/ppermute | solution.py:44
  54.7 5.2 %collective-permute-done.3.came_ref = f32[1,384,384]{2,1,0:T(8,128)S(1)} collective-permute-done((f32[1,384,384]{2,1,0:T(8,128)S(1)}, f32[1,384,384]{2,1,0:T(8,128)S(1)}, u32[]{:S(2)}, u32[]{:S(2)}) %collective-permute-start.3) | collective-permute-done | bytes 589856 | tf_op jit(solution)/shard_map/ppermute | solution.py:44
  60.0 2.1 collective-permute-start.5
  62.1 4.6 %collective-permute-start.6 = (f32[1,6]{1,0:T(1,128)S(1)}, f32[1,6]{1,0:T(1,128)S(1)}, u32[]{:S(2)}, u32[]{:S(2)}) collective-permute-start(f32[1,6]{1,0:T(1,128)S(1)} %maximum_bitcast_fusion.ours_ref), channel_id=1, source_target_pairs={{0,8},{8,0},{16,24},{24,16},{1,9},{9,1},{17,25},{25,17},{2,10},{10... | collective-permute-start | bytes 80 | tf_op jit(solution)/shard_map/ppermute | solution.py:30
  68.4 11.2 %collective-permute-done.8.refs_0_.refs_1_ = f32[1,384,1024]{2,1,0:T(8,128)S(1)} collective-permute-done((f32[1,384,1024]{2,1,0:T(8,128)S(1)}, f32[1,384,1024]{2,1,0:T(8,128)S(1)}, u32[]{:S(2)}, u32[]{:S(2)}) %collective-permute-start.8) | collective-permute-done | bytes 1572896 | tf_op jit(solution)/shard_map/ppermute | solution.py:30
  79.6 3.8 %shard_map.68 = (f32[1,384,384]{2,1,0:T(8,128)S(1)}, f32[1,384,384]{2,1,0:T(8,128)S(1)}) custom-call(s32[2,2]{1,0:T(2,128)S(1)} %copy-done.21, s32[4]{0:T(128)S(1)} %pad_add_fusion.state_ref, f32[2,768,1024]{2,1,0:T(8,128)S(1)} %bitcast.7, f32[1,96,384]{2,1,0:T(8,128)S(1)} %get-tuple-element.41.token_ref, ...), custom_call_target="tpu_custom_call" | custom-call | flops 1 | bytes 1 | tf_op jit(solution)/shard_map/pallas_call | solution.py:196
  83.5 1.8 collective-permute-start.9
  85.3 2.6 %collective-permute-start.12 = (f32[1,96,768]{2,1,0:T(8,128)S(1)}, f32[1,96,768]{2,1,0:T(8,128)S(1)}, u32[]{:S(2)}, u32[]{:S(2)}) collective-permute-start(f32[1,96,768]{2,1,0:T(8,128)S(1)} %shard_map.66.token_ref.one_ref), channel_id=1, source_target_pairs={{0,4},{1,5},{2,6},{3,7},{4,0},{5,1},{6,2},{7,3},{8,12},{9,13},{10,... | collective-permute-start | bytes 884744 | tf_op jit(solution)/shard_map/ppermute | solution.py:44
  88.2 19.0 %collective-permute-done.10.right_ref = f32[1,96,384]{2,1,0:T(8,128)S(1)} collective-permute-done((f32[1,96,384]{2,1,0:T(8,128)S(1)}, f32[1,96,384]{2,1,0:T(8,128)S(1)}, u32[]{:S(2)}, u32[]{:S(2)}) %collective-permute-start.10) | collective-permute-done | bytes 147488 | tf_op jit(solution)/shard_map/ppermute | solution.py:44
  108.2 1.6 collective-permute-start.11
  109.8 5.2 %collective-permute-done.11.two_ref = f32[1,96,384]{2,1,0:T(8,128)S(1)} collective-permute-done((f32[1,96,384]{2,1,0:T(8,128)S(1)}, f32[1,96,384]{2,1,0:T(8,128)S(1)}, u32[]{:S(2)}, u32[]{:S(2)}) %collective-permute-start.11) | collective-permute-done | bytes 147488 | tf_op jit(solution)/shard_map/ppermute | solution.py:30
  116.1 6.3 %collective-permute-done.13.came_ref = f32[1,192,384]{2,1,0:T(8,128)S(1)} collective-permute-done((f32[1,192,384]{2,1,0:T(8,128)S(1)}, f32[1,192,384]{2,1,0:T(8,128)S(1)}, u32[]{:S(2)}, u32[]{:S(2)}) %collective-permute-start.13) | collective-permute-done | bytes 294944 | tf_op jit(solution)/shard_map/ppermute | solution.py:44
  123.0 1.4 collective-permute-start.18
  124.4 3.6 %collective-permute-start.15 = (f32[2,96,384]{2,1,0:T(8,128)S(1)}, f32[2,96,384]{2,1,0:T(8,128)S(1)}, u32[]{:S(2)}, u32[]{:S(2)}) collective-permute-start(f32[2,96,384]{2,1,0:T(8,128)S(1)} %shard_map.71.refs_0_.one_ref), channel_id=1, source_target_pairs={{0,4},{1,5},{2,6},{3,7},{4,0},{5,1},{6,2},{7,3},{8,12},{9,13},{10,... | collective-permute-start | bytes 884744 | tf_op jit(solution)/shard_map/ppermute | solution.py:44
  128.0 10.6 %collective-permute-done.15.two_ref = f32[2,96,384]{2,1,0:T(8,128)S(1)} collective-permute-done((f32[2,96,384]{2,1,0:T(8,128)S(1)}, f32[2,96,384]{2,1,0:T(8,128)S(1)}, u32[]{:S(2)}, u32[]{:S(2)}) %collective-permute-start.15) | collective-permute-done | bytes 294944 | tf_op jit(solution)/shard_map/ppermute | solution.py:44
  138.7 2.0 collective-permute-done.14.right_ref
  143.3 3.4 %collective-permute-done.17.two_ref = f32[1,96,384]{2,1,0:T(8,128)S(1)} collective-permute-done((f32[1,96,384]{2,1,0:T(8,128)S(1)}, f32[1,96,384]{2,1,0:T(8,128)S(1)}, u32[]{:S(2)}, u32[]{:S(2)}) %collective-permute-start.17) | collective-permute-done | bytes 147488 | tf_op jit(solution)/shard_map/ppermute | solution.py:30
  148.7 4.8 %collective-permute-done.20.two_ref = f32[2,192,384]{2,1,0:T(8,128)S(1)} collective-permute-done((f32[2,192,384]{2,1,0:T(8,128)S(1)}, f32[2,192,384]{2,1,0:T(8,128)S(1)}, u32[]{:S(2)}, u32[]{:S(2)}) %collective-permute-start.20) | collective-permute-done | bytes 589856 | tf_op jit(solution)/shard_map/ppermute | solution.py:44
  153.6 4.0 %collective-permute-done.19.two_ref = f32[2,96,384]{2,1,0:T(8,128)S(1)} collective-permute-done((f32[2,96,384]{2,1,0:T(8,128)S(1)}, f32[2,96,384]{2,1,0:T(8,128)S(1)}, u32[]{:S(2)}, u32[]{:S(2)}) %collective-permute-start.19) | collective-permute-done | bytes 294944 | tf_op jit(solution)/shard_map/ppermute | solution.py:44
  157.8 6.8 %collective-permute-start.23 = (f32[1,768,768]{2,1,0:T(8,128)S(1)}, f32[1,768,768]{2,1,0:T(8,128)S(1)}, u32[]{:S(2)}, u32[]{:S(2)}) collective-permute-start(f32[1,768,768]{2,1,0:T(8,128)S(1)} %shard_map.83.refs_0_), channel_id=1, source_target_pairs={{0,8},{8,0},{16,24},{24,16},{1,9},{9,1},{17,25},{25,17},{2,10},{10... | collective-permute-start | bytes 7077896 | tf_op jit(solution)/shard_map/ppermute | solution.py:30
  166.4 1.5 shard_map.84.token_ref
  170.2 1.7 copy-done.15
  171.8 4.5 %shard_map.85 = (bf16[2,1,1536,768]{3,2,1,0:T(8,128)(2,1)}, f32[96,768]{1,0:T(8,128)S(1)}) custom-call(s32[4]{0:T(128)S(1)} %pad_add_fusion.state_ref, f32[1,768,256]{2,1,0:T(8,128)} %shard_map.84.token_ref, f32[1,768,768]{2,1,0:T(8,128)S(1)} %shard_map.83.refs_0_, f32[1,768,768]{2,1,0:T(8,128)S(1)} %copy-done.15), custom_call_target="tpu_custom_call" | custom-call | flops 1 | bytes 1 | tf_op jit(solution)/shard_map/pallas_call | solution.py:334
  176.3 7.8 %collective-permute-done.24.refs_1_ = f32[1,768,256]{2,1,0:T(8,128)S(1)} collective-permute-done((f32[1,768,256]{2,1,0:T(8,128)S(1)}, f32[1,768,256]{2,1,0:T(8,128)S(1)}, u32[]{:S(2)}, u32[]{:S(2)}) %collective-permute-start.24) | collective-permute-done | bytes 786464 | tf_op jit(solution)/shard_map/ppermute | solution.py:30
  187.9 1.4 shard_map.88.refs_0_.refs_1_
  189.3 1.5 shard_map.89.token_ref
  191.7 2.3 copy-done.7
  194.0 7.5 %shard_map.90 = (f32[2,768,1024]{2,1,0:T(8,128)}, f32[8,128]{1,0:T(8,128)S(1)}) custom-call(s32[2,2]{1,0:T(2,128)S(1)} %copy-done.21, s32[4]{0:T(128)S(1)} %pad_add_fusion.state_ref, bf16[2,1,1536,768]{3,2,1,0:T(8,128)(2,1)S(1)} %copy-done.7, f32[1,768,256]{2,1,0:T(8,128)} %shard_map.89.token_ref, f32[2,768,1024]{2,1,0:T(8,128)} %collective-permute-done.1.refs_0_), custom_call_target="tpu_custom_call" | custom-call | flops 1 | bytes 1 | tf_op jit(solution)/shard_map/pallas_call | solution.py:390
  201.5 7.7 %shard_map.91 = (f32[2,768,1024]{2,1,0:T(8,128)}, f32[8,128]{1,0:T(8,128)S(1)}) custom-call(s32[2,2]{1,0:T(2,128)S(1)} %copy-done.21, s32[4]{0:T(128)S(1)} %pad_add_fusion.state_ref, bf16[2,1,1536,768]{3,2,1,0:T(8,128)(2,1)S(1)} %copy-done.7, f32[8,128]{1,0:T(8,128)S(1)} %get-tuple-element.51.token_ref, ...), custom_call_target="tpu_custom_call", output_to_operand_aliasing={{0}: (5, {})} | custom-call | flops 1 | bytes 1 | tf_op jit(solution)/shard_map/pallas_call | solution.py:390
  209.2 1.4 shard_map.93.token_ref.refs_2_.refs_3_
  212.0 1.7 copy-done.2
  213.6 4.5 %shard_map.94 = (bf16[2,1,1536,768]{3,2,1,0:T(8,128)(2,1)}, f32[96,768]{1,0:T(8,128)S(1)}) custom-call(s32[4]{0:T(128)S(1)} %pad_add_fusion.state_ref, f32[2,768,384]{2,1,0:T(8,128)S(1)} %copy-done.2, f32[2,768,384]{2,1,0:T(8,128)S(1)} %shard_map.88.refs_0_.refs_1_, f32[2,768,384]{2,1,0:T(8,128)S(1)} %shard_map.88.refs_0_.refs_1_, ...), custom_call_target="tpu_custom_call" | custom-call | flops 1 | bytes 1 | tf_op jit(solution)/shard_map/pallas_call | solution.py:334
  219.5 4.4 %collective-permute-done.28.refs_1_.refs_3_ = f32[1,768,256]{2,1,0:T(8,128)} collective-permute-done((f32[1,768,256]{2,1,0:T(8,128)}, f32[1,768,256]{2,1,0:T(8,128)}, u32[]{:S(2)}, u32[]{:S(2)}) %collective-permute-start.28) | collective-permute-done | bytes 786464 | tf_op jit(solution)/shard_map/ppermute | solution.py:30
  223.9 2.3 copy-done.5
  226.2 1.4 copy-done.9
  227.6 8.6 %shard_map.96 = (f32[2,768,1024]{2,1,0:T(8,128)}, f32[8,128]{1,0:T(8,128)S(1)}) custom-call(s32[2,2]{1,0:T(2,128)S(1)} %copy-done.21, s32[4]{0:T(128)S(1)} %pad_add_fusion.state_ref, bf16[2,1,1536,768]{3,2,1,0:T(8,128)(2,1)S(1)} %copy-done.5, f32[8,128]{1,0:T(8,128)S(1)} %shard_map.95.token_ref, ...), custom_call_target="tpu_custom_call", output_to_operand_aliasing={{0}: (6, {})} | custom-call | flops 1 | bytes 1 | tf_op jit(solution)/shard_map/pallas_call | solution.py:390
  236.4 2.3 copy-done.6
  238.8 8.0 %shard_map.97 = (f32[2,768,1024]{2,1,0:T(8,128)}, f32[8,128]{1,0:T(8,128)}) custom-call(s32[2,2]{1,0:T(2,128)S(1)} %copy-done.21, s32[4]{0:T(128)S(1)} %pad_add_fusion.state_ref, bf16[2,1,1536,768]{3,2,1,0:T(8,128)(2,1)S(1)} %copy-done.6, f32[8,128]{1,0:T(8,128)S(1)} %get-tuple-element.57.token_ref, ...), custom_call_target="tpu_custom_call", output_to_operand_aliasing={{0}: (8, {})} | custom-call | flops 1 | bytes 1 | tf_op jit(solution)/shard_map/pallas_call | solution.py:390
  (126 shorter events, 27.4 us)
Async XLA Ops:
  0.6 10.6 %collective-permute-start.1 = (f32[2,768,1024]{2,1,0:T(8,128)}, f32[2,768,1024]{2,1,0:T(8,128)}, u32[]{:S(2)}, u32[]{:S(2)}) collective-permute-start(f32[2,768,1024]{2,1,0:T(8,128)} %source_ref.11), channel_id=1, source_target_pairs={{0,8},{8,0},{16,24},{24,16},{1,9},{9,1},{17,25},{25,17},{2,10},{10... | collective-permute-start | bytes 18874376 | tf_op jit(solution)/shard_map/ppermute | solution.py:30
  2.7 2.8 %copy-start = (f32[2,768,1024]{2,1,0:T(8,128)S(1)}, f32[2,768,1024]{2,1,0:T(8,128)}, u32[]{:S(2)}) copy-start(f32[2,768,1024]{2,1,0:T(8,128)} %source_ref.11) | copy-start | bytes 18874372
  6.9 4.4 %slice-start = ((s8[6291456]{0:T(1024)(128)(4,1)}), s8[4194304]{0:T(1024)(128)(4,1)S(1)}, s32[]{:S(2)}) async-start(s8[6291456]{0:T(1024)(128)(4,1)} %bitcast.6), calls=%async_computation | async-start | bytes 8388608
  7.6 3.7 %slice-start.1 = ((s8[6291456]{0:T(1024)(128)(4,1)}), s8[2097152]{0:T(1024)(128)(4,1)S(1)}, s32[]{:S(2)}) async-start(s8[6291456]{0:T(1024)(128)(4,1)} %bitcast.6), calls=%async_computation.1 | async-start | bytes 4194304
  7.6 3.7 %copy-start.21 = (s32[2,2]{1,0:T(2,128)S(1)}, s32[2,2]{1,0:T(2,128)}, u32[]{:S(2)}) copy-start(s32[2,2]{1,0:T(2,128)} %plan_ref.25) | copy-start | bytes 52
  7.6 38.6 %collective-permute-start = (f32[1,392,1024]{2,1,0:T(8,128)S(1)}, f32[1,392,1024]{2,1,0:T(8,128)S(1)}, u32[]{:S(2)}, u32[]{:S(2)}) collective-permute-start(f32[1,392,1024]{2,1,0:T(8,128)S(1)} %shard_map.59.refs_0_), channel_id=1, source_target_pairs={{0,16},{16,0},{8,24},{24,8},{1,17},{17,1},{9,25},{25,9},{2,18},{18... | collective-permute-start | bytes 4816904 | tf_op jit(solution)/shard_map/ppermute | solution.py:30
  18.6 17.1 %collective-permute-start.2 = (f32[1,384,768]{2,1,0:T(8,128)S(1)}, f32[1,384,768]{2,1,0:T(8,128)S(1)}, u32[]{:S(2)}, u32[]{:S(2)}) collective-permute-start(f32[1,384,768]{2,1,0:T(8,128)S(1)} %get-tuple-element.32.token_ref), channel_id=1, source_target_pairs={{0,1},{1,0},{2,3},{3,2},{4,5},{5,4},{6,7},{7,6},{8,10},{9,11},{10,... | collective-permute-start | bytes 3538952 | tf_op jit(solution)/shard_map/ppermute | solution.py:44
  21.6 58.1 %collective-permute-start.8 = (f32[1,384,1024]{2,1,0:T(8,128)S(1)}, f32[1,384,1024]{2,1,0:T(8,128)S(1)}, u32[]{:S(2)}, u32[]{:S(2)}) collective-permute-start(f32[1,384,1024]{2,1,0:T(8,128)S(1)} %shard_map.60.token_ref), channel_id=1, source_target_pairs={{0,16},{16,0},{8,24},{24,8},{1,17},{17,1},{9,25},{25,9},{2,18},{18... | collective-permute-start | bytes 4718600 | tf_op jit(solution)/shard_map/ppermute | solution.py:30
  35.9 16.1 %collective-permute-start.4 = (f32[1,192,768]{2,1,0:T(8,128)S(1)}, f32[1,192,768]{2,1,0:T(8,128)S(1)}, u32[]{:S(2)}, u32[]{:S(2)}) collective-permute-start(f32[1,192,768]{2,1,0:T(8,128)S(1)} %get-tuple-element.33.token_ref), channel_id=1, source_target_pairs={{0,2},{1,3},{2,0},{3,1},{4,6},{5,7},{6,4},{7,5},{8,9},{9,8},{10,11... | collective-permute-start | bytes 1769480 | tf_op jit(solution)/shard_map/ppermute | solution.py:44
  46.2 94.5 %copy-start.3 = (f32[1,392,1024]{2,1,0:T(8,128)}, f32[1,392,1024]{2,1,0:T(8,128)S(1)}, u32[]{:S(2)}) copy-start(f32[1,392,1024]{2,1,0:T(8,128)S(1)} %collective-permute-done.refs_0_.theirs_ref) | copy-start | bytes 4816900
  50.0 9.9 %collective-permute-start.3 = (f32[1,384,384]{2,1,0:T(8,128)S(1)}, f32[1,384,384]{2,1,0:T(8,128)S(1)}, u32[]{:S(2)}, u32[]{:S(2)}) collective-permute-start(f32[1,384,384]{2,1,0:T(8,128)S(1)} %get-tuple-element.35.token_ref), channel_id=1, source_target_pairs={{0,1},{1,0},{2,3},{3,2},{4,5},{5,4},{6,7},{7,6},{8,10},{9,11},{10,... | collective-permute-start | bytes 1769480 | tf_op jit(solution)/shard_map/ppermute | solution.py:44
  52.0 14.7 %copy-start.23 = (f32[768]{0:T(1024)S(1)}, f32[768]{0:T(1024)}, u32[]{:S(2)}) copy-start(f32[768]{0:T(1024)} %refs_1_.1) | copy-start | bytes 9220
  52.1 15.5 %collective-permute-start.7 = (f32[1,96,768]{2,1,0:T(8,128)S(1)}, f32[1,96,768]{2,1,0:T(8,128)S(1)}, u32[]{:S(2)}, u32[]{:S(2)}) collective-permute-start(f32[1,96,768]{2,1,0:T(8,128)S(1)} %get-tuple-element.37.token_ref), channel_id=1, source_target_pairs={{0,4},{1,5},{2,6},{3,7},{4,0},{5,1},{6,2},{7,3},{8,12},{9,13},{10,... | collective-permute-start | bytes 884744 | tf_op jit(solution)/shard_map/ppermute | solution.py:44
  60.0 8.3 %collective-permute-start.5 = (f32[1,192,384]{2,1,0:T(8,128)S(1)}, f32[1,192,384]{2,1,0:T(8,128)S(1)}, u32[]{:S(2)}, u32[]{:S(2)}) collective-permute-start(f32[1,192,384]{2,1,0:T(8,128)S(1)} %get-tuple-element.39.token_ref), channel_id=1, source_target_pairs={{0,2},{1,3},{2,0},{3,1},{4,6},{5,7},{6,4},{7,5},{8,9},{9,8},{10,11... | collective-permute-start | bytes 884744 | tf_op jit(solution)/shard_map/ppermute | solution.py:44
  62.1 5.5 %collective-permute-start.6 = (f32[1,6]{1,0:T(1,128)S(1)}, f32[1,6]{1,0:T(1,128)S(1)}, u32[]{:S(2)}, u32[]{:S(2)}) collective-permute-start(f32[1,6]{1,0:T(1,128)S(1)} %maximum_bitcast_fusion.ours_ref), channel_id=1, source_target_pairs={{0,8},{8,0},{16,24},{24,16},{1,9},{9,1},{17,25},{25,17},{2,10},{10... | collective-permute-start | bytes 80 | tf_op jit(solution)/shard_map/ppermute | solution.py:30
  79.6 3.8 %copy-start.8 = (f32[1,384,1024]{2,1,0:T(8,128)}, f32[1,384,1024]{2,1,0:T(8,128)S(1)}, u32[]{:S(2)}) copy-start(f32[1,384,1024]{2,1,0:T(8,128)S(1)} %collective-permute-done.8.refs_0_.refs_1_) | copy-start | bytes 4718596
  83.5 32.1 %collective-permute-start.9 = (f32[1,384,384]{2,1,0:T(8,128)S(1)}, f32[1,384,384]{2,1,0:T(8,128)S(1)}, u32[]{:S(2)}, u32[]{:S(2)}) collective-permute-start(f32[1,384,384]{2,1,0:T(8,128)S(1)} %get-tuple-element.43.token_ref), channel_id=1, source_target_pairs={{0,1},{1,0},{2,3},{3,2},{4,5},{5,4},{6,7},{7,6},{8,10},{9,11},{10,... | collective-permute-start | bytes 1769480 | tf_op jit(solution)/shard_map/ppermute | solution.py:44
  85.3 22.8 %collective-permute-start.12 = (f32[1,96,768]{2,1,0:T(8,128)S(1)}, f32[1,96,768]{2,1,0:T(8,128)S(1)}, u32[]{:S(2)}, u32[]{:S(2)}) collective-permute-start(f32[1,96,768]{2,1,0:T(8,128)S(1)} %shard_map.66.token_ref.one_ref), channel_id=1, source_target_pairs={{0,4},{1,5},{2,6},{3,7},{4,0},{5,1},{6,2},{7,3},{8,12},{9,13},{10,... | collective-permute-start | bytes 884744 | tf_op jit(solution)/shard_map/ppermute | solution.py:44
  87.9 19.4 %collective-permute-start.10 = (f32[1,96,384]{2,1,0:T(8,128)S(1)}, f32[1,96,384]{2,1,0:T(8,128)S(1)}, u32[]{:S(2)}, u32[]{:S(2)}) collective-permute-start(f32[1,96,384]{2,1,0:T(8,128)S(1)} %get-tuple-element.41.token_ref), channel_id=1, source_target_pairs={{0,4},{1,5},{2,6},{3,7},{4,0},{5,1},{6,2},{7,3},{8,12},{9,13},{10,... | collective-permute-start | bytes 442376 | tf_op jit(solution)/shard_map/ppermute | solution.py:44
  108.1 14.4 %collective-permute-start.16 = (f32[1,192,768]{2,1,0:T(8,128)S(1)}, f32[1,192,768]{2,1,0:T(8,128)S(1)}, u32[]{:S(2)}, u32[]{:S(2)}) collective-permute-start(f32[1,192,768]{2,1,0:T(8,128)S(1)} %shard_map.70.token_ref.one_ref), channel_id=1, source_target_pairs={{0,2},{1,3},{2,0},{3,1},{4,6},{5,7},{6,4},{7,5},{8,9},{9,8},{10,11... | collective-permute-start | bytes 1769480 | tf_op jit(solution)/shard_map/ppermute | solution.py:44
  108.2 6.8 %collective-permute-start.11 = (f32[1,96,384]{2,1,0:T(8,128)S(1)}, f32[1,96,384]{2,1,0:T(8,128)S(1)}, u32[]{:S(2)}, u32[]{:S(2)}) collective-permute-start(f32[1,96,384]{2,1,0:T(8,128)S(1)} %shard_map.69.token_ref.one_ref), channel_id=1, source_target_pairs={{0,16},{16,0},{8,24},{24,8},{1,17},{17,1},{9,25},{25,9},{2,18},{18... | collective-permute-start | bytes 442376 | tf_op jit(solution)/shard_map/ppermute | solution.py:30
  115.7 6.8 %collective-permute-start.13 = (f32[1,192,384]{2,1,0:T(8,128)S(1)}, f32[1,192,384]{2,1,0:T(8,128)S(1)}, u32[]{:S(2)}, u32[]{:S(2)}) collective-permute-start(f32[1,192,384]{2,1,0:T(8,128)S(1)} %get-tuple-element.46.token_ref), channel_id=1, source_target_pairs={{0,2},{1,3},{2,0},{3,1},{4,6},{5,7},{6,4},{7,5},{8,9},{9,8},{10,11... | collective-permute-start | bytes 884744 | tf_op jit(solution)/shard_map/ppermute | solution.py:44
  122.6 35.0 %collective-permute-start.22 = (f32[1,384,768]{2,1,0:T(8,128)S(1)}, f32[1,384,768]{2,1,0:T(8,128)S(1)}, u32[]{:S(2)}, u32[]{:S(2)}) collective-permute-start(f32[1,384,768]{2,1,0:T(8,128)S(1)} %shard_map.75.token_ref.one_ref), channel_id=1, source_target_pairs={{0,1},{1,0},{2,3},{3,2},{4,5},{5,4},{6,7},{7,6},{8,10},{9,11},{10,... | collective-permute-start | bytes 3538952 | tf_op jit(solution)/shard_map/ppermute | solution.py:44
  123.0 19.4 %collective-permute-start.18 = (f32[1,768,256]{2,1,0:T(8,128)S(1)}, f32[1,768,256]{2,1,0:T(8,128)S(1)}, u32[]{:S(2)}, u32[]{:S(2)}) collective-permute-start(f32[1,768,256]{2,1,0:T(8,128)S(1)} %shard_map.72.token_ref), channel_id=1, source_target_pairs={{0,16},{16,0},{8,24},{24,8},{1,17},{17,1},{9,25},{25,9},{2,18},{18... | collective-permute-start | bytes 2359304 | tf_op jit(solution)/shard_map/ppermute | solution.py:30
  124.4 14.2 %collective-permute-start.15 = (f32[2,96,384]{2,1,0:T(8,128)S(1)}, f32[2,96,384]{2,1,0:T(8,128)S(1)}, u32[]{:S(2)}, u32[]{:S(2)}) collective-permute-start(f32[2,96,384]{2,1,0:T(8,128)S(1)} %shard_map.71.refs_0_.one_ref), channel_id=1, source_target_pairs={{0,4},{1,5},{2,6},{3,7},{4,0},{5,1},{6,2},{7,3},{8,12},{9,13},{10,... | collective-permute-start | bytes 884744 | tf_op jit(solution)/shard_map/ppermute | solution.py:44
  128.0 12.7 %collective-permute-start.14 = (f32[1,96,384]{2,1,0:T(8,128)S(1)}, f32[1,96,384]{2,1,0:T(8,128)S(1)}, u32[]{:S(2)}, u32[]{:S(2)}) collective-permute-start(f32[1,96,384]{2,1,0:T(8,128)S(1)} %get-tuple-element.48.token_ref), channel_id=1, source_target_pairs={{0,4},{1,5},{2,6},{3,7},{4,0},{5,1},{6,2},{7,3},{8,12},{9,13},{10,... | collective-permute-start | bytes 442376 | tf_op jit(solution)/shard_map/ppermute | solution.py:44
  138.6 14.9 %collective-permute-start.20 = (f32[2,192,384]{2,1,0:T(8,128)S(1)}, f32[2,192,384]{2,1,0:T(8,128)S(1)}, u32[]{:S(2)}, u32[]{:S(2)}) collective-permute-start(f32[2,192,384]{2,1,0:T(8,128)S(1)} %shard_map.76.token_ref.one_ref), channel_id=1, source_target_pairs={{0,2},{1,3},{2,0},{3,1},{4,6},{5,7},{6,4},{7,5},{8,9},{9,8},{10,11... | collective-permute-start | bytes 1769480 | tf_op jit(solution)/shard_map/ppermute | solution.py:44
  141.5 5.2 %collective-permute-start.17 = (f32[1,96,384]{2,1,0:T(8,128)S(1)}, f32[1,96,384]{2,1,0:T(8,128)S(1)}, u32[]{:S(2)}, u32[]{:S(2)}) collective-permute-start(f32[1,96,384]{2,1,0:T(8,128)S(1)} %shard_map.77.refs_0_.one_ref), channel_id=1, source_target_pairs={{0,16},{16,0},{8,24},{24,8},{1,17},{17,1},{9,25},{25,9},{2,18},{18... | collective-permute-start | bytes 442376 | tf_op jit(solution)/shard_map/ppermute | solution.py:30
  146.7 10.8 %collective-permute-start.19 = (f32[2,96,384]{2,1,0:T(8,128)S(1)}, f32[2,96,384]{2,1,0:T(8,128)S(1)}, u32[]{:S(2)}, u32[]{:S(2)}) collective-permute-start(f32[2,96,384]{2,1,0:T(8,128)S(1)} %shard_map.79.refs_0_.one_ref), channel_id=1, source_target_pairs={{0,4},{1,5},{2,6},{3,7},{4,0},{5,1},{6,2},{7,3},{8,12},{9,13},{10,... | collective-permute-start | bytes 884744 | tf_op jit(solution)/shard_map/ppermute | solution.py:44
  157.8 11.0 %collective-permute-start.23 = (f32[1,768,768]{2,1,0:T(8,128)S(1)}, f32[1,768,768]{2,1,0:T(8,128)S(1)}, u32[]{:S(2)}, u32[]{:S(2)}) collective-permute-start(f32[1,768,768]{2,1,0:T(8,128)S(1)} %shard_map.83.refs_0_), channel_id=1, source_target_pairs={{0,8},{8,0},{16,24},{24,16},{1,9},{9,1},{17,25},{25,17},{2,10},{10... | collective-permute-start | bytes 7077896 | tf_op jit(solution)/shard_map/ppermute | solution.py:30
  164.6 19.5 %collective-permute-start.24 = (f32[1,768,256]{2,1,0:T(8,128)S(1)}, f32[1,768,256]{2,1,0:T(8,128)S(1)}, u32[]{:S(2)}, u32[]{:S(2)}) collective-permute-start(f32[1,768,256]{2,1,0:T(8,128)S(1)} %shard_map.80.token_ref), channel_id=1, source_target_pairs={{0,16},{16,0},{8,24},{24,8},{1,17},{17,1},{9,25},{25,9},{2,18},{18... | collective-permute-start | bytes 2359304 | tf_op jit(solution)/shard_map/ppermute | solution.py:30
  165.9 18.2 %collective-permute-start.21 = (f32[2,192,384]{2,1,0:T(8,128)S(1)}, f32[2,192,384]{2,1,0:T(8,128)S(1)}, u32[]{:S(2)}, u32[]{:S(2)}) collective-permute-start(f32[2,192,384]{2,1,0:T(8,128)S(1)} %shard_map.82.token_ref.one_ref), channel_id=1, source_target_pairs={{0,2},{1,3},{2,0},{3,1},{4,6},{5,7},{6,4},{7,5},{8,9},{9,8},{10,11... | collective-permute-start | bytes 1769480 | tf_op jit(solution)/shard_map/ppermute | solution.py:44
  165.9 22.0 %collective-permute-start.26 = (f32[2,384,384]{2,1,0:T(8,128)S(1)}, f32[2,384,384]{2,1,0:T(8,128)}, u32[]{:S(2)}, u32[]{:S(2)}) collective-permute-start(f32[2,384,384]{2,1,0:T(8,128)S(1)} %shard_map.81.token_ref.one_ref), channel_id=1, source_target_pairs={{0,1},{1,0},{2,3},{3,2},{4,5},{5,4},{6,7},{7,6},{8,10},{9,11},{10,... | collective-permute-start | bytes 3538952 | tf_op jit(solution)/shard_map/ppermute | solution.py:44
  176.3 9.8 %copy-start.16 = (f32[96,768]{1,0:T(8,128)}, f32[96,768]{1,0:T(8,128)S(1)}, u32[]{:S(2)}) copy-start(f32[96,768]{1,0:T(8,128)S(1)} %get-tuple-element.49.refs_0_) | copy-start | bytes 884740
  186.2 23.0 %collective-permute-start.25 = (f32[2,384,384]{2,1,0:T(8,128)S(1)}, f32[2,384,384]{2,1,0:T(8,128)}, u32[]{:S(2)}, u32[]{:S(2)}) collective-permute-start(f32[2,384,384]{2,1,0:T(8,128)S(1)} %shard_map.87.token_ref.one_ref), channel_id=1, source_target_pairs={{0,1},{1,0},{2,3},{3,2},{4,5},{5,4},{6,7},{7,6},{8,10},{9,11},{10,... | collective-permute-start | bytes 3538952 | tf_op jit(solution)/shard_map/ppermute | solution.py:44
  186.7 22.5 %collective-permute-start.27 = (f32[1,768,256]{2,1,0:T(8,128)}, f32[1,768,256]{2,1,0:T(8,128)}, u32[]{:S(2)}, u32[]{:S(2)}) collective-permute-start(f32[1,768,256]{2,1,0:T(8,128)} %shard_map.84.token_ref), channel_id=1, source_target_pairs={{0,16},{16,0},{8,24},{24,8},{1,17},{17,1},{9,25},{25,9},{2,18},{18... | collective-permute-start | bytes 2359304 | tf_op jit(solution)/shard_map/ppermute | solution.py:30
  190.8 33.0 %collective-permute-start.28 = (f32[1,768,256]{2,1,0:T(8,128)}, f32[1,768,256]{2,1,0:T(8,128)}, u32[]{:S(2)}, u32[]{:S(2)}) collective-permute-start(f32[1,768,256]{2,1,0:T(8,128)} %shard_map.89.token_ref), channel_id=1, source_target_pairs={{0,16},{16,0},{8,24},{24,8},{1,17},{17,1},{9,25},{25,9},{2,18},{18... | collective-permute-start | bytes 2359304 | tf_op jit(solution)/shard_map/ppermute | solution.py:30
  191.7 2.3 copy-start.7
  213.6 4.5 %copy-start.17 = (f32[96,768]{1,0:T(8,128)S(1)}, f32[96,768]{1,0:T(8,128)}, u32[]{:S(2)}) copy-start(f32[96,768]{1,0:T(8,128)} %copy-done.16) | copy-start | bytes 884740
  218.1 5.7 %copy-start.4 = (f32[1,392,1024]{2,1,0:T(8,128)S(1)}, f32[1,392,1024]{2,1,0:T(8,128)}, u32[]{:S(2)}) copy-start(f32[1,392,1024]{2,1,0:T(8,128)} %copy-done.3) | copy-start | bytes 4816900
  218.2 5.7 %copy-start.24 = (f32[96,768]{1,0:T(8,128)}, f32[96,768]{1,0:T(8,128)S(1)}, u32[]{:S(2)}) copy-start(f32[96,768]{1,0:T(8,128)S(1)} %add.44) | copy-start | bytes 884740
  218.2 18.0 %collective-permute-start.29 = (f32[96,384]{1,0:T(8,128)S(1)}, f32[96,384]{1,0:T(8,128)S(1)}, u32[]{:S(2)}, u32[]{:S(2)}) collective-permute-start(f32[96,384]{1,0:T(8,128)S(1)} %constant_dynamic-slice_fusion.1), channel_id=1, source_target_pairs={{0,16},{16,0},{8,24},{24,8},{1,17},{17,1},{9,25},{25,9},{2,18},{18... | collective-permute-start | bytes 442376 | tf_op jit(solution)/shard_map/ppermute | solution.py:30
  223.9 2.3 copy-start.5
  227.6 8.6 %copy-start.25 = (f32[96,768]{1,0:T(8,128)S(1)}, f32[96,768]{1,0:T(8,128)}, u32[]{:S(2)}) copy-start(f32[96,768]{1,0:T(8,128)} %copy-done.24) | copy-start | bytes 884740
  227.6 8.8 %copy-start.11 = (f32[1,768,256]{2,1,0:T(8,128)S(1)}, f32[1,768,256]{2,1,0:T(8,128)}, u32[]{:S(2)}) copy-start(f32[1,768,256]{2,1,0:T(8,128)} %copy-done.10) | copy-start | bytes 2359300
  227.6 8.8 %copy-start.13 = (f32[1,768,256]{2,1,0:T(8,128)S(1)}, f32[1,768,256]{2,1,0:T(8,128)}, u32[]{:S(2)}) copy-start(f32[1,768,256]{2,1,0:T(8,128)} %copy-done.12) | copy-start | bytes 2359300
  236.3 10.5 %collective-permute-start.30 = (f32[96,192]{1,0:T(8,128)S(1)}, f32[96,192]{1,0:T(8,128)S(1)}, u32[]{:S(2)}, u32[]{:S(2)}) collective-permute-start(f32[96,192]{1,0:T(8,128)S(1)} %constant_dynamic-slice_fusion), channel_id=1, source_target_pairs={{0,8},{8,0},{16,24},{24,16},{1,9},{9,1},{17,25},{25,17},{2,10},{10... | collective-permute-start | bytes 221192 | tf_op jit(solution)/shard_map/ppermute | solution.py:30
  236.4 2.3 copy-start.6
  (11 other events, 13.8 us)

commit v9 on v8

--- a/solution.py
+++ b/solution.py
@@ -554,7 +554,7 @@
             for stage in range(bits):
                 times.append(times[-1] + 3 + (wide / 2 if stage == 1 else wide))
             if tuned and turn > 0 and cut == cuts - 1:
-                times = [70.0, 80.0, 84.0, 95.0, 101.5, 104.0, 120.0, 130.0]
+                times = [70.0, 70.5, 72.0, 79.0, 86.0, 100.0, 120.0, 130.0]
             elif tuned and turn == 0:
                 times[-1] = 104.2
             elif tuned:
@@ -564,7 +564,7 @@
     for turn in range(1, rounds):
         begin = 0.0 if tuned else 74.0 + 137.0 * (turn - 1)
         plain = ((0.0, 20.0), (17.0, 37.0), (34.0, 56.0), (51.0, 75.0))
-        ordered = ((79.0, 101.1), (102.0, 119.7), (104.5, 129.0), (120.5, 136.5))
+        ordered = ((69.9, 71.2), (87.0, 119.7), (104.5, 129.0), (120.5, 136.5))
         for piece, (send, there) in enumerate(ordered if tuned else plain):
             tasks += [(begin + send, send_piece(turn, piece)), (begin + there, gate_piece(turn, piece))]
     for turn in range(rounds):

time: 248 us -> 251 us (1.012)
  starting transfers between devices: 48.2 us -> 56.5 us
  waiting for transfers between devices: 107 us -> 101 us
    ppermute x18, starting transfers between devices: 23.5 us -> 36 us  [across(): return lax.ppermute(block, ('pair', 'aux'), route)]
    ppermute x13, waiting for transfers between devices: 41.9 us -> 32.3 us  [swapped(): return lax.ppermute(block, axis, route)]
    ppermute x18, waiting for transfers between devices: 64.6 us -> 69.1 us  [across(): return lax.ppermute(block, ('pair', 'aux'), route)]
    ppermute x13, starting transfers between devices: 24.7 us -> 20.5 us  [swapped(): return lax.ppermute(block, axis, route)]
  transfers between devices with their start and end apart: 31 -> 31, of which waited for: 17 -> 17; matrix products, arithmetic and copies ran while one was open for 1% -> 1% of each run, Pallas kernels for 26% -> 25%
where the time goes in v9:
time: 251 us; the launch traced here: 250 us
  waiting for transfers between devices  101 us (40%)
  Pallas kernels  67.5 us (27%)
  starting transfers between devices  56.5 us (23%)
  local copies, waits for them, and re-layouts  21 us (8%)
    ppermute x18, waiting for transfers between devices, across(): return lax.ppermute(block, ('pair', 'aux'), route)  69.1 us
    ppermute x18, starting transfers between devices, across(): return lax.ppermute(block, ('pair', 'aux'), route)  36 us
    ppermute x13, waiting for transfers between devices, swapped(): return lax.ppermute(block, axis, route)  32.3 us
    pallas_call x4, Pallas kernels, gradient_terms(): pl.pallas_call(functools.partial(gradient_kernel, len(sources), turn > 0,...  31.7 us
    unnamed x56, local copies, waits for them, and re-layouts  20.7 us
    ppermute x13, starting transfers between devices, swapped(): return lax.ppermute(block, axis, route)  20.5 us
    pallas_call x3, Pallas kernels, integral(): pl.pallas_call(functools.partial(integral_kernel, turn, blocks), out_shap...  15 us
    pallas_call x2, Pallas kernels, tildes(): pl.pallas_call(functools.partial(tilde_kernel, blocks, places), out_shape...  8.96 us
  transfers between devices with their start and end apart: 31, of which 17 were waited for; matrix products, arithmetic and copies ran while one was open for 1% of the time, Pallas kernels for 25%

profile of v9, /device:TPU:0, one launch (start us, length us, event | category | flops | bytes accessed | tf_op | source)
XLA Modules:
  0.0 249.7 jit_solution(716670129222335665)
XLA Ops:
  2.7 2.8 %copy-done = f32[2,768,1024]{2,1,0:T(8,128)S(1)} copy-done((f32[2,768,1024]{2,1,0:T(8,128)S(1)}, f32[2,768,1024]{2,1,0:T(8,128)}, u32[]{:S(2)}) %copy-start) | copy-done | bytes 6291480
  7.6 2.6 %collective-permute-start = (f32[1,392,1024]{2,1,0:T(8,128)S(1)}, f32[1,392,1024]{2,1,0:T(8,128)S(1)}, u32[]{:S(2)}, u32[]{:S(2)}) collective-permute-start(f32[1,392,1024]{2,1,0:T(8,128)S(1)} %shard_map.59.refs_0_), channel_id=1, source_target_pairs={{0,16},{16,0},{8,24},{24,8},{1,17},{17,1},{9,25},{25,9},{2,18},{18... | collective-permute-start | bytes 4816904 | tf_op jit(solution)/shard_map/ppermute | solution.py:30
  11.3 7.3 %shard_map.61 = (f32[1,384,768]{2,1,0:T(8,128)S(1)}, f32[1,384,768]{2,1,0:T(8,128)S(1)}) custom-call(s32[2,2]{1,0:T(2,128)S(1)} %copy-done.21, s32[4]{0:T(128)S(1)} %pad_add_fusion.state_ref, f32[2,768,1024]{2,1,0:T(8,128)S(1)} %bitcast.7, f32[1,384,1024]{2,1,0:T(8,128)S(1)} %shard_map.60.token_ref, f32[2,768,1024]{2,1,0:T(8,128)} %collective-permute-done.1.refs_0_), custom_call_target="tpu_custom_call" | custom-call | flops 1 | bytes 1 | tf_op jit(solution)/shard_map/pallas_call | solution.py:196
  18.6 2.9 %collective-permute-start.2 = (f32[1,384,768]{2,1,0:T(8,128)S(1)}, f32[1,384,768]{2,1,0:T(8,128)S(1)}, u32[]{:S(2)}, u32[]{:S(2)}) collective-permute-start(f32[1,384,768]{2,1,0:T(8,128)S(1)} %get-tuple-element.32.token_ref), channel_id=1, source_target_pairs={{0,1},{1,0},{2,3},{3,2},{4,5},{5,4},{6,7},{7,6},{8,10},{9,11},{10,... | collective-permute-start | bytes 3538952 | tf_op jit(solution)/shard_map/ppermute | solution.py:44
  21.6 1.5 collective-permute-start.8
  23.1 12.7 %collective-permute-done.2.came_ref = f32[1,384,768]{2,1,0:T(8,128)S(1)} collective-permute-done((f32[1,384,768]{2,1,0:T(8,128)S(1)}, f32[1,384,768]{2,1,0:T(8,128)S(1)}, u32[]{:S(2)}, u32[]{:S(2)}) %collective-permute-start.2) | collective-permute-done | bytes 1179680 | tf_op jit(solution)/shard_map/ppermute | solution.py:44
  35.9 2.2 collective-permute-start.4
  38.1 8.1 %collective-permute-done.refs_0_.theirs_ref = f32[1,392,1024]{2,1,0:T(8,128)S(1)} collective-permute-done((f32[1,392,1024]{2,1,0:T(8,128)S(1)}, f32[1,392,1024]{2,1,0:T(8,128)S(1)}, u32[]{:S(2)}, u32[]{:S(2)}) %collective-permute-start) | collective-permute-done | bytes 1605664 | tf_op jit(solution)/shard_map/ppermute | solution.py:30
  46.2 3.8 %shard_map.63 = (f32[1,384,384]{2,1,0:T(8,128)S(1)}, f32[1,384,384]{2,1,0:T(8,128)S(1)}) custom-call(s32[2,2]{1,0:T(2,128)S(1)} %copy-done.21, s32[4]{0:T(128)S(1)} %pad_add_fusion.state_ref, f32[2,768,1024]{2,1,0:T(8,128)S(1)} %bitcast.7, f32[1,192,768]{2,1,0:T(8,128)S(1)} %get-tuple-element.33.token_ref, ...), custom_call_target="tpu_custom_call" | custom-call | flops 1 | bytes 1 | tf_op jit(solution)/shard_map/pallas_call | solution.py:196
  50.0 2.0 collective-permute-start.3
  52.1 2.7 %collective-permute-start.7 = (f32[1,96,768]{2,1,0:T(8,128)S(1)}, f32[1,96,768]{2,1,0:T(8,128)S(1)}, u32[]{:S(2)}, u32[]{:S(2)}) collective-permute-start(f32[1,96,768]{2,1,0:T(8,128)S(1)} %get-tuple-element.37.token_ref), channel_id=1, source_target_pairs={{0,4},{1,5},{2,6},{3,7},{4,0},{5,1},{6,2},{7,3},{8,12},{9,13},{10,... | collective-permute-start | bytes 884744 | tf_op jit(solution)/shard_map/ppermute | solution.py:44
  54.7 5.2 %collective-permute-done.3.came_ref = f32[1,384,384]{2,1,0:T(8,128)S(1)} collective-permute-done((f32[1,384,384]{2,1,0:T(8,128)S(1)}, f32[1,384,384]{2,1,0:T(8,128)S(1)}, u32[]{:S(2)}, u32[]{:S(2)}) %collective-permute-start.3) | collective-permute-done | bytes 589856 | tf_op jit(solution)/shard_map/ppermute | solution.py:44
  60.0 2.1 collective-permute-start.5
  62.1 4.6 %collective-permute-start.6 = (f32[1,6]{1,0:T(1,128)S(1)}, f32[1,6]{1,0:T(1,128)S(1)}, u32[]{:S(2)}, u32[]{:S(2)}) collective-permute-start(f32[1,6]{1,0:T(1,128)S(1)} %maximum_bitcast_fusion.ours_ref), channel_id=1, source_target_pairs={{0,8},{8,0},{16,24},{24,16},{1,9},{9,1},{17,25},{25,17},{2,10},{10... | collective-permute-start | bytes 80 | tf_op jit(solution)/shard_map/ppermute | solution.py:30
  69.0 10.6 %collective-permute-done.8.refs_0_.refs_1_ = f32[1,384,1024]{2,1,0:T(8,128)S(1)} collective-permute-done((f32[1,384,1024]{2,1,0:T(8,128)S(1)}, f32[1,384,1024]{2,1,0:T(8,128)S(1)}, u32[]{:S(2)}, u32[]{:S(2)}) %collective-permute-start.8) | collective-permute-done | bytes 1572896 | tf_op jit(solution)/shard_map/ppermute | solution.py:30
  79.6 3.8 %shard_map.69 = (f32[1,384,384]{2,1,0:T(8,128)S(1)}, f32[1,384,384]{2,1,0:T(8,128)S(1)}) custom-call(s32[2,2]{1,0:T(2,128)S(1)} %copy-done.21, s32[4]{0:T(128)S(1)} %pad_add_fusion.state_ref, f32[2,768,1024]{2,1,0:T(8,128)S(1)} %bitcast.7, f32[1,768,256]{2,1,0:T(8,128)S(1)} %shard_map.68.token_ref, f32[1,384,1024]{2,1,0:T(8,128)S(1)} %collective-permute-done.8.refs_0_.refs_1_), custom_call_target="tpu_custom_call" | custom-call | flops 1 | bytes 1 | tf_op jit(solution)/shard_map/pallas_call | solution.py:196
  83.5 1.8 collective-permute-start.9
  86.8 6.7 %collective-permute-done.9.came_ref = f32[1,384,384]{2,1,0:T(8,128)S(1)} collective-permute-done((f32[1,384,384]{2,1,0:T(8,128)S(1)}, f32[1,384,384]{2,1,0:T(8,128)S(1)}, u32[]{:S(2)}, u32[]{:S(2)}) %collective-permute-start.9) | collective-permute-done | bytes 589856 | tf_op jit(solution)/shard_map/ppermute | solution.py:44
  93.5 1.9 collective-permute-start.10
  95.4 2.6 %collective-permute-start.15 = (f32[1,96,768]{2,1,0:T(8,128)S(1)}, f32[1,96,768]{2,1,0:T(8,128)S(1)}, u32[]{:S(2)}, u32[]{:S(2)}) collective-permute-start(f32[1,96,768]{2,1,0:T(8,128)S(1)} %shard_map.66.token_ref.one_ref), channel_id=1, source_target_pairs={{0,4},{1,5},{2,6},{3,7},{4,0},{5,1},{6,2},{7,3},{8,12},{9,13},{10,... | collective-permute-start | bytes 884744 | tf_op jit(solution)/shard_map/ppermute | solution.py:44
  98.3 18.0 %collective-permute-done.11.right_ref = f32[1,96,384]{2,1,0:T(8,128)S(1)} collective-permute-done((f32[1,96,384]{2,1,0:T(8,128)S(1)}, f32[1,96,384]{2,1,0:T(8,128)S(1)}, u32[]{:S(2)}, u32[]{:S(2)}) %collective-permute-start.11) | collective-permute-done | bytes 147488 | tf_op jit(solution)/shard_map/ppermute | solution.py:44
  118.0 1.5 collective-permute-start.14
  119.5 3.4 %collective-permute-start.13 = (f32[1,96,384]{2,1,0:T(8,128)S(1)}, f32[1,96,384]{2,1,0:T(8,128)S(1)}, u32[]{:S(2)}, u32[]{:S(2)}) collective-permute-start(f32[1,96,384]{2,1,0:T(8,128)S(1)} %get-tuple-element.48.token_ref), channel_id=1, source_target_pairs={{0,4},{1,5},{2,6},{3,7},{4,0},{5,1},{6,2},{7,3},{8,12},{9,13},{10,... | collective-permute-start | bytes 442376 | tf_op jit(solution)/shard_map/ppermute | solution.py:44
  123.2 4.7 %collective-permute-done.13.right_ref = f32[1,96,384]{2,1,0:T(8,128)S(1)} collective-permute-done((f32[1,96,384]{2,1,0:T(8,128)S(1)}, f32[1,96,384]{2,1,0:T(8,128)S(1)}, u32[]{:S(2)}, u32[]{:S(2)}) %collective-permute-start.13) | collective-permute-done | bytes 147488 | tf_op jit(solution)/shard_map/ppermute | solution.py:44
  128.6 7.3 %collective-permute-done.17.two_ref = f32[1,192,768]{2,1,0:T(8,128)S(1)} collective-permute-done((f32[1,192,768]{2,1,0:T(8,128)S(1)}, f32[1,192,768]{2,1,0:T(8,128)S(1)}, u32[]{:S(2)}, u32[]{:S(2)}) %collective-permute-start.17) | collective-permute-done | bytes 589856 | tf_op jit(solution)/shard_map/ppermute | solution.py:44
  137.2 2.0 collective-permute-start.16
  139.2 3.1 %collective-permute-done.16.two_ref = f32[1,96,384]{2,1,0:T(8,128)S(1)} collective-permute-done((f32[1,96,384]{2,1,0:T(8,128)S(1)}, f32[1,96,384]{2,1,0:T(8,128)S(1)}, u32[]{:S(2)}, u32[]{:S(2)}) %collective-permute-start.16) | collective-permute-done | bytes 147488 | tf_op jit(solution)/shard_map/ppermute | solution.py:30
  143.0 3.9 %collective-permute-done.19.two_ref = f32[2,96,384]{2,1,0:T(8,128)S(1)} collective-permute-done((f32[2,96,384]{2,1,0:T(8,128)S(1)}, f32[2,96,384]{2,1,0:T(8,128)S(1)}, u32[]{:S(2)}, u32[]{:S(2)}) %collective-permute-start.19) | collective-permute-done | bytes 294944 | tf_op jit(solution)/shard_map/ppermute | solution.py:44
  146.9 3.0 %collective-permute-start.22 = (f32[2,192,384]{2,1,0:T(8,128)S(1)}, f32[2,192,384]{2,1,0:T(8,128)S(1)}, u32[]{:S(2)}, u32[]{:S(2)}) collective-permute-start(f32[2,192,384]{2,1,0:T(8,128)S(1)} %shard_map.80.token_ref.one_ref), channel_id=1, source_target_pairs={{0,2},{1,3},{2,0},{3,1},{4,6},{5,7},{6,4},{7,5},{8,9},{9,8},{10,11... | collective-permute-start | bytes 1769480 | tf_op jit(solution)/shard_map/ppermute | solution.py:44
  149.9 3.4 %collective-permute-start.18 = (f32[2,96,384]{2,1,0:T(8,128)S(1)}, f32[2,96,384]{2,1,0:T(8,128)S(1)}, u32[]{:S(2)}, u32[]{:S(2)}) collective-permute-start(f32[2,96,384]{2,1,0:T(8,128)S(1)} %shard_map.78.refs_0_.one_ref), channel_id=1, source_target_pairs={{0,4},{1,5},{2,6},{3,7},{4,0},{5,1},{6,2},{7,3},{8,12},{9,13},{10,... | collective-permute-start | bytes 884744 | tf_op jit(solution)/shard_map/ppermute | solution.py:44
  153.3 10.3 %collective-permute-done.18.two_ref = f32[2,96,384]{2,1,0:T(8,128)S(1)} collective-permute-done((f32[2,96,384]{2,1,0:T(8,128)S(1)}, f32[2,96,384]{2,1,0:T(8,128)S(1)}, u32[]{:S(2)}, u32[]{:S(2)}) %collective-permute-start.18) | collective-permute-done | bytes 294944 | tf_op jit(solution)/shard_map/ppermute | solution.py:44
  165.6 4.0 %collective-permute-start.20 = (f32[2,192,384]{2,1,0:T(8,128)S(1)}, f32[2,192,384]{2,1,0:T(8,128)S(1)}, u32[]{:S(2)}, u32[]{:S(2)}) collective-permute-start(f32[2,192,384]{2,1,0:T(8,128)S(1)} %shard_map.81.token_ref.one_ref), channel_id=1, source_target_pairs={{0,2},{1,3},{2,0},{3,1},{4,6},{5,7},{6,4},{7,5},{8,9},{9,8},{10,11... | collective-permute-start | bytes 1769480 | tf_op jit(solution)/shard_map/ppermute | solution.py:44
  170.3 1.5 shard_map.84.token_ref
  173.2 1.7 copy-done.15
  174.9 4.5 %shard_map.85 = (bf16[2,1,1536,768]{3,2,1,0:T(8,128)(2,1)}, f32[96,768]{1,0:T(8,128)S(1)}) custom-call(s32[4]{0:T(128)S(1)} %pad_add_fusion.state_ref, f32[1,768,256]{2,1,0:T(8,128)} %shard_map.84.token_ref, f32[1,768,768]{2,1,0:T(8,128)S(1)} %shard_map.83.refs_0_, f32[1,768,768]{2,1,0:T(8,128)S(1)} %copy-done.15), custom_call_target="tpu_custom_call" | custom-call | flops 1 | bytes 1 | tf_op jit(solution)/shard_map/pallas_call | solution.py:334
  179.4 5.0 %collective-permute-done.24.refs_1_ = f32[1,768,256]{2,1,0:T(8,128)S(1)} collective-permute-done((f32[1,768,256]{2,1,0:T(8,128)S(1)}, f32[1,768,256]{2,1,0:T(8,128)S(1)}, u32[]{:S(2)}, u32[]{:S(2)}) %collective-permute-start.24) | collective-permute-done | bytes 786464 | tf_op jit(solution)/shard_map/ppermute | solution.py:30
  189.9 1.5 shard_map.89.token_ref
  192.6 2.3 copy-done.7
  194.9 7.5 %shard_map.90 = (f32[2,768,1024]{2,1,0:T(8,128)}, f32[8,128]{1,0:T(8,128)S(1)}) custom-call(s32[2,2]{1,0:T(2,128)S(1)} %copy-done.21, s32[4]{0:T(128)S(1)} %pad_add_fusion.state_ref, bf16[2,1,1536,768]{3,2,1,0:T(8,128)(2,1)S(1)} %copy-done.7, f32[1,768,256]{2,1,0:T(8,128)} %shard_map.89.token_ref, f32[2,768,1024]{2,1,0:T(8,128)} %collective-permute-done.1.refs_0_), custom_call_target="tpu_custom_call" | custom-call | flops 1 | bytes 1 | tf_op jit(solution)/shard_map/pallas_call | solution.py:390
  202.4 7.7 %shard_map.91 = (f32[2,768,1024]{2,1,0:T(8,128)}, f32[8,128]{1,0:T(8,128)S(1)}) custom-call(s32[2,2]{1,0:T(2,128)S(1)} %copy-done.21, s32[4]{0:T(128)S(1)} %pad_add_fusion.state_ref, bf16[2,1,1536,768]{3,2,1,0:T(8,128)(2,1)S(1)} %copy-done.7, f32[8,128]{1,0:T(8,128)S(1)} %get-tuple-element.51.token_ref, ...), custom_call_target="tpu_custom_call", output_to_operand_aliasing={{0}: (5, {})} | custom-call | flops 1 | bytes 1 | tf_op jit(solution)/shard_map/pallas_call | solution.py:390
  212.9 1.7 copy-done.2
  214.5 4.5 %shard_map.94 = (bf16[2,1,1536,768]{3,2,1,0:T(8,128)(2,1)}, f32[96,768]{1,0:T(8,128)S(1)}) custom-call(s32[4]{0:T(128)S(1)} %pad_add_fusion.state_ref, f32[2,768,384]{2,1,0:T(8,128)S(1)} %copy-done.2, f32[2,768,384]{2,1,0:T(8,128)S(1)} %shard_map.88.refs_0_.refs_1_, f32[2,768,384]{2,1,0:T(8,128)S(1)} %shard_map.88.refs_0_.refs_1_, ...), custom_call_target="tpu_custom_call" | custom-call | flops 1 | bytes 1 | tf_op jit(solution)/shard_map/pallas_call | solution.py:334
  220.1 4.2 %collective-permute-done.28.refs_1_.refs_3_ = f32[1,768,256]{2,1,0:T(8,128)} collective-permute-done((f32[1,768,256]{2,1,0:T(8,128)}, f32[1,768,256]{2,1,0:T(8,128)}, u32[]{:S(2)}, u32[]{:S(2)}) %collective-permute-start.28) | collective-permute-done | bytes 786464 | tf_op jit(solution)/shard_map/ppermute | solution.py:30
  224.3 2.3 copy-done.5
  228.0 8.6 %shard_map.96 = (f32[2,768,1024]{2,1,0:T(8,128)}, f32[8,128]{1,0:T(8,128)S(1)}) custom-call(s32[2,2]{1,0:T(2,128)S(1)} %copy-done.21, s32[4]{0:T(128)S(1)} %pad_add_fusion.state_ref, bf16[2,1,1536,768]{3,2,1,0:T(8,128)(2,1)S(1)} %copy-done.5, f32[8,128]{1,0:T(8,128)S(1)} %shard_map.95.token_ref, ...), custom_call_target="tpu_custom_call", output_to_operand_aliasing={{0}: (6, {})} | custom-call | flops 1 | bytes 1 | tf_op jit(solution)/shard_map/pallas_call | solution.py:390
  236.8 1.8 collective-permute-start.30
  238.6 2.3 copy-done.6
  241.0 8.0 %shard_map.97 = (f32[2,768,1024]{2,1,0:T(8,128)}, f32[8,128]{1,0:T(8,128)}) custom-call(s32[2,2]{1,0:T(2,128)S(1)} %copy-done.21, s32[4]{0:T(128)S(1)} %pad_add_fusion.state_ref, bf16[2,1,1536,768]{3,2,1,0:T(8,128)(2,1)S(1)} %copy-done.6, f32[8,128]{1,0:T(8,128)S(1)} %get-tuple-element.57.token_ref, ...), custom_call_target="tpu_custom_call", output_to_operand_aliasing={{0}: (8, {})} | custom-call | flops 1 | bytes 1 | tf_op jit(solution)/shard_map/pallas_call | solution.py:390
  (126 shorter events, 31.1 us)
Async XLA Ops:
  0.6 10.6 %collective-permute-start.1 = (f32[2,768,1024]{2,1,0:T(8,128)}, f32[2,768,1024]{2,1,0:T(8,128)}, u32[]{:S(2)}, u32[]{:S(2)}) collective-permute-start(f32[2,768,1024]{2,1,0:T(8,128)} %source_ref.11), channel_id=1, source_target_pairs={{0,8},{8,0},{16,24},{24,16},{1,9},{9,1},{17,25},{25,17},{2,10},{10... | collective-permute-start | bytes 18874376 | tf_op jit(solution)/shard_map/ppermute | solution.py:30
  2.7 2.8 %copy-start = (f32[2,768,1024]{2,1,0:T(8,128)S(1)}, f32[2,768,1024]{2,1,0:T(8,128)}, u32[]{:S(2)}) copy-start(f32[2,768,1024]{2,1,0:T(8,128)} %source_ref.11) | copy-start | bytes 18874372
  6.9 4.4 %slice-start = ((s8[6291456]{0:T(1024)(128)(4,1)}), s8[4194304]{0:T(1024)(128)(4,1)S(1)}, s32[]{:S(2)}) async-start(s8[6291456]{0:T(1024)(128)(4,1)} %bitcast.6), calls=%async_computation | async-start | bytes 8388608
  7.6 3.7 %slice-start.1 = ((s8[6291456]{0:T(1024)(128)(4,1)}), s8[2097152]{0:T(1024)(128)(4,1)S(1)}, s32[]{:S(2)}) async-start(s8[6291456]{0:T(1024)(128)(4,1)} %bitcast.6), calls=%async_computation.1 | async-start | bytes 4194304
  7.6 3.7 %copy-start.21 = (s32[2,2]{1,0:T(2,128)S(1)}, s32[2,2]{1,0:T(2,128)}, u32[]{:S(2)}) copy-start(s32[2,2]{1,0:T(2,128)} %plan_ref.25) | copy-start | bytes 52
  7.6 38.6 %collective-permute-start = (f32[1,392,1024]{2,1,0:T(8,128)S(1)}, f32[1,392,1024]{2,1,0:T(8,128)S(1)}, u32[]{:S(2)}, u32[]{:S(2)}) collective-permute-start(f32[1,392,1024]{2,1,0:T(8,128)S(1)} %shard_map.59.refs_0_), channel_id=1, source_target_pairs={{0,16},{16,0},{8,24},{24,8},{1,17},{17,1},{9,25},{25,9},{2,18},{18... | collective-permute-start | bytes 4816904 | tf_op jit(solution)/shard_map/ppermute | solution.py:30
  18.6 17.1 %collective-permute-start.2 = (f32[1,384,768]{2,1,0:T(8,128)S(1)}, f32[1,384,768]{2,1,0:T(8,128)S(1)}, u32[]{:S(2)}, u32[]{:S(2)}) collective-permute-start(f32[1,384,768]{2,1,0:T(8,128)S(1)} %get-tuple-element.32.token_ref), channel_id=1, source_target_pairs={{0,1},{1,0},{2,3},{3,2},{4,5},{5,4},{6,7},{7,6},{8,10},{9,11},{10,... | collective-permute-start | bytes 3538952 | tf_op jit(solution)/shard_map/ppermute | solution.py:44
  21.6 58.1 %collective-permute-start.8 = (f32[1,384,1024]{2,1,0:T(8,128)S(1)}, f32[1,384,1024]{2,1,0:T(8,128)S(1)}, u32[]{:S(2)}, u32[]{:S(2)}) collective-permute-start(f32[1,384,1024]{2,1,0:T(8,128)S(1)} %shard_map.60.token_ref), channel_id=1, source_target_pairs={{0,16},{16,0},{8,24},{24,8},{1,17},{17,1},{9,25},{25,9},{2,18},{18... | collective-permute-start | bytes 4718600 | tf_op jit(solution)/shard_map/ppermute | solution.py:30
  35.9 16.1 %collective-permute-start.4 = (f32[1,192,768]{2,1,0:T(8,128)S(1)}, f32[1,192,768]{2,1,0:T(8,128)S(1)}, u32[]{:S(2)}, u32[]{:S(2)}) collective-permute-start(f32[1,192,768]{2,1,0:T(8,128)S(1)} %get-tuple-element.33.token_ref), channel_id=1, source_target_pairs={{0,2},{1,3},{2,0},{3,1},{4,6},{5,7},{6,4},{7,5},{8,9},{9,8},{10,11... | collective-permute-start | bytes 1769480 | tf_op jit(solution)/shard_map/ppermute | solution.py:44
  46.2 81.7 %copy-start.3 = (f32[1,392,1024]{2,1,0:T(8,128)}, f32[1,392,1024]{2,1,0:T(8,128)S(1)}, u32[]{:S(2)}) copy-start(f32[1,392,1024]{2,1,0:T(8,128)S(1)} %collective-permute-done.refs_0_.theirs_ref) | copy-start | bytes 4816900
  50.0 9.9 %collective-permute-start.3 = (f32[1,384,384]{2,1,0:T(8,128)S(1)}, f32[1,384,384]{2,1,0:T(8,128)S(1)}, u32[]{:S(2)}, u32[]{:S(2)}) collective-permute-start(f32[1,384,384]{2,1,0:T(8,128)S(1)} %get-tuple-element.35.token_ref), channel_id=1, source_target_pairs={{0,1},{1,0},{2,3},{3,2},{4,5},{5,4},{6,7},{7,6},{8,10},{9,11},{10,... | collective-permute-start | bytes 1769480 | tf_op jit(solution)/shard_map/ppermute | solution.py:44
  52.0 14.7 %copy-start.23 = (f32[768]{0:T(1024)S(1)}, f32[768]{0:T(1024)}, u32[]{:S(2)}) copy-start(f32[768]{0:T(1024)} %refs_1_.1) | copy-start | bytes 9220
  52.1 15.5 %collective-permute-start.7 = (f32[1,96,768]{2,1,0:T(8,128)S(1)}, f32[1,96,768]{2,1,0:T(8,128)S(1)}, u32[]{:S(2)}, u32[]{:S(2)}) collective-permute-start(f32[1,96,768]{2,1,0:T(8,128)S(1)} %get-tuple-element.37.token_ref), channel_id=1, source_target_pairs={{0,4},{1,5},{2,6},{3,7},{4,0},{5,1},{6,2},{7,3},{8,12},{9,13},{10,... | collective-permute-start | bytes 884744 | tf_op jit(solution)/shard_map/ppermute | solution.py:44
  60.0 8.3 %collective-permute-start.5 = (f32[1,192,384]{2,1,0:T(8,128)S(1)}, f32[1,192,384]{2,1,0:T(8,128)S(1)}, u32[]{:S(2)}, u32[]{:S(2)}) collective-permute-start(f32[1,192,384]{2,1,0:T(8,128)S(1)} %get-tuple-element.39.token_ref), channel_id=1, source_target_pairs={{0,2},{1,3},{2,0},{3,1},{4,6},{5,7},{6,4},{7,5},{8,9},{9,8},{10,11... | collective-permute-start | bytes 884744 | tf_op jit(solution)/shard_map/ppermute | solution.py:44
  62.1 5.5 %collective-permute-start.6 = (f32[1,6]{1,0:T(1,128)S(1)}, f32[1,6]{1,0:T(1,128)S(1)}, u32[]{:S(2)}, u32[]{:S(2)}) collective-permute-start(f32[1,6]{1,0:T(1,128)S(1)} %maximum_bitcast_fusion.ours_ref), channel_id=1, source_target_pairs={{0,8},{8,0},{16,24},{24,16},{1,9},{9,1},{17,25},{25,17},{2,10},{10... | collective-permute-start | bytes 80 | tf_op jit(solution)/shard_map/ppermute | solution.py:30
  79.6 3.8 %copy-start.8 = (f32[1,384,1024]{2,1,0:T(8,128)}, f32[1,384,1024]{2,1,0:T(8,128)S(1)}, u32[]{:S(2)}) copy-start(f32[1,384,1024]{2,1,0:T(8,128)S(1)} %collective-permute-done.8.refs_0_.refs_1_) | copy-start | bytes 4718596
  83.5 9.9 %collective-permute-start.9 = (f32[1,384,384]{2,1,0:T(8,128)S(1)}, f32[1,384,384]{2,1,0:T(8,128)S(1)}, u32[]{:S(2)}, u32[]{:S(2)}) collective-permute-start(f32[1,384,384]{2,1,0:T(8,128)S(1)} %get-tuple-element.43.token_ref), channel_id=1, source_target_pairs={{0,1},{1,0},{2,3},{3,2},{4,5},{5,4},{6,7},{7,6},{8,10},{9,11},{10,... | collective-permute-start | bytes 1769480 | tf_op jit(solution)/shard_map/ppermute | solution.py:44
  85.3 31.9 %collective-permute-start.12 = (f32[1,768,256]{2,1,0:T(8,128)S(1)}, f32[1,768,256]{2,1,0:T(8,128)S(1)}, u32[]{:S(2)}, u32[]{:S(2)}) collective-permute-start(f32[1,768,256]{2,1,0:T(8,128)S(1)} %shard_map.68.token_ref), channel_id=1, source_target_pairs={{0,16},{16,0},{8,24},{24,8},{1,17},{17,1},{9,25},{25,9},{2,18},{18... | collective-permute-start | bytes 2359304 | tf_op jit(solution)/shard_map/ppermute | solution.py:30
  93.5 23.6 %collective-permute-start.10 = (f32[1,192,384]{2,1,0:T(8,128)S(1)}, f32[1,192,384]{2,1,0:T(8,128)S(1)}, u32[]{:S(2)}, u32[]{:S(2)}) collective-permute-start(f32[1,192,384]{2,1,0:T(8,128)S(1)} %get-tuple-element.45.token_ref), channel_id=1, source_target_pairs={{0,2},{1,3},{2,0},{3,1},{4,6},{5,7},{6,4},{7,5},{8,9},{9,8},{10,11... | collective-permute-start | bytes 884744 | tf_op jit(solution)/shard_map/ppermute | solution.py:44
  95.4 21.8 %collective-permute-start.15 = (f32[1,96,768]{2,1,0:T(8,128)S(1)}, f32[1,96,768]{2,1,0:T(8,128)S(1)}, u32[]{:S(2)}, u32[]{:S(2)}) collective-permute-start(f32[1,96,768]{2,1,0:T(8,128)S(1)} %shard_map.66.token_ref.one_ref), channel_id=1, source_target_pairs={{0,4},{1,5},{2,6},{3,7},{4,0},{5,1},{6,2},{7,3},{8,12},{9,13},{10,... | collective-permute-start | bytes 884744 | tf_op jit(solution)/shard_map/ppermute | solution.py:44
  98.0 18.4 %collective-permute-start.11 = (f32[1,96,384]{2,1,0:T(8,128)S(1)}, f32[1,96,384]{2,1,0:T(8,128)S(1)}, u32[]{:S(2)}, u32[]{:S(2)}) collective-permute-start(f32[1,96,384]{2,1,0:T(8,128)S(1)} %get-tuple-element.41.refs_0_), channel_id=1, source_target_pairs={{0,4},{1,5},{2,6},{3,7},{4,0},{5,1},{6,2},{7,3},{8,12},{9,13},{10,... | collective-permute-start | bytes 442376 | tf_op jit(solution)/shard_map/ppermute | solution.py:44
  117.1 6.1 %copy-start.10 = (f32[1,768,256]{2,1,0:T(8,128)}, f32[1,768,256]{2,1,0:T(8,128)S(1)}, u32[]{:S(2)}) copy-start(f32[1,768,256]{2,1,0:T(8,128)S(1)} %collective-permute-done.12.refs_1_.refs_0_) | copy-start | bytes 2359300
  117.3 18.7 %collective-permute-start.17 = (f32[1,192,768]{2,1,0:T(8,128)S(1)}, f32[1,192,768]{2,1,0:T(8,128)S(1)}, u32[]{:S(2)}, u32[]{:S(2)}) collective-permute-start(f32[1,192,768]{2,1,0:T(8,128)S(1)} %shard_map.74.token_ref.one_ref), channel_id=1, source_target_pairs={{0,2},{1,3},{2,0},{3,1},{4,6},{5,7},{6,4},{7,5},{8,9},{9,8},{10,11... | collective-permute-start | bytes 1769480 | tf_op jit(solution)/shard_map/ppermute | solution.py:44
  118.0 5.1 %collective-permute-start.14 = (f32[1,96,384]{2,1,0:T(8,128)S(1)}, f32[1,96,384]{2,1,0:T(8,128)S(1)}, u32[]{:S(2)}, u32[]{:S(2)}) collective-permute-start(f32[1,96,384]{2,1,0:T(8,128)S(1)} %shard_map.71.refs_0_.one_ref), channel_id=1, source_target_pairs={{0,16},{16,0},{8,24},{24,8},{1,17},{17,1},{9,25},{25,9},{2,18},{18... | collective-permute-start | bytes 442376 | tf_op jit(solution)/shard_map/ppermute | solution.py:30
  119.5 8.3 %collective-permute-start.13 = (f32[1,96,384]{2,1,0:T(8,128)S(1)}, f32[1,96,384]{2,1,0:T(8,128)S(1)}, u32[]{:S(2)}, u32[]{:S(2)}) collective-permute-start(f32[1,96,384]{2,1,0:T(8,128)S(1)} %get-tuple-element.48.token_ref), channel_id=1, source_target_pairs={{0,4},{1,5},{2,6},{3,7},{4,0},{5,1},{6,2},{7,3},{8,12},{9,13},{10,... | collective-permute-start | bytes 442376 | tf_op jit(solution)/shard_map/ppermute | solution.py:44
  136.0 28.2 %collective-permute-start.21 = (f32[1,384,768]{2,1,0:T(8,128)S(1)}, f32[1,384,768]{2,1,0:T(8,128)S(1)}, u32[]{:S(2)}, u32[]{:S(2)}) collective-permute-start(f32[1,384,768]{2,1,0:T(8,128)S(1)} %shard_map.77.token_ref.one_ref), channel_id=1, source_target_pairs={{0,1},{1,0},{2,3},{3,2},{4,5},{5,4},{6,7},{7,6},{8,10},{9,11},{10,... | collective-permute-start | bytes 3538952 | tf_op jit(solution)/shard_map/ppermute | solution.py:44
  136.1 10.8 %collective-permute-start.19 = (f32[2,96,384]{2,1,0:T(8,128)S(1)}, f32[2,96,384]{2,1,0:T(8,128)S(1)}, u32[]{:S(2)}, u32[]{:S(2)}) collective-permute-start(f32[2,96,384]{2,1,0:T(8,128)S(1)} %shard_map.75.token_ref.one_ref), channel_id=1, source_target_pairs={{0,4},{1,5},{2,6},{3,7},{4,0},{5,1},{6,2},{7,3},{8,12},{9,13},{10,... | collective-permute-start | bytes 884744 | tf_op jit(solution)/shard_map/ppermute | solution.py:44
  137.2 5.2 %collective-permute-start.16 = (f32[1,96,384]{2,1,0:T(8,128)S(1)}, f32[1,96,384]{2,1,0:T(8,128)S(1)}, u32[]{:S(2)}, u32[]{:S(2)}) collective-permute-start(f32[1,96,384]{2,1,0:T(8,128)S(1)} %shard_map.76.token_ref.one_ref), channel_id=1, source_target_pairs={{0,16},{16,0},{8,24},{24,8},{1,17},{17,1},{9,25},{25,9},{2,18},{18... | collective-permute-start | bytes 442376 | tf_op jit(solution)/shard_map/ppermute | solution.py:30
  146.9 17.2 %collective-permute-start.22 = (f32[2,192,384]{2,1,0:T(8,128)S(1)}, f32[2,192,384]{2,1,0:T(8,128)S(1)}, u32[]{:S(2)}, u32[]{:S(2)}) collective-permute-start(f32[2,192,384]{2,1,0:T(8,128)S(1)} %shard_map.80.token_ref.one_ref), channel_id=1, source_target_pairs={{0,2},{1,3},{2,0},{3,1},{4,6},{5,7},{6,4},{7,5},{8,9},{9,8},{10,11... | collective-permute-start | bytes 1769480 | tf_op jit(solution)/shard_map/ppermute | solution.py:44
  149.9 13.7 %collective-permute-start.18 = (f32[2,96,384]{2,1,0:T(8,128)S(1)}, f32[2,96,384]{2,1,0:T(8,128)S(1)}, u32[]{:S(2)}, u32[]{:S(2)}) collective-permute-start(f32[2,96,384]{2,1,0:T(8,128)S(1)} %shard_map.78.refs_0_.one_ref), channel_id=1, source_target_pairs={{0,4},{1,5},{2,6},{3,7},{4,0},{5,1},{6,2},{7,3},{8,12},{9,13},{10,... | collective-permute-start | bytes 884744 | tf_op jit(solution)/shard_map/ppermute | solution.py:44
  164.3 7.5 %collective-permute-start.23 = (f32[1,768,768]{2,1,0:T(8,128)S(1)}, f32[1,768,768]{2,1,0:T(8,128)S(1)}, u32[]{:S(2)}, u32[]{:S(2)}) collective-permute-start(f32[1,768,768]{2,1,0:T(8,128)S(1)} %shard_map.83.refs_0_), channel_id=1, source_target_pairs={{0,8},{8,0},{16,24},{24,16},{1,9},{9,1},{17,25},{25,17},{2,10},{10... | collective-permute-start | bytes 7077896 | tf_op jit(solution)/shard_map/ppermute | solution.py:30
  164.4 20.0 %collective-permute-start.24 = (f32[1,768,256]{2,1,0:T(8,128)S(1)}, f32[1,768,256]{2,1,0:T(8,128)S(1)}, u32[]{:S(2)}, u32[]{:S(2)}) collective-permute-start(f32[1,768,256]{2,1,0:T(8,128)S(1)} %shard_map.79.token_ref), channel_id=1, source_target_pairs={{0,16},{16,0},{8,24},{24,8},{1,17},{17,1},{9,25},{25,9},{2,18},{18... | collective-permute-start | bytes 2359304 | tf_op jit(solution)/shard_map/ppermute | solution.py:30
  165.6 18.8 %collective-permute-start.20 = (f32[2,192,384]{2,1,0:T(8,128)S(1)}, f32[2,192,384]{2,1,0:T(8,128)S(1)}, u32[]{:S(2)}, u32[]{:S(2)}) collective-permute-start(f32[2,192,384]{2,1,0:T(8,128)S(1)} %shard_map.81.token_ref.one_ref), channel_id=1, source_target_pairs={{0,2},{1,3},{2,0},{3,1},{4,6},{5,7},{6,4},{7,5},{8,9},{9,8},{10,11... | collective-permute-start | bytes 1769480 | tf_op jit(solution)/shard_map/ppermute | solution.py:44
  169.6 18.9 %collective-permute-start.26 = (f32[2,384,384]{2,1,0:T(8,128)S(1)}, f32[2,384,384]{2,1,0:T(8,128)}, u32[]{:S(2)}, u32[]{:S(2)}) collective-permute-start(f32[2,384,384]{2,1,0:T(8,128)S(1)} %shard_map.82.token_ref.one_ref), channel_id=1, source_target_pairs={{0,1},{1,0},{2,3},{3,2},{4,5},{5,4},{6,7},{7,6},{8,10},{9,11},{10,... | collective-permute-start | bytes 3538952 | tf_op jit(solution)/shard_map/ppermute | solution.py:44
  179.4 7.0 %copy-start.16 = (f32[96,768]{1,0:T(8,128)}, f32[96,768]{1,0:T(8,128)S(1)}, u32[]{:S(2)}) copy-start(f32[96,768]{1,0:T(8,128)S(1)} %get-tuple-element.49.refs_0_) | copy-start | bytes 884740
  186.4 23.7 %collective-permute-start.25 = (f32[2,384,384]{2,1,0:T(8,128)S(1)}, f32[2,384,384]{2,1,0:T(8,128)}, u32[]{:S(2)}, u32[]{:S(2)}) collective-permute-start(f32[2,384,384]{2,1,0:T(8,128)S(1)} %shard_map.87.token_ref.one_ref), channel_id=1, source_target_pairs={{0,1},{1,0},{2,3},{3,2},{4,5},{5,4},{6,7},{7,6},{8,10},{9,11},{10,... | collective-permute-start | bytes 3538952 | tf_op jit(solution)/shard_map/ppermute | solution.py:44
  187.6 22.5 %collective-permute-start.27 = (f32[1,768,256]{2,1,0:T(8,128)}, f32[1,768,256]{2,1,0:T(8,128)}, u32[]{:S(2)}, u32[]{:S(2)}) collective-permute-start(f32[1,768,256]{2,1,0:T(8,128)} %shard_map.84.token_ref), channel_id=1, source_target_pairs={{0,16},{16,0},{8,24},{24,8},{1,17},{17,1},{9,25},{25,9},{2,18},{18... | collective-permute-start | bytes 2359304 | tf_op jit(solution)/shard_map/ppermute | solution.py:30
  191.5 32.8 %collective-permute-start.28 = (f32[1,768,256]{2,1,0:T(8,128)}, f32[1,768,256]{2,1,0:T(8,128)}, u32[]{:S(2)}, u32[]{:S(2)}) collective-permute-start(f32[1,768,256]{2,1,0:T(8,128)} %shard_map.89.token_ref), channel_id=1, source_target_pairs={{0,16},{16,0},{8,24},{24,8},{1,17},{17,1},{9,25},{25,9},{2,18},{18... | collective-permute-start | bytes 2359304 | tf_op jit(solution)/shard_map/ppermute | solution.py:30
  214.5 4.5 %copy-start.17 = (f32[96,768]{1,0:T(8,128)S(1)}, f32[96,768]{1,0:T(8,128)}, u32[]{:S(2)}) copy-start(f32[96,768]{1,0:T(8,128)} %copy-done.16) | copy-start | bytes 884740
  219.0 5.3 %copy-start.4 = (f32[1,392,1024]{2,1,0:T(8,128)S(1)}, f32[1,392,1024]{2,1,0:T(8,128)}, u32[]{:S(2)}) copy-start(f32[1,392,1024]{2,1,0:T(8,128)} %copy-done.3) | copy-start | bytes 4816900
  219.0 5.2 %copy-start.24 = (f32[96,768]{1,0:T(8,128)}, f32[96,768]{1,0:T(8,128)S(1)}, u32[]{:S(2)}) copy-start(f32[96,768]{1,0:T(8,128)S(1)} %add.44) | copy-start | bytes 884740
  219.1 17.5 %collective-permute-start.29 = (f32[96,384]{1,0:T(8,128)S(1)}, f32[96,384]{1,0:T(8,128)S(1)}, u32[]{:S(2)}, u32[]{:S(2)}) collective-permute-start(f32[96,384]{1,0:T(8,128)S(1)} %constant_dynamic-slice_fusion.1), channel_id=1, source_target_pairs={{0,16},{16,0},{8,24},{24,8},{1,17},{17,1},{9,25},{25,9},{2,18},{18... | collective-permute-start | bytes 442376 | tf_op jit(solution)/shard_map/ppermute | solution.py:30
  224.3 2.3 copy-start.5
  228.0 8.6 %copy-start.25 = (f32[96,768]{1,0:T(8,128)S(1)}, f32[96,768]{1,0:T(8,128)}, u32[]{:S(2)}) copy-start(f32[96,768]{1,0:T(8,128)} %copy-done.24) | copy-start | bytes 884740
  228.0 10.6 %copy-start.11 = (f32[1,768,256]{2,1,0:T(8,128)S(1)}, f32[1,768,256]{2,1,0:T(8,128)}, u32[]{:S(2)}) copy-start(f32[1,768,256]{2,1,0:T(8,128)} %copy-done.10) | copy-start | bytes 2359300
  228.0 10.6 %copy-start.13 = (f32[1,768,256]{2,1,0:T(8,128)S(1)}, f32[1,768,256]{2,1,0:T(8,128)}, u32[]{:S(2)}) copy-start(f32[1,768,256]{2,1,0:T(8,128)} %copy-done.12) | copy-start | bytes 2359300
  236.8 12.2 %collective-permute-start.30 = (f32[96,192]{1,0:T(8,128)S(1)}, f32[96,192]{1,0:T(8,128)S(1)}, u32[]{:S(2)}, u32[]{:S(2)}) collective-permute-start(f32[96,192]{1,0:T(8,128)S(1)} %constant_dynamic-slice_fusion), channel_id=1, source_target_pairs={{0,8},{8,0},{16,24},{24,16},{1,9},{9,1},{17,25},{25,17},{2,10},{10... | collective-permute-start | bytes 221192 | tf_op jit(solution)/shard_map/ppermute | solution.py:30
  238.6 2.3 copy-start.6
  (11 other events, 15.2 us)

commit v10 on v8

--- a/solution.py
+++ b/solution.py
@@ -570,7 +570,7 @@
     for turn in range(rounds):
         steps = [make_tilde(turn), add_terms(turn, True), add_terms(turn, False)]
         if turn == 0 and rounds > 1:
-            times = [119.5, 121.0, 122.0] if tuned else [time + 1 for time in late[cuts][-4:-1]]
+            times = [119.5, 119.6, 122.0] if tuned else [time + 1 for time in late[cuts][-4:-1]]
             tasks += list(zip(times, steps))
         else:
             tasks += [(late[-1][-1] + 6 + index, step_) for index, step_ in enumerate(steps)]

time: 248 us -> 252 us (1.016)
  local copies, waits for them, and re-layouts: 22 us -> 25.2 us
    unnamed x56 -> x58, local copies, waits for them, and re-layouts: 21.6 us -> 24.9 us
where the time goes in v10:
time: 252 us; the launch traced here: 251 us
  waiting for transfers between devices  106 us (42%)
  Pallas kernels  68.4 us (27%)
  starting transfers between devices  48.1 us (19%)
  local copies, waits for them, and re-layouts  25.2 us (10%)
    ppermute x18, waiting for transfers between devices, across(): return lax.ppermute(block, ('pair', 'aux'), route)  63.7 us
    ppermute x13, waiting for transfers between devices, swapped(): return lax.ppermute(block, axis, route)  42.4 us
    pallas_call x4, Pallas kernels, gradient_terms(): pl.pallas_call(functools.partial(gradient_kernel, len(sources), turn > 0,...  31.7 us
    unnamed x58, local copies, waits for them, and re-layouts  24.9 us
    ppermute x13, starting transfers between devices, swapped(): return lax.ppermute(block, axis, route)  24.4 us
    ppermute x18, starting transfers between devices, across(): return lax.ppermute(block, ('pair', 'aux'), route)  23.8 us
    pallas_call x3, Pallas kernels, integral(): pl.pallas_call(functools.partial(integral_kernel, turn, blocks), out_shap...  15 us
    pallas_call x2, Pallas kernels, tildes(): pl.pallas_call(functools.partial(tilde_kernel, blocks, places), out_shape...  8.93 us
  transfers between devices with their start and end apart: 31, of which 17 were waited for; matrix products, arithmetic and copies ran while one was open for 1% of the time, Pallas kernels for 26%

profile of v10, /device:TPU:0, one launch (start us, length us, event | category | flops | bytes accessed | tf_op | source)
XLA Modules:
  0.0 251.2 jit_solution(7205970835318126507)
XLA Ops:
  2.7 2.8 %copy-done = f32[2,768,1024]{2,1,0:T(8,128)S(1)} copy-done((f32[2,768,1024]{2,1,0:T(8,128)S(1)}, f32[2,768,1024]{2,1,0:T(8,128)}, u32[]{:S(2)}) %copy-start) | copy-done | bytes 6291480
  7.6 2.6 %collective-permute-start = (f32[1,392,1024]{2,1,0:T(8,128)S(1)}, f32[1,392,1024]{2,1,0:T(8,128)S(1)}, u32[]{:S(2)}, u32[]{:S(2)}) collective-permute-start(f32[1,392,1024]{2,1,0:T(8,128)S(1)} %shard_map.59.refs_0_), channel_id=1, source_target_pairs={{0,16},{16,0},{8,24},{24,8},{1,17},{17,1},{9,25},{25,9},{2,18},{18... | collective-permute-start | bytes 4816904 | tf_op jit(solution)/shard_map/ppermute | solution.py:30
  11.3 7.3 %shard_map.61 = (f32[1,384,768]{2,1,0:T(8,128)S(1)}, f32[1,384,768]{2,1,0:T(8,128)S(1)}) custom-call(s32[2,2]{1,0:T(2,128)S(1)} %copy-done.22, s32[4]{0:T(128)S(1)} %pad_add_fusion.state_ref, f32[2,768,1024]{2,1,0:T(8,128)S(1)} %bitcast.7, f32[1,384,1024]{2,1,0:T(8,128)S(1)} %shard_map.60.token_ref, f32[2,768,1024]{2,1,0:T(8,128)} %collective-permute-done.1.refs_0_), custom_call_target="tpu_custom_call" | custom-call | flops 1 | bytes 1 | tf_op jit(solution)/shard_map/pallas_call | solution.py:196
  18.6 2.9 %collective-permute-start.2 = (f32[1,384,768]{2,1,0:T(8,128)S(1)}, f32[1,384,768]{2,1,0:T(8,128)S(1)}, u32[]{:S(2)}, u32[]{:S(2)}) collective-permute-start(f32[1,384,768]{2,1,0:T(8,128)S(1)} %get-tuple-element.32.token_ref), channel_id=1, source_target_pairs={{0,1},{1,0},{2,3},{3,2},{4,5},{5,4},{6,7},{7,6},{8,10},{9,11},{10,... | collective-permute-start | bytes 3538952 | tf_op jit(solution)/shard_map/ppermute | solution.py:44
  21.6 1.5 collective-permute-start.8
  23.1 12.7 %collective-permute-done.2.came_ref = f32[1,384,768]{2,1,0:T(8,128)S(1)} collective-permute-done((f32[1,384,768]{2,1,0:T(8,128)S(1)}, f32[1,384,768]{2,1,0:T(8,128)S(1)}, u32[]{:S(2)}, u32[]{:S(2)}) %collective-permute-start.2) | collective-permute-done | bytes 1179680 | tf_op jit(solution)/shard_map/ppermute | solution.py:44
  35.9 2.2 collective-permute-start.4
  38.1 8.1 %collective-permute-done.refs_0_.theirs_ref = f32[1,392,1024]{2,1,0:T(8,128)S(1)} collective-permute-done((f32[1,392,1024]{2,1,0:T(8,128)S(1)}, f32[1,392,1024]{2,1,0:T(8,128)S(1)}, u32[]{:S(2)}, u32[]{:S(2)}) %collective-permute-start) | collective-permute-done | bytes 1605664 | tf_op jit(solution)/shard_map/ppermute | solution.py:30
  46.2 3.8 %shard_map.63 = (f32[1,384,384]{2,1,0:T(8,128)S(1)}, f32[1,384,384]{2,1,0:T(8,128)S(1)}) custom-call(s32[2,2]{1,0:T(2,128)S(1)} %copy-done.22, s32[4]{0:T(128)S(1)} %pad_add_fusion.state_ref, f32[2,768,1024]{2,1,0:T(8,128)S(1)} %bitcast.7, f32[1,192,768]{2,1,0:T(8,128)S(1)} %get-tuple-element.33.token_ref, ...), custom_call_target="tpu_custom_call" | custom-call | flops 1 | bytes 1 | tf_op jit(solution)/shard_map/pallas_call | solution.py:196
  50.0 2.0 collective-permute-start.3
  52.1 2.7 %collective-permute-start.7 = (f32[1,96,768]{2,1,0:T(8,128)S(1)}, f32[1,96,768]{2,1,0:T(8,128)S(1)}, u32[]{:S(2)}, u32[]{:S(2)}) collective-permute-start(f32[1,96,768]{2,1,0:T(8,128)S(1)} %get-tuple-element.37.token_ref), channel_id=1, source_target_pairs={{0,4},{1,5},{2,6},{3,7},{4,0},{5,1},{6,2},{7,3},{8,12},{9,13},{10,... | collective-permute-start | bytes 884744 | tf_op jit(solution)/shard_map/ppermute | solution.py:44
  54.7 5.2 %collective-permute-done.3.came_ref = f32[1,384,384]{2,1,0:T(8,128)S(1)} collective-permute-done((f32[1,384,384]{2,1,0:T(8,128)S(1)}, f32[1,384,384]{2,1,0:T(8,128)S(1)}, u32[]{:S(2)}, u32[]{:S(2)}) %collective-permute-start.3) | collective-permute-done | bytes 589856 | tf_op jit(solution)/shard_map/ppermute | solution.py:44
  60.0 2.1 collective-permute-start.5
  62.1 4.6 %collective-permute-start.6 = (f32[1,6]{1,0:T(1,128)S(1)}, f32[1,6]{1,0:T(1,128)S(1)}, u32[]{:S(2)}, u32[]{:S(2)}) collective-permute-start(f32[1,6]{1,0:T(1,128)S(1)} %maximum_bitcast_fusion.ours_ref), channel_id=1, source_target_pairs={{0,8},{8,0},{16,24},{24,16},{1,9},{9,1},{17,25},{25,17},{2,10},{10... | collective-permute-start | bytes 80 | tf_op jit(solution)/shard_map/ppermute | solution.py:30
  68.4 11.2 %collective-permute-done.8.refs_0_.refs_1_ = f32[1,384,1024]{2,1,0:T(8,128)S(1)} collective-permute-done((f32[1,384,1024]{2,1,0:T(8,128)S(1)}, f32[1,384,1024]{2,1,0:T(8,128)S(1)}, u32[]{:S(2)}, u32[]{:S(2)}) %collective-permute-start.8) | collective-permute-done | bytes 1572896 | tf_op jit(solution)/shard_map/ppermute | solution.py:30
  79.6 3.8 %shard_map.68 = (f32[1,384,384]{2,1,0:T(8,128)S(1)}, f32[1,384,384]{2,1,0:T(8,128)S(1)}) custom-call(s32[2,2]{1,0:T(2,128)S(1)} %copy-done.22, s32[4]{0:T(128)S(1)} %pad_add_fusion.state_ref, f32[2,768,1024]{2,1,0:T(8,128)S(1)} %bitcast.7, f32[1,96,384]{2,1,0:T(8,128)S(1)} %get-tuple-element.41.token_ref, ...), custom_call_target="tpu_custom_call" | custom-call | flops 1 | bytes 1 | tf_op jit(solution)/shard_map/pallas_call | solution.py:196
  83.5 1.8 collective-permute-start.9
  85.3 2.6 %collective-permute-start.12 = (f32[1,96,768]{2,1,0:T(8,128)S(1)}, f32[1,96,768]{2,1,0:T(8,128)S(1)}, u32[]{:S(2)}, u32[]{:S(2)}) collective-permute-start(f32[1,96,768]{2,1,0:T(8,128)S(1)} %shard_map.66.token_ref.one_ref), channel_id=1, source_target_pairs={{0,4},{1,5},{2,6},{3,7},{4,0},{5,1},{6,2},{7,3},{8,12},{9,13},{10,... | collective-permute-start | bytes 884744 | tf_op jit(solution)/shard_map/ppermute | solution.py:44
  88.2 19.0 %collective-permute-done.10.right_ref = f32[1,96,384]{2,1,0:T(8,128)S(1)} collective-permute-done((f32[1,96,384]{2,1,0:T(8,128)S(1)}, f32[1,96,384]{2,1,0:T(8,128)S(1)}, u32[]{:S(2)}, u32[]{:S(2)}) %collective-permute-start.10) | collective-permute-done | bytes 147488 | tf_op jit(solution)/shard_map/ppermute | solution.py:44
  108.2 1.6 collective-permute-start.11
  109.8 5.2 %collective-permute-done.11.two_ref = f32[1,96,384]{2,1,0:T(8,128)S(1)} collective-permute-done((f32[1,96,384]{2,1,0:T(8,128)S(1)}, f32[1,96,384]{2,1,0:T(8,128)S(1)}, u32[]{:S(2)}, u32[]{:S(2)}) %collective-permute-start.11) | collective-permute-done | bytes 147488 | tf_op jit(solution)/shard_map/ppermute | solution.py:30
  116.1 6.3 %collective-permute-done.13.came_ref = f32[1,192,384]{2,1,0:T(8,128)S(1)} collective-permute-done((f32[1,192,384]{2,1,0:T(8,128)S(1)}, f32[1,192,384]{2,1,0:T(8,128)S(1)}, u32[]{:S(2)}, u32[]{:S(2)}) %collective-permute-start.13) | collective-permute-done | bytes 294944 | tf_op jit(solution)/shard_map/ppermute | solution.py:44
  124.4 3.6 %collective-permute-start.15 = (f32[2,96,384]{2,1,0:T(8,128)S(1)}, f32[2,96,384]{2,1,0:T(8,128)S(1)}, u32[]{:S(2)}, u32[]{:S(2)}) collective-permute-start(f32[2,96,384]{2,1,0:T(8,128)S(1)} %shard_map.71.refs_0_.one_ref), channel_id=1, source_target_pairs={{0,4},{1,5},{2,6},{3,7},{4,0},{5,1},{6,2},{7,3},{8,12},{9,13},{10,... | collective-permute-start | bytes 884744 | tf_op jit(solution)/shard_map/ppermute | solution.py:44
  128.0 10.6 %collective-permute-done.15.two_ref = f32[2,96,384]{2,1,0:T(8,128)S(1)} collective-permute-done((f32[2,96,384]{2,1,0:T(8,128)S(1)}, f32[2,96,384]{2,1,0:T(8,128)S(1)}, u32[]{:S(2)}, u32[]{:S(2)}) %collective-permute-start.15) | collective-permute-done | bytes 294944 | tf_op jit(solution)/shard_map/ppermute | solution.py:44
  138.7 2.0 collective-permute-done.14.right_ref
  143.3 3.4 %collective-permute-done.17.two_ref = f32[1,96,384]{2,1,0:T(8,128)S(1)} collective-permute-done((f32[1,96,384]{2,1,0:T(8,128)S(1)}, f32[1,96,384]{2,1,0:T(8,128)S(1)}, u32[]{:S(2)}, u32[]{:S(2)}) %collective-permute-start.17) | collective-permute-done | bytes 147488 | tf_op jit(solution)/shard_map/ppermute | solution.py:30
  148.1 1.5 shard_map.80.token_ref
  149.6 3.9 %collective-permute-done.20.two_ref = f32[2,192,384]{2,1,0:T(8,128)S(1)} collective-permute-done((f32[2,192,384]{2,1,0:T(8,128)S(1)}, f32[2,192,384]{2,1,0:T(8,128)S(1)}, u32[]{:S(2)}, u32[]{:S(2)}) %collective-permute-start.20) | collective-permute-done | bytes 589856 | tf_op jit(solution)/shard_map/ppermute | solution.py:44
  153.6 4.0 %collective-permute-done.19.two_ref = f32[2,96,384]{2,1,0:T(8,128)S(1)} collective-permute-done((f32[2,96,384]{2,1,0:T(8,128)S(1)}, f32[2,96,384]{2,1,0:T(8,128)S(1)}, u32[]{:S(2)}, u32[]{:S(2)}) %collective-permute-start.19) | collective-permute-done | bytes 294944 | tf_op jit(solution)/shard_map/ppermute | solution.py:44
  157.8 6.8 %collective-permute-start.23 = (f32[1,768,768]{2,1,0:T(8,128)S(1)}, f32[1,768,768]{2,1,0:T(8,128)S(1)}, u32[]{:S(2)}, u32[]{:S(2)}) collective-permute-start(f32[1,768,768]{2,1,0:T(8,128)S(1)} %shard_map.83.refs_0_), channel_id=1, source_target_pairs={{0,8},{8,0},{16,24},{24,16},{1,9},{9,1},{17,25},{25,17},{2,10},{10... | collective-permute-start | bytes 7077896 | tf_op jit(solution)/shard_map/ppermute | solution.py:30
  166.4 1.5 shard_map.84.token_ref
  170.2 1.7 copy-done.16
  171.8 4.5 %shard_map.85 = (bf16[2,1,1536,768]{3,2,1,0:T(8,128)(2,1)}, f32[96,768]{1,0:T(8,128)S(1)}) custom-call(s32[4]{0:T(128)S(1)} %pad_add_fusion.state_ref, f32[1,768,256]{2,1,0:T(8,128)} %shard_map.84.token_ref, f32[1,768,768]{2,1,0:T(8,128)S(1)} %shard_map.83.refs_0_, f32[1,768,768]{2,1,0:T(8,128)S(1)} %copy-done.16), custom_call_target="tpu_custom_call" | custom-call | flops 1 | bytes 1 | tf_op jit(solution)/shard_map/pallas_call | solution.py:334
  176.3 2.4 copy-done.7
  178.7 7.5 %shard_map.86 = (f32[2,768,1024]{2,1,0:T(8,128)}, f32[8,128]{1,0:T(8,128)S(1)}) custom-call(s32[2,2]{1,0:T(2,128)S(1)} %copy-done.22, s32[4]{0:T(128)S(1)} %pad_add_fusion.state_ref, bf16[2,1,1536,768]{3,2,1,0:T(8,128)(2,1)S(1)} %copy-done.7, f32[96,768]{1,0:T(8,128)S(1)} %get-tuple-element.50.token_ref, f32[2,768,1024]{2,1,0:T(8,128)} %collective-permute-done.1.refs_0_), custom_call_target="tpu_custom_call" | custom-call | flops 1 | bytes 1 | tf_op jit(solution)/shard_map/pallas_call | solution.py:390
  190.8 1.4 shard_map.89.refs_0_.refs_1_
  192.3 1.5 shard_map.90.token_ref
  194.9 2.3 copy-done.8
  197.2 7.7 %shard_map.91 = (f32[2,768,1024]{2,1,0:T(8,128)}, f32[8,128]{1,0:T(8,128)S(1)}) custom-call(s32[2,2]{1,0:T(2,128)S(1)} %copy-done.22, s32[4]{0:T(128)S(1)} %pad_add_fusion.state_ref, bf16[2,1,1536,768]{3,2,1,0:T(8,128)(2,1)S(1)} %copy-done.8, f32[1,768,256]{2,1,0:T(8,128)} %shard_map.90.token_ref, ...), custom_call_target="tpu_custom_call", output_to_operand_aliasing={{0}: (5, {})} | custom-call | flops 1 | bytes 1 | tf_op jit(solution)/shard_map/pallas_call | solution.py:390
  204.9 5.8 %collective-permute-done.27.refs_1_.refs_2_ = f32[1,768,256]{2,1,0:T(8,128)} collective-permute-done((f32[1,768,256]{2,1,0:T(8,128)}, f32[1,768,256]{2,1,0:T(8,128)}, u32[]{:S(2)}, u32[]{:S(2)}) %collective-permute-start.27) | collective-permute-done | bytes 786464 | tf_op jit(solution)/shard_map/ppermute | solution.py:30
  210.6 1.4 shard_map.93.token_ref.refs_2_.refs_3_
  213.5 1.7 copy-done.2
  215.1 4.5 %shard_map.94 = (bf16[2,1,1536,768]{3,2,1,0:T(8,128)(2,1)}, f32[96,768]{1,0:T(8,128)S(1)}) custom-call(s32[4]{0:T(128)S(1)} %pad_add_fusion.state_ref, f32[2,768,384]{2,1,0:T(8,128)S(1)} %copy-done.2, f32[2,768,384]{2,1,0:T(8,128)S(1)} %shard_map.89.refs_0_.refs_1_, f32[2,768,384]{2,1,0:T(8,128)S(1)} %shard_map.89.refs_0_.refs_1_, ...), custom_call_target="tpu_custom_call" | custom-call | flops 1 | bytes 1 | tf_op jit(solution)/shard_map/pallas_call | solution.py:334
  220.7 6.8 %collective-permute-done.28.refs_1_.refs_3_ = f32[1,768,256]{2,1,0:T(8,128)} collective-permute-done((f32[1,768,256]{2,1,0:T(8,128)}, f32[1,768,256]{2,1,0:T(8,128)}, u32[]{:S(2)}, u32[]{:S(2)}) %collective-permute-start.28) | collective-permute-done | bytes 786464 | tf_op jit(solution)/shard_map/ppermute | solution.py:30
  227.5 2.3 copy-done.5
  231.3 8.6 %shard_map.96 = (f32[2,768,1024]{2,1,0:T(8,128)}, f32[8,128]{1,0:T(8,128)S(1)}) custom-call(s32[2,2]{1,0:T(2,128)S(1)} %copy-done.22, s32[4]{0:T(128)S(1)} %pad_add_fusion.state_ref, bf16[2,1,1536,768]{3,2,1,0:T(8,128)(2,1)S(1)} %copy-done.5, f32[8,128]{1,0:T(8,128)S(1)} %shard_map.95.token_ref, ...), custom_call_target="tpu_custom_call", output_to_operand_aliasing={{0}: (6, {})} | custom-call | flops 1 | bytes 1 | tf_op jit(solution)/shard_map/pallas_call | solution.py:390
  240.1 2.3 copy-done.6
  242.4 8.0 %shard_map.97 = (f32[2,768,1024]{2,1,0:T(8,128)}, f32[8,128]{1,0:T(8,128)}) custom-call(s32[2,2]{1,0:T(2,128)S(1)} %copy-done.22, s32[4]{0:T(128)S(1)} %pad_add_fusion.state_ref, bf16[2,1,1536,768]{3,2,1,0:T(8,128)(2,1)S(1)} %copy-done.6, f32[8,128]{1,0:T(8,128)S(1)} %get-tuple-element.57.token_ref, ...), custom_call_target="tpu_custom_call", output_to_operand_aliasing={{0}: (8, {})} | custom-call | flops 1 | bytes 1 | tf_op jit(solution)/shard_map/pallas_call | solution.py:390
  (128 shorter events, 30.4 us)
Async XLA Ops:
  0.6 10.6 %collective-permute-start.1 = (f32[2,768,1024]{2,1,0:T(8,128)}, f32[2,768,1024]{2,1,0:T(8,128)}, u32[]{:S(2)}, u32[]{:S(2)}) collective-permute-start(f32[2,768,1024]{2,1,0:T(8,128)} %source_ref.11), channel_id=1, source_target_pairs={{0,8},{8,0},{16,24},{24,16},{1,9},{9,1},{17,25},{25,17},{2,10},{10... | collective-permute-start | bytes 18874376 | tf_op jit(solution)/shard_map/ppermute | solution.py:30
  2.7 2.8 %copy-start = (f32[2,768,1024]{2,1,0:T(8,128)S(1)}, f32[2,768,1024]{2,1,0:T(8,128)}, u32[]{:S(2)}) copy-start(f32[2,768,1024]{2,1,0:T(8,128)} %source_ref.11) | copy-start | bytes 18874372
  6.9 4.4 %slice-start = ((s8[6291456]{0:T(1024)(128)(4,1)}), s8[4194304]{0:T(1024)(128)(4,1)S(1)}, s32[]{:S(2)}) async-start(s8[6291456]{0:T(1024)(128)(4,1)} %bitcast.6), calls=%async_computation | async-start | bytes 8388608
  7.6 3.7 %slice-start.1 = ((s8[6291456]{0:T(1024)(128)(4,1)}), s8[2097152]{0:T(1024)(128)(4,1)S(1)}, s32[]{:S(2)}) async-start(s8[6291456]{0:T(1024)(128)(4,1)} %bitcast.6), calls=%async_computation.1 | async-start | bytes 4194304
  7.6 3.7 %copy-start.22 = (s32[2,2]{1,0:T(2,128)S(1)}, s32[2,2]{1,0:T(2,128)}, u32[]{:S(2)}) copy-start(s32[2,2]{1,0:T(2,128)} %plan_ref.25) | copy-start | bytes 52
  7.6 38.6 %collective-permute-start = (f32[1,392,1024]{2,1,0:T(8,128)S(1)}, f32[1,392,1024]{2,1,0:T(8,128)S(1)}, u32[]{:S(2)}, u32[]{:S(2)}) collective-permute-start(f32[1,392,1024]{2,1,0:T(8,128)S(1)} %shard_map.59.refs_0_), channel_id=1, source_target_pairs={{0,16},{16,0},{8,24},{24,8},{1,17},{17,1},{9,25},{25,9},{2,18},{18... | collective-permute-start | bytes 4816904 | tf_op jit(solution)/shard_map/ppermute | solution.py:30
  18.6 17.1 %collective-permute-start.2 = (f32[1,384,768]{2,1,0:T(8,128)S(1)}, f32[1,384,768]{2,1,0:T(8,128)S(1)}, u32[]{:S(2)}, u32[]{:S(2)}) collective-permute-start(f32[1,384,768]{2,1,0:T(8,128)S(1)} %get-tuple-element.32.token_ref), channel_id=1, source_target_pairs={{0,1},{1,0},{2,3},{3,2},{4,5},{5,4},{6,7},{7,6},{8,10},{9,11},{10,... | collective-permute-start | bytes 3538952 | tf_op jit(solution)/shard_map/ppermute | solution.py:44
  21.6 58.1 %collective-permute-start.8 = (f32[1,384,1024]{2,1,0:T(8,128)S(1)}, f32[1,384,1024]{2,1,0:T(8,128)S(1)}, u32[]{:S(2)}, u32[]{:S(2)}) collective-permute-start(f32[1,384,1024]{2,1,0:T(8,128)S(1)} %shard_map.60.token_ref), channel_id=1, source_target_pairs={{0,16},{16,0},{8,24},{24,8},{1,17},{17,1},{9,25},{25,9},{2,18},{18... | collective-permute-start | bytes 4718600 | tf_op jit(solution)/shard_map/ppermute | solution.py:30
  35.9 16.1 %collective-permute-start.4 = (f32[1,192,768]{2,1,0:T(8,128)S(1)}, f32[1,192,768]{2,1,0:T(8,128)S(1)}, u32[]{:S(2)}, u32[]{:S(2)}) collective-permute-start(f32[1,192,768]{2,1,0:T(8,128)S(1)} %get-tuple-element.33.token_ref), channel_id=1, source_target_pairs={{0,2},{1,3},{2,0},{3,1},{4,6},{5,7},{6,4},{7,5},{8,9},{9,8},{10,11... | collective-permute-start | bytes 1769480 | tf_op jit(solution)/shard_map/ppermute | solution.py:44
  46.2 94.5 %copy-start.3 = (f32[1,392,1024]{2,1,0:T(8,128)}, f32[1,392,1024]{2,1,0:T(8,128)S(1)}, u32[]{:S(2)}) copy-start(f32[1,392,1024]{2,1,0:T(8,128)S(1)} %collective-permute-done.refs_0_.theirs_ref) | copy-start | bytes 4816900
  50.0 9.9 %collective-permute-start.3 = (f32[1,384,384]{2,1,0:T(8,128)S(1)}, f32[1,384,384]{2,1,0:T(8,128)S(1)}, u32[]{:S(2)}, u32[]{:S(2)}) collective-permute-start(f32[1,384,384]{2,1,0:T(8,128)S(1)} %get-tuple-element.35.token_ref), channel_id=1, source_target_pairs={{0,1},{1,0},{2,3},{3,2},{4,5},{5,4},{6,7},{7,6},{8,10},{9,11},{10,... | collective-permute-start | bytes 1769480 | tf_op jit(solution)/shard_map/ppermute | solution.py:44
  52.0 14.7 %copy-start.24 = (f32[768]{0:T(1024)S(1)}, f32[768]{0:T(1024)}, u32[]{:S(2)}) copy-start(f32[768]{0:T(1024)} %refs_1_.1) | copy-start | bytes 9220
  52.1 15.5 %collective-permute-start.7 = (f32[1,96,768]{2,1,0:T(8,128)S(1)}, f32[1,96,768]{2,1,0:T(8,128)S(1)}, u32[]{:S(2)}, u32[]{:S(2)}) collective-permute-start(f32[1,96,768]{2,1,0:T(8,128)S(1)} %get-tuple-element.37.token_ref), channel_id=1, source_target_pairs={{0,4},{1,5},{2,6},{3,7},{4,0},{5,1},{6,2},{7,3},{8,12},{9,13},{10,... | collective-permute-start | bytes 884744 | tf_op jit(solution)/shard_map/ppermute | solution.py:44
  60.0 8.3 %collective-permute-start.5 = (f32[1,192,384]{2,1,0:T(8,128)S(1)}, f32[1,192,384]{2,1,0:T(8,128)S(1)}, u32[]{:S(2)}, u32[]{:S(2)}) collective-permute-start(f32[1,192,384]{2,1,0:T(8,128)S(1)} %get-tuple-element.39.token_ref), channel_id=1, source_target_pairs={{0,2},{1,3},{2,0},{3,1},{4,6},{5,7},{6,4},{7,5},{8,9},{9,8},{10,11... | collective-permute-start | bytes 884744 | tf_op jit(solution)/shard_map/ppermute | solution.py:44
  62.1 5.5 %collective-permute-start.6 = (f32[1,6]{1,0:T(1,128)S(1)}, f32[1,6]{1,0:T(1,128)S(1)}, u32[]{:S(2)}, u32[]{:S(2)}) collective-permute-start(f32[1,6]{1,0:T(1,128)S(1)} %maximum_bitcast_fusion.ours_ref), channel_id=1, source_target_pairs={{0,8},{8,0},{16,24},{24,16},{1,9},{9,1},{17,25},{25,17},{2,10},{10... | collective-permute-start | bytes 80 | tf_op jit(solution)/shard_map/ppermute | solution.py:30
  79.6 3.8 %copy-start.9 = (f32[1,384,1024]{2,1,0:T(8,128)}, f32[1,384,1024]{2,1,0:T(8,128)S(1)}, u32[]{:S(2)}) copy-start(f32[1,384,1024]{2,1,0:T(8,128)S(1)} %collective-permute-done.8.refs_0_.refs_1_) | copy-start | bytes 4718596
  83.5 32.1 %collective-permute-start.9 = (f32[1,384,384]{2,1,0:T(8,128)S(1)}, f32[1,384,384]{2,1,0:T(8,128)S(1)}, u32[]{:S(2)}, u32[]{:S(2)}) collective-permute-start(f32[1,384,384]{2,1,0:T(8,128)S(1)} %get-tuple-element.43.token_ref), channel_id=1, source_target_pairs={{0,1},{1,0},{2,3},{3,2},{4,5},{5,4},{6,7},{7,6},{8,10},{9,11},{10,... | collective-permute-start | bytes 1769480 | tf_op jit(solution)/shard_map/ppermute | solution.py:44
  85.3 22.8 %collective-permute-start.12 = (f32[1,96,768]{2,1,0:T(8,128)S(1)}, f32[1,96,768]{2,1,0:T(8,128)S(1)}, u32[]{:S(2)}, u32[]{:S(2)}) collective-permute-start(f32[1,96,768]{2,1,0:T(8,128)S(1)} %shard_map.66.token_ref.one_ref), channel_id=1, source_target_pairs={{0,4},{1,5},{2,6},{3,7},{4,0},{5,1},{6,2},{7,3},{8,12},{9,13},{10,... | collective-permute-start | bytes 884744 | tf_op jit(solution)/shard_map/ppermute | solution.py:44
  87.9 19.4 %collective-permute-start.10 = (f32[1,96,384]{2,1,0:T(8,128)S(1)}, f32[1,96,384]{2,1,0:T(8,128)S(1)}, u32[]{:S(2)}, u32[]{:S(2)}) collective-permute-start(f32[1,96,384]{2,1,0:T(8,128)S(1)} %get-tuple-element.41.token_ref), channel_id=1, source_target_pairs={{0,4},{1,5},{2,6},{3,7},{4,0},{5,1},{6,2},{7,3},{8,12},{9,13},{10,... | collective-permute-start | bytes 442376 | tf_op jit(solution)/shard_map/ppermute | solution.py:44
  108.1 14.4 %collective-permute-start.16 = (f32[1,192,768]{2,1,0:T(8,128)S(1)}, f32[1,192,768]{2,1,0:T(8,128)S(1)}, u32[]{:S(2)}, u32[]{:S(2)}) collective-permute-start(f32[1,192,768]{2,1,0:T(8,128)S(1)} %shard_map.70.token_ref.one_ref), channel_id=1, source_target_pairs={{0,2},{1,3},{2,0},{3,1},{4,6},{5,7},{6,4},{7,5},{8,9},{9,8},{10,11... | collective-permute-start | bytes 1769480 | tf_op jit(solution)/shard_map/ppermute | solution.py:44
  108.2 6.8 %collective-permute-start.11 = (f32[1,96,384]{2,1,0:T(8,128)S(1)}, f32[1,96,384]{2,1,0:T(8,128)S(1)}, u32[]{:S(2)}, u32[]{:S(2)}) collective-permute-start(f32[1,96,384]{2,1,0:T(8,128)S(1)} %shard_map.69.token_ref.one_ref), channel_id=1, source_target_pairs={{0,16},{16,0},{8,24},{24,8},{1,17},{17,1},{9,25},{25,9},{2,18},{18... | collective-permute-start | bytes 442376 | tf_op jit(solution)/shard_map/ppermute | solution.py:30
  115.7 6.8 %collective-permute-start.13 = (f32[1,192,384]{2,1,0:T(8,128)S(1)}, f32[1,192,384]{2,1,0:T(8,128)S(1)}, u32[]{:S(2)}, u32[]{:S(2)}) collective-permute-start(f32[1,192,384]{2,1,0:T(8,128)S(1)} %get-tuple-element.46.token_ref), channel_id=1, source_target_pairs={{0,2},{1,3},{2,0},{3,1},{4,6},{5,7},{6,4},{7,5},{8,9},{9,8},{10,11... | collective-permute-start | bytes 884744 | tf_op jit(solution)/shard_map/ppermute | solution.py:44
  122.6 35.0 %collective-permute-start.22 = (f32[1,384,768]{2,1,0:T(8,128)S(1)}, f32[1,384,768]{2,1,0:T(8,128)S(1)}, u32[]{:S(2)}, u32[]{:S(2)}) collective-permute-start(f32[1,384,768]{2,1,0:T(8,128)S(1)} %shard_map.75.token_ref.one_ref), channel_id=1, source_target_pairs={{0,1},{1,0},{2,3},{3,2},{4,5},{5,4},{6,7},{7,6},{8,10},{9,11},{10,... | collective-permute-start | bytes 3538952 | tf_op jit(solution)/shard_map/ppermute | solution.py:44
  123.0 19.4 %collective-permute-start.18 = (f32[1,768,256]{2,1,0:T(8,128)S(1)}, f32[1,768,256]{2,1,0:T(8,128)S(1)}, u32[]{:S(2)}, u32[]{:S(2)}) collective-permute-start(f32[1,768,256]{2,1,0:T(8,128)S(1)} %shard_map.72.token_ref), channel_id=1, source_target_pairs={{0,16},{16,0},{8,24},{24,8},{1,17},{17,1},{9,25},{25,9},{2,18},{18... | collective-permute-start | bytes 2359304 | tf_op jit(solution)/shard_map/ppermute | solution.py:30
  124.4 14.2 %collective-permute-start.15 = (f32[2,96,384]{2,1,0:T(8,128)S(1)}, f32[2,96,384]{2,1,0:T(8,128)S(1)}, u32[]{:S(2)}, u32[]{:S(2)}) collective-permute-start(f32[2,96,384]{2,1,0:T(8,128)S(1)} %shard_map.71.refs_0_.one_ref), channel_id=1, source_target_pairs={{0,4},{1,5},{2,6},{3,7},{4,0},{5,1},{6,2},{7,3},{8,12},{9,13},{10,... | collective-permute-start | bytes 884744 | tf_op jit(solution)/shard_map/ppermute | solution.py:44
  128.0 12.7 %collective-permute-start.14 = (f32[1,96,384]{2,1,0:T(8,128)S(1)}, f32[1,96,384]{2,1,0:T(8,128)S(1)}, u32[]{:S(2)}, u32[]{:S(2)}) collective-permute-start(f32[1,96,384]{2,1,0:T(8,128)S(1)} %get-tuple-element.48.token_ref), channel_id=1, source_target_pairs={{0,4},{1,5},{2,6},{3,7},{4,0},{5,1},{6,2},{7,3},{8,12},{9,13},{10,... | collective-permute-start | bytes 442376 | tf_op jit(solution)/shard_map/ppermute | solution.py:44
  138.7 14.9 %collective-permute-start.20 = (f32[2,192,384]{2,1,0:T(8,128)S(1)}, f32[2,192,384]{2,1,0:T(8,128)S(1)}, u32[]{:S(2)}, u32[]{:S(2)}) collective-permute-start(f32[2,192,384]{2,1,0:T(8,128)S(1)} %shard_map.76.token_ref.one_ref), channel_id=1, source_target_pairs={{0,2},{1,3},{2,0},{3,1},{4,6},{5,7},{6,4},{7,5},{8,9},{9,8},{10,11... | collective-permute-start | bytes 1769480 | tf_op jit(solution)/shard_map/ppermute | solution.py:44
  141.5 5.2 %collective-permute-start.17 = (f32[1,96,384]{2,1,0:T(8,128)S(1)}, f32[1,96,384]{2,1,0:T(8,128)S(1)}, u32[]{:S(2)}, u32[]{:S(2)}) collective-permute-start(f32[1,96,384]{2,1,0:T(8,128)S(1)} %shard_map.77.refs_0_.one_ref), channel_id=1, source_target_pairs={{0,16},{16,0},{8,24},{24,8},{1,17},{17,1},{9,25},{25,9},{2,18},{18... | collective-permute-start | bytes 442376 | tf_op jit(solution)/shard_map/ppermute | solution.py:30
  146.7 10.8 %collective-permute-start.19 = (f32[2,96,384]{2,1,0:T(8,128)S(1)}, f32[2,96,384]{2,1,0:T(8,128)S(1)}, u32[]{:S(2)}, u32[]{:S(2)}) collective-permute-start(f32[2,96,384]{2,1,0:T(8,128)S(1)} %shard_map.79.refs_0_.one_ref), channel_id=1, source_target_pairs={{0,4},{1,5},{2,6},{3,7},{4,0},{5,1},{6,2},{7,3},{8,12},{9,13},{10,... | collective-permute-start | bytes 884744 | tf_op jit(solution)/shard_map/ppermute | solution.py:44
  157.8 11.0 %collective-permute-start.23 = (f32[1,768,768]{2,1,0:T(8,128)S(1)}, f32[1,768,768]{2,1,0:T(8,128)S(1)}, u32[]{:S(2)}, u32[]{:S(2)}) collective-permute-start(f32[1,768,768]{2,1,0:T(8,128)S(1)} %shard_map.83.refs_0_), channel_id=1, source_target_pairs={{0,8},{8,0},{16,24},{24,16},{1,9},{9,1},{17,25},{25,17},{2,10},{10... | collective-permute-start | bytes 7077896 | tf_op jit(solution)/shard_map/ppermute | solution.py:30
  164.6 21.6 %collective-permute-start.24 = (f32[1,768,256]{2,1,0:T(8,128)}, f32[1,768,256]{2,1,0:T(8,128)S(1)}, u32[]{:S(2)}, u32[]{:S(2)}) collective-permute-start(f32[1,768,256]{2,1,0:T(8,128)} %shard_map.80.token_ref), channel_id=1, source_target_pairs={{0,16},{16,0},{8,24},{24,8},{1,17},{17,1},{9,25},{25,9},{2,18},{18... | collective-permute-start | bytes 2359304 | tf_op jit(solution)/shard_map/ppermute | solution.py:30
  165.9 21.2 %collective-permute-start.21 = (f32[2,192,384]{2,1,0:T(8,128)S(1)}, f32[2,192,384]{2,1,0:T(8,128)S(1)}, u32[]{:S(2)}, u32[]{:S(2)}) collective-permute-start(f32[2,192,384]{2,1,0:T(8,128)S(1)} %shard_map.82.token_ref.one_ref), channel_id=1, source_target_pairs={{0,2},{1,3},{2,0},{3,1},{4,6},{5,7},{6,4},{7,5},{8,9},{9,8},{10,11... | collective-permute-start | bytes 1769480 | tf_op jit(solution)/shard_map/ppermute | solution.py:44
  165.9 24.9 %collective-permute-start.26 = (f32[2,384,384]{2,1,0:T(8,128)S(1)}, f32[2,384,384]{2,1,0:T(8,128)}, u32[]{:S(2)}, u32[]{:S(2)}) collective-permute-start(f32[2,384,384]{2,1,0:T(8,128)S(1)} %shard_map.81.token_ref.one_ref), channel_id=1, source_target_pairs={{0,1},{1,0},{2,3},{3,2},{4,5},{5,4},{6,7},{7,6},{8,10},{9,11},{10,... | collective-permute-start | bytes 3538952 | tf_op jit(solution)/shard_map/ppermute | solution.py:44
  176.3 9.9 %copy-start.17 = (f32[96,768]{1,0:T(8,128)}, f32[96,768]{1,0:T(8,128)S(1)}, u32[]{:S(2)}) copy-start(f32[96,768]{1,0:T(8,128)S(1)} %get-tuple-element.50.token_ref) | copy-start | bytes 884740
  176.3 2.4 copy-start.7
  189.1 21.5 %collective-permute-start.25 = (f32[2,384,384]{2,1,0:T(8,128)S(1)}, f32[2,384,384]{2,1,0:T(8,128)}, u32[]{:S(2)}, u32[]{:S(2)}) collective-permute-start(f32[2,384,384]{2,1,0:T(8,128)S(1)} %shard_map.88.token_ref.one_ref), channel_id=1, source_target_pairs={{0,1},{1,0},{2,3},{3,2},{4,5},{5,4},{6,7},{7,6},{8,10},{9,11},{10,... | collective-permute-start | bytes 3538952 | tf_op jit(solution)/shard_map/ppermute | solution.py:44
  189.9 20.8 %collective-permute-start.27 = (f32[1,768,256]{2,1,0:T(8,128)}, f32[1,768,256]{2,1,0:T(8,128)}, u32[]{:S(2)}, u32[]{:S(2)}) collective-permute-start(f32[1,768,256]{2,1,0:T(8,128)} %shard_map.84.token_ref), channel_id=1, source_target_pairs={{0,16},{16,0},{8,24},{24,8},{1,17},{17,1},{9,25},{25,9},{2,18},{18... | collective-permute-start | bytes 2359304 | tf_op jit(solution)/shard_map/ppermute | solution.py:30
  193.8 33.7 %collective-permute-start.28 = (f32[1,768,256]{2,1,0:T(8,128)}, f32[1,768,256]{2,1,0:T(8,128)}, u32[]{:S(2)}, u32[]{:S(2)}) collective-permute-start(f32[1,768,256]{2,1,0:T(8,128)} %shard_map.90.token_ref), channel_id=1, source_target_pairs={{0,16},{16,0},{8,24},{24,8},{1,17},{17,1},{9,25},{25,9},{2,18},{18... | collective-permute-start | bytes 2359304 | tf_op jit(solution)/shard_map/ppermute | solution.py:30
  215.1 4.5 %copy-start.18 = (f32[96,768]{1,0:T(8,128)S(1)}, f32[96,768]{1,0:T(8,128)}, u32[]{:S(2)}) copy-start(f32[96,768]{1,0:T(8,128)} %copy-done.17) | copy-start | bytes 884740
  219.6 7.9 %copy-start.4 = (f32[1,392,1024]{2,1,0:T(8,128)S(1)}, f32[1,392,1024]{2,1,0:T(8,128)}, u32[]{:S(2)}) copy-start(f32[1,392,1024]{2,1,0:T(8,128)} %copy-done.3) | copy-start | bytes 4816900
  219.7 7.9 %copy-start.25 = (f32[96,768]{1,0:T(8,128)}, f32[96,768]{1,0:T(8,128)S(1)}, u32[]{:S(2)}) copy-start(f32[96,768]{1,0:T(8,128)S(1)} %add.44) | copy-start | bytes 884740
  219.7 20.1 %collective-permute-start.29 = (f32[96,384]{1,0:T(8,128)S(1)}, f32[96,384]{1,0:T(8,128)S(1)}, u32[]{:S(2)}, u32[]{:S(2)}) collective-permute-start(f32[96,384]{1,0:T(8,128)S(1)} %constant_dynamic-slice_fusion.1), channel_id=1, source_target_pairs={{0,16},{16,0},{8,24},{24,8},{1,17},{17,1},{9,25},{25,9},{2,18},{18... | collective-permute-start | bytes 442376 | tf_op jit(solution)/shard_map/ppermute | solution.py:30
  227.5 2.3 copy-start.5
  231.3 8.6 %copy-start.26 = (f32[96,768]{1,0:T(8,128)S(1)}, f32[96,768]{1,0:T(8,128)}, u32[]{:S(2)}) copy-start(f32[96,768]{1,0:T(8,128)} %copy-done.25) | copy-start | bytes 884740
  231.3 8.8 %copy-start.12 = (f32[1,768,256]{2,1,0:T(8,128)S(1)}, f32[1,768,256]{2,1,0:T(8,128)}, u32[]{:S(2)}) copy-start(f32[1,768,256]{2,1,0:T(8,128)} %copy-done.11) | copy-start | bytes 2359300
  231.3 8.8 %copy-start.14 = (f32[1,768,256]{2,1,0:T(8,128)S(1)}, f32[1,768,256]{2,1,0:T(8,128)}, u32[]{:S(2)}) copy-start(f32[1,768,256]{2,1,0:T(8,128)} %copy-done.13) | copy-start | bytes 2359300
  240.0 10.5 %collective-permute-start.30 = (f32[96,192]{1,0:T(8,128)S(1)}, f32[96,192]{1,0:T(8,128)S(1)}, u32[]{:S(2)}, u32[]{:S(2)}) collective-permute-start(f32[96,192]{1,0:T(8,128)S(1)} %constant_dynamic-slice_fusion), channel_id=1, source_target_pairs={{0,8},{8,0},{16,24},{24,16},{1,9},{9,1},{17,25},{25,17},{2,10},{10... | collective-permute-start | bytes 221192 | tf_op jit(solution)/shard_map/ppermute | solution.py:30
  240.1 2.3 copy-start.6
  (12 other events, 14.9 us)
